TPU v7x, 32 devices: a whole 2x2x4 slice. The times are simulated.
32 devices in a mesh: section: 4 (over y, core), dp: 8 (over z, x).
Axes of the slice: x: 2, y: 2, z: 4, core: 2. Of those that a mesh axis runs over, the one named last changes fastest.
Arguments:
- tokens: bfloat16 [16, 280, 768], P('dp'), may hold values from -6 to 6
- lengths: int32 [16], P('dp'), may hold values from 5 to 40, as said below
- cotangent: bfloat16 [16, 280, 768], P('dp'), may hold values from -6 to 6
- attend_gain: float32 [4, 768], P('section', 'dp'), may hold values from 0.1 to 1.9
- attend_shift: float32 [4, 768], P('section', 'dp'), may hold values from -1.75 to 1.75
- joint_weight: float32 [4, 768, 2304], P('section', 'dp'), may hold values from -0.21875 to 0.21875
- joint_bias: float32 [4, 1536], P('section', 'dp'), may hold values from -3 to 3
- output_weight: float32 [4, 768, 768], P('section', 'dp'), may hold values from -1.25 to 1.25
- output_bias: float32 [4, 768], P('section', 'dp'), may hold values from -1.75 to 1.75
- feed_gain: float32 [4, 768], P('section', 'dp'), may hold values from 0.1 to 1.9
- feed_shift: float32 [4, 768], P('section', 'dp'), may hold values from -1.75 to 1.75
- up_weight: float32 [4, 768, 3072], P('section', 'dp'), may hold values from -0.21875 to 0.21875
- up_bias: float32 [4, 3072], P('section', 'dp'), may hold values from -3 to 3
- down_weight: float32 [4, 3072, 768], P('section', 'dp'), may hold values from -0.109375 to 0.109375
- down_bias: float32 [4, 768], P('section', 'dp'), may hold values from -1.75 to 1.75
Outputs:
- outputs: bfloat16 [16, 280, 768], P('dp', None, 'section')
- token_grad: bfloat16 [16, 280, 768], P('dp', None, 'section')
- grad_attend_gain: float32 [4, 768], P('section', 'dp')
- grad_attend_shift: float32 [4, 768], P('section', 'dp')
- grad_joint_weight: float32 [4, 768, 2304], P('section', 'dp')
- grad_joint_bias: float32 [4, 1536], P('section', 'dp')
- grad_output_weight: float32 [4, 768, 768], P('section', 'dp')
- grad_output_bias: float32 [4, 768], P('section', 'dp')
- grad_feed_gain: float32 [4, 768], P('section', 'dp')
- grad_feed_shift: float32 [4, 768], P('section', 'dp')
- grad_up_weight: float32 [4, 768, 3072], P('section', 'dp')
- grad_up_bias: float32 [4, 3072], P('section', 'dp')
- grad_down_weight: float32 [4, 3072, 768], P('section', 'dp')
- grad_down_bias: float32 [4, 768], P('section', 'dp')
Inputs may be any that keep to these rules, and one draw needn't show every extreme that they name: `lengths`: in every draw some pair has a caption of exactly 40 rows and some pair one of exactly the least length.
All inputs are finite; a program needn't handle non-finite values.
Results may differ from a plain program's by a relative error of at most 0.015.
Values may be sent and summed in bfloat16 or wider, within the bound.
No kernel may reach another device: no remote copies, remote signals or barrier semaphores. Data moves between devices by JAX's collectives and lax.ppermute only.
A program may use at most 320 MiB of HBM per device.

v0:
```python
import jax
import jax.numpy as jnp
from jax import lax
from jax.sharding import PartitionSpec as P

HEADS = 12
FF = 3072
CAPTION = 40
MICRO = 2


def from_behind(value, axis, by):
    peers = lax.axis_size(axis)
    pairs = [(i, i + by) for i in range(peers) if 0 <= i + by < peers]
    return lax.ppermute(value, axis, pairs)


def normalize(stream, gain, shift):
    average = jnp.mean(stream, axis=-1, keepdims=True)
    centered = stream - average
    spread = jnp.mean(centered * centered, axis=-1, keepdims=True)
    return centered * lax.rsqrt(spread + 1e-06) * gain + shift


def gelu_exact(entries):
    return jax.nn.gelu(entries, approximate=False)


def key_valid(lengths, seq_len):
    places = lax.broadcasted_iota(jnp.int32, (lengths.shape[0], seq_len), 1)
    return (places < lengths[:, None]) | (places >= CAPTION)


def unpack(gathered):
    return tuple((item[0] if item.ndim == 3 else item[0].astype(jnp.float32) for item in gathered))


def split_heads(joined, model_width):
    pair_count, seq_len = (joined.shape[0], joined.shape[1])
    shaped = joined.reshape(pair_count, seq_len, 3, HEADS, model_width // HEADS)
    return (shaped[:, :, 0], shaped[:, :, 1], shaped[:, :, 2])


def blank_saved(per_micro, seq_len, model_width):
    return (
        jnp.zeros((per_micro, seq_len, model_width), jnp.float32),
        jnp.zeros((per_micro, seq_len, 3 * model_width), jnp.bfloat16),
        jnp.zeros((per_micro, HEADS, seq_len), jnp.float32),
        jnp.zeros((per_micro, seq_len, model_width), jnp.bfloat16),
        jnp.zeros((per_micro, seq_len, model_width), jnp.float32),
        jnp.zeros((per_micro, seq_len, FF), jnp.float32),
        jnp.zeros((per_micro, seq_len, FF), jnp.bfloat16),
    )


def place(buffer, item, slot, live):
    previous = lax.dynamic_index_in_dim(buffer, slot, 0, False)
    return lax.dynamic_update_index_in_dim(buffer, jnp.where(live, item, previous), slot, 0)


def forward_part(stream, usable, params):
    (
        attend_gain,
        attend_shift,
        joint_weight,
        joint_bias,
        output_weight,
        output_bias,
        feed_gain,
        feed_shift,
        up_weight,
        up_bias,
        down_weight,
        down_bias,
    ) = params
    pair_count, seq_len, model_width = stream.shape
    factor = (model_width // HEADS) ** (-0.5)
    normed = normalize(stream, attend_gain, attend_shift).astype(jnp.bfloat16)
    bias_full = jnp.concatenate(
        [joint_bias[:model_width], jnp.zeros((model_width,), jnp.float32), joint_bias[model_width:]]
    )
    joined = (
        jnp.einsum("psd,df->psf", normed, joint_weight, preferred_element_type=jnp.float32)
        + bias_full
    ).astype(jnp.bfloat16)
    query_rows, key_rows, value_rows = split_heads(joined, model_width)
    scores = (
        jnp.einsum("pqhe,pkhe->phqk", query_rows, key_rows, preferred_element_type=jnp.float32)
        * factor
    )
    scores = jnp.where(usable[:, None, None, :], scores, -1e30)
    highest = jnp.max(scores, axis=-1, keepdims=True)
    raised = jnp.exp(scores - highest)
    summed = jnp.sum(raised, axis=-1, keepdims=True)
    weights_soft = (raised / summed).astype(jnp.bfloat16)
    context = jnp.einsum(
        "phqk,pkhe->pqhe", weights_soft, value_rows, preferred_element_type=jnp.float32
    )
    context = context.reshape(pair_count, seq_len, model_width).astype(jnp.bfloat16)
    middle = (
        stream
        + jnp.einsum("psd,de->pse", context, output_weight, preferred_element_type=jnp.float32)
        + output_bias
    )
    normed_two = normalize(middle, feed_gain, feed_shift).astype(jnp.bfloat16)
    hidden = (
        jnp.einsum("psd,df->psf", normed_two, up_weight, preferred_element_type=jnp.float32)
        + up_bias
    )
    activated = gelu_exact(hidden).astype(jnp.bfloat16)
    leaving = (
        middle
        + jnp.einsum("psf,fd->psd", activated, down_weight, preferred_element_type=jnp.float32)
        + down_bias
    )
    logsum = (highest + jnp.log(summed))[..., 0]
    return (leaving, (stream, joined, logsum, context, middle, hidden, activated))


def backward_part(upstream, saved, usable, params):
    (
        attend_gain,
        attend_shift,
        joint_weight,
        joint_bias,
        output_weight,
        output_bias,
        feed_gain,
        feed_shift,
        up_weight,
        up_bias,
        down_weight,
        down_bias,
    ) = params
    stream, joined, logsum, context, middle, hidden, activated = saved
    pair_count, seq_len, model_width = stream.shape
    factor = (model_width // HEADS) ** (-0.5)
    branch_two = upstream.astype(jnp.bfloat16)
    grad_down_weight = jnp.einsum(
        "psf,psd->fd", activated, branch_two, preferred_element_type=jnp.float32
    )
    grad_down_bias = jnp.sum(branch_two.astype(jnp.float32), axis=(0, 1))
    d_activated = jnp.einsum(
        "psd,fd->psf", branch_two, down_weight, preferred_element_type=jnp.float32
    )
    gelu_pull = jax.vjp(gelu_exact, hidden)[1]
    d_hidden = gelu_pull(d_activated)[0].astype(jnp.bfloat16)
    normed_two, feed_pull = jax.vjp(normalize, middle, feed_gain, feed_shift)
    grad_up_weight = jnp.einsum(
        "psd,psf->df", normed_two.astype(jnp.bfloat16), d_hidden, preferred_element_type=jnp.float32
    )
    grad_up_bias = jnp.sum(d_hidden.astype(jnp.float32), axis=(0, 1))
    d_normed_two = jnp.einsum(
        "psf,df->psd", d_hidden, up_weight, preferred_element_type=jnp.float32
    )
    d_middle, grad_feed_gain, grad_feed_shift = feed_pull(d_normed_two)
    d_middle = d_middle + upstream
    branch_one = d_middle.astype(jnp.bfloat16)
    grad_output_weight = jnp.einsum(
        "psd,pse->de", context, branch_one, preferred_element_type=jnp.float32
    )
    grad_output_bias = jnp.sum(branch_one.astype(jnp.float32), axis=(0, 1))
    d_context = jnp.einsum(
        "pse,de->psd", branch_one, output_weight, preferred_element_type=jnp.float32
    ).astype(jnp.bfloat16)
    d_context = d_context.reshape(pair_count, seq_len, HEADS, model_width // HEADS)
    query_rows, key_rows, value_rows = split_heads(joined, model_width)
    scores = (
        jnp.einsum("pqhe,pkhe->phqk", query_rows, key_rows, preferred_element_type=jnp.float32)
        * factor
    )
    weights_soft = jnp.where(usable[:, None, None, :], jnp.exp(scores - logsum[..., None]), 0.0)
    d_value = jnp.einsum(
        "phqk,pqhe->pkhe",
        weights_soft.astype(jnp.bfloat16),
        d_context,
        preferred_element_type=jnp.float32,
    )
    d_weights = jnp.einsum(
        "pqhe,pkhe->phqk", d_context, value_rows, preferred_element_type=jnp.float32
    )
    inner = jnp.sum(weights_soft * d_weights, axis=-1, keepdims=True)
    d_scores = (weights_soft * (d_weights - inner)).astype(jnp.bfloat16)
    d_query = (
        jnp.einsum("phqk,pkhe->pqhe", d_scores, key_rows, preferred_element_type=jnp.float32)
        * factor
    )
    d_key = (
        jnp.einsum("phqk,pqhe->pkhe", d_scores, query_rows, preferred_element_type=jnp.float32)
        * factor
    )
    d_joined = (
        jnp.stack([d_query, d_key, d_value], axis=2)
        .reshape(pair_count, seq_len, 3 * model_width)
        .astype(jnp.bfloat16)
    )
    normed, attend_pull = jax.vjp(normalize, stream, attend_gain, attend_shift)
    grad_joint_weight = jnp.einsum(
        "psd,psf->df", normed.astype(jnp.bfloat16), d_joined, preferred_element_type=jnp.float32
    )
    joint_sums = jnp.sum(d_joined.astype(jnp.float32), axis=(0, 1))
    grad_joint_bias = jnp.concatenate([joint_sums[:model_width], joint_sums[2 * model_width :]])
    d_normed = jnp.einsum("psf,df->psd", d_joined, joint_weight, preferred_element_type=jnp.float32)
    d_stream, grad_attend_gain, grad_attend_shift = attend_pull(d_normed)
    d_stream = d_stream + d_middle
    grads = (
        grad_attend_gain,
        grad_attend_shift,
        grad_joint_weight,
        grad_joint_bias,
        grad_output_weight,
        grad_output_bias,
        grad_feed_gain,
        grad_feed_shift,
        grad_up_weight,
        grad_up_bias,
        grad_down_weight,
        grad_down_bias,
    )
    return (d_stream, tuple((item[None] for item in grads)))


def shards(
    tokens,
    lengths,
    cotangent,
    attend_gain,
    attend_shift,
    joint_weight,
    joint_bias,
    output_weight,
    output_bias,
    feed_gain,
    feed_shift,
    up_weight,
    up_bias,
    down_weight,
    down_bias,
):
    section_count = lax.axis_size("section")
    section_index = lax.axis_index("section")
    pair_count, seq_len, model_width = tokens.shape
    per_micro = pair_count // MICRO
    shaped = (MICRO, per_micro, seq_len, model_width)
    token_blocks = tokens.reshape(shaped)
    cotangent_blocks = cotangent.reshape(shaped)
    usable_blocks = key_valid(lengths, seq_len).reshape(MICRO, per_micro, seq_len)
    params = unpack(
        (
            lax.all_gather(attend_gain.astype(jnp.bfloat16), "dp", axis=1, tiled=True),
            lax.all_gather(attend_shift.astype(jnp.bfloat16), "dp", axis=1, tiled=True),
            lax.all_gather(joint_weight.astype(jnp.bfloat16), "dp", axis=1, tiled=True),
            lax.all_gather(joint_bias.astype(jnp.bfloat16), "dp", axis=1, tiled=True),
            lax.all_gather(output_weight.astype(jnp.bfloat16), "dp", axis=1, tiled=True),
            lax.all_gather(output_bias.astype(jnp.bfloat16), "dp", axis=1, tiled=True),
            lax.all_gather(feed_gain.astype(jnp.bfloat16), "dp", axis=1, tiled=True),
            lax.all_gather(feed_shift.astype(jnp.bfloat16), "dp", axis=1, tiled=True),
            lax.all_gather(up_weight.astype(jnp.bfloat16), "dp", axis=1, tiled=True),
            lax.all_gather(up_bias.astype(jnp.bfloat16), "dp", axis=1, tiled=True),
            lax.all_gather(down_weight.astype(jnp.bfloat16), "dp", axis=1, tiled=True),
            lax.all_gather(down_bias.astype(jnp.bfloat16), "dp", axis=1, tiled=True),
        )
    )
    kept_blank = blank_saved(per_micro, seq_len, model_width)
    row_blank = jnp.zeros(shaped[1:], jnp.float32)
    buffers = tuple((jnp.zeros((MICRO,) + item.shape, item.dtype) for item in kept_blank))
    finals = jnp.zeros(shaped, jnp.float32)
    arriving = jnp.zeros(shaped[1:], jnp.bfloat16)
    sweeps = MICRO + section_count - 1
    for clock in range(sweeps):
        index = clock - section_index
        live = (index >= 0) & (index < MICRO)
        slot = jnp.clip(index, 0, MICRO - 1)
        first_rows = lax.dynamic_index_in_dim(token_blocks, slot, 0, False)
        source = jnp.where(section_index == 0, first_rows, arriving).astype(jnp.float32)
        usable = lax.dynamic_index_in_dim(usable_blocks, slot, 0, False)
        leaving, saved = lax.cond(
            live, forward_part, lambda *rest: (row_blank, kept_blank), source, usable, params
        )
        buffers = tuple((place(buffer, item, slot, live) for buffer, item in zip(buffers, saved)))
        finals = place(finals, leaving, slot, live)
        if clock + 1 < sweeps:
            arriving = from_behind(leaving.astype(jnp.bfloat16), "section", 1)
    back_params = unpack(
        (
            lax.all_gather(attend_gain.astype(jnp.bfloat16), "dp", axis=1, tiled=True),
            lax.all_gather(attend_shift.astype(jnp.bfloat16), "dp", axis=1, tiled=True),
            lax.all_gather(joint_weight.astype(jnp.bfloat16), "dp", axis=1, tiled=True),
            lax.all_gather(joint_bias.astype(jnp.bfloat16), "dp", axis=1, tiled=True),
            lax.all_gather(output_weight.astype(jnp.bfloat16), "dp", axis=1, tiled=True),
            lax.all_gather(output_bias.astype(jnp.bfloat16), "dp", axis=1, tiled=True),
            lax.all_gather(feed_gain.astype(jnp.bfloat16), "dp", axis=1, tiled=True),
            lax.all_gather(feed_shift.astype(jnp.bfloat16), "dp", axis=1, tiled=True),
            lax.all_gather(up_weight.astype(jnp.bfloat16), "dp", axis=1, tiled=True),
            lax.all_gather(up_bias.astype(jnp.bfloat16), "dp", axis=1, tiled=True),
            lax.all_gather(down_weight.astype(jnp.bfloat16), "dp", axis=1, tiled=True),
            lax.all_gather(down_bias.astype(jnp.bfloat16), "dp", axis=1, tiled=True),
        )
    )
    totals = tuple((jnp.zeros((1,) + item.shape, jnp.float32) for item in back_params))

    def step_back(upstream, saved, usable, running):
        d_stream, grads = backward_part(upstream, saved, usable, back_params)
        return (d_stream, tuple((total + grad for total, grad in zip(running, grads))))

    def step_spare(upstream, saved, usable, running):
        return (row_blank, running)

    input_grads = jnp.zeros(shaped, jnp.float32)
    returning = jnp.zeros(shaped[1:], jnp.bfloat16)
    for clock in range(sweeps):
        index = clock - (section_count - 1 - section_index)
        live = (index >= 0) & (index < MICRO)
        slot = jnp.clip(index, 0, MICRO - 1)
        last_rows = lax.dynamic_index_in_dim(cotangent_blocks, slot, 0, False)
        upstream = jnp.where(section_index == section_count - 1, last_rows, returning).astype(
            jnp.float32
        )
        saved = tuple((lax.dynamic_index_in_dim(buffer, slot, 0, False) for buffer in buffers))
        usable = lax.dynamic_index_in_dim(usable_blocks, slot, 0, False)
        d_stream, totals = lax.cond(live, step_back, step_spare, upstream, saved, usable, totals)
        input_grads = place(input_grads, d_stream, slot, live)
        if clock + 1 < sweeps:
            returning = from_behind(d_stream.astype(jnp.bfloat16), "section", -1)
    shares = (
        lax.psum_scatter(
            totals[0].astype(jnp.bfloat16), "dp", scatter_dimension=1, tiled=True
        ).astype(jnp.float32),
        lax.psum_scatter(
            totals[1].astype(jnp.bfloat16), "dp", scatter_dimension=1, tiled=True
        ).astype(jnp.float32),
        lax.psum_scatter(
            totals[2].astype(jnp.bfloat16), "dp", scatter_dimension=1, tiled=True
        ).astype(jnp.float32),
        lax.psum_scatter(
            totals[3].astype(jnp.bfloat16), "dp", scatter_dimension=1, tiled=True
        ).astype(jnp.float32),
        lax.psum_scatter(
            totals[4].astype(jnp.bfloat16), "dp", scatter_dimension=1, tiled=True
        ).astype(jnp.float32),
        lax.psum_scatter(
            totals[5].astype(jnp.bfloat16), "dp", scatter_dimension=1, tiled=True
        ).astype(jnp.float32),
        lax.psum_scatter(
            totals[6].astype(jnp.bfloat16), "dp", scatter_dimension=1, tiled=True
        ).astype(jnp.float32),
        lax.psum_scatter(
            totals[7].astype(jnp.bfloat16), "dp", scatter_dimension=1, tiled=True
        ).astype(jnp.float32),
        lax.psum_scatter(
            totals[8].astype(jnp.bfloat16), "dp", scatter_dimension=1, tiled=True
        ).astype(jnp.float32),
        lax.psum_scatter(
            totals[9].astype(jnp.bfloat16), "dp", scatter_dimension=1, tiled=True
        ).astype(jnp.float32),
        lax.psum_scatter(
            totals[10].astype(jnp.bfloat16), "dp", scatter_dimension=1, tiled=True
        ).astype(jnp.float32),
        lax.psum_scatter(
            totals[11].astype(jnp.bfloat16), "dp", scatter_dimension=1, tiled=True
        ).astype(jnp.float32),
    )
    out_term = jnp.where(section_index == section_count - 1, finals, 0.0).reshape(
        pair_count, seq_len, model_width
    )
    in_term = jnp.where(section_index == 0, input_grads, 0.0).reshape(
        pair_count, seq_len, model_width
    )
    out_pieces, in_pieces = (
        lax.all_to_all(
            out_term.astype(jnp.bfloat16)[None], "section", split_axis=3, concat_axis=0, tiled=True
        ),
        lax.all_to_all(
            in_term.astype(jnp.bfloat16)[None], "section", split_axis=3, concat_axis=0, tiled=True
        ),
    )
    outputs = out_pieces[section_count - 1]
    token_grad = in_pieces[0]
    return (outputs, token_grad) + tuple(shares)


def solution(mesh):
    return jax.shard_map(
        shards,
        mesh=mesh,
        in_specs=(
            P("dp", None, None),
            P("dp"),
            P("dp", None, None),
            P("section", "dp"),
            P("section", "dp"),
            P("section", "dp", None),
            P("section", "dp"),
            P("section", "dp", None),
            P("section", "dp"),
            P("section", "dp"),
            P("section", "dp"),
            P("section", "dp", None),
            P("section", "dp"),
            P("section", "dp", None),
            P("section", "dp"),
        ),
        out_specs=(
            P("dp", None, "section"),
            P("dp", None, "section"),
            P("section", "dp"),
            P("section", "dp"),
            P("section", "dp", None),
            P("section", "dp"),
            P("section", "dp", None),
            P("section", "dp"),
            P("section", "dp"),
            P("section", "dp"),
            P("section", "dp", None),
            P("section", "dp"),
            P("section", "dp", None),
            P("section", "dp"),
        ),
        check_vma=False,
    )
```

profile of v0, /device:TPU:0, one launch (start us, length us, event | category | flops | bytes accessed | tf_op | source)
XLA Modules:
  0.0 2312.9 jit_solution(16879791048445275437)
XLA Ops:
  19.4 39.1 %all-reduce.7 = (bf16[768]{0:T(1024)(128)(2,1)S(1)}, bf16[768]{0:T(1024)(128)(2,1)S(1)}, bf16[1536]{0:T(1024)(128)(2,1)S(1)}, bf16[768]{0:T(1024)(128)(2,1)S(1)}...) all-reduce(bf16[768]{0:T(1024)(128)(2,1)S(1)} %dynamic-update-slice, ...), channel_id=1, replica_groups=mesh['section'=4,'dp'=8] {'dp'}, use_global_device_ids=true, to_apply=%add | all-reduce | flops 6144 | bytes 24576
  58.6 26.1 %all_gather.53 = bf16[1,3072]{1,0:T(2,128)(2,1)S(1)} all-gather(bf16[1,384]{1,0:T(2,128)(2,1)S(1)} %convert_element_type.1170), channel_id=1, replica_groups=mesh['section'=4,'dp'=8] {'dp'}, dimensions={1}, use_global_device_ids=true | all-gather | bytes 6912 | tf_op jit(solution)/shard_map/all_gather | solution.py:259
  86.5 35.2 %all-gather.5.cloned.1.call-done = bf16[1,768,2304]{2,1,0:T(8,128)(2,1)} async-done(((bf16[1,96,2304]{2,1,0:T(8,128)(2,1)}), bf16[1,768,2304]{2,1,0:T(8,128)(2,1)}) %all-gather.5.cloned.1.call-update) | async-done | bytes 3538960 | tf_op jit(solution)/shard_map/all_gather | solution.py:252
  121.8 81.2 %all-gather.9.cloned.1.call-done = bf16[1,768,3072]{2,1,0:T(8,128)(2,1)} async-done(((bf16[1,96,3072]{2,1,0:T(8,128)(2,1)}), bf16[1,768,3072]{2,1,0:T(8,128)(2,1)}) %all-gather.9.cloned.1.call-update) | async-done | bytes 4718608 | tf_op jit(solution)/shard_map/all_gather | solution.py:258
  202.9 80.7 %all-gather.11.cloned.1.call-done = bf16[1,3072,768]{2,1,0:T(8,128)(2,1)} async-done(((bf16[1,384,768]{2,1,0:T(8,128)(2,1)}), bf16[1,3072,768]{2,1,0:T(8,128)(2,1)}) %all-gather.11.cloned.1.call-update) | async-done | bytes 4718608 | tf_op jit(solution)/shard_map/all_gather | solution.py:260
  283.6 34.6 %conditional.10 = (f32[1,280,768]{2,1,0:T(8,128)S(1)}, f32[1,280,768]{2,1,0:T(8,128)S(1)}, f32[1,12,280]{2,1,0:T(8,128)}, f32[1,280,768]{2,1,0:T(8,128)}, f32[1,...) conditional(s32[]{:T(128)} %convert_element_type.1147, ...), branch_computations={%region_0.1_spmd, %region_1.8_spmd} | conditional | flops 4278760192 | bytes 97017240 | solution.py:277
  297.5 12.2 fusion.5
  326.9 20.9 dynamic_update_slice.141
  355.4 15.0 dynamic_update_slice.161
  378.0 23.0 dynamic_update_slice.166
  443.1 45.8 %conditional.11 = (f32[1,280,768]{2,1,0:T(8,128)}, f32[1,280,768]{2,1,0:T(8,128)}, f32[1,12,280]{2,1,0:T(8,128)}, f32[1,280,768]{2,1,0:T(8,128)}, f32[1,280,3072...) conditional(s32[]{:T(128)} %convert_element_type.1177, ...), branch_computations={%region_8.9_spmd, %region_9.16_spmd} | conditional | flops 4278760192 | bytes 80319160 | solution.py:277
  466.7 12.3 fusion.39
  496.4 23.1 dynamic_update_slice.142
  538.2 20.9 dynamic_update_slice.162
  568.1 23.1 dynamic_update_slice.167
  629.9 15.9 conditional.12
  653.3 23.1 dynamic_update_slice.143
  693.7 20.9 dynamic_update_slice.163
  723.3 23.1 dynamic_update_slice.168
  793.4 10.4 collective-permute-start.3
  809.5 20.9 dynamic_update_slice.164
  844.0 23.1 dynamic_update_slice.169
  913.2 20.9 dynamic_update_slice.165
  940.8 23.1 dynamic_update_slice.170
  973.0 20.0 conditional.15
  1036.1 226.6 %collective-permute-done.6 = bf16[1,280,768]{2,1,0:T(8,128)(2,1)} collective-permute-done((bf16[1,280,768]{2,1,0:T(8,128)(2,1)}, bf16[1,280,768]{2,1,0:T(8,128)(2,1)}, u32[]{:S(2)}, u32[]{:S(2)}) %collective-permute-start.6) | collective-permute-done | bytes 430112 | tf_op jit(solution)/shard_map/ppermute | solution.py:15
  1264.8 88.0 %conditional.18 = (f32[1,280,768]{2,1,0:T(8,128)}, f32[1,768]{1,0:T(1,128)}, f32[1,768]{1,0:T(1,128)}, f32[1,768,2304]{2,1,0:T(8,128)}, f32[1,1536]{1,0:T(1,128)...) conditional(s32[]{:T(128)} %convert_element_type.1199, ...), branch_computations={%region_97.98_spmd, %region_98.116_spmd} | conditional | flops 8631179264 | bytes 240354976 | solution.py:321
  1278.3 12.6 convert_reduce_fusion.13
  1340.9 10.5 bitcast_add_fusion.14
  1366.7 83.4 %conditional.19 = (f32[1,768]{1,0:T(1,128)}, f32[1,768]{1,0:T(1,128)}, f32[1,768,2304]{2,1,0:T(8,128)}, f32[1,1536]{1,0:T(1,128)}, f32[1,768,768]{2,1,0:T(8,128)...) conditional(s32[]{:T(128)} %convert_element_type.1202, ...), branch_computations={%region_116.117_spmd, %region_117.135_spmd} | conditional | flops 8631180288 | bytes 233516896 | solution.py:321
  1380.7 12.4 convert_reduce_fusion.17
  1434.6 10.6 bitcast_add_fusion.20
  1488.3 15.0 dynamic_update_slice.144
  1512.7 15.0 dynamic_update_slice.145
  1538.7 20.9 dynamic_update_slice.181
  1566.8 20.9 dynamic_update_slice.182
  1594.9 20.9 dynamic_update_slice.183
  1624.3 20.9 dynamic_update_slice.184
  1649.1 20.9 dynamic_update_slice.185
  1684.3 17.6 reduce-scatter.45.cloned.1.call-done
  1703.2 62.0 %reduce-scatter.47.cloned.1.call-done = bf16[96,1]{1,0:T(8,128)(2,1)} async-done(((bf16[768,1]{1,0:T(8,128)(2,1)}), bf16[96,1]{1,0:T(8,128)(2,1)}) %reduce-scatter.47.cloned.1.call-update) | async-done | bytes 208
  1766.6 61.9 %reduce-scatter.51.cloned.1.call-done = bf16[96,1]{1,0:T(8,128)(2,1)} async-done(((bf16[768,1]{1,0:T(8,128)(2,1)}), bf16[96,1]{1,0:T(8,128)(2,1)}) %reduce-scatter.51.cloned.1.call-update) | async-done | bytes 208
  1829.8 62.4 %reduce-scatter.41.cloned.1.call-done = bf16[192,1]{1,0:T(8,128)(2,1)} async-done(((bf16[1536,1]{1,0:T(8,128)(2,1)}), bf16[192,1]{1,0:T(8,128)(2,1)}) %reduce-scatter.41.cloned.1.call-update) | async-done | bytes 400
  1893.7 63.2 %reduce-scatter.49.cloned.1.call-done = bf16[384,1]{1,0:T(8,128)(2,1)} async-done(((bf16[3072,1]{1,0:T(8,128)(2,1)}), bf16[384,1]{1,0:T(8,128)(2,1)}) %reduce-scatter.49.cloned.1.call-update) | async-done | bytes 784
  1962.7 61.2 %reduce-scatter.31.cloned.1.call-done = bf16[1,96,768]{2,1,0:T(8,128)(2,1)} async-done(((bf16[1,768,768]{2,1,0:T(8,128)(2,1)}), bf16[1,96,768]{2,1,0:T(8,128)(2,1)}) %reduce-scatter.31.cloned.1.call-update) | async-done | bytes 147472 | tf_op jit(solution)/shard_map/reduce_scatter | solution.py:338
  2025.5 80.4 %reduce-scatter.29.cloned.1.call-done = bf16[1,96,2304]{2,1,0:T(8,128)(2,1)} async-done(((bf16[1,768,2304]{2,1,0:T(8,128)(2,1)}), bf16[1,96,2304]{2,1,0:T(8,128)(2,1)}) %reduce-scatter.29.cloned.1.call-update) | async-done | bytes 442384 | tf_op jit(solution)/shard_map/reduce_scatter | solution.py:332
  2107.9 96.9 %reduce-scatter.33.cloned.1.call-done = bf16[1,96,3072]{2,1,0:T(8,128)(2,1)} async-done(((bf16[1,768,3072]{2,1,0:T(8,128)(2,1)}), bf16[1,96,3072]{2,1,0:T(8,128)(2,1)}) %reduce-scatter.33.cloned.1.call-update) | async-done | bytes 589840 | tf_op jit(solution)/shard_map/reduce_scatter | solution.py:350
  2207.0 97.0 %reduce-scatter.35.cloned.1.call-done = bf16[1,384,768]{2,1,0:T(8,128)(2,1)} async-done(((bf16[1,3072,768]{2,1,0:T(8,128)(2,1)}), bf16[1,384,768]{2,1,0:T(8,128)(2,1)}) %reduce-scatter.35.cloned.1.call-update) | async-done | bytes 589840 | tf_op jit(solution)/shard_map/reduce_scatter | solution.py:356
  (796 shorter events, 714.9 us)
Async XLA Ops:
  7.2 79.4 %all-gather.7.cloned.1.call-start = ((), (), s32[]{:S(2)}) async-start(), calls=%async_computation.15 | async-start | bytes 1327104 | tf_op jit(solution)/shard_map/all_gather | solution.py:254
  8.9 49.7 %copy-start.269 = (f32[1,384]{1,0:T(1,128)S(1)}, f32[1,384]{1,0:T(1,128)}, u32[]{:S(2)}) copy-start(f32[1,384]{1,0:T(1,128)} %param.47) | copy-start | bytes 4612
  8.9 76.5 %copy-start.57 = (bf16[2,280,768]{2,1,0:T(8,128)(2,1)S(1)}, bf16[2,280,768]{2,1,0:T(8,128)(2,1)}, u32[]{:S(2)}) copy-start(bf16[2,280,768]{2,1,0:T(8,128)(2,1)} %param.35) | copy-start | bytes 2580484
  9.0 112.8 %all-gather.5.cloned.1.call-start = ((), (), s32[]{:S(2)}) async-start(), calls=%async_computation.14 | async-start | bytes 3981312 | tf_op jit(solution)/shard_map/all_gather | solution.py:252
  11.1 74.4 %copy-start.62 = (bf16[2,280,768]{2,1,0:T(8,128)(2,1)S(1)}, bf16[2,280,768]{2,1,0:T(8,128)(2,1)}, u32[]{:S(2)}) copy-start(bf16[2,280,768]{2,1,0:T(8,128)(2,1)} %param.37) | copy-start | bytes 2580484
  11.1 75.3 %copy-start.270 = (s32[2]{0:T(128)S(1)}, s32[2]{0:T(128)}, u32[]{:S(2)}) copy-start(s32[2]{0:T(128)} %param.36) | copy-start | bytes 28
  11.2 191.8 %all-gather.9.cloned.1.call-start = ((), (), s32[]{:S(2)}) async-start(), calls=%async_computation.16 | async-start | bytes 5308416 | tf_op jit(solution)/shard_map/all_gather | solution.py:258
  13.4 270.2 %all-gather.11.cloned.1.call-start = ((), (), s32[]{:S(2)}) async-start(), calls=%async_computation.17 | async-start | bytes 5308416 | tf_op jit(solution)/shard_map/all_gather | solution.py:260
  15.7 1664.6 %reduce-scatter.37.cloned.1.call-start = ((), (), s32[]{:S(2)}) async-start(), calls=%async_computation.22 | async-start | bytes 221184
  58.6 225.0 %copy-start.178 = (f32[768]{0:T(1024)}, f32[768]{0:T(1024)S(1)}, u32[]{:S(2)}) copy-start(f32[768]{0:T(1024)S(1)} %convert_element_type.1240) | copy-start | bytes 9220
  58.6 225.0 %copy-start.118 = (f32[1536]{0:T(1024)}, f32[1536]{0:T(1024)S(1)}, u32[]{:S(2)}) copy-start(f32[1536]{0:T(1024)S(1)} %convert_element_type.1241) | copy-start | bytes 18436
  58.6 225.0 %copy-start.126 = (f32[768]{0:T(1024)}, f32[768]{0:T(1024)S(1)}, u32[]{:S(2)}) copy-start(f32[768]{0:T(1024)S(1)} %convert_element_type.1242) | copy-start | bytes 9220
  84.8 198.8 %copy-start.242 = (f32[1,3072]{1,0:T(1,128)}, f32[1,3072]{1,0:T(1,128)S(1)}, u32[]{:S(2)}) copy-start(f32[1,3072]{1,0:T(1,128)S(1)} %convert_element_type.1237) | copy-start | bytes 36868
  296.4 13.2 copy-start.80
  296.4 13.2 slice-start.20
  324.0 118.1 %collective-permute-start = (bf16[1,280,768]{2,1,0:T(8,128)(2,1)}, bf16[1,280,768]{2,1,0:T(8,128)(2,1)}, u32[]{:S(2)}, u32[]{:S(2)}) collective-permute-start(bf16[1,280,768]{2,1,0:T(8,128)(2,1)} %get-tuple-element.2496), channel_id=1, source_target_pairs={{0,8},{8,16},{16,24},{1,9},{9,17},{17,25},{2,10},{10,18},{18,26},{... | collective-permute-start | bytes 1290248 | tf_op jit(solution)/shard_map/ppermute | solution.py:15
  462.3 16.7 copy-start.81
  462.4 16.7 slice-start.22
  519.5 109.4 %collective-permute-start.1 = (bf16[1,280,768]{2,1,0:T(8,128)(2,1)}, bf16[1,280,768]{2,1,0:T(8,128)(2,1)}, u32[]{:S(2)}, u32[]{:S(2)}) collective-permute-start(bf16[1,280,768]{2,1,0:T(8,128)(2,1)} %get-tuple-element.2494), channel_id=1, source_target_pairs={{0,8},{8,16},{16,24},{1,9},{9,17},{17,25},{2,10},{10,18},{18,26},{... | collective-permute-start | bytes 1290248 | tf_op jit(solution)/shard_map/ppermute | solution.py:15
  676.4 103.2 %collective-permute-start.2 = (bf16[1,280,768]{2,1,0:T(8,128)(2,1)}, bf16[1,280,768]{2,1,0:T(8,128)(2,1)}, u32[]{:S(2)}, u32[]{:S(2)}) collective-permute-start(bf16[1,280,768]{2,1,0:T(8,128)(2,1)} %get-tuple-element.2492), channel_id=1, source_target_pairs={{0,8},{8,16},{16,24},{1,9},{9,17},{17,25},{2,10},{10,18},{18,26},{... | collective-permute-start | bytes 1290248 | tf_op jit(solution)/shard_map/ppermute | solution.py:15
  790.4 13.5 copy-start.73
  793.4 102.3 %collective-permute-start.3 = (bf16[1,280,768]{2,1,0:T(8,128)(2,1)}, bf16[1,280,768]{2,1,0:T(8,128)(2,1)}, u32[]{:S(2)}, u32[]{:S(2)}) collective-permute-start(bf16[1,280,768]{2,1,0:T(8,128)(2,1)} %get-tuple-element.2490), channel_id=1, source_target_pairs={{0,8},{8,16},{16,24},{1,9},{9,17},{17,25},{2,10},{10,18},{18,26},{... | collective-permute-start | bytes 1290248 | tf_op jit(solution)/shard_map/ppermute | solution.py:15
  994.2 11.3 collective-permute-start.4
  1015.4 9.8 collective-permute-start.5
  1034.8 227.9 %collective-permute-start.6 = (bf16[1,280,768]{2,1,0:T(8,128)(2,1)}, bf16[1,280,768]{2,1,0:T(8,128)(2,1)}, u32[]{:S(2)}, u32[]{:S(2)}) collective-permute-start(bf16[1,280,768]{2,1,0:T(8,128)(2,1)} %convert_element_type.1200), channel_id=1, source_target_pairs={{8,0},{16,8},{24,16},{9,1},{17,9},{25,17},{10,2},{18,10},{26,18},{... | collective-permute-start | bytes 1290248 | tf_op jit(solution)/shard_map/ppermute | solution.py:15
  1276.3 14.6 slice-start.16
  1278.2 15.5 copy-start.216
  1278.3 15.0 copy-start.198
  1278.3 12.6 copy-start.9
  1278.3 12.6 copy-start.191
  1278.3 12.6 slice-start.17
  1354.8 9.8 collective-permute-start.7
  1378.2 17.4 copy-start.193
  1378.2 15.0 slice-start.18
  1380.7 14.9 copy-start.200
  1451.6 230.0 %reduce-scatter.39.cloned.1.call-start = ((), (), s32[]{:S(2)}) async-start(), calls=%async_computation.23 | async-start | bytes 221184
  1453.2 229.7 %reduce-scatter.43.cloned.1.call-start = ((), (), s32[]{:S(2)}) async-start(), calls=%async_computation.25 | async-start | bytes 221184
  1454.8 247.0 %reduce-scatter.45.cloned.1.call-start = ((), (), s32[]{:S(2)}) async-start(), calls=%async_computation.26 | async-start | bytes 221184
  1456.4 308.8 %reduce-scatter.47.cloned.1.call-start = ((), (), s32[]{:S(2)}) async-start(), calls=%async_computation.27 | async-start | bytes 221184
  1458.0 370.4 %reduce-scatter.51.cloned.1.call-start = ((), (), s32[]{:S(2)}) async-start(), calls=%async_computation.29 | async-start | bytes 221184
  1459.6 432.6 %reduce-scatter.41.cloned.1.call-start = ((), (), s32[]{:S(2)}) async-start(), calls=%async_computation.24 | async-start | bytes 442368
  1461.4 495.5 %reduce-scatter.49.cloned.1.call-start = ((), (), s32[]{:S(2)}) async-start(), calls=%async_computation.28 | async-start | bytes 884736
  1463.5 560.4 %reduce-scatter.31.cloned.1.call-start = ((), (), s32[]{:S(2)}) async-start(), calls=%async_computation.19 | async-start | bytes 1327104 | tf_op jit(solution)/shard_map/reduce_scatter | solution.py:338
  1466.3 639.6 %reduce-scatter.29.cloned.1.call-start = ((), (), s32[]{:S(2)}) async-start(), calls=%async_computation.18 | async-start | bytes 3981312 | tf_op jit(solution)/shard_map/reduce_scatter | solution.py:332
  1471.7 733.2 %reduce-scatter.33.cloned.1.call-start = ((), (), s32[]{:S(2)}) async-start(), calls=%async_computation.20 | async-start | bytes 5308416 | tf_op jit(solution)/shard_map/reduce_scatter | solution.py:350
  1478.3 825.7 %reduce-scatter.35.cloned.1.call-start = ((), (), s32[]{:S(2)}) async-start(), calls=%async_computation.21 | async-start | bytes 5308416 | tf_op jit(solution)/shard_map/reduce_scatter | solution.py:356
  1529.7 142.3 %all-to-all-start = ((bf16[1,2,280,768]{2,1,0,3:T(2,128)(2,1)}), bf16[1,2,280,768]{2,1,0,3:T(2,128)(2,1)S(1)}, u32[]{:S(2)}, u32[]{:S(2)}) async-start(bf16[1,2,280,768]{2,1,0,3:T(2,128)(2,1)} %fusion.544), calls=%async_computation | async-start | bytes 2359296 | tf_op jit(solution)/shard_map/all_to_all | solution.py:370
  1672.0 286.5 %all-to-all-start.1 = ((bf16[1,2,280,768]{2,1,0,3:T(2,128)(2,1)}), bf16[1,2,280,768]{2,1,0,3:T(2,128)(2,1)S(1)}, u32[]{:S(2)}, u32[]{:S(2)}) async-start(bf16[1,2,280,768]{2,1,0,3:T(2,128)(2,1)} %fusion.545), calls=%async_computation.1 | async-start | bytes 2359296 | tf_op jit(solution)/shard_map/all_to_all | solution.py:373
  (150 other events, 804.9 us)
Sparse Core Ops, SparseCore 0:
  10.8 43.9 all-gather.6
  57.5 64.2 all-gather.4
  124.5 78.3 all-gather.8
  205.5 78.0 all-gather.10
  1451.8 59.4 reduce-scatter.36
  1514.9 60.0 reduce-scatter.38
  1578.3 60.0 reduce-scatter.42
  1641.7 60.1 reduce-scatter.44
  1705.1 60.0 reduce-scatter.46
  1768.3 60.1 reduce-scatter.50
  1831.8 60.4 reduce-scatter.40
  1895.4 61.4 reduce-scatter.48
  1960.7 63.1 reduce-scatter.30
  2027.8 78.0 reduce-scatter.28
  2109.9 94.9 reduce-scatter.32
  2208.8 95.1 reduce-scatter.34
where the time goes:
time: 2350 us; the launch traced here: 2310 us
  waiting for transfers between devices  1050 us (45%)
  local copies, waits for them, and re-layouts  758 us (32%)
  other arithmetic  198 us (8%)
  matrix products  166 us (7%)
  blocking collectives  65.3 us (3%)
  starting transfers between devices  31.5 us (1%)
  loops' own time  24.6 us (1%)
    dynamic_update_slice x20, local copies, waits for them, and re-layouts, place(): lax.dynamic_update_index_in_dim(buffer, jnp.where(live, item, previous),...  415 us
    unnamed x24, waiting for transfers between devices  267 us
    ppermute x8, waiting for transfers between devices, from_behind(): return lax.ppermute(value, axis, pairs)  254 us
    dynamic_slice x44, local copies, waits for them, and re-layouts, place(): previous = lax.dynamic_index_in_dim(buffer, slot, 0, False)  133 us
    reduce_scatter x1, waiting for transfers between devices, shards(): lax.psum_scatter(totals[10].astype(jnp.bfloat16), 'dp', scatter_dimension...  97 us
    reduce_scatter x1, waiting for transfers between devices, shards(): lax.psum_scatter(totals[8].astype(jnp.bfloat16), 'dp', scatter_dimension=...  96.9 us
    all_gather x1, waiting for transfers between devices, shards(): lax.all_gather(up_weight.astype(jnp.bfloat16), 'dp', axis=1, tiled=True)  81.2 us
    all_gather x1, waiting for transfers between devices, shards(): lax.all_gather(down_weight.astype(jnp.bfloat16), 'dp', axis=1, tiled=True)  80.7 us
  transfers between devices with their start and end apart: 26, of which 16 were waited for; matrix products, arithmetic and copies ran while one was open for 29% of the time, Pallas kernels for 0%

commit v1 on v0

v1 whole, which is shorter than its diff:
```python
import functools

import jax
import jax.numpy as jnp
from jax import lax
from jax.experimental import pallas as pl
from jax.experimental.pallas import tpu as pltpu
from jax.sharding import PartitionSpec as P

D = 768
HEADS = 12
FF = 3072
CAPTION = 40
ROWS = 288
CHUNKS = 12
HALF = 6
EPS = 1e-6
BF = jnp.bfloat16
F32 = jnp.float32
PAIRED = 2 * (D // HEADS)
VMEM_LIMIT = 58 * 2**20
WIDE = FF + 2 * D
AG, AS, BQ, BV, OB, FG, FS, DB, UB = 0, 1, 2, 3, 4, 5, 6, 7, 8


def dot(a, b, ca=1, cb=0):
    return lax.dot_general(a, b, (((ca,), (cb,)), ((), ())), preferred_element_type=F32)


def spread_of(v):
    mean = jnp.mean(v, axis=-1, keepdims=True)
    cent = v - mean
    return cent, lax.rsqrt(jnp.mean(cent * cent, axis=-1, keepdims=True) + EPS)


def gelu_pair(h):
    x = jnp.abs(h) * (0.5**0.5)
    t = 1.0 / (1.0 + 0.5 * x)
    poly = jnp.full_like(t, 0.17087277)
    for c in (-0.82215223, 1.48851587, -1.13520398, 0.27886807, -0.18628806, 0.09678418,
              0.37409196, 1.00002368, -1.26551223):
        poly = poly * t + c
    gauss = jnp.exp(-x * x)
    tail = 0.5 * t * gauss * jnp.exp(poly)
    phi = jnp.where(h < 0.0, tail, 1.0 - tail)
    return h * phi, phi + h * gauss * 0.3989422804014327


def square(block):
    return block.reshape(D, D)


def weight_copies(w, wv, wd, sems):
    per, q = wd.shape[1], wd.shape[2]
    out = [pltpu.make_async_copy(w.at[:, k], wv.at[k], sems.at[k]) for k in range(8)]
    for b in range(4):
        if q == 4:
            src = w.at[pl.ds(b * per, per), pl.ds(8, 4)]
        else:
            src = w.at[:, pl.ds(8 + b, 1)]
        out.append(pltpu.make_async_copy(src, wd.at[b], sems.at[8 + b]))
    return out


def start_weights(pick, wa, wb, wv, wd, sems, order):
    @pl.when(pick == 0)
    def _():
        c = weight_copies(wa, wv, wd, sems)
        for k in order:
            c[k].start()

    @pl.when(pick != 0)
    def _():
        c = weight_copies(wb, wv, wd, sems)
        for k in order:
            c[k].start()

    return weight_copies(wa, wv, wd, sems)


def handing(core, keep, send, sems, waits):
    def hand_on(src, first, at):
        wide = src.shape[1]
        sem = sems.at[len(waits)]
        mine = (core == 0) == first

        @pl.when(mine)
        def _():
            pltpu.make_async_copy(src, keep.at[:, pl.ds(at, wide)], sem).start()

        @pl.when(jnp.logical_not(mine))
        def _():
            pltpu.make_async_copy(src, send.at[:, pl.ds(at, wide)], sem).start()

        waits.append(pltpu.make_async_copy(src, keep.at[:, pl.ds(at, wide)], sem))

    return hand_on


def forward_kernel(save, pick_ref, core_ref, x_ref, mask_ref, vec_ref, wa, wb, *rest):
    outs = []
    if save:
        y_ref, lse_ref, mid_ref, j_hbm, gp_hbm, keep, send = rest[:7]
        wv, wd, jn, ctx, act, gp, nrm, nt, sems, osems = rest[7:]
        hand_on = handing(core_ref[0], keep, send, osems, outs)
    else:
        y_ref = rest[0]
        wv, wd, jn, ctx, act, gp, nrm, nt, sems, osems = rest[1:]
    copies = start_weights(pick_ref[0], wa, wb, wv, wd, sems, range(12))

    def flush(src, dst):
        c = pltpu.make_async_copy(src, dst, osems.at[len(outs)])
        c.start()
        outs.append(c)

    x = x_ref[...].astype(F32)
    cent, inv = spread_of(x)
    nrm[...] = (cent * inv * vec_ref[AG:AG + 1, :] + vec_ref[AS:AS + 1, :]).astype(BF)
    if save:
        hand_on(nrm, True, D)
        hand_on(nrm, False, FF + D)
    for k in range(3):
        copies[k].wait()
        r = dot(nrm[...], square(wv[k]))
        if k == 0:
            r = r + vec_ref[BQ:BQ + 1, :]
        if k == 2:
            r = r + vec_ref[BV:BV + 1, :]
        jn[:, k * D:(k + 1) * D] = r.astype(BF)
    if save:
        flush(jn, j_hbm)
    usable = mask_ref[0:1, :] > 0.5
    lane = lax.broadcasted_iota(jnp.int32, (ROWS, PAIRED), 1)
    low = lane < PAIRED // 2

    def heads(i, lse):
        at = pl.multiple_of(i * PAIRED, PAIRED)
        q2 = jn[:, pl.ds(at, PAIRED)] * BF(0.125)
        k2 = jn[:, pl.ds(D + at, PAIRED)]
        v2 = jn[:, pl.ds(2 * D + at, PAIRED)]
        zero = jnp.zeros_like(q2)
        both = []
        for h in range(2):
            s = dot(jnp.where(low == (h == 0), q2, zero), k2, 1, 1)
            s = jnp.where(usable, s, -1e30)
            top = jnp.max(s, axis=-1, keepdims=True)
            e = jnp.exp(s - top)
            total = jnp.sum(e, axis=-1, keepdims=True)
            p = (e * (1.0 / total)).astype(BF)
            both.append(dot(p, v2))
            if save:
                lse = jnp.where(lane == 2 * i + h, top + jnp.log(total), lse)
        ctx[:, pl.ds(at, PAIRED)] = jnp.where(low, both[0], both[1]).astype(BF)
        return lse

    lse = lax.fori_loop(0, HEADS // 2, heads, jnp.zeros((ROWS, PAIRED), F32))
    if save:
        lse_ref[...] = lse
        hand_on(ctx, False, FF)
    copies[3].wait()
    middle = x_ref[...].astype(F32) + dot(ctx[...], square(wv[3])) + vec_ref[OB:OB + 1, :]
    if save:
        mid_ref[...] = middle
    cent, inv = spread_of(middle)
    nt[...] = (cent * inv * vec_ref[FG:FG + 1, :] + vec_ref[FS:FS + 1, :]).astype(BF)
    if save:
        hand_on(nt, True, 0)
    acc = middle + vec_ref[DB:DB + 1, :]
    for b in range(4):
        copies[4 + b].wait()
        h = dot(nt[...], square(wv[4 + b])) + vec_ref[UB + b:UB + b + 1, :]
        a, g = gelu_pair(h)
        act[:, b * D:(b + 1) * D] = a.astype(BF)
        if save:
            gp[:, b * D:(b + 1) * D] = g.astype(BF)
        copies[8 + b].wait()
        acc = acc + dot(act[:, b * D:(b + 1) * D], square(wd[b]))
    y_ref[...] = acc.astype(BF)
    if save:
        hand_on(act, False, 0)
        flush(gp, gp_hbm)
        for c in outs:
            c.wait()


def weight_scratch(shape):
    n, _, r, _ = shape
    per, q = (n // 4, 4) if n > 1 else (1, 1)
    return [pltpu.VMEM((8, n, r, D), BF), pltpu.VMEM((4, per, q, r, D), BF)]


ANYS = pl.BlockSpec(memory_space=pl.ANY)
VM = pl.BlockSpec(memory_space=pltpu.VMEM)
SM = pl.BlockSpec(memory_space=pltpu.SMEM)


def forward_layer(save, pick, core, x, mask, vec, wa, wb):
    def sd(cols, t=BF):
        return jax.ShapeDtypeStruct((ROWS, cols), t)

    shapes, specs = [sd(D)], [VM]
    if save:
        shapes += [sd(PAIRED, F32), sd(D, F32), sd(3 * D), sd(FF), sd(WIDE), sd(WIDE)]
        specs += [VM, VM] + [ANYS] * 4
    return pl.pallas_call(
        functools.partial(forward_kernel, save),
        out_shape=shapes,
        in_specs=[SM, SM, VM, VM, VM, ANYS, ANYS],
        out_specs=specs,
        scratch_shapes=weight_scratch(wa.shape) + [
            pltpu.VMEM((ROWS, 3 * D), BF), pltpu.VMEM((ROWS, D), BF), pltpu.VMEM((ROWS, FF), BF),
            pltpu.VMEM((ROWS, FF), BF), pltpu.VMEM((ROWS, D), BF), pltpu.VMEM((ROWS, D), BF),
            pltpu.SemaphoreType.DMA((12,)), pltpu.SemaphoreType.DMA((7,))],
        compiler_params=pltpu.CompilerParams(vmem_limit_bytes=VMEM_LIMIT),
        cost_estimate=pl.CostEstimate(flops=2 * ROWS * D * D * 13, bytes_accessed=24 * D * D + 2**22, transcendentals=0),
        name="forward_layer",
    )(pick, core, x, mask, vec, wa, wb)


def backward_kernel(save, pick_ref, core_ref, g_ref, x_ref, lse_ref, mid_ref, mask_ref, vec_ref, wa, wb,
                    j_hbm, gp_hbm, *rest):
    if save:
        ds_ref, gv_ref, keep_hbm, send_hbm = rest[:4]
        wv, wd, jn, gp, dh, dj, b1, sems, isems, osems = rest[4:]
    else:
        ds_ref = rest[0]
        wv, wd, jn, gp, dh, dj, b1, sems, isems, osems = rest[1:]
    gp_in = pltpu.make_async_copy(gp_hbm, gp, isems.at[0])
    gp_in.start()
    copies = start_weights(pick_ref[0], wa, wb, wv, wd, sems, (8, 4, 9, 5, 10, 6, 11, 7, 3, 0, 1, 2))
    j_in = pltpu.make_async_copy(j_hbm, jn, isems.at[1])
    j_in.start()
    waits = []
    hand_on = handing(core_ref[0], keep_hbm, send_hbm, osems, waits) if save else lambda *a: None
    hand_on(g_ref, False, 0)
    g = g_ref[...]
    d_nt = jnp.zeros((ROWS, D), F32)
    gp_in.wait()
    for b in range(4):
        copies[8 + b].wait()
        da = dot(g, square(wd[b]), 1, 1)
        cols = slice(b * D, (b + 1) * D)
        d = da * gp[:, cols].astype(F32)
        dh[:, cols] = d.astype(BF)
        if save:
            gv_ref[UB + b:UB + b + 1, :] = jnp.sum(dh[:, cols].astype(F32), axis=0, keepdims=True)
        copies[4 + b].wait()
        d_nt = d_nt + dot(dh[:, cols], square(wv[4 + b]), 1, 1)
    hand_on(dh, True, 0)

    def norm_back(v, dy, gain, row):
        cent, inv = spread_of(v)
        hat = cent * inv
        if save:
            gv_ref[row:row + 1, :] = jnp.sum(dy * hat, axis=0, keepdims=True)
            gv_ref[row + 1:row + 2, :] = jnp.sum(dy, axis=0, keepdims=True)
        t = dy * gain
        return inv * (t - jnp.mean(t, axis=-1, keepdims=True) - hat * jnp.mean(t * hat, axis=-1, keepdims=True))

    d_mid = g_ref[...].astype(F32) + norm_back(mid_ref[...], d_nt, vec_ref[FG:FG + 1, :], FG)
    b1[...] = d_mid.astype(BF)
    if save:
        gv_ref[DB:DB + 1, :] = jnp.sum(g_ref[...].astype(F32), axis=0, keepdims=True)
        gv_ref[OB:OB + 1, :] = jnp.sum(b1[...].astype(F32), axis=0, keepdims=True)
    hand_on(b1, False, D)
    copies[3].wait()
    dj[:, :D] = dot(b1[...], square(wv[3]), 1, 1).astype(BF)
    j_in.wait()
    usable = mask_ref[0:1, :] > 0.5
    lane = lax.broadcasted_iota(jnp.int32, (ROWS, PAIRED), 1)
    low = lane < PAIRED // 2

    def heads(i, carry):
        at = pl.multiple_of(i * PAIRED, PAIRED)
        q2 = jn[:, pl.ds(at, PAIRED)] * BF(0.125)
        k2 = jn[:, pl.ds(D + at, PAIRED)]
        v2 = jn[:, pl.ds(2 * D + at, PAIRED)]
        do2 = dj[:, pl.ds(at, PAIRED)]
        zero = jnp.zeros_like(q2)
        lse_all = lse_ref[...]
        res = []
        for h in range(2):
            here = low == (h == 0)
            lse = jnp.sum(jnp.where(lane == 2 * i + h, lse_all, 0.0), axis=-1, keepdims=True)
            s = dot(jnp.where(here, q2, zero), k2, 1, 1)
            p = jnp.where(usable, jnp.exp(s - lse), 0.0)
            dp = dot(jnp.where(here, do2, zero), v2, 1, 1)
            inner = jnp.sum(p * dp, axis=-1, keepdims=True)
            dsc = (p * (dp - inner)).astype(BF)
            res.append((dot(dsc, k2) * 0.125, dot(dsc, q2, 0, 0), dot(p.astype(BF), do2, 0, 0)))
        for c in range(3):
            dj[:, pl.ds(c * D + at, PAIRED)] = jnp.where(low, res[0][c], res[1][c]).astype(BF)
        return carry

    lax.fori_loop(0, HEADS // 2, heads, 0)
    hand_on(dj.at[:, pl.ds(0, 2 * D)], True, FF)
    hand_on(dj.at[:, pl.ds(2 * D, D)], False, 2 * D)
    if save:
        gv_ref[BQ:BQ + 1, :] = jnp.sum(dj[:, :D].astype(F32), axis=0, keepdims=True)
        gv_ref[BV:BV + 1, :] = jnp.sum(dj[:, 2 * D:].astype(F32), axis=0, keepdims=True)
        gv_ref[UB + 4:, :] = jnp.zeros((4, D), F32)
    d_n = jnp.zeros((ROWS, D), F32)
    for k in range(3):
        copies[k].wait()
        d_n = d_n + dot(dj[:, k * D:(k + 1) * D], square(wv[k]), 1, 1)
    ds_ref[...] = (d_mid + norm_back(x_ref[...].astype(F32), d_n, vec_ref[AG:AG + 1, :], AG)).astype(BF)
    for c in waits:
        c.wait()


def backward_layer(save, pick, core, g, x, mask, vec, wa, wb, saved):
    lse, mid, jn, gp = saved

    def sd(cols, t=BF, rows=ROWS):
        return jax.ShapeDtypeStruct((rows, cols), t)

    shapes, specs = [sd(D)], [VM]
    if save:
        shapes += [sd(D, F32, 16), sd(WIDE), sd(WIDE)]
        specs += [VM, ANYS, ANYS]
    return pl.pallas_call(
        functools.partial(backward_kernel, save),
        out_shape=shapes,
        in_specs=[SM, SM] + [VM] * 6 + [ANYS] * 4,
        out_specs=specs,
        scratch_shapes=weight_scratch(wa.shape) + [
            pltpu.VMEM((ROWS, 3 * D), BF), pltpu.VMEM((ROWS, FF), BF), pltpu.VMEM((ROWS, FF), BF),
            pltpu.VMEM((ROWS, 3 * D), BF), pltpu.VMEM((ROWS, D), BF),
            pltpu.SemaphoreType.DMA((12,)), pltpu.SemaphoreType.DMA((2,)), pltpu.SemaphoreType.DMA((5,))],
        compiler_params=pltpu.CompilerParams(vmem_limit_bytes=VMEM_LIMIT),
        cost_estimate=pl.CostEstimate(flops=2 * ROWS * D * D * 14, bytes_accessed=24 * D * D + 2**23, transcendentals=0),
        name="backward_layer",
    )(pick, core, g, x, lse, mid, mask, vec, wa, wb, jn, gp)


def product_kernel(core_ref, fk, bk, fr, br, out_ref):
    n, _, r, _ = out_ref.shape

    def both(a, b, at, wide=D):
        return jnp.concatenate([a[:, at:at + wide], b[:, at:at + wide]], axis=0)

    @pl.when(core_ref[0] == 0)
    def _():
        for c in range(HALF):
            left = both(fk, fr, 0 if c < 4 else D)
            out_ref[:, c] = dot(left, both(bk, br, c * D), 0, 0).astype(BF).reshape(n, r, D)

    @pl.when(core_ref[0] != 0)
    def _():
        for c in range(HALF):
            left = both(fk, fr, c * D)
            val = dot(left, both(bk, br, 0 if c < 4 else (c - 3) * D), 0, 0).astype(BF)
            if c < 4 and n > 1:
                out_ref[c * (n // 4):(c + 1) * (n // 4), 0:4] = val.reshape(n // 4, 4, r, D)
            else:
                out_ref[:, c] = val.reshape(n, r, D)


def weight_products(n, core, fk, bk, fr, br):
    return pl.pallas_call(
        product_kernel,
        out_shape=jax.ShapeDtypeStruct((n, HALF, D // n, D), BF),
        in_specs=[SM] + [VM] * 4,
        out_specs=VM,
        compiler_params=pltpu.CompilerParams(vmem_limit_bytes=VMEM_LIMIT),
        cost_estimate=pl.CostEstimate(flops=2 * 2 * ROWS * D * D * 6, bytes_accessed=2**24, transcendentals=0),
        name="weight_products",
    )(core, fk, bk, fr, br)


def moved(value, axis, by):
    peers = lax.axis_size(axis)
    return lax.ppermute(value, axis, [(i, i + by) for i in range(peers) if 0 <= i + by < peers])


def swapped(value):
    peers = lax.axis_size("section")
    return lax.ppermute(value, "section", [(i, i ^ 1) for i in range(peers)])


def pack_shard(joint, output, up, down):
    r = output.shape[0]
    pieces = [joint[:, k * D:(k + 1) * D] for k in range(3)] + [output]
    pieces += [up[:, k * D:(k + 1) * D] for k in range(4)]
    return jnp.concatenate([jnp.stack(pieces), down.reshape(4, r, D)]).astype(BF)


def kernel_form(n, g):
    r = D // n
    if r % 16 == 0:
        return g
    cut = jnp.swapaxes(g[:, :8], 0, 1).reshape(8, D, D)
    return jnp.concatenate([cut, g[:, 8:].reshape(4, D, D)])[None]


def vector_block(v, n):
    r = D // n
    parts = [v[:, 0:r], v[:, r:2 * r], v[:, 2 * r:4 * r], v[:, 4 * r:5 * r], v[:, 5 * r:6 * r], v[:, 6 * r:7 * r],
             v[:, 7 * r:8 * r], v[:, 8 * r:]]
    rows = jnp.concatenate([p.reshape(-1) for p in parts]).reshape(12, D)
    return jnp.concatenate([rows, jnp.zeros((4, D), v.dtype)]).astype(F32)


def vector_parts(rows, n):
    cuts = [rows[0:1], rows[1:2], rows[2:4], rows[4:5], rows[5:6], rows[6:7], rows[7:8], rows[8:12]]
    return jnp.concatenate([c.reshape(n, -1) for c in cuts], axis=1)


def shards(tokens, lengths, cotangent, attend_gain, attend_shift, joint_weight, joint_bias, output_weight,
           output_bias, feed_gain, feed_shift, up_weight, up_bias, down_weight, down_bias):
    n = lax.axis_size("dp")
    r = D // n
    nk = n if r % 16 == 0 else 1
    sections = lax.axis_size("section")
    stages = sections // 2
    index = lax.axis_index("section")
    core, stage = index % 2, index // 2
    seq = tokens.shape[1]
    coref = core.reshape(1)
    picks = [(core != s).astype(jnp.int32).reshape(1) for s in range(2)]

    packed = pack_shard(joint_weight[0], output_weight[0], up_weight[0], down_weight[0])
    small = jnp.concatenate([v[0] for v in (attend_gain, attend_shift, joint_bias, output_bias, feed_gain, feed_shift,
                                            down_bias, up_bias)]).astype(BF)
    small = lax.all_gather(small, "dp")
    mine = lax.all_gather(packed, "dp")
    small_other = swapped(small)
    vec_own, vec_oth = vector_block(small, n), vector_block(small_other, n)
    vecs = [jnp.where(core == s, vec_own, vec_oth) for s in range(2)]
    other = swapped(mine)
    wa, wb = kernel_form(n, mine), kernel_form(n, other)

    def own_pair(a):
        return lax.dynamic_index_in_dim(a, core, 0, False)

    def padded(a):
        return jnp.pad(a, ((0, ROWS - seq), (0, 0)))

    places = lax.broadcasted_iota(jnp.int32, (8, ROWS), 1)
    mask = (((places < own_pair(lengths)) | (places >= CAPTION)) & (places < seq)).astype(F32)
    own_tokens = padded(own_pair(tokens))
    own_cotangent = padded(own_pair(cotangent))

    x = own_tokens
    for t in range(stages):
        last = t == stages - 1
        start, saved = x, []
        for s in range(2):
            got = forward_layer(last, picks[s], coref, x, mask, vecs[s], wa, wb)
            saved.append((x,) + tuple(got[1:]))
            x = got[0]
        if not last:
            x = jnp.where(stage == 0, own_tokens, moved(x, "section", 2))
    leaving = x
    forward_got = [swapped(saved[s][6]) for s in range(2)]

    g = own_cotangent
    products, vec_grads = [None, None], [None, None]
    for t in range(stages):
        last = t == stages - 1
        for s in (1, 0):
            xin, lse, mid, jn, gp, fk, _ = saved[s]
            got = backward_layer(last, picks[s], coref, g, xin, mask, vecs[s], wa, wb, (lse, mid, jn, gp))
            g = got[0]
            if last:
                vec_grads[s] = got[1]
                products[s] = weight_products(nk, coref, fk, got[2], forward_got[s], swapped(got[3]))
        if not last:
            g = jnp.where(stage == stages - 1, own_cotangent, moved(g, "section", -2))

    reduced = [None, None]
    for s in (1, 0):
        p = products[s]
        if nk == 1:
            col = jnp.swapaxes(p[0].reshape(HALF, n, r, D), 0, 1)
            row = jnp.concatenate([jnp.swapaxes(p[0, :4].reshape(n, 4, r, D), 0, 0), col[:, 4:]], axis=1)
            p = jnp.where(core == 0, col, row)
        reduced[s] = lax.psum_scatter(p, "dp", scatter_dimension=0)
    keep = jnp.where(core == 0, reduced[0], reduced[1])
    away = swapped(jnp.where(core == 0, reduced[1], reduced[0]))
    first = jnp.where(core == 0, keep, away).astype(F32)
    second = jnp.where(core == 0, away, keep).astype(F32)
    grad_up = jnp.concatenate([first[k] for k in range(4)], axis=1)
    grad_joint = jnp.concatenate([first[4], first[5], second[5]], axis=1)
    grad_down = second[:4].reshape(4 * r, D)
    grad_out = second[4]

    vec_keep = jnp.where(core == 0, vec_grads[0], vec_grads[1])
    vec_send = jnp.where(core == 0, vec_grads[1], vec_grads[0])
    vec_sum = vec_keep + swapped(vec_send)
    v = lax.psum_scatter(vector_parts(vec_sum, n), "dp", scatter_dimension=0)

    ends = jnp.where(stage == 0, g, leaving)[:seq].reshape(seq, sections, D // sections)
    pieces = lax.all_to_all(ends, "section", split_axis=1, concat_axis=0, tiled=True).reshape(sections, seq, D // sections)
    outputs = pieces[sections - 2:]
    token_grad = pieces[:2]
    return (outputs, token_grad, v[None, 0:r], v[None, r:2 * r], grad_joint[None], v[None, 2 * r:4 * r], grad_out[None],
            v[None, 4 * r:5 * r], v[None, 5 * r:6 * r], v[None, 6 * r:7 * r], grad_up[None], v[None, 8 * r:],
            grad_down[None], v[None, 7 * r:8 * r])


def solution(mesh):
    vec, mat = P("section", "dp"), P("section", "dp", None)
    rows = P("dp", None, None)
    out = P("dp", None, "section")
    return jax.shard_map(
        shards,
        mesh=mesh,
        in_specs=(rows, P("dp"), rows, vec, vec, mat, vec, mat, vec, vec, vec, mat, vec, mat, vec),
        out_specs=(out, out, vec, vec, mat, vec, mat, vec, vec, vec, mat, vec, mat, vec),
        check_vma=False,
    )
```

time: 2350 us -> 799 us (0.34); the launches traced: 2310 us -> 793 us
  local copies, waits for them, and re-layouts: 758 us -> 23.2 us
  waiting for transfers between devices: 1050 us -> 468 us
  Pallas kernels: 0 us -> 203 us
  other arithmetic: 198 us -> 9.19 us
  matrix products: 166 us -> 0 us
  loops' own time: 24.6 us -> 0 us
    dynamic_update_slice x20 -> x0, local copies, waits for them, and re-layouts: 415 us -> none  [place(): lax.dynamic_update_index_in_dim(buffer, jnp.where(live, item, previous),...]
    unnamed x24 -> x3, waiting for transfers between devices: 267 us -> 0.05 us
    ppermute x8 -> x10, waiting for transfers between devices: 254 us -> 35.5 us  [the longest x2 21.9 us: moved(): lax.ppermute(value, axis, [(i, i + by) for i in range(peers) if 0 <= i +...]
    pallas_call x0 -> x10, Pallas kernels: none -> 203 us  [the longest x4 92.9 us: backward_layer(): pl.pallas_call(functools.partial(backward_kernel, save), out_shape=shapes...]
    dot_general x38 -> x0, matrix products: 166 us -> none  [the longest x2 25 us: backward_part(): jnp.einsum('psd,fd->psf', branch_two, down_weight, preferred_element_type...]
    dynamic_slice x46 -> x1, local copies, waits for them, and re-layouts: 136 us -> 0.59 us  [own_pair(): return lax.dynamic_index_in_dim(a, core, 0, False)]
    reduce_scatter x4 -> x2, waiting for transfers between devices: 335 us -> 234 us  [shards(): reduced[s] = lax.psum_scatter(p, 'dp', scatter_dimension=0)]
    broadcast_in_dim x36 -> x0, local copies, waits for them, and re-layouts: 99.2 us -> none  [the longest x16 66.8 us: place(): lax.dynamic_update_index_in_dim(buffer, jnp.where(live, item, previous),...]
  transfers between devices with their start and end apart: 26 -> 14, of which waited for: 16 -> 8; matrix products, arithmetic and copies ran while one was open for 29% -> 2% of each run, Pallas kernels for 0% -> 8%
where the time goes in v1:
time: 799 us; the launch traced here: 793 us
  waiting for transfers between devices  468 us (59%)
  Pallas kernels  203 us (25%)
  blocking collectives  66.1 us (8%)
  local copies, waits for them, and re-layouts  23.2 us (3%)
  between operations  14.7 us (2%)
  starting transfers between devices  9.22 us (1%)
  other arithmetic  9.19 us (1%)
    reduce_scatter x2, waiting for transfers between devices, shards(): reduced[s] = lax.psum_scatter(p, 'dp', scatter_dimension=0)  234 us
    all_gather x1, waiting for transfers between devices, shards(): mine = lax.all_gather(packed, 'dp')  198 us
    pallas_call x4, Pallas kernels, backward_layer(): pl.pallas_call(functools.partial(backward_kernel, save), out_shape=shapes...  92.9 us
    pallas_call x4, Pallas kernels, forward_layer(): pl.pallas_call(functools.partial(forward_kernel, save), out_shape=shapes,...  84.2 us
    unnamed x1, blocking collectives  35.6 us
    all_gather x1, blocking collectives, shards(): small = lax.all_gather(small, 'dp')  30.6 us
    pallas_call x2, Pallas kernels, weight_products(): pl.pallas_call(product_kernel, out_shape=jax.ShapeDtypeStruct((n, HALF, D...  25.8 us
    ppermute x2, waiting for transfers between devices, moved(): lax.ppermute(value, axis, [(i, i + by) for i in range(peers) if 0 <= i +...  21.9 us
  transfers between devices with their start and end apart: 14, of which 8 were waited for; matrix products, arithmetic and copies ran while one was open for 2% of the time, Pallas kernels for 8%

profile of v1, /device:TPU:0, one launch (start us, length us, event | category | flops | bytes accessed | tf_op | source)
XLA Modules:
  0.0 793.1 jit_solution(1307192976658200212)
XLA Ops:
  7.3 1.4 convert_bitcast_fusion.1
  9.1 1.1 copy-done.10
  10.4 1.2 copy-done.8
  11.7 198.4 %all-gather.3.cloned.1.call-done.wa = bf16[8,12,96,768]{3,2,1,0:T(8,128)(2,1)} async-done(((bf16[1,12,96,768]{3,2,1,0:T(8,128)(2,1)}), bf16[8,12,96,768]{3,2,1,0:T(8,128)(2,1)}) %all-gather.3.cloned.1.call-update) | async-done | bytes 14155792 | tf_op jit(solution)/shard_map/all_gather | solution.py:426
  210.4 30.6 %all-gather = bf16[8,1,1152]{2,1,0:T(2,128)(2,1)S(1)} all-gather(bf16[1,1,1152]{2,1,0:T(2,128)(2,1)S(1)} %bitcast.90), channel_id=1, replica_groups=mesh['section'=4,'dp'=8] {'dp'}, dimensions={0}, use_global_device_ids=true | all-gather | bytes 20736 | tf_op jit(solution)/shard_map/all_gather | solution.py:425
  241.8 0.6 dynamic_slice.13
  243.9 0.7 fusion.11
  244.6 0.8 pad.10.x_ref
  247.8 0.7 convert_select_fusion
  248.4 0.6 iota.13.mask_ref
  249.0 20.2 %forward_layer.4.x_ref = bf16[288,768]{1,0:T(8,128)(2,1)} custom-call(s32[1]{0:T(128)} %bitcast.pick_ref, s32[1]{0:T(128)} %bitcast.1.core_ref, bf16[288,768]{1,0:T(8,128)(2,1)} %pad.10.x_ref, f32[8,288]{1,0:T(8,128)} %iota.13.mask_ref, f32[16,768]{1,0:T(8,128)} %get-tuple-element.77.vec_ref, bf16[8,12,96,768]{3,2,1,0:T(8,128)(2,1)} %all-gather.3.cloned.1.call-done.wa, ...), custom_call_target="tpu_custom_call" | custom-call | flops 4416602112 | bytes 18350080 | tf_op jit(solution)/shard_map/forward_layer/pallas_call | solution.py:205
  269.2 19.9 %forward_layer.5 = bf16[288,768]{1,0:T(8,128)(2,1)} custom-call(s32[1]{0:T(128)} %bitcast.2.pick_ref, s32[1]{0:T(128)} %bitcast.1.core_ref, bf16[288,768]{1,0:T(8,128)(2,1)} %forward_layer.4.x_ref, f32[8,288]{1,0:T(8,128)} %iota.13.mask_ref, f32[16,768]{1,0:T(8,128)} %get-tuple-element.76.vec_ref, bf16[8,12,96,768]{3,2,1,0:T(8,128)(2,1)} %all-gather.3.cloned.1.call-done.wa, ...), custom_call_target="tpu_custom_call" | custom-call | flops 4416602112 | bytes 18350080 | tf_op jit(solution)/shard_map/forward_layer/pallas_call | solution.py:205
  289.1 3.4 collective-permute-start.2
  292.6 0.8 pad.9.g_ref
  293.4 9.5 %collective-permute-done.2 = bf16[288,768]{1,0:T(8,128)(2,1)S(1)} collective-permute-done((bf16[288,768]{1,0:T(8,128)(2,1)}, bf16[288,768]{1,0:T(8,128)(2,1)S(1)}, u32[]{:S(2)}, u32[]{:S(2)}) %collective-permute-start.2) | collective-permute-done | bytes 442400 | tf_op jit(solution)/shard_map/ppermute | solution.py:373
  302.9 0.9 broadcast_select_fusion.2.x_ref
  303.8 21.9 %forward_layer.6 = (bf16[288,768]{1,0:T(8,128)(2,1)}, f32[288,128]{1,0:T(8,128)}, f32[288,768]{1,0:T(8,128)}, bf16[288,2304]{1,0:T(8,128)(2,1)}, bf16[288,3072]{...) custom-call(s32[1]{0:T(128)} %bitcast.pick_ref, s32[1]{0:T(128)} %bitcast.1.core_ref, ...), custom_call_target="tpu_custom_call" | custom-call | flops 4416602112 | bytes 18350080 | tf_op jit(solution)/shard_map/forward_layer/pallas_call | solution.py:205
  325.7 22.2 %forward_layer.7 = (bf16[288,768]{1,0:T(8,128)(2,1)}, f32[288,128]{1,0:T(8,128)}, f32[288,768]{1,0:T(8,128)}, bf16[288,2304]{1,0:T(8,128)(2,1)}, bf16[288,3072]{...) custom-call(s32[1]{0:T(128)} %bitcast.2.pick_ref, s32[1]{0:T(128)} %bitcast.1.core_ref, ...), custom_call_target="tpu_custom_call" | custom-call | flops 4416602112 | bytes 18350080 | tf_op jit(solution)/shard_map/forward_layer/pallas_call | solution.py:205
  347.9 22.7 %backward_layer.4.g_ref = bf16[288,768]{1,0:T(8,128)(2,1)} custom-call(s32[1]{0:T(128)} %bitcast.2.pick_ref, s32[1]{0:T(128)} %bitcast.1.core_ref, bf16[288,768]{1,0:T(8,128)(2,1)} %pad.9.g_ref, bf16[288,768]{1,0:T(8,128)(2,1)} %get-tuple-element.36.x_ref, f32[288,128]{1,0:T(8,128)} %get-tuple-element.37.lse_ref, f32[288,768]{1,0:T(8,128)} %get-tuple-element.38.mid_ref, ...), custom_call_target="tpu_custom_call" | custom-call | flops 4756340736 | bytes 22544384 | tf_op jit(solution)/shard_map/backward_layer/pallas_call | solution.py:321
  370.6 23.2 %backward_layer.5 = bf16[288,768]{1,0:T(8,128)(2,1)} custom-call(s32[1]{0:T(128)} %bitcast.pick_ref, s32[1]{0:T(128)} %bitcast.1.core_ref, bf16[288,768]{1,0:T(8,128)(2,1)} %backward_layer.4.g_ref, bf16[288,768]{1,0:T(8,128)(2,1)} %broadcast_select_fusion.2.x_ref, f32[288,128]{1,0:T(8,128)} %get-tuple-element.41.lse_ref, ...), custom_call_target="tpu_custom_call" | custom-call | flops 4756340736 | bytes 22544384 | tf_op jit(solution)/shard_map/backward_layer/pallas_call | solution.py:321
  393.8 1.3 collective-permute-start.3
  395.1 12.5 %collective-permute-done.3 = bf16[288,768]{1,0:T(8,128)(2,1)S(1)} collective-permute-done((bf16[288,768]{1,0:T(8,128)(2,1)}, bf16[288,768]{1,0:T(8,128)(2,1)S(1)}, u32[]{:S(2)}, u32[]{:S(2)}) %collective-permute-start.3) | collective-permute-done | bytes 442400 | tf_op jit(solution)/shard_map/ppermute | solution.py:373
  407.6 0.9 broadcast_select_fusion.1.g_ref
  408.5 23.4 %backward_layer.6 = (bf16[288,768]{1,0:T(8,128)(2,1)}, f32[16,768]{1,0:T(8,128)}, bf16[288,4608]{1,0:T(8,128)(2,1)}, bf16[288,4608]{1,0:T(8,128)(2,1)}) custom-call(s32[1]{0:T(128)} %bitcast.2.pick_ref, s32[1]{0:T(128)} %bitcast.1.core_ref, bf16[288,768]{1,0:T(8,128)(2,1)} %broadcast_select_fusion.1.g_ref, bf16[288,768]{1,0:T(8,128)(2,1)} %get-tuple-element.36.x_ref, ...), custom_call_target="tpu_custom_call" | custom-call | flops 4756340736 | bytes 22544384 | tf_op jit(solution)/shard_map/backward_layer/pallas_call | solution.py:321
  431.9 23.7 %backward_layer.7 = (bf16[288,768]{1,0:T(8,128)(2,1)}, f32[16,768]{1,0:T(8,128)}, bf16[288,4608]{1,0:T(8,128)(2,1)}, bf16[288,4608]{1,0:T(8,128)(2,1)}) custom-call(s32[1]{0:T(128)} %bitcast.pick_ref, s32[1]{0:T(128)} %bitcast.1.core_ref, bf16[288,768]{1,0:T(8,128)(2,1)} %get-tuple-element.45.g_ref, bf16[288,768]{1,0:T(8,128)(2,1)} %broadcast_select_fusion.2.x_ref, ...), custom_call_target="tpu_custom_call" | custom-call | flops 4756340736 | bytes 22544384 | tf_op jit(solution)/shard_map/backward_layer/pallas_call | solution.py:321
  455.7 5.1 collective-permute-done.6.br
  460.9 1.6 copy-done.6
  462.4 12.8 %weight_products.2 = bf16[8,6,96,768]{3,2,1,0:T(8,128)(2,1)} custom-call(s32[1]{0:T(128)} %bitcast.1.core_ref, bf16[288,4608]{1,0:T(8,128)(2,1)} %get-tuple-element.50.fk, bf16[288,4608]{1,0:T(8,128)(2,1)} %get-tuple-element.51.bk, bf16[288,4608]{1,0:T(8,128)(2,1)} %copy-done.4, bf16[288,4608]{1,0:T(8,128)(2,1)} %copy-done.6), custom_call_target="tpu_custom_call" | custom-call | flops 4076863488 | bytes 16777216 | tf_op jit(solution)/shard_map/weight_products/pallas_call | solution.py:360
  475.9 4.7 collective-permute-done.7.fr
  480.6 3.8 collective-permute-done.8.br
  484.4 1.5 copy-done.7
  485.9 13.0 %weight_products.3 = bf16[8,6,96,768]{3,2,1,0:T(8,128)(2,1)} custom-call(s32[1]{0:T(128)} %bitcast.1.core_ref, bf16[288,4608]{1,0:T(8,128)(2,1)} %get-tuple-element.54.fk, bf16[288,4608]{1,0:T(8,128)(2,1)} %get-tuple-element.55.bk, bf16[288,4608]{1,0:T(8,128)(2,1)} %copy-done.5, bf16[288,4608]{1,0:T(8,128)(2,1)} %copy-done.7), custom_call_target="tpu_custom_call" | custom-call | flops 4076863488 | bytes 16777216 | tf_op jit(solution)/shard_map/weight_products/pallas_call | solution.py:360
  498.9 0.6 copy-done.26
  499.5 0.6 dynamic-slice
  500.3 101.3 %reduce-scatter.3.cloned.1.call-done = bf16[1,6,96,768]{3,2,1,0:T(8,128)(2,1)} async-done(((bf16[8,6,96,768]{3,2,1,0:T(8,128)(2,1)}), bf16[1,6,96,768]{3,2,1,0:T(8,128)(2,1)}) %reduce-scatter.3.cloned.1.call-update) | async-done | bytes 884752 | tf_op jit(solution)/shard_map/reduce_scatter | solution.py:478
  601.6 132.2 %reduce-scatter.5.cloned.1.call-done = bf16[1,6,96,768]{3,2,1,0:T(8,128)(2,1)} async-done(((bf16[8,6,96,768]{3,2,1,0:T(8,128)(2,1)}), bf16[1,6,96,768]{3,2,1,0:T(8,128)(2,1)}) %reduce-scatter.5.cloned.1.call-update) | async-done | bytes 884752 | tf_op jit(solution)/shard_map/reduce_scatter | solution.py:478
  733.8 2.2 select_bitcast_fusion
  736.6 0.9 copy.31
  737.5 3.5 all-to-all-start
  741.7 35.6 %all-reduce.4 = f32[8,1152]{1,0:T(8,128)S(1)} all-reduce(f32[8,1152]{1,0:T(8,128)S(1)} %concatenate.76), channel_id=2, replica_groups=mesh['section'=4,'dp'=8] {'dp'}, use_global_device_ids=true, to_apply=%region_0.1.clone | all-reduce | flops 9216 | bytes 73728
  777.3 1.3 dynamic-slice.8
  778.6 1.3 dynamic-slice.4
  779.9 1.3 fusion.13
  781.1 0.8 slice_bitcast_fusion.7
  782.2 0.8 fusion.12
  783.0 1.1 slice.270
  784.2 1.0 maximum_bitcast_fusion.1
  785.2 1.1 maximum_bitcast_fusion
  (152 shorter events, 8.1 us)
Async XLA Ops:
  7.2 236.7 %copy-start = (bf16[2,280,768]{2,1,0:T(8,128)(2,1)S(1)}, bf16[2,280,768]{2,1,0:T(8,128)(2,1)}, u32[]{:S(2)}) copy-start(bf16[2,280,768]{2,1,0:T(8,128)(2,1)} %param.15) | copy-start | bytes 2580484
  7.2 1.8 copy-start.13
  7.2 202.9 %all-gather.3.cloned.1.call-start = ((), (), s32[]{:S(2)}) async-start(), calls=%async_computation.3 | async-start | bytes 15925248 | tf_op jit(solution)/shard_map/all_gather | solution.py:426
  7.3 1.6 copy-start.9
  8.9 1.3 copy-start.10
  10.2 199.9 %copy-start.17 = (f32[1,384]{1,0:T(1,128)S(1)}, f32[1,384]{1,0:T(1,128)}, u32[]{:S(2)}) copy-start(f32[1,384]{1,0:T(1,128)} %param.27) | copy-start | bytes 4612
  10.2 199.9 %copy-start.18 = (f32[1,192]{1,0:T(1,128)S(1)}, f32[1,192]{1,0:T(1,128)}, u32[]{:S(2)}) copy-start(f32[1,192]{1,0:T(1,128)} %param.21) | copy-start | bytes 2308
  10.3 199.9 %copy-start.19 = (f32[1,96]{1,0:T(1,128)S(1)}, f32[1,96]{1,0:T(1,128)}, u32[]{:S(2)}) copy-start(f32[1,96]{1,0:T(1,128)} %param.18) | copy-start | bytes 1156
  10.3 199.9 %copy-start.20 = (f32[1,96]{1,0:T(1,128)S(1)}, f32[1,96]{1,0:T(1,128)}, u32[]{:S(2)}) copy-start(f32[1,96]{1,0:T(1,128)} %param.19) | copy-start | bytes 1156
  10.3 199.9 %copy-start.21 = (f32[1,96]{1,0:T(1,128)S(1)}, f32[1,96]{1,0:T(1,128)}, u32[]{:S(2)}) copy-start(f32[1,96]{1,0:T(1,128)} %param.23) | copy-start | bytes 1156
  10.3 199.9 %copy-start.22 = (f32[1,96]{1,0:T(1,128)S(1)}, f32[1,96]{1,0:T(1,128)}, u32[]{:S(2)}) copy-start(f32[1,96]{1,0:T(1,128)} %param.24) | copy-start | bytes 1156
  10.3 199.9 %copy-start.23 = (f32[1,96]{1,0:T(1,128)S(1)}, f32[1,96]{1,0:T(1,128)}, u32[]{:S(2)}) copy-start(f32[1,96]{1,0:T(1,128)} %param.25) | copy-start | bytes 1156
  10.3 199.9 %copy-start.24 = (f32[1,96]{1,0:T(1,128)S(1)}, f32[1,96]{1,0:T(1,128)}, u32[]{:S(2)}) copy-start(f32[1,96]{1,0:T(1,128)} %param.29) | copy-start | bytes 1156
  10.3 231.5 %copy-start.25 = (s32[2]{0:T(128)S(1)}, s32[2]{0:T(128)}, u32[]{:S(2)}) copy-start(s32[2]{0:T(128)} %param.16) | copy-start | bytes 28
  10.4 1.2 copy-start.8
  11.6 590.0 %reduce-scatter.3.cloned.1.call-start = ((), (), s32[]{:S(2)}) async-start(), calls=%async_computation.4 | async-start | bytes 7962624 | tf_op jit(solution)/shard_map/reduce_scatter | solution.py:478
  210.1 38.3 %collective-permute-start.1 = (bf16[8,12,96,768]{3,2,1,0:T(8,128)(2,1)}, bf16[8,12,96,768]{3,2,1,0:T(8,128)(2,1)}, u32[]{:S(2)}, u32[]{:S(2)}) collective-permute-start(bf16[8,12,96,768]{3,2,1,0:T(8,128)(2,1)} %all-gather.3.cloned.1.call-done.wa), channel_id=1, source_target_pairs={{0,8},{8,0},{16,24},{24,16},{1,9},{9,1},{17,25},{25,17},{2,10},{10... | collective-permute-start | bytes 42467336 | tf_op jit(solution)/shard_map/ppermute | solution.py:378
  241.0 4.5 collective-permute-start
  269.2 23.4 %copy-start.14 = (bf16[2,280,768]{2,1,0:T(8,128)(2,1)S(1)}, bf16[2,280,768]{2,1,0:T(8,128)(2,1)}, u32[]{:S(2)}) copy-start(bf16[2,280,768]{2,1,0:T(8,128)(2,1)} %param.17) | copy-start | bytes 2580484
  289.1 13.8 %collective-permute-start.2 = (bf16[288,768]{1,0:T(8,128)(2,1)}, bf16[288,768]{1,0:T(8,128)(2,1)S(1)}, u32[]{:S(2)}, u32[]{:S(2)}) collective-permute-start(bf16[288,768]{1,0:T(8,128)(2,1)} %forward_layer.5), channel_id=1, source_target_pairs={{0,16},{8,24},{1,17},{9,25},{2,18},{10,26},{3,19},{11,27},{4,20},{... | collective-permute-start | bytes 1327112 | tf_op jit(solution)/shard_map/ppermute | solution.py:373
  393.8 13.9 %collective-permute-start.3 = (bf16[288,768]{1,0:T(8,128)(2,1)}, bf16[288,768]{1,0:T(8,128)(2,1)S(1)}, u32[]{:S(2)}, u32[]{:S(2)}) collective-permute-start(bf16[288,768]{1,0:T(8,128)(2,1)} %backward_layer.5), channel_id=1, source_target_pairs={{16,0},{24,8},{17,1},{25,9},{18,2},{26,10},{19,3},{27,11},{20,4},{... | collective-permute-start | bytes 1327112 | tf_op jit(solution)/shard_map/ppermute | solution.py:373
  395.1 60.7 %collective-permute-start.5 = (bf16[288,4608]{1,0:T(8,128)(2,1)}, bf16[288,4608]{1,0:T(8,128)(2,1)S(1)}, u32[]{:S(2)}, u32[]{:S(2)}) collective-permute-start(bf16[288,4608]{1,0:T(8,128)(2,1)} %get-tuple-element.52), channel_id=1, source_target_pairs={{0,8},{8,0},{16,24},{24,16},{1,9},{9,1},{17,25},{25,17},{2,10},{10... | collective-permute-start | bytes 7962632 | tf_op jit(solution)/shard_map/ppermute | solution.py:378
  455.6 5.2 collective-permute-start.6
  455.7 5.1 copy-start.4
  460.9 1.6 copy-start.6
  475.3 258.6 %reduce-scatter.5.cloned.1.call-start = ((), (), s32[]{:S(2)}) async-start(), calls=%async_computation.5 | async-start | bytes 7962624 | tf_op jit(solution)/shard_map/reduce_scatter | solution.py:478
  475.3 5.2 collective-permute-start.7
  475.5 8.9 %collective-permute-start.8 = (bf16[288,4608]{1,0:T(8,128)(2,1)}, bf16[288,4608]{1,0:T(8,128)(2,1)S(1)}, u32[]{:S(2)}, u32[]{:S(2)}) collective-permute-start(bf16[288,4608]{1,0:T(8,128)(2,1)} %get-tuple-element.57), channel_id=1, source_target_pairs={{0,8},{8,0},{16,24},{24,16},{1,9},{9,1},{17,25},{25,17},{2,10},{10... | collective-permute-start | bytes 7962632 | tf_op jit(solution)/shard_map/ppermute | solution.py:378
  480.6 3.8 copy-start.5
  484.4 1.5 copy-start.7
  498.8 0.7 copy-start.26
  498.8 1.2 copy-start.15
  498.8 1.2 copy-start.16
  498.9 237.1 %copy-start.11 = (bf16[288,768]{1,0:T(8,128)(2,1)S(1)}, bf16[288,768]{1,0:T(8,128)(2,1)}, u32[]{:S(2)}) copy-start(bf16[288,768]{1,0:T(8,128)(2,1)} %get-tuple-element.47) | copy-start | bytes 1327108
  498.9 237.1 %copy-start.12 = (bf16[288,768]{1,0:T(8,128)(2,1)S(1)}, bf16[288,768]{1,0:T(8,128)(2,1)}, u32[]{:S(2)}) copy-start(bf16[288,768]{1,0:T(8,128)(2,1)} %get-tuple-element.46) | copy-start | bytes 1327108
  500.1 240.9 %collective-permute-start.4 = (f32[16,768]{1,0:T(8,128)S(1)}, f32[16,768]{1,0:T(8,128)S(1)}, u32[]{:S(2)}, u32[]{:S(2)}) collective-permute-start(f32[16,768]{1,0:T(8,128)S(1)} %broadcast_select_fusion.3), channel_id=1, source_target_pairs={{0,8},{8,0},{16,24},{24,16},{1,9},{9,1},{17,25},{25,17},{2,10},{10... | collective-permute-start | bytes 147464 | tf_op jit(solution)/shard_map/ppermute | solution.py:378
  736.0 45.9 %collective-permute-start.9 = (bf16[6,96,768]{2,1,0:T(8,128)(2,1)}, bf16[6,96,768]{2,1,0:T(8,128)(2,1)S(1)}, u32[]{:S(2)}, u32[]{:S(2)}) collective-permute-start(bf16[6,96,768]{2,1,0:T(8,128)(2,1)} %select_bitcast_fusion), channel_id=1, source_target_pairs={{0,8},{8,0},{16,24},{24,16},{1,9},{9,1},{17,25},{25,17},{2,10},{10... | collective-permute-start | bytes 2654216 | tf_op jit(solution)/shard_map/ppermute | solution.py:378
  736.6 45.4 %copy-start.2 = (bf16[1,6,96,768]{3,2,1,0:T(8,128)(2,1)S(1)}, bf16[1,6,96,768]{3,2,1,0:T(8,128)(2,1)}, u32[]{:S(2)}) copy-start(bf16[1,6,96,768]{3,2,1,0:T(8,128)(2,1)} %reduce-scatter.3.cloned.1.call-done) | copy-start | bytes 2654212
  736.6 45.4 %copy-start.3 = (bf16[1,6,96,768]{3,2,1,0:T(8,128)(2,1)S(1)}, bf16[1,6,96,768]{3,2,1,0:T(8,128)(2,1)}, u32[]{:S(2)}) copy-start(bf16[1,6,96,768]{3,2,1,0:T(8,128)(2,1)} %reduce-scatter.5.cloned.1.call-done) | copy-start | bytes 2654212
  737.5 43.6 %all-to-all-start = ((bf16[280,4,192]{2,0,1:T(8,128)(2,1)}), bf16[280,4,192]{2,0,1:T(8,128)(2,1)S(1)}, u32[]{:S(2)}, u32[]{:S(2)}) async-start(bf16[280,4,192]{2,0,1:T(8,128)(2,1)} %copy.31), calls=%async_computation | async-start | bytes 1146880 | tf_op jit(solution)/shard_map/all_to_all | solution.py:494
  784.2 2.1 copy-start.1
Sparse Core Ops, SparseCore 0:
  11.8 198.2 all-gather.2
  475.4 126.1 reduce-scatter.2
  605.7 128.0 reduce-scatter.4

commit v2 on v1

v2 whole, which is shorter than its diff:
```python
import functools

import jax
import jax.numpy as jnp
from jax import lax
from jax.experimental import pallas as pl
from jax.experimental.pallas import tpu as pltpu
from jax.sharding import PartitionSpec as P

D = 768
HEADS = 12
FF = 3072
CAPTION = 40
ROWS = 288
HALF = 6
TAIL = 16
EPS = 1e-6
BF = jnp.bfloat16
F32 = jnp.float32
PAIRED = 2 * (D // HEADS)
VMEM_LIMIT = 60 * 2**20
WIDE = FF + 2 * D
AG, AS, BQ, BV, OB, FG, FS, DB, UB = 0, 1, 2, 3, 4, 5, 6, 7, 8

ANYS = pl.BlockSpec(memory_space=pl.ANY)
VM = pl.BlockSpec(memory_space=pltpu.VMEM)
SM = pl.BlockSpec(memory_space=pltpu.SMEM)


def dot(a, b, ca=1, cb=0):
    return lax.dot_general(a, b, (((ca,), (cb,)), ((), ())), preferred_element_type=F32)


def spread_of(v):
    mean = jnp.mean(v, axis=-1, keepdims=True)
    cent = v - mean
    return cent, lax.rsqrt(jnp.mean(cent * cent, axis=-1, keepdims=True) + EPS)


def square(block):
    return block.reshape(D, D)


def weight_scratch(count):
    n, r, per = (8, D // 8, 2) if count > 1 else (1, D, 1)
    return [pltpu.VMEM((8, n, r, D), BF), pltpu.VMEM((4, per, D // per, D), BF), pltpu.VMEM((n, TAIL, D), BF),
            pltpu.SemaphoreType.DMA((13,))]


def start_weights(which, info, sets, scratch, order):
    wv, wd, tv, sems = scratch
    r = wv.shape[2]

    def start(block, j, part):
        if part == 12:
            pltpu.make_async_copy(block.at[pl.ds(12 * r, TAIL)], tv.at[j], sems.at[12]).start()
        elif part < 8:
            pltpu.make_async_copy(block.at[pl.ds(part * r, r)], wv.at[part, j], sems.at[part]).start()
        elif len(sets[0]) == 1:
            pltpu.make_async_copy(block.at[pl.ds(part * r, r)], wd.at[part - 8, 0], sems.at[part]).start()
        elif part == 8:
            b = j // 2
            pltpu.make_async_copy(block.at[pl.ds(8 * r, 4 * r)], wd.at[b, j % 2], sems.at[8 + b]).start()

    for number, blocks in enumerate(sets):
        if len(blocks) == 1:

            @pl.when(info[which] == number)
            def _():
                for part in order:
                    start(blocks[0], 0, part)

            continue
        for middle in (0, 1):

            @pl.when((info[which] == number) & (info[4] == middle))
            def _():
                held = [(0, 0), (1, 1), (2, 3), (4, 2)] if middle else [(0, 0), (1, 1), (3, 2), (5, 3)]
                spots = [(blocks[far * 6 + at], (info[2] ^ flip) * 2 + (info[3] ^ far)) for far in (0, 1) for at, flip in held]
                for part in order:
                    for block, j in spots:
                        start(block, j, part)

    waits = [pltpu.make_async_copy(wv.at[k], wv.at[k], sems.at[k]) for k in range(8)]
    waits += [pltpu.make_async_copy(wd.at[b], wd.at[b], sems.at[8 + b]) for b in range(4)]
    return waits + [pltpu.make_async_copy(tv, tv, sems.at[12])]


def vectors(tv):
    total = tv[0].astype(F32)
    for j in range(1, tv.shape[0]):
        total = total + tv[j].astype(F32)
    return total


def handing(core, keep, send, sems, waits):
    def hand_on(src, first, at):
        wide = src.shape[1]
        sem = sems.at[len(waits)]
        mine = (core == 0) == first

        @pl.when(mine)
        def _():
            pltpu.make_async_copy(src, keep.at[:, pl.ds(at, wide)], sem).start()

        @pl.when(jnp.logical_not(mine))
        def _():
            pltpu.make_async_copy(src, send.at[:, pl.ds(at, wide)], sem).start()

        waits.append(pltpu.make_async_copy(src, keep.at[:, pl.ds(at, wide)], sem))

    return hand_on


def forward_one(save, core, x, usable, copies, scratch, work, osems, saved, outs):
    wv, wd, tv, _ = scratch
    jn, ctx, act, gp, nrm, nt, vec = work
    if save:
        lse_ref, mid_ref, j_hbm, gp_hbm, keep, send = saved
        hand_on = handing(core, keep, send, osems, outs)

        def flush(src, dst):
            c = pltpu.make_async_copy(src, dst, osems.at[len(outs)])
            c.start()
            outs.append(c)

    copies[12].wait()
    vec[...] = vectors(tv)
    cent, inv = spread_of(x)
    nrm[...] = (cent * inv * vec[AG:AG + 1, :] + vec[AS:AS + 1, :]).astype(BF)
    if save:
        hand_on(nrm, True, D)
        hand_on(nrm, False, FF + D)
    for k in range(3):
        copies[k].wait()
        r = dot(nrm[...], square(wv[k]))
        if k == 0:
            r = r + vec[BQ:BQ + 1, :]
        if k == 2:
            r = r + vec[BV:BV + 1, :]
        jn[:, k * D:(k + 1) * D] = r.astype(BF)
    if save:
        flush(jn, j_hbm)
    lane = lax.broadcasted_iota(jnp.int32, (ROWS, PAIRED), 1)
    low = lane < PAIRED // 2
    lse = jnp.zeros((ROWS, PAIRED), F32)
    for i in range(HEADS // 2):
        at = i * PAIRED
        q2 = jn[:, at:at + PAIRED] * BF(0.125)
        k2 = jn[:, D + at:D + at + PAIRED]
        v2 = jn[:, 2 * D + at:2 * D + at + PAIRED]
        zero = jnp.zeros_like(q2)
        both = []
        for h in range(2):
            s = dot(jnp.where(low == (h == 0), q2, zero), k2, 1, 1)
            s = jnp.where(usable, s, -1e30)
            top = jnp.max(s, axis=-1, keepdims=True)
            e = jnp.exp(s - top)
            total = jnp.sum(e, axis=-1, keepdims=True)
            both.append(dot(e.astype(BF), v2) * (1.0 / total))
            if save:
                lse = jnp.where(lane == 2 * i + h, top + jnp.log(total), lse)
        ctx[:, at:at + PAIRED] = jnp.where(low, both[0], both[1]).astype(BF)
    if save:
        lse_ref[...] = lse
        hand_on(ctx, False, FF)
    for k in range(3, 12):
        copies[k].wait()
    middle = x + dot(ctx[...], square(wv[3])) + vec[OB:OB + 1, :]
    if save:
        mid_ref[...] = middle
    cent, inv = spread_of(middle)
    nt[...] = (cent * inv * vec[FG:FG + 1, :] + vec[FS:FS + 1, :]).astype(BF)
    if save:
        hand_on(nt, True, 0)
    acc = middle + vec[DB:DB + 1, :]
    for b in range(4):
        cols = slice(b * D, (b + 1) * D)
        h = dot(nt[...], square(wv[4 + b])) + vec[UB + b:UB + b + 1, :]
        phi = 0.5 + 0.5 * lax.erf(h * (0.5**0.5))
        a = (h * phi).astype(BF)
        if save:
            act[:, cols] = a
            gp[:, cols] = (phi + h * jnp.exp(-0.5 * h * h) * 0.3989422804014327).astype(BF)
        acc = acc + dot(a, square(wd[b]))
    if save:
        hand_on(act, False, 0)
        flush(gp, gp_hbm)
    return acc.astype(BF)


def forward_kernel(save, count, info, x_ref, mask_ref, *rest):
    sets, rest = (rest[:count], rest[count:2 * count]), rest[2 * count:]
    wide = 14 if save else 2
    results, rest = rest[:wide], rest[wide:]
    scratch = [rest[0:4], rest[4:8]]
    rest = rest[8:]
    copies = [start_weights(s, info, sets, scratch[s], (12,) + tuple(range(12))) for s in range(2)]
    usable = mask_ref[0:1, :] > 0.5
    outs = []
    x = x_ref[...]
    for s in range(2):
        work, rest = rest[:7], rest[7:]
        saved = results[2 + 6 * s:8 + 6 * s] if save else ()
        x = forward_one(save, info[5], x.astype(F32), usable, copies[s], scratch[s], work, rest[7 * (1 - s)], saved, outs)
        results[s][...] = x
    for c in outs:
        c.wait()


def forward_stage(save, info, x, mask, wa, wb):
    def sd(cols, t=BF):
        return jax.ShapeDtypeStruct((ROWS, cols), t)

    shapes, specs = [sd(D)] * 2, [VM] * 2
    if save:
        shapes += [sd(PAIRED, F32), sd(D, F32), sd(3 * D), sd(FF), sd(WIDE), sd(WIDE)] * 2
        specs += ([VM, VM] + [ANYS] * 4) * 2
    work = [pltpu.VMEM((ROWS, 3 * D), BF), pltpu.VMEM((ROWS, D), BF), pltpu.VMEM((ROWS, FF), BF),
            pltpu.VMEM((ROWS, FF), BF), pltpu.VMEM((ROWS, D), BF), pltpu.VMEM((ROWS, D), BF), pltpu.VMEM((16, D), F32)]
    return pl.pallas_call(
        functools.partial(forward_kernel, save, len(wa)),
        out_shape=shapes,
        in_specs=[SM, VM, VM] + [ANYS] * (2 * len(wa)),
        out_specs=specs,
        scratch_shapes=weight_scratch(len(wa)) * 2 + work * 2 + [pltpu.SemaphoreType.DMA((14,))],
        compiler_params=pltpu.CompilerParams(vmem_limit_bytes=VMEM_LIMIT),
        cost_estimate=pl.CostEstimate(flops=2 * ROWS * D * D * 26, bytes_accessed=48 * D * D + 2**23, transcendentals=0),
        name="forward_stage",
    )(info, x, mask, *wa, *wb)


def backward_one(save, core, g_ref, x_ref, lse_ref, mid_ref, j_hbm, gp_hbm, usable, copies, scratch, work, isems, osems, results,
                 waits):
    wv, wd, tv, _ = scratch
    jn, gp, dh, dj, b1, vec = work
    hand_on = lambda *a: None
    if save:
        gv_ref, keep_hbm, send_hbm = results
        hand_on = handing(core, keep_hbm, send_hbm, osems, waits)
    hand_on(g_ref, False, 0)
    copies[12].wait()
    vec[...] = vectors(tv)
    d_nt = None
    for b in range(4):
        cols = slice(b * D, (b + 1) * D)
        copies[8 + b].wait()
        if b == 0:
            pltpu.make_async_copy(gp_hbm, gp, isems.at[0]).wait()
        da = dot(g_ref[...], square(wd[b]), 1, 1)
        d = (da * gp[:, cols].astype(F32)).astype(BF)
        dh[:, cols] = d
        copies[4 + b].wait()
        part = dot(d, square(wv[4 + b]), 1, 1)
        d_nt = part if d_nt is None else d_nt + part
    hand_on(dh, True, 0)

    def norm_back(v, dy, gain, row):
        cent, inv = spread_of(v)
        hat = cent * inv
        if save:
            gv_ref[row:row + 1, :] = jnp.sum(dy * hat, axis=0, keepdims=True)
            gv_ref[row + 1:row + 2, :] = jnp.sum(dy, axis=0, keepdims=True)
        t = dy * gain
        return inv * (t - jnp.mean(t, axis=-1, keepdims=True) - hat * jnp.mean(t * hat, axis=-1, keepdims=True))

    d_mid = g_ref[...].astype(F32) + norm_back(mid_ref[...], d_nt, vec[FG:FG + 1, :], FG)
    b1[...] = d_mid.astype(BF)
    hand_on(b1, False, D)
    if save:
        for b in range(4):
            gv_ref[UB + b:UB + b + 1, :] = jnp.sum(dh[:, b * D:(b + 1) * D].astype(F32), axis=0, keepdims=True)
        gv_ref[DB:DB + 1, :] = jnp.sum(g_ref[...].astype(F32), axis=0, keepdims=True)
        gv_ref[OB:OB + 1, :] = jnp.sum(b1[...].astype(F32), axis=0, keepdims=True)
    copies[3].wait()
    d_ctx = dot(b1[...], square(wv[3]), 1, 1).astype(BF)
    pltpu.make_async_copy(j_hbm, jn, isems.at[1]).wait()
    for k in range(3):
        copies[k].wait()
    lane = lax.broadcasted_iota(jnp.int32, (ROWS, PAIRED), 1)
    low = lane < PAIRED // 2
    for i in range(HEADS // 2):
        at = i * PAIRED
        q2 = jn[:, at:at + PAIRED] * BF(0.125)
        k2 = jn[:, D + at:D + at + PAIRED]
        v2 = jn[:, 2 * D + at:2 * D + at + PAIRED]
        do2 = d_ctx[:, at:at + PAIRED]
        zero = jnp.zeros_like(q2)
        res = []
        for h in range(2):
            here = low == (h == 0)
            s = dot(jnp.where(here, q2, zero), k2, 1, 1)
            p = jnp.where(usable, jnp.exp(s - lse_ref[:, 2 * i + h:2 * i + h + 1]), 0.0)
            dp = dot(jnp.where(here, do2, zero), v2, 1, 1)
            inner = jnp.sum(p * dp, axis=-1, keepdims=True)
            dsc = (p * (dp - inner)).astype(BF)
            res.append((dot(dsc, k2) * 0.125, dot(dsc, q2, 0, 0), dot(p.astype(BF), do2, 0, 0)))
        for c in range(3):
            dj[:, c * D + at:c * D + at + PAIRED] = jnp.where(low, res[0][c], res[1][c]).astype(BF)
    hand_on(dj.at[:, pl.ds(0, 2 * D)], True, FF)
    hand_on(dj.at[:, pl.ds(2 * D, D)], False, 2 * D)
    if save:
        gv_ref[BQ:BQ + 1, :] = jnp.sum(dj[:, :D].astype(F32), axis=0, keepdims=True)
        gv_ref[BV:BV + 1, :] = jnp.sum(dj[:, 2 * D:].astype(F32), axis=0, keepdims=True)
        gv_ref[UB + 4:, :] = jnp.zeros((4, D), F32)
    d_n = dot(dj[:, :D], square(wv[0]), 1, 1)
    for k in (1, 2):
        d_n = d_n + dot(dj[:, k * D:(k + 1) * D], square(wv[k]), 1, 1)
    return (d_mid + norm_back(x_ref[...].astype(F32), d_n, vec[AG:AG + 1, :], AG)).astype(BF)


def backward_kernel(save, layers, count, info, g_ref, mask_ref, *rest):
    m = len(layers)
    kept, rest = [rest[5 * i:5 * i + 5] for i in range(m)], rest[5 * m:]
    rest = rest[1:] if save else rest
    sets, rest = (rest[:count], rest[count:2 * count]), rest[2 * count:]
    wide = 4 if save else 1
    results, rest = rest[:wide], rest[wide:]
    scratch, rest = [rest[4 * i:4 * i + 4] for i in range(m)], rest[4 * m:]
    work, (gs, isems, osems) = [rest[6 * i:6 * i + 6] for i in range(m)], rest[6 * m:]
    copies = []
    for i in range(m):
        pltpu.make_async_copy(kept[i][4], work[i][1], isems.at[i, 0]).start()
        copies.append(start_weights(layers[i], info, sets, scratch[i], (12, 8, 9, 10, 11, 4, 5, 6, 7, 3, 0, 1, 2)))
        pltpu.make_async_copy(kept[i][3], work[i][0], isems.at[i, 1]).start()
    usable = mask_ref[0:1, :] > 0.5
    waits = []
    for i in range(m):
        x_ref, lse_ref, mid_ref, j_hbm, gp_hbm = kept[i]
        g = backward_one(save, info[5], g_ref if i == 0 else gs, x_ref, lse_ref, mid_ref, j_hbm, gp_hbm, usable, copies[i],
                         scratch[i], work[i], isems.at[i], osems, results[1:], waits)
        if i + 1 < m:
            gs[...] = g
        else:
            results[0][...] = g
    for c in waits:
        c.wait()


def backward_layers(save, layers, info, g, mask, saved, wa, wb, behind):
    def sd(cols, t=BF, rows=ROWS):
        return jax.ShapeDtypeStruct((rows, cols), t)

    shapes, specs = [sd(D)], [VM]
    if save:
        shapes += [sd(D, F32, 16), sd(WIDE), sd(WIDE)]
        specs += [VM, ANYS, ANYS]
    m = len(layers)
    work = [pltpu.VMEM((ROWS, 3 * D), BF), pltpu.VMEM((ROWS, FF), BF), pltpu.VMEM((ROWS, FF), BF),
            pltpu.VMEM((ROWS, 3 * D), BF), pltpu.VMEM((ROWS, D), BF), pltpu.VMEM((16, D), F32)]
    kept = [a for s in layers for a in saved[s]]
    return pl.pallas_call(
        functools.partial(backward_kernel, save, layers, len(wa)),
        out_shape=shapes,
        in_specs=[SM, VM, VM] + [VM, VM, VM, ANYS, ANYS] * m + [ANYS] * (save + 2 * len(wa)),
        out_specs=specs,
        scratch_shapes=weight_scratch(len(wa)) * m + work * m + [
            pltpu.VMEM((ROWS, D), BF), pltpu.SemaphoreType.DMA((m, 2)), pltpu.SemaphoreType.DMA((5,))],
        compiler_params=pltpu.CompilerParams(vmem_limit_bytes=VMEM_LIMIT),
        cost_estimate=pl.CostEstimate(flops=2 * ROWS * D * D * 14 * m, bytes_accessed=m * (24 * D * D + 2**23), transcendentals=0),
        name="backward_layers",
    )(info, g, mask, *kept, *([behind] if save else []), *wa, *wb)


def product_kernel(n, info, slots, gv, fk, bk, fr, br, *rest):
    outs, (held, sems) = rest[:-2], rest[-2:]
    r = D // n

    def both(a, b, at):
        return jnp.concatenate([a[:, at:at + D], b[:, at:at + D]], axis=0)

    for j in range(n):
        held[j, HALF * r:] = gv[...].astype(BF)

    @pl.when(info[5] == 0)
    def _():
        for c in range(HALF):
            val = dot(both(fk, fr, 0 if c < 4 else D), both(bk, br, c * D), 0, 0).astype(BF)
            for j in range(n):
                held[slots[j], c * r:(c + 1) * r] = val[j * r:(j + 1) * r]

    @pl.when(info[5] != 0)
    def _():
        for c in range(HALF):
            val = dot(both(fk, fr, c * D), both(bk, br, 0 if c < 4 else (c - 3) * D), 0, 0).astype(BF)
            if c < 4 and n > 1:
                for i in range(n // 4):
                    held[slots[c * (n // 4) + i], :4 * r] = val[i * 4 * r:(i + 1) * 4 * r]
            else:
                for j in range(n):
                    held[slots[j], c * r:(c + 1) * r] = val[j * r:(j + 1) * r]

    for j in range(n):
        pltpu.make_async_copy(held.at[j], outs[j], sems.at[j]).start()
    for j in range(n):
        pltpu.make_async_copy(held.at[j], outs[j], sems.at[j]).wait()


def weight_products(n, info, slots, gv, fk, bk, fr, br):
    shape = (HALF * (D // n) + TAIL, D)
    return pl.pallas_call(
        functools.partial(product_kernel, n),
        out_shape=[jax.ShapeDtypeStruct(shape, BF)] * n,
        in_specs=[SM, SM] + [VM] * 5,
        out_specs=[ANYS] * n,
        scratch_shapes=[pltpu.VMEM((n,) + shape, BF), pltpu.SemaphoreType.DMA((n,))],
        compiler_params=pltpu.CompilerParams(vmem_limit_bytes=VMEM_LIMIT),
        cost_estimate=pl.CostEstimate(flops=2 * 2 * ROWS * D * D * 6, bytes_accessed=2**24, transcendentals=0),
        name="weight_products",
    )(info, slots, gv, fk, bk, fr, br)


def moved(value, axis, by):
    peers = lax.axis_size(axis)
    return lax.ppermute(value, axis, [(i, i + by) for i in range(peers) if 0 <= i + by < peers])


def swapped(value):
    peers = lax.axis_size("section")
    return lax.ppermute(value, "section", [(i, i ^ 1) for i in range(peers)])


def vector_tail(n, spot, attend_gain, attend_shift, joint_bias, output_bias, feed_gain, feed_shift, down_bias, up_bias):
    lane = jnp.arange(D)

    def row(v, times, at, live=True):
        return jnp.where((lane // v.shape[0] == at) & live, jnp.tile(v, times), 0.0)

    half, quarter = n // 2, n // 4
    rows = [row(attend_gain, n, spot), row(attend_shift, n, spot)]
    rows += [row(joint_bias, half, spot % half, spot // half == k) for k in range(2)]
    rows += [row(v, n, spot) for v in (output_bias, feed_gain, feed_shift, down_bias)]
    rows += [row(up_bias, quarter, spot % quarter, spot // quarter == k) for k in range(4)]
    return jnp.concatenate([jnp.stack(rows), jnp.zeros((4, D), F32)])


def pack_shard(joint, output, up, down, tail):
    pieces = [joint[:, k * D:(k + 1) * D] for k in range(3)] + [output]
    pieces += [up[:, k * D:(k + 1) * D] for k in range(4)]
    return jnp.concatenate(pieces + [down, tail]).astype(BF)


def kernel_form(n, g, tail):
    r = D // n
    cut = jnp.swapaxes(g[:, :8 * r].reshape(n, 8, r, D), 0, 1).reshape(8 * D, D)
    return [jnp.concatenate([cut, g[:, 8 * r:12 * r].reshape(FF, D), tail.astype(BF)])]


IN, OUT, MID, PAIR = ((0, 1), (3, 2)), ((1, 0), (2, 3)), ((1, 2), (2, 1)), ((0, 1), (1, 0), (2, 3), (3, 2))
ENDS, MIDS = (0, 3), (1, 2)


def along(value, moves):
    return lax.ppermute(value, "dp", [(2 * a + x, 2 * b + x) for a, b in moves for x in range(2)])


def across(value, lines=(0, 1, 2, 3)):
    return lax.ppermute(value, "dp", [(2 * z + x, 2 * z + 1 - x) for z in lines for x in range(2)])


def core_swap(value, lines=(0, 1, 2, 3)):
    n, peers = lax.axis_size("dp"), lax.axis_size("section")
    pairs = [(s * n + 2 * z + x, (s ^ 1) * n + 2 * z + x) for s in range(peers) for z in lines for x in range(2)]
    return lax.ppermute(value, ("section", "dp"), pairs)


def gather_blocks(own):
    one = along(own, PAIR)
    mid = along(own, MID)
    far = along(mid, OUT)
    back = along(one, MID)
    last = along(back, OUT)
    column = [own, one, mid, far, back, last]
    lines = [(0, 1, 2, 3), (0, 1, 2, 3), MIDS, ENDS, MIDS, ENDS]
    mine = column + [across(b, l) for b, l in zip(column, lines)]
    return mine, [core_swap(b, l) for b, l in zip(mine, lines * 2)]


def add(*terms):
    total = terms[0].astype(F32)
    for t in terms[1:]:
        total = total + t.astype(F32)
    return total.astype(BF)


def scatter_blocks(blocks):
    s = [add(blocks[k], across(blocks[4 + k])) for k in range(4)]
    a1 = along(s[0], IN)
    a2 = along(s[1], IN)
    b2 = along(add(s[0], a1), MID)
    a3 = along(s[2], IN)
    b3 = along(add(s[1], a2), MID)
    c3 = along(add(s[2], b2), OUT)
    return add(s[3], a3, b3, c3)


def shards(tokens, lengths, cotangent, attend_gain, attend_shift, joint_weight, joint_bias, output_weight,
           output_bias, feed_gain, feed_shift, up_weight, up_bias, down_weight, down_bias):
    n = lax.axis_size("dp")
    r = D // n
    lined = n == 8
    nk = n if lined else 1
    sections = lax.axis_size("section")
    stages = sections // 2
    index = lax.axis_index("section")
    core, stage = index % 2, index // 2
    seq = tokens.shape[1]
    spot = lax.axis_index("dp")
    z, column = spot // 2, spot % 2
    middle = (z == 1) | (z == 2)
    info = jnp.stack([core, 1 - core, z, column, middle.astype(jnp.int32), core]).astype(jnp.int32)
    if lined:
        order = jnp.array([[3, 2, 1, 0], [2, 3, 1, 0], [0, 1, 3, 2], [0, 1, 2, 3]], jnp.int32)[z]
        slots = jnp.stack([order[j // 2] + jnp.where(column == j % 2, 0, 4) for j in range(8)]).astype(jnp.int32)
    else:
        slots = jnp.zeros((1,), jnp.int32)

    tail = vector_tail(n, spot, attend_gain[0], attend_shift[0], joint_bias[0], output_bias[0], feed_gain[0], feed_shift[0],
                       down_bias[0], up_bias[0])
    packed = pack_shard(joint_weight[0], output_weight[0], up_weight[0], down_weight[0], tail)
    if lined:
        wa, wb = gather_blocks(packed)
    else:
        gathered = lax.all_gather(packed, "dp")
        tails = lax.psum(tail.astype(BF).astype(F32), "dp")
        wa, wb = kernel_form(n, gathered, tails), kernel_form(n, swapped(gathered), swapped(tails))

    def own_pair(a):
        return lax.dynamic_index_in_dim(a, core, 0, False)

    def padded(a):
        return jnp.pad(a, ((0, ROWS - seq), (0, 0)))

    places = lax.broadcasted_iota(jnp.int32, (8, ROWS), 1)
    mask = (((places < own_pair(lengths)) | (places >= CAPTION)) & (places < seq)).astype(F32)
    own_tokens = padded(own_pair(tokens))
    own_cotangent = padded(own_pair(cotangent))

    x = own_tokens
    for t in range(stages):
        last = t == stages - 1
        got = forward_stage(last, info, x, mask, wa, wb)
        if not last:
            x = jnp.where(stage == 0, own_tokens, moved(got[1], "section", 2))
    leaving = got[1]
    saved = [(x, *got[2:6]), (got[0], *got[8:12])]
    kept = [got[6], got[12]]
    received = [swapped(got[7]), swapped(got[13])]

    g = own_cotangent
    for t in range(stages - 1):
        g = backward_layers(False, (1, 0), info, g, mask, saved, wa, wb, None)[0]
        g = jnp.where(stage == stages - 1, own_cotangent, moved(g, "section", -2))
    products = [None, None]
    behind = mask
    for s in (1, 0):
        g, gv, bk, bs = backward_layers(True, (s,), info, g, mask, saved, wa, wb, behind)
        products[s] = weight_products(nk, info, slots, gv, kept[s], bk, received[s], swapped(bs))
        behind = products[s][0]

    ends = jnp.where(stage == 0, g, leaving)[:seq].reshape(seq, sections, D // sections)
    pieces = lax.all_to_all(ends, "section", split_axis=1, concat_axis=0, tiled=True).reshape(sections, seq, D // sections)
    outputs = pieces[sections - 2:]
    token_grad = pieces[:2]

    reduced = [None, None]
    for s in (1, 0):
        if lined:
            reduced[s] = scatter_blocks(products[s])
        else:
            p = products[s][0]
            col = jnp.swapaxes(p[:HALF * D].reshape(HALF, n, r, D), 0, 1).reshape(n, HALF * r, D)
            row = jnp.concatenate([p[:4 * D].reshape(n, 4 * r, D), col[:, 4 * r:]], axis=1)
            total = lax.psum_scatter(jnp.where(core == 0, col, row), "dp", scatter_dimension=0)
            reduced[s] = jnp.concatenate([total, lax.psum(p[HALF * D:], "dp")])
    sent = [lax.ppermute(reduced[s], "section", [(i, i ^ 1) for i in range(sections) if i % 2 != s]) for s in range(2)]
    keep = jnp.where(core == 0, reduced[0], reduced[1])
    away = jnp.where(core == 0, sent[0], sent[1])
    first = jnp.where(core == 0, keep, away).astype(F32)
    second = jnp.where(core == 0, away, keep).astype(F32)
    grad_up = jnp.concatenate([first[k * r:(k + 1) * r] for k in range(4)], axis=1)
    grad_joint = jnp.concatenate([first[4 * r:5 * r], first[5 * r:6 * r], second[5 * r:6 * r]], axis=1)
    grad_down = second[:4 * r]
    grad_out = second[4 * r:5 * r]
    v = first[6 * r:] + second[6 * r:]
    half, quarter = n // 2, n // 4
    vec = lax.dynamic_slice(v, (0, r * spot), (16, r))
    grad_jb = lax.dynamic_slice(v, (BQ + spot // half, 2 * r * (spot % half)), (1, 2 * r))
    grad_ub = lax.dynamic_slice(v, (UB + spot // quarter, 4 * r * (spot % quarter)), (1, 4 * r))
    return (outputs, token_grad, vec[AG:AG + 1], vec[AS:AS + 1], grad_joint[None], grad_jb, grad_out[None],
            vec[OB:OB + 1], vec[FG:FG + 1], vec[FS:FS + 1], grad_up[None], grad_ub, grad_down[None], vec[DB:DB + 1])


def solution(mesh):
    vec, mat = P("section", "dp"), P("section", "dp", None)
    rows = P("dp", None, None)
    out = P("dp", None, "section")
    return jax.shard_map(
        shards,
        mesh=mesh,
        in_specs=(rows, P("dp"), rows, vec, vec, mat, vec, mat, vec, vec, vec, mat, vec, mat, vec),
        out_specs=(out, out, vec, vec, mat, vec, mat, vec, vec, vec, mat, vec, mat, vec),
        check_vma=False,
    )
```

time: 799 us -> 570 us (0.71)
  waiting for transfers between devices: 468 us -> 259 us
  starting transfers between devices: 9.22 us -> 109 us
  blocking collectives: 66.1 us -> 0 us
  Pallas kernels: 203 us -> 149 us
    reduce_scatter x2 -> x0, waiting for transfers between devices: 234 us -> none  [shards(): reduced[s] = lax.psum_scatter(p, 'dp', scatter_dimension=0)]
    ppermute x0 -> x45, waiting for transfers between devices: none -> 226 us  [the longest x17 122 us: along(): lax.ppermute(value, 'dp', [(2 * a + x, 2 * b + x) for a, b in moves for x...]
    all_gather x1 -> x0, waiting for transfers between devices: 198 us -> none  [shards(): mine = lax.all_gather(packed, 'dp')]
    ppermute x0 -> x45, starting transfers between devices: none -> 100 us  [the longest x17 58.4 us: along(): lax.ppermute(value, 'dp', [(2 * a + x, 2 * b + x) for a, b in moves for x...]
    pallas_call x10 -> x7, Pallas kernels: 203 us -> 149 us  [the longest x3 74.3 us: backward_layers(): pl.pallas_call(functools.partial(backward_kernel, save, layers, len(wa)),...]
    unnamed x1 -> x0, blocking collectives: 35.6 us -> none
    all_gather x1 -> x0, blocking collectives: 30.6 us -> none  [shards(): small = lax.all_gather(small, 'dp')]
    ppermute x8 -> x4, waiting for transfers between devices: 13.6 us -> 2.98 us  [swapped(): return lax.ppermute(value, 'section', [(i, i ^ 1) for i in range(peers)])]
  transfers between devices with their start and end apart: 14 -> 52, of which waited for: 8 -> 22; matrix products, arithmetic and copies ran while one was open for 2% -> 3% of each run, Pallas kernels for 8% -> 12%
where the time goes in v2:
time: 570 us; the launch traced here: 564 us
  waiting for transfers between devices  259 us (45%)
  Pallas kernels  149 us (26%)
  starting transfers between devices  109 us (19%)
  local copies, waits for them, and re-layouts  23.9 us (4%)
  other arithmetic  14.9 us (3%)
  between operations  7.27 us (1%)
    ppermute x17, waiting for transfers between devices, along(): lax.ppermute(value, 'dp', [(2 * a + x, 2 * b + x) for a, b in moves for x...  122 us
    ppermute x14, waiting for transfers between devices, across(): lax.ppermute(value, 'dp', [(2 * z + x, 2 * z + 1 - x) for z in lines for...  104 us
    pallas_call x3, Pallas kernels, backward_layers(): pl.pallas_call(functools.partial(backward_kernel, save, layers, len(wa)),...  74.3 us
    ppermute x17, starting transfers between devices, along(): lax.ppermute(value, 'dp', [(2 * a + x, 2 * b + x) for a, b in moves for x...  58.4 us
    pallas_call x2, Pallas kernels, forward_stage(): pl.pallas_call(functools.partial(forward_kernel, save, len(wa)), out_shap...  48.8 us
    pallas_call x2, Pallas kernels, weight_products(): pl.pallas_call(functools.partial(product_kernel, n), out_shape=[jax.Shape...  26.3 us
    ppermute x14, starting transfers between devices, across(): lax.ppermute(value, 'dp', [(2 * z + x, 2 * z + 1 - x) for z in lines for...  24.6 us
    ppermute x2, waiting for transfers between devices, moved(): lax.ppermute(value, axis, [(i, i + by) for i in range(peers) if 0 <= i +...  20.4 us
  transfers between devices with their start and end apart: 52, of which 22 were waited for; matrix products, arithmetic and copies ran while one was open for 3% of the time, Pallas kernels for 12%

profile of v2, /device:TPU:0, one launch (start us, length us, event | category | flops | bytes accessed | tf_op | source)
XLA Modules:
  0.0 563.7 jit_solution(7895326562275279224)
XLA Ops:
  7.3 7.5 %concatenate.10.rest_0_.rest_10_.rest_6_ = bf16[1168,768]{1,0:T(8,128)(2,1)S(1)} concatenate(bf16[96,768]{1,0:T(8,128)(2,1)} %get-tuple-element.139, bf16[96,768]{1,0:T(8,128)(2,1)} %get-tuple-element.140, bf16[96,768]{1,0:T(8,128)(2,1)} %get-tuple-element.141, bf16[96,768]{1,0:T(8,128)(2,1)} %convert_bitcast_fusion.3, bf16[96,768]{1,0:T(8,128)(2,1)} %get-tuple-element.109, ...), dimensions={0} | concatenate | bytes 3588096 | tf_op jit(solution)/shard_map/concatenate | solution.py:440
  15.6 5.8 %collective-permute-start = (bf16[1168,768]{1,0:T(8,128)(2,1)S(1)}, bf16[1168,768]{1,0:T(8,128)(2,1)S(1)}, u32[]{:S(2)}, u32[]{:S(2)}) collective-permute-start(bf16[1168,768]{1,0:T(8,128)(2,1)S(1)} %concatenate.10.rest_0_.rest_10_.rest_6_), channel_id=1, source_target_pairs={{0,2},{1,3},{2,0},{3,1},{4,6},{5,7},{6,4},{7,5},{8,10},{9,11},{10,... | collective-permute-start | bytes 5382152 | tf_op jit(solution)/shard_map/ppermute | solution.py:454
  24.2 36.1 %collective-permute-done.rest_1_.rest_11_.rest_7_ = bf16[1168,768]{1,0:T(8,128)(2,1)S(1)} collective-permute-done((bf16[1168,768]{1,0:T(8,128)(2,1)S(1)}, bf16[1168,768]{1,0:T(8,128)(2,1)S(1)}, u32[]{:S(2)}, u32[]{:S(2)}) %collective-permute-start) | collective-permute-done | bytes 1794080 | tf_op jit(solution)/shard_map/ppermute | solution.py:454
  61.0 1.6 collective-permute-start.6
  62.6 1.9 collective-permute-start.7
  64.4 35.7 %collective-permute-done.2.rest_3_.rest_13_.rest_9_ = bf16[1168,768]{1,0:T(8,128)(2,1)S(1)} collective-permute-done((bf16[1168,768]{1,0:T(8,128)(2,1)S(1)}, bf16[1168,768]{1,0:T(8,128)(2,1)S(1)}, u32[]{:S(2)}, u32[]{:S(2)}) %collective-permute-start.2) | collective-permute-done | bytes 1794080 | tf_op jit(solution)/shard_map/ppermute | solution.py:454
  102.4 3.4 collective-permute-start.8
  105.8 1.9 collective-permute-start.9
  107.7 2.0 collective-permute-start.14
  110.6 34.5 %collective-permute-done.4.rest_5_.rest_15_.rest_11_ = bf16[1168,768]{1,0:T(8,128)(2,1)} collective-permute-done((bf16[1168,768]{1,0:T(8,128)(2,1)S(1)}, bf16[1168,768]{1,0:T(8,128)(2,1)}, u32[]{:S(2)}, u32[]{:S(2)}) %collective-permute-start.4) | collective-permute-done | bytes 1794080 | tf_op jit(solution)/shard_map/ppermute | solution.py:454
  145.8 3.4 collective-permute-start.10
  149.2 1.9 collective-permute-start.19
  151.2 1.9 collective-permute-start.16
  153.1 2.4 collective-permute-start.20
  155.6 1.9 collective-permute-start.21
  157.5 31.3 %collective-permute-done.10.rest_11_.rest_21_.rest_17_ = bf16[1168,768]{1,0:T(8,128)(2,1)} collective-permute-done((bf16[1168,768]{1,0:T(8,128)(2,1)}, bf16[1168,768]{1,0:T(8,128)(2,1)}, u32[]{:S(2)}, u32[]{:S(2)}) %collective-permute-start.10) | collective-permute-done | bytes 1794080 | tf_op jit(solution)/shard_map/ppermute | solution.py:458
  188.9 1.9 collective-permute-start.22
  195.4 22.7 %forward_stage.2 = (bf16[288,768]{1,0:T(8,128)(2,1)}, bf16[288,768]{1,0:T(8,128)(2,1)}) custom-call(s32[6]{0:T(128)} %stack.67.info, bf16[288,768]{1,0:T(8,128)(2,1)} %pad.8.x_ref, f32[8,288]{1,0:T(8,128)} %iota.36.mask_ref.rest_5_, bf16[1168,768]{1,0:T(8,128)(2,1)} %copy-done.2, bf16[1168,768]{1,0:T(8,128)(2,1)} %copy-done.4, bf16[1168,768]{1,0:T(8,128)(2,1)} %copy-done.3, ...), custom_call_target="tpu_custom_call" | custom-call | flops 8833204224 | bytes 36700160 | tf_op jit(solution)/shard_map/forward_stage/pallas_call | solution.py:221
  218.2 3.5 collective-permute-start.23
  223.5 8.2 %collective-permute-done.23 = bf16[288,768]{1,0:T(8,128)(2,1)S(1)} collective-permute-done((bf16[288,768]{1,0:T(8,128)(2,1)}, bf16[288,768]{1,0:T(8,128)(2,1)S(1)}, u32[]{:S(2)}, u32[]{:S(2)}) %collective-permute-start.23) | collective-permute-done | bytes 442400 | tf_op jit(solution)/shard_map/ppermute | solution.py:415
  232.5 26.0 %forward_stage.3 = (bf16[288,768]{1,0:T(8,128)(2,1)}, bf16[288,768]{1,0:T(8,128)(2,1)}, f32[288,128]{1,0:T(8,128)}, f32[288,768]{1,0:T(8,128)}, bf16[288,2304]{1...) custom-call(s32[6]{0:T(128)} %stack.67.info, ...), custom_call_target="tpu_custom_call" | custom-call | flops 8833204224 | bytes 36700160 | tf_op jit(solution)/shard_map/forward_stage/pallas_call | solution.py:221
  258.6 34.5 %backward_layers.3 = bf16[288,768]{1,0:T(8,128)(2,1)} custom-call(s32[6]{0:T(128)} %stack.67.info, bf16[288,768]{1,0:T(8,128)(2,1)} %pad.7.g_ref, f32[8,288]{1,0:T(8,128)} %iota.36.mask_ref.rest_5_, bf16[288,768]{1,0:T(8,128)(2,1)} %get-tuple-element.54.rest_0_, f32[288,128]{1,0:T(8,128)} %get-tuple-element.55.rest_1_, ...), custom_call_target="tpu_custom_call" | custom-call | flops 9512681472 | bytes 45088768 | tf_op jit(solution)/shard_map/backward_layers/pallas_call | solution.py:352
  294.5 12.2 %collective-permute-done.24 = bf16[288,768]{1,0:T(8,128)(2,1)S(1)} collective-permute-done((bf16[288,768]{1,0:T(8,128)(2,1)}, bf16[288,768]{1,0:T(8,128)(2,1)S(1)}, u32[]{:S(2)}, u32[]{:S(2)}) %collective-permute-start.24) | collective-permute-done | bytes 442400 | tf_op jit(solution)/shard_map/ppermute | solution.py:415
  307.6 19.9 %backward_layers.4 = (bf16[288,768]{1,0:T(8,128)(2,1)}, f32[16,768]{1,0:T(8,128)}, bf16[288,4608]{1,0:T(8,128)(2,1)}, bf16[288,4608]{1,0:T(8,128)(2,1)}) custom-call(s32[6]{0:T(128)} %stack.67.info, bf16[288,768]{1,0:T(8,128)(2,1)} %broadcast_select_fusion.2.g_ref, f32[8,288]{1,0:T(8,128)} %iota.36.mask_ref.rest_5_, ...), custom_call_target="tpu_custom_call" | custom-call | flops 4756340736 | bytes 22544384 | tf_op jit(solution)/shard_map/backward_layers/pallas_call | solution.py:352
  335.2 13.1 %weight_products.2 = (bf16[592,768]{1,0:T(8,128)(2,1)}, bf16[592,768]{1,0:T(8,128)(2,1)}, bf16[592,768]{1,0:T(8,128)(2,1)}, bf16[592,768]{1,0:T(8,128)(2,1)}, bf...) custom-call(s32[6]{0:T(128)} %stack.67.info, ...), custom_call_target="tpu_custom_call" | custom-call | flops 4076863488 | bytes 16777216 | tf_op jit(solution)/shard_map/weight_products/pallas_call | solution.py:401
  348.3 19.9 %backward_layers.5 = (bf16[288,768]{1,0:T(8,128)(2,1)}, f32[16,768]{1,0:T(8,128)}, bf16[288,4608]{1,0:T(8,128)(2,1)}, bf16[288,4608]{1,0:T(8,128)(2,1)}) custom-call(s32[6]{0:T(128)} %stack.67.info, bf16[288,768]{1,0:T(8,128)(2,1)} %get-tuple-element.63.g_ref, f32[8,288]{1,0:T(8,128)} %iota.36.mask_ref.rest_5_, ...), custom_call_target="tpu_custom_call" | custom-call | flops 4756340736 | bytes 22544384 | tf_op jit(solution)/shard_map/backward_layers/pallas_call | solution.py:352
  370.5 3.0 collective-permute-done.28.br
  375.0 13.2 %weight_products.3 = (bf16[592,768]{1,0:T(8,128)(2,1)}, bf16[592,768]{1,0:T(8,128)(2,1)}, bf16[592,768]{1,0:T(8,128)(2,1)}, bf16[592,768]{1,0:T(8,128)(2,1)}, bf...) custom-call(s32[6]{0:T(128)} %stack.67.info, ...), custom_call_target="tpu_custom_call" | custom-call | flops 4076863488 | bytes 16777216 | tf_op jit(solution)/shard_map/weight_products/pallas_call | solution.py:401
  389.7 2.0 collective-permute-done.45
  391.9 7.4 %collective-permute-start.46 = (bf16[592,768]{1,0:T(8,128)(2,1)S(1)}, bf16[592,768]{1,0:T(8,128)(2,1)S(1)}, u32[]{:S(2)}, u32[]{:S(2)}) collective-permute-start(bf16[592,768]{1,0:T(8,128)(2,1)S(1)} %add_convert_fusion.3), channel_id=1, source_target_pairs={{0,2},{1,3},{6,4},{7,5},{8,10},{9,11},{14,12},{15,13},{16,18},{17,... | collective-permute-start | bytes 2727944 | tf_op jit(solution)/shard_map/ppermute | solution.py:454
  399.4 1.5 collective-permute-start.32
  400.9 10.3 %collective-permute-done.42 = bf16[592,768]{1,0:T(8,128)(2,1)S(1)} collective-permute-done((bf16[592,768]{1,0:T(8,128)(2,1)S(1)}, bf16[592,768]{1,0:T(8,128)(2,1)S(1)}, u32[]{:S(2)}, u32[]{:S(2)}) %collective-permute-start.42) | collective-permute-done | bytes 909344 | tf_op jit(solution)/shard_map/ppermute | solution.py:458
  411.5 7.4 %collective-permute-start.43 = (bf16[592,768]{1,0:T(8,128)(2,1)S(1)}, bf16[592,768]{1,0:T(8,128)(2,1)S(1)}, u32[]{:S(2)}, u32[]{:S(2)}) collective-permute-start(bf16[592,768]{1,0:T(8,128)(2,1)S(1)} %add_convert_fusion.5), channel_id=1, source_target_pairs={{0,2},{1,3},{6,4},{7,5},{8,10},{9,11},{14,12},{15,13},{16,18},{17,... | collective-permute-start | bytes 2727944 | tf_op jit(solution)/shard_map/ppermute | solution.py:454
  418.9 11.8 %collective-permute-done.35 = bf16[592,768]{1,0:T(8,128)(2,1)S(1)} collective-permute-done((bf16[592,768]{1,0:T(8,128)(2,1)}, bf16[592,768]{1,0:T(8,128)(2,1)S(1)}, u32[]{:S(2)}, u32[]{:S(2)}) %collective-permute-start.35) | collective-permute-done | bytes 909344 | tf_op jit(solution)/shard_map/ppermute | solution.py:458
  431.0 7.4 %collective-permute-start.36 = (bf16[592,768]{1,0:T(8,128)(2,1)S(1)}, bf16[592,768]{1,0:T(8,128)(2,1)S(1)}, u32[]{:S(2)}, u32[]{:S(2)}) collective-permute-start(bf16[592,768]{1,0:T(8,128)(2,1)S(1)} %add_convert_fusion.11), channel_id=1, source_target_pairs={{0,2},{1,3},{6,4},{7,5},{8,10},{9,11},{14,12},{15,13},{16,18},{17,... | collective-permute-start | bytes 2727944 | tf_op jit(solution)/shard_map/ppermute | solution.py:454
  441.0 9.2 %collective-permute-done.32 = bf16[592,768]{1,0:T(8,128)(2,1)S(1)} collective-permute-done((bf16[592,768]{1,0:T(8,128)(2,1)S(1)}, bf16[592,768]{1,0:T(8,128)(2,1)S(1)}, u32[]{:S(2)}, u32[]{:S(2)}) %collective-permute-start.32) | collective-permute-done | bytes 909344 | tf_op jit(solution)/shard_map/ppermute | solution.py:458
  451.9 7.4 %collective-permute-start.33 = (bf16[592,768]{1,0:T(8,128)(2,1)S(1)}, bf16[592,768]{1,0:T(8,128)(2,1)S(1)}, u32[]{:S(2)}, u32[]{:S(2)}) collective-permute-start(bf16[592,768]{1,0:T(8,128)(2,1)S(1)} %add_convert_fusion.13), channel_id=1, source_target_pairs={{0,2},{1,3},{6,4},{7,5},{8,10},{9,11},{14,12},{15,13},{16,18},{17,... | collective-permute-start | bytes 2727944 | tf_op jit(solution)/shard_map/ppermute | solution.py:454
  460.6 9.1 %collective-permute-done.40 = bf16[592,768]{1,0:T(8,128)(2,1)S(1)} collective-permute-done((bf16[592,768]{1,0:T(8,128)(2,1)S(1)}, bf16[592,768]{1,0:T(8,128)(2,1)S(1)}, u32[]{:S(2)}, u32[]{:S(2)}) %collective-permute-start.40) | collective-permute-done | bytes 909344 | tf_op jit(solution)/shard_map/ppermute | solution.py:458
  472.3 16.9 %collective-permute-done.30 = bf16[592,768]{1,0:T(8,128)(2,1)S(1)} collective-permute-done((bf16[592,768]{1,0:T(8,128)(2,1)S(1)}, bf16[592,768]{1,0:T(8,128)(2,1)S(1)}, u32[]{:S(2)}, u32[]{:S(2)}) %collective-permute-start.30) | collective-permute-done | bytes 909344 | tf_op jit(solution)/shard_map/ppermute | solution.py:458
  490.4 7.6 %collective-permute-start.41 = (bf16[592,768]{1,0:T(8,128)(2,1)S(1)}, bf16[592,768]{1,0:T(8,128)(2,1)S(1)}, u32[]{:S(2)}, u32[]{:S(2)}) collective-permute-start(bf16[592,768]{1,0:T(8,128)(2,1)S(1)} %get-tuple-element.93), channel_id=1, source_target_pairs={{0,2},{1,3},{6,4},{7,5},{8,10},{9,11},{14,12},{15,13},{16,18},{17,... | collective-permute-start | bytes 2727944 | tf_op jit(solution)/shard_map/ppermute | solution.py:454
  500.3 8.3 %collective-permute-done.39 = bf16[592,768]{1,0:T(8,128)(2,1)S(1)} collective-permute-done((bf16[592,768]{1,0:T(8,128)(2,1)S(1)}, bf16[592,768]{1,0:T(8,128)(2,1)S(1)}, u32[]{:S(2)}, u32[]{:S(2)}) %collective-permute-start.39) | collective-permute-done | bytes 909344 | tf_op jit(solution)/shard_map/ppermute | solution.py:458
  510.7 4.4 collective-permute-done.48
  515.1 5.7 %collective-permute-start.31 = (bf16[592,768]{1,0:T(8,128)(2,1)S(1)}, bf16[592,768]{1,0:T(8,128)(2,1)S(1)}, u32[]{:S(2)}, u32[]{:S(2)}) collective-permute-start(bf16[592,768]{1,0:T(8,128)(2,1)S(1)} %get-tuple-element.95), channel_id=1, source_target_pairs={{0,2},{1,3},{6,4},{7,5},{8,10},{9,11},{14,12},{15,13},{16,18},{17,... | collective-permute-start | bytes 2727944 | tf_op jit(solution)/shard_map/ppermute | solution.py:454
  521.5 2.2 collective-permute-start.50
  523.7 3.9 collective-permute-done.29
  527.6 10.2 %collective-permute-done.38 = bf16[592,768]{1,0:T(8,128)(2,1)S(1)} collective-permute-done((bf16[592,768]{1,0:T(8,128)(2,1)S(1)}, bf16[592,768]{1,0:T(8,128)(2,1)S(1)}, u32[]{:S(2)}, u32[]{:S(2)}) %collective-permute-start.38) | collective-permute-done | bytes 909344 | tf_op jit(solution)/shard_map/ppermute | solution.py:454
  542.4 3.5 all-to-all-start
  545.9 9.3 %all-to-all-done = bf16[280,4,192]{2,0,1:T(8,128)(2,1)S(1)} async-done(((bf16[280,4,192]{2,0,1:T(8,128)(2,1)}), bf16[280,4,192]{2,0,1:T(8,128)(2,1)S(1)}, u32[]{:S(2)}, u32[]{:S(2)}) %all-to-all-start) | async-done | bytes 430112 | tf_op jit(solution)/shard_map/all_to_all | solution.py:562
  (220 shorter events, 59.7 us)
Async XLA Ops:
  14.8 8.1 %collective-permute-start.1 = (bf16[1168,768]{1,0:T(8,128)(2,1)S(1)}, bf16[1168,768]{1,0:T(8,128)(2,1)S(1)}, u32[]{:S(2)}, u32[]{:S(2)}) collective-permute-start(bf16[1168,768]{1,0:T(8,128)(2,1)S(1)} %concatenate.10.rest_0_.rest_10_.rest_6_), channel_id=1, source_target_pairs={{2,4},{3,5},{4,2},{5,3},{10,12},{11,13},{12,10},{13,11},{18,20},{1... | collective-permute-start | bytes 5382152 | tf_op jit(solution)/shard_map/ppermute | solution.py:454
  15.6 44.7 %collective-permute-start = (bf16[1168,768]{1,0:T(8,128)(2,1)S(1)}, bf16[1168,768]{1,0:T(8,128)(2,1)S(1)}, u32[]{:S(2)}, u32[]{:S(2)}) collective-permute-start(bf16[1168,768]{1,0:T(8,128)(2,1)S(1)} %concatenate.10.rest_0_.rest_10_.rest_6_), channel_id=1, source_target_pairs={{0,2},{1,3},{2,0},{3,1},{4,6},{5,7},{6,4},{7,5},{8,10},{9,11},{10,... | collective-permute-start | bytes 5382152 | tf_op jit(solution)/shard_map/ppermute | solution.py:454
  21.4 41.2 %collective-permute-start.5 = (bf16[1168,768]{1,0:T(8,128)(2,1)S(1)}, bf16[1168,768]{1,0:T(8,128)(2,1)S(1)}, u32[]{:S(2)}, u32[]{:S(2)}) collective-permute-start(bf16[1168,768]{1,0:T(8,128)(2,1)S(1)} %concatenate.10.rest_0_.rest_10_.rest_6_), channel_id=1, source_target_pairs={{0,1},{1,0},{2,3},{3,2},{4,5},{5,4},{6,7},{7,6},{8,9},{9,8},{10,11... | collective-permute-start | bytes 5382152 | tf_op jit(solution)/shard_map/ppermute | solution.py:458
  22.9 41.6 %collective-permute-start.11 = (bf16[1168,768]{1,0:T(8,128)(2,1)S(1)}, bf16[1168,768]{1,0:T(8,128)(2,1)S(1)}, u32[]{:S(2)}, u32[]{:S(2)}) collective-permute-start(bf16[1168,768]{1,0:T(8,128)(2,1)S(1)} %concatenate.10.rest_0_.rest_10_.rest_6_), channel_id=1, source_target_pairs={{0,8},{1,9},{2,10},{3,11},{4,12},{5,13},{6,14},{7,15},{8,0},{9,1},... | collective-permute-start | bytes 5382152 | tf_op jit(solution)/shard_map/ppermute | solution.py:464
  22.9 77.2 %collective-permute-start.2 = (bf16[1168,768]{1,0:T(8,128)(2,1)S(1)}, bf16[1168,768]{1,0:T(8,128)(2,1)S(1)}, u32[]{:S(2)}, u32[]{:S(2)}) collective-permute-start(bf16[1168,768]{1,0:T(8,128)(2,1)S(1)} %collective-permute-done.1.rest_2_.rest_12_.rest_8_), channel_id=1, source_target_pairs={{2,0},{3,1},{4,6},{5,7},{10,8},{11,9},{12,14},{13,15},{18,16},{19,... | collective-permute-start | bytes 5382152 | tf_op jit(solution)/shard_map/ppermute | solution.py:454
  60.2 40.7 %collective-permute-start.3 = (bf16[1168,768]{1,0:T(8,128)(2,1)S(1)}, bf16[1168,768]{1,0:T(8,128)(2,1)S(1)}, u32[]{:S(2)}, u32[]{:S(2)}) collective-permute-start(bf16[1168,768]{1,0:T(8,128)(2,1)S(1)} %collective-permute-done.rest_1_.rest_11_.rest_7_), channel_id=1, source_target_pairs={{2,4},{3,5},{4,2},{5,3},{10,12},{11,13},{12,10},{13,11},{18,20},{1... | collective-permute-start | bytes 5382152 | tf_op jit(solution)/shard_map/ppermute | solution.py:454
  61.0 40.1 %collective-permute-start.6 = (bf16[1168,768]{1,0:T(8,128)(2,1)S(1)}, bf16[1168,768]{1,0:T(8,128)(2,1)S(1)}, u32[]{:S(2)}, u32[]{:S(2)}) collective-permute-start(bf16[1168,768]{1,0:T(8,128)(2,1)S(1)} %collective-permute-done.rest_1_.rest_11_.rest_7_), channel_id=1, source_target_pairs={{0,1},{1,0},{2,3},{3,2},{4,5},{5,4},{6,7},{7,6},{8,9},{9,8},{10,11... | collective-permute-start | bytes 5382152 | tf_op jit(solution)/shard_map/ppermute | solution.py:458
  62.6 39.8 %collective-permute-start.7 = (bf16[1168,768]{1,0:T(8,128)(2,1)S(1)}, bf16[1168,768]{1,0:T(8,128)(2,1)}, u32[]{:S(2)}, u32[]{:S(2)}) collective-permute-start(bf16[1168,768]{1,0:T(8,128)(2,1)S(1)} %collective-permute-done.1.rest_2_.rest_12_.rest_8_), channel_id=1, source_target_pairs={{2,3},{3,2},{4,5},{5,4},{10,11},{11,10},{12,13},{13,12},{18,19},{1... | collective-permute-start | bytes 5382152 | tf_op jit(solution)/shard_map/ppermute | solution.py:458
  64.4 41.3 %collective-permute-start.12 = (bf16[1168,768]{1,0:T(8,128)(2,1)S(1)}, bf16[1168,768]{1,0:T(8,128)(2,1)S(1)}, u32[]{:S(2)}, u32[]{:S(2)}) collective-permute-start(bf16[1168,768]{1,0:T(8,128)(2,1)S(1)} %collective-permute-done.rest_1_.rest_11_.rest_7_), channel_id=1, source_target_pairs={{0,8},{1,9},{2,10},{3,11},{4,12},{5,13},{6,14},{7,15},{8,0},{9,1},... | collective-permute-start | bytes 5382152 | tf_op jit(solution)/shard_map/ppermute | solution.py:464
  100.9 8.9 %collective-permute-start.17 = (bf16[1168,768]{1,0:T(8,128)(2,1)S(1)}, bf16[1168,768]{1,0:T(8,128)(2,1)S(1)}, u32[]{:S(2)}, u32[]{:S(2)}) collective-permute-start(bf16[1168,768]{1,0:T(8,128)(2,1)S(1)} %collective-permute-done.5.rest_6_.rest_16_.rest_12_), channel_id=1, source_target_pairs={{0,8},{1,9},{2,10},{3,11},{4,12},{5,13},{6,14},{7,15},{8,0},{9,1},... | collective-permute-start | bytes 5382152 | tf_op jit(solution)/shard_map/ppermute | solution.py:464
  101.1 44.0 %collective-permute-start.4 = (bf16[1168,768]{1,0:T(8,128)(2,1)S(1)}, bf16[1168,768]{1,0:T(8,128)(2,1)}, u32[]{:S(2)}, u32[]{:S(2)}) collective-permute-start(bf16[1168,768]{1,0:T(8,128)(2,1)S(1)} %collective-permute-done.3.rest_4_.rest_14_.rest_10_), channel_id=1, source_target_pairs={{2,0},{3,1},{4,6},{5,7},{10,8},{11,9},{12,14},{13,15},{18,16},{19,... | collective-permute-start | bytes 5382152 | tf_op jit(solution)/shard_map/ppermute | solution.py:454
  102.4 43.5 %collective-permute-start.8 = (bf16[1168,768]{1,0:T(8,128)(2,1)S(1)}, bf16[1168,768]{1,0:T(8,128)(2,1)}, u32[]{:S(2)}, u32[]{:S(2)}) collective-permute-start(bf16[1168,768]{1,0:T(8,128)(2,1)S(1)} %collective-permute-done.2.rest_3_.rest_13_.rest_9_), channel_id=1, source_target_pairs={{0,1},{1,0},{6,7},{7,6},{8,9},{9,8},{14,15},{15,14},{16,17},{17,16... | collective-permute-start | bytes 5382152 | tf_op jit(solution)/shard_map/ppermute | solution.py:458
  105.8 43.4 %collective-permute-start.9 = (bf16[1168,768]{1,0:T(8,128)(2,1)S(1)}, bf16[1168,768]{1,0:T(8,128)(2,1)}, u32[]{:S(2)}, u32[]{:S(2)}) collective-permute-start(bf16[1168,768]{1,0:T(8,128)(2,1)S(1)} %collective-permute-done.3.rest_4_.rest_14_.rest_10_), channel_id=1, source_target_pairs={{2,3},{3,2},{4,5},{5,4},{10,11},{11,10},{12,13},{13,12},{18,19},{1... | collective-permute-start | bytes 5382152 | tf_op jit(solution)/shard_map/ppermute | solution.py:458
  107.7 43.4 %collective-permute-start.14 = (bf16[1168,768]{1,0:T(8,128)(2,1)S(1)}, bf16[1168,768]{1,0:T(8,128)(2,1)S(1)}, u32[]{:S(2)}, u32[]{:S(2)}) collective-permute-start(bf16[1168,768]{1,0:T(8,128)(2,1)S(1)} %collective-permute-done.2.rest_3_.rest_13_.rest_9_), channel_id=1, source_target_pairs={{0,8},{1,9},{6,14},{7,15},{8,0},{9,1},{14,6},{15,7},{16,24},{17,25... | collective-permute-start | bytes 5382152 | tf_op jit(solution)/shard_map/ppermute | solution.py:464
  109.8 43.3 %collective-permute-start.15 = (bf16[1168,768]{1,0:T(8,128)(2,1)S(1)}, bf16[1168,768]{1,0:T(8,128)(2,1)S(1)}, u32[]{:S(2)}, u32[]{:S(2)}) collective-permute-start(bf16[1168,768]{1,0:T(8,128)(2,1)S(1)} %collective-permute-done.3.rest_4_.rest_14_.rest_10_), channel_id=1, source_target_pairs={{2,10},{3,11},{4,12},{5,13},{10,2},{11,3},{12,4},{13,5},{18,26},{1... | collective-permute-start | bytes 5382152 | tf_op jit(solution)/shard_map/ppermute | solution.py:464
  145.1 10.5 %collective-permute-start.18 = (bf16[1168,768]{1,0:T(8,128)(2,1)S(1)}, bf16[1168,768]{1,0:T(8,128)(2,1)S(1)}, u32[]{:S(2)}, u32[]{:S(2)}) collective-permute-start(bf16[1168,768]{1,0:T(8,128)(2,1)S(1)} %collective-permute-done.6.rest_7_.rest_17_.rest_13_), channel_id=1, source_target_pairs={{0,8},{1,9},{2,10},{3,11},{4,12},{5,13},{6,14},{7,15},{8,0},{9,1},... | collective-permute-start | bytes 5382152 | tf_op jit(solution)/shard_map/ppermute | solution.py:464
  145.8 43.0 %collective-permute-start.10 = (bf16[1168,768]{1,0:T(8,128)(2,1)}, bf16[1168,768]{1,0:T(8,128)(2,1)}, u32[]{:S(2)}, u32[]{:S(2)}) collective-permute-start(bf16[1168,768]{1,0:T(8,128)(2,1)} %collective-permute-done.4.rest_5_.rest_15_.rest_11_), channel_id=1, source_target_pairs={{0,1},{1,0},{6,7},{7,6},{8,9},{9,8},{14,15},{15,14},{16,17},{17,16... | collective-permute-start | bytes 5382152 | tf_op jit(solution)/shard_map/ppermute | solution.py:458
  149.2 44.9 %collective-permute-start.19 = (bf16[1168,768]{1,0:T(8,128)(2,1)}, bf16[1168,768]{1,0:T(8,128)(2,1)}, u32[]{:S(2)}, u32[]{:S(2)}) collective-permute-start(bf16[1168,768]{1,0:T(8,128)(2,1)} %collective-permute-done.7.rest_8_.rest_18_.rest_14_), channel_id=1, source_target_pairs={{2,10},{3,11},{4,12},{5,13},{10,2},{11,3},{12,4},{13,5},{18,26},{1... | collective-permute-start | bytes 5382152 | tf_op jit(solution)/shard_map/ppermute | solution.py:464
  151.2 43.0 %collective-permute-start.16 = (bf16[1168,768]{1,0:T(8,128)(2,1)}, bf16[1168,768]{1,0:T(8,128)(2,1)}, u32[]{:S(2)}, u32[]{:S(2)}) collective-permute-start(bf16[1168,768]{1,0:T(8,128)(2,1)} %collective-permute-done.4.rest_5_.rest_15_.rest_11_), channel_id=1, source_target_pairs={{0,8},{1,9},{6,14},{7,15},{8,0},{9,1},{14,6},{15,7},{16,24},{17,25... | collective-permute-start | bytes 5382152 | tf_op jit(solution)/shard_map/ppermute | solution.py:464
  153.1 41.1 %collective-permute-start.20 = (bf16[1168,768]{1,0:T(8,128)(2,1)}, bf16[1168,768]{1,0:T(8,128)(2,1)}, u32[]{:S(2)}, u32[]{:S(2)}) collective-permute-start(bf16[1168,768]{1,0:T(8,128)(2,1)} %collective-permute-done.8.rest_9_.rest_19_.rest_15_), channel_id=1, source_target_pairs={{0,8},{1,9},{6,14},{7,15},{8,0},{9,1},{14,6},{15,7},{16,24},{17,25... | collective-permute-start | bytes 5382152 | tf_op jit(solution)/shard_map/ppermute | solution.py:464
  155.6 38.6 %collective-permute-start.21 = (bf16[1168,768]{1,0:T(8,128)(2,1)}, bf16[1168,768]{1,0:T(8,128)(2,1)}, u32[]{:S(2)}, u32[]{:S(2)}) collective-permute-start(bf16[1168,768]{1,0:T(8,128)(2,1)} %collective-permute-done.9.rest_10_.rest_20_.rest_16_), channel_id=1, source_target_pairs={{2,10},{3,11},{4,12},{5,13},{10,2},{11,3},{12,4},{13,5},{18,26},{1... | collective-permute-start | bytes 5382152 | tf_op jit(solution)/shard_map/ppermute | solution.py:464
  218.2 13.5 %collective-permute-start.23 = (bf16[288,768]{1,0:T(8,128)(2,1)}, bf16[288,768]{1,0:T(8,128)(2,1)S(1)}, u32[]{:S(2)}, u32[]{:S(2)}) collective-permute-start(bf16[288,768]{1,0:T(8,128)(2,1)} %get-tuple-element.53), channel_id=1, source_target_pairs={{0,16},{8,24},{1,17},{9,25},{2,18},{10,26},{3,19},{11,27},{4,20},{... | collective-permute-start | bytes 1327112 | tf_op jit(solution)/shard_map/ppermute | solution.py:415
  293.1 13.6 %collective-permute-start.24 = (bf16[288,768]{1,0:T(8,128)(2,1)}, bf16[288,768]{1,0:T(8,128)(2,1)S(1)}, u32[]{:S(2)}, u32[]{:S(2)}) collective-permute-start(bf16[288,768]{1,0:T(8,128)(2,1)} %backward_layers.3), channel_id=1, source_target_pairs={{16,0},{24,8},{17,1},{25,9},{18,2},{26,10},{19,3},{27,11},{20,4},{... | collective-permute-start | bytes 1327112 | tf_op jit(solution)/shard_map/ppermute | solution.py:415
  294.4 40.7 %collective-permute-start.25 = (bf16[288,4608]{1,0:T(8,128)(2,1)S(1)}, bf16[288,4608]{1,0:T(8,128)(2,1)}, u32[]{:S(2)}, u32[]{:S(2)}) collective-permute-start(bf16[288,4608]{1,0:T(8,128)(2,1)S(1)} %copy-done.37), channel_id=1, source_target_pairs={{0,8},{8,0},{16,24},{24,16},{1,9},{9,1},{17,25},{25,17},{2,10},{10... | collective-permute-start | bytes 7962632 | tf_op jit(solution)/shard_map/ppermute | solution.py:420
  334.7 35.9 %collective-permute-start.27 = (bf16[288,4608]{1,0:T(8,128)(2,1)}, bf16[288,4608]{1,0:T(8,128)(2,1)}, u32[]{:S(2)}, u32[]{:S(2)}) collective-permute-start(bf16[288,4608]{1,0:T(8,128)(2,1)} %get-tuple-element.75), channel_id=1, source_target_pairs={{0,8},{8,0},{16,24},{24,16},{1,9},{9,1},{17,25},{25,17},{2,10},{10... | collective-permute-start | bytes 7962632 | tf_op jit(solution)/shard_map/ppermute | solution.py:420
  368.5 23.2 %collective-permute-start.45 = (bf16[592,768]{1,0:T(8,128)(2,1)}, bf16[592,768]{1,0:T(8,128)(2,1)S(1)}, u32[]{:S(2)}, u32[]{:S(2)}) collective-permute-start(bf16[592,768]{1,0:T(8,128)(2,1)} %get-tuple-element.91), channel_id=1, source_target_pairs={{0,1},{1,0},{2,3},{3,2},{4,5},{5,4},{6,7},{7,6},{8,9},{9,8},{10,11... | collective-permute-start | bytes 2727944 | tf_op jit(solution)/shard_map/ppermute | solution.py:458
  369.9 41.3 %collective-permute-start.42 = (bf16[592,768]{1,0:T(8,128)(2,1)S(1)}, bf16[592,768]{1,0:T(8,128)(2,1)S(1)}, u32[]{:S(2)}, u32[]{:S(2)}) collective-permute-start(bf16[592,768]{1,0:T(8,128)(2,1)S(1)} %copy-done.43), channel_id=1, source_target_pairs={{0,1},{1,0},{2,3},{3,2},{4,5},{5,4},{6,7},{7,6},{8,9},{9,8},{10,11... | collective-permute-start | bytes 2727944 | tf_op jit(solution)/shard_map/ppermute | solution.py:458
  388.2 42.5 %collective-permute-start.35 = (bf16[592,768]{1,0:T(8,128)(2,1)}, bf16[592,768]{1,0:T(8,128)(2,1)S(1)}, u32[]{:S(2)}, u32[]{:S(2)}) collective-permute-start(bf16[592,768]{1,0:T(8,128)(2,1)} %get-tuple-element.84), channel_id=1, source_target_pairs={{0,1},{1,0},{2,3},{3,2},{4,5},{5,4},{6,7},{7,6},{8,9},{9,8},{10,11... | collective-permute-start | bytes 2727944 | tf_op jit(solution)/shard_map/ppermute | solution.py:458
  391.9 48.0 %collective-permute-start.46 = (bf16[592,768]{1,0:T(8,128)(2,1)S(1)}, bf16[592,768]{1,0:T(8,128)(2,1)S(1)}, u32[]{:S(2)}, u32[]{:S(2)}) collective-permute-start(bf16[592,768]{1,0:T(8,128)(2,1)S(1)} %add_convert_fusion.3), channel_id=1, source_target_pairs={{0,2},{1,3},{6,4},{7,5},{8,10},{9,11},{14,12},{15,13},{16,18},{17,... | collective-permute-start | bytes 2727944 | tf_op jit(solution)/shard_map/ppermute | solution.py:454
  399.4 50.8 %collective-permute-start.32 = (bf16[592,768]{1,0:T(8,128)(2,1)S(1)}, bf16[592,768]{1,0:T(8,128)(2,1)S(1)}, u32[]{:S(2)}, u32[]{:S(2)}) collective-permute-start(bf16[592,768]{1,0:T(8,128)(2,1)S(1)} %copy-done.44), channel_id=1, source_target_pairs={{0,1},{1,0},{2,3},{3,2},{4,5},{5,4},{6,7},{7,6},{8,9},{9,8},{10,11... | collective-permute-start | bytes 2727944 | tf_op jit(solution)/shard_map/ppermute | solution.py:458
  411.5 40.4 %collective-permute-start.43 = (bf16[592,768]{1,0:T(8,128)(2,1)S(1)}, bf16[592,768]{1,0:T(8,128)(2,1)S(1)}, u32[]{:S(2)}, u32[]{:S(2)}) collective-permute-start(bf16[592,768]{1,0:T(8,128)(2,1)S(1)} %add_convert_fusion.5), channel_id=1, source_target_pairs={{0,2},{1,3},{6,4},{7,5},{8,10},{9,11},{14,12},{15,13},{16,18},{17,... | collective-permute-start | bytes 2727944 | tf_op jit(solution)/shard_map/ppermute | solution.py:454
  431.0 28.5 %collective-permute-start.36 = (bf16[592,768]{1,0:T(8,128)(2,1)S(1)}, bf16[592,768]{1,0:T(8,128)(2,1)S(1)}, u32[]{:S(2)}, u32[]{:S(2)}) collective-permute-start(bf16[592,768]{1,0:T(8,128)(2,1)S(1)} %add_convert_fusion.11), channel_id=1, source_target_pairs={{0,2},{1,3},{6,4},{7,5},{8,10},{9,11},{14,12},{15,13},{16,18},{17,... | collective-permute-start | bytes 2727944 | tf_op jit(solution)/shard_map/ppermute | solution.py:454
  438.4 31.2 %collective-permute-start.40 = (bf16[592,768]{1,0:T(8,128)(2,1)S(1)}, bf16[592,768]{1,0:T(8,128)(2,1)S(1)}, u32[]{:S(2)}, u32[]{:S(2)}) collective-permute-start(bf16[592,768]{1,0:T(8,128)(2,1)S(1)} %copy-done.41), channel_id=1, source_target_pairs={{0,1},{1,0},{2,3},{3,2},{4,5},{5,4},{6,7},{7,6},{8,9},{9,8},{10,11... | collective-permute-start | bytes 2727944 | tf_op jit(solution)/shard_map/ppermute | solution.py:458
  440.2 30.9 %collective-permute-start.47 = (bf16[592,768]{1,0:T(8,128)(2,1)S(1)}, bf16[592,768]{1,0:T(8,128)(2,1)S(1)}, u32[]{:S(2)}, u32[]{:S(2)}) collective-permute-start(bf16[592,768]{1,0:T(8,128)(2,1)S(1)} %add_convert_fusion.2), channel_id=1, source_target_pairs={{2,4},{3,5},{4,2},{5,3},{10,12},{11,13},{12,10},{13,11},{18,20},{1... | collective-permute-start | bytes 2727944 | tf_op jit(solution)/shard_map/ppermute | solution.py:454
  450.2 39.0 %collective-permute-start.30 = (bf16[592,768]{1,0:T(8,128)(2,1)S(1)}, bf16[592,768]{1,0:T(8,128)(2,1)S(1)}, u32[]{:S(2)}, u32[]{:S(2)}) collective-permute-start(bf16[592,768]{1,0:T(8,128)(2,1)S(1)} %copy-done.42), channel_id=1, source_target_pairs={{0,1},{1,0},{2,3},{3,2},{4,5},{5,4},{6,7},{7,6},{8,9},{9,8},{10,11... | collective-permute-start | bytes 2727944 | tf_op jit(solution)/shard_map/ppermute | solution.py:458
  451.9 38.6 %collective-permute-start.33 = (bf16[592,768]{1,0:T(8,128)(2,1)S(1)}, bf16[592,768]{1,0:T(8,128)(2,1)S(1)}, u32[]{:S(2)}, u32[]{:S(2)}) collective-permute-start(bf16[592,768]{1,0:T(8,128)(2,1)S(1)} %add_convert_fusion.13), channel_id=1, source_target_pairs={{0,2},{1,3},{6,4},{7,5},{8,10},{9,11},{14,12},{15,13},{16,18},{17,... | collective-permute-start | bytes 2727944 | tf_op jit(solution)/shard_map/ppermute | solution.py:454
  459.7 38.6 %collective-permute-start.37 = (bf16[592,768]{1,0:T(8,128)(2,1)S(1)}, bf16[592,768]{1,0:T(8,128)(2,1)S(1)}, u32[]{:S(2)}, u32[]{:S(2)}) collective-permute-start(bf16[592,768]{1,0:T(8,128)(2,1)S(1)} %add_convert_fusion.10), channel_id=1, source_target_pairs={{2,4},{3,5},{4,2},{5,3},{10,12},{11,13},{12,10},{13,11},{18,20},{1... | collective-permute-start | bytes 2727944 | tf_op jit(solution)/shard_map/ppermute | solution.py:454
  469.7 39.0 %collective-permute-start.39 = (bf16[592,768]{1,0:T(8,128)(2,1)S(1)}, bf16[592,768]{1,0:T(8,128)(2,1)S(1)}, u32[]{:S(2)}, u32[]{:S(2)}) collective-permute-start(bf16[592,768]{1,0:T(8,128)(2,1)S(1)} %copy-done.39), channel_id=1, source_target_pairs={{0,1},{1,0},{2,3},{3,2},{4,5},{5,4},{6,7},{7,6},{8,9},{9,8},{10,11... | collective-permute-start | bytes 2727944 | tf_op jit(solution)/shard_map/ppermute | solution.py:458
  471.1 38.3 %collective-permute-start.44 = (bf16[592,768]{1,0:T(8,128)(2,1)S(1)}, bf16[592,768]{1,0:T(8,128)(2,1)S(1)}, u32[]{:S(2)}, u32[]{:S(2)}) collective-permute-start(bf16[592,768]{1,0:T(8,128)(2,1)S(1)} %add_convert_fusion.4), channel_id=1, source_target_pairs={{2,4},{3,5},{4,2},{5,3},{10,12},{11,13},{12,10},{13,11},{18,20},{1... | collective-permute-start | bytes 2727944 | tf_op jit(solution)/shard_map/ppermute | solution.py:454
  489.1 25.9 %collective-permute-start.48 = (bf16[592,768]{1,0:T(8,128)(2,1)S(1)}, bf16[592,768]{1,0:T(8,128)(2,1)S(1)}, u32[]{:S(2)}, u32[]{:S(2)}) collective-permute-start(bf16[592,768]{1,0:T(8,128)(2,1)S(1)} %get-tuple-element.92), channel_id=1, source_target_pairs={{2,0},{3,1},{4,6},{5,7},{10,8},{11,9},{12,14},{13,15},{18,16},{19,... | collective-permute-start | bytes 2727944 | tf_op jit(solution)/shard_map/ppermute | solution.py:454
  490.4 30.3 %collective-permute-start.41 = (bf16[592,768]{1,0:T(8,128)(2,1)S(1)}, bf16[592,768]{1,0:T(8,128)(2,1)S(1)}, u32[]{:S(2)}, u32[]{:S(2)}) collective-permute-start(bf16[592,768]{1,0:T(8,128)(2,1)S(1)} %get-tuple-element.93), channel_id=1, source_target_pairs={{0,2},{1,3},{6,4},{7,5},{8,10},{9,11},{14,12},{15,13},{16,18},{17,... | collective-permute-start | bytes 2727944 | tf_op jit(solution)/shard_map/ppermute | solution.py:454
  498.3 29.2 %collective-permute-start.29 = (bf16[592,768]{1,0:T(8,128)(2,1)S(1)}, bf16[592,768]{1,0:T(8,128)(2,1)S(1)}, u32[]{:S(2)}, u32[]{:S(2)}) collective-permute-start(bf16[592,768]{1,0:T(8,128)(2,1)S(1)} %copy-done.40), channel_id=1, source_target_pairs={{0,1},{1,0},{2,3},{3,2},{4,5},{5,4},{6,7},{7,6},{8,9},{9,8},{10,11... | collective-permute-start | bytes 2727944 | tf_op jit(solution)/shard_map/ppermute | solution.py:458
  508.6 18.9 %collective-permute-start.34 = (bf16[592,768]{1,0:T(8,128)(2,1)S(1)}, bf16[592,768]{1,0:T(8,128)(2,1)S(1)}, u32[]{:S(2)}, u32[]{:S(2)}) collective-permute-start(bf16[592,768]{1,0:T(8,128)(2,1)S(1)} %add_convert_fusion.12), channel_id=1, source_target_pairs={{2,4},{3,5},{4,2},{5,3},{10,12},{11,13},{12,10},{13,11},{18,20},{1... | collective-permute-start | bytes 2727944 | tf_op jit(solution)/shard_map/ppermute | solution.py:454
  509.4 28.4 %collective-permute-start.38 = (bf16[592,768]{1,0:T(8,128)(2,1)S(1)}, bf16[592,768]{1,0:T(8,128)(2,1)S(1)}, u32[]{:S(2)}, u32[]{:S(2)}) collective-permute-start(bf16[592,768]{1,0:T(8,128)(2,1)S(1)} %get-tuple-element.94), channel_id=1, source_target_pairs={{2,0},{3,1},{4,6},{5,7},{10,8},{11,9},{12,14},{13,15},{18,16},{19,... | collective-permute-start | bytes 2727944 | tf_op jit(solution)/shard_map/ppermute | solution.py:454
  515.1 23.9 %collective-permute-start.31 = (bf16[592,768]{1,0:T(8,128)(2,1)S(1)}, bf16[592,768]{1,0:T(8,128)(2,1)S(1)}, u32[]{:S(2)}, u32[]{:S(2)}) collective-permute-start(bf16[592,768]{1,0:T(8,128)(2,1)S(1)} %get-tuple-element.95), channel_id=1, source_target_pairs={{0,2},{1,3},{6,4},{7,5},{8,10},{9,11},{14,12},{15,13},{16,18},{17,... | collective-permute-start | bytes 2727944 | tf_op jit(solution)/shard_map/ppermute | solution.py:454
  521.5 34.6 %collective-permute-start.50 = (bf16[592,768]{1,0:T(8,128)(2,1)S(1)}, bf16[592,768]{1,0:T(8,128)(2,1)}, u32[]{:S(2)}, u32[]{:S(2)}) collective-permute-start(bf16[592,768]{1,0:T(8,128)(2,1)S(1)} %add_convert_fusion), channel_id=1, source_target_pairs={{0,8},{16,24},{1,9},{17,25},{2,10},{18,26},{3,11},{19,27},{4,12},{... | collective-permute-start | bytes 2727944 | tf_op jit(solution)/shard_map/ppermute | solution.py:576
  539.6 16.4 %collective-permute-start.49 = (bf16[592,768]{1,0:T(8,128)(2,1)S(1)}, bf16[592,768]{1,0:T(8,128)(2,1)}, u32[]{:S(2)}, u32[]{:S(2)}) collective-permute-start(bf16[592,768]{1,0:T(8,128)(2,1)S(1)} %add_convert_fusion.8), channel_id=1, source_target_pairs={{8,0},{24,16},{9,1},{25,17},{10,2},{26,18},{11,3},{27,19},{12,4},{... | collective-permute-start | bytes 2727944 | tf_op jit(solution)/shard_map/ppermute | solution.py:576
  542.4 12.8 %all-to-all-start = ((bf16[280,4,192]{2,0,1:T(8,128)(2,1)}), bf16[280,4,192]{2,0,1:T(8,128)(2,1)S(1)}, u32[]{:S(2)}, u32[]{:S(2)}) async-start(bf16[280,4,192]{2,0,1:T(8,128)(2,1)} %copy.30), calls=%async_computation | async-start | bytes 1146880 | tf_op jit(solution)/shard_map/all_to_all | solution.py:562
  (49 other events, 1365.3 us)

commit v3 on v2

--- a/solution.py
+++ b/solution.py
@@ -52,34 +52,37 @@
     r = wv.shape[2]
 
     def start(block, j, part):
-        if part == 12:
-            pltpu.make_async_copy(block.at[pl.ds(12 * r, TAIL)], tv.at[j], sems.at[12]).start()
-        elif part < 8:
+        if len(sets[0]) == 1:
+            rows = block.at[pl.ds(part * r, r if part < 12 else TAIL)]
+            dst = wv.at[part, 0] if part < 8 else wd.at[part - 8, 0] if part < 12 else tv.at[0]
+            pltpu.make_async_copy(rows, dst, sems.at[part]).start()
+        elif part == 12:
+            pltpu.make_async_copy(block.at[pl.ds(10 * r, TAIL)], tv.at[j], sems.at[12]).start()
+        elif part < 6:
             pltpu.make_async_copy(block.at[pl.ds(part * r, r)], wv.at[part, j], sems.at[part]).start()
-        elif len(sets[0]) == 1:
-            pltpu.make_async_copy(block.at[pl.ds(part * r, r)], wd.at[part - 8, 0], sems.at[part]).start()
         elif part == 8:
             b = j // 2
-            pltpu.make_async_copy(block.at[pl.ds(8 * r, 4 * r)], wd.at[b, j % 2], sems.at[8 + b]).start()
+            pltpu.make_async_copy(block.at[pl.ds(6 * r, 4 * r)], wd.at[b, j % 2], sems.at[8 + b]).start()
 
     for number, blocks in enumerate(sets):
-        if len(blocks) == 1:
-
-            @pl.when(info[which] == number)
-            def _():
+
+        @pl.when(info[which] == number)
+        def _():
+            if len(blocks) == 1:
                 for part in order:
                     start(blocks[0], 0, part)
-
-            continue
-        for middle in (0, 1):
-
-            @pl.when((info[which] == number) & (info[4] == middle))
-            def _():
-                held = [(0, 0), (1, 1), (2, 3), (4, 2)] if middle else [(0, 0), (1, 1), (3, 2), (5, 3)]
-                spots = [(blocks[far * 6 + at], (info[2] ^ flip) * 2 + (info[3] ^ far)) for far in (0, 1) for at, flip in held]
-                for part in order:
-                    for block, j in spots:
-                        start(block, j, part)
+                return
+            lines = [info[2], info[2] ^ 1, info[2] ^ info[6], info[2] ^ (info[6] ^ 1)]
+            spots = [(blocks[4 * far + k], lines[k] * 2 + (info[3] ^ far)) for far in (0, 1) for k in range(4)]
+            for part in order:
+                if part in (6, 7):
+                    for far in (0, 1):
+                        for k in range(4):
+                            rows = blocks[8 + k].at[pl.ds((2 * far + part - 6) * r, r)]
+                            pltpu.make_async_copy(rows, wv.at[part, lines[k] * 2 + (info[3] ^ far)], sems.at[part]).start()
+                    continue
+                for block, j in spots:
+                    start(block, j, part)
 
     waits = [pltpu.make_async_copy(wv.at[k], wv.at[k], sems.at[k]) for k in range(8)]
     waits += [pltpu.make_async_copy(wd.at[b], wd.at[b], sems.at[8 + b]) for b in range(4)]
@@ -362,52 +365,124 @@
     )(info, g, mask, *kept, *([behind] if save else []), *wa, *wb)
 
 
-def product_kernel(n, info, slots, gv, fk, bk, fr, br, *rest):
-    outs, (held, sems) = rest[:-2], rest[-2:]
+def product_kernel(n, joined, info, slots, gv, fk_hbm, bk_hbm, fr_hbm, br_hbm, *rest):
+    outs = [rest[0].at[j] for j in range(n)] if joined else rest[:n]
+    f, b, held, isems, osems = rest[-5:]
     r = D // n
-
-    def both(a, b, at):
-        return jnp.concatenate([a[:, at:at + D], b[:, at:at + D]], axis=0)
+    flat = HALF
+    loads = {}
+
+    def load(first, core):
+        mine = range(2 if core == 0 else HALF) if first else range(HALF if core == 0 else 3)
+        for k in mine:
+            dst, own, other = (f, fk_hbm, fr_hbm) if first else (b, bk_hbm, br_hbm)
+            sem = isems.at[0 if first else 1, k]
+            for half, src in enumerate((own, other)):
+                pltpu.make_async_copy(src.at[:, pl.ds(k * D, D)], dst.at[k, pl.ds(half * ROWS, ROWS)], sem).start()
+            loads[core, first, k] = pltpu.make_async_copy(dst.at[k], dst.at[k], sem)
+
+    def operand(first, core, k):
+        wait = loads.pop((core, first, k), None)
+        if wait is not None:
+            wait.wait()
+        return (f if first else b)[k]
 
     for j in range(n):
-        held[j, HALF * r:] = gv[...].astype(BF)
+        held[j, flat * r:] = gv[...].astype(BF)
+        pltpu.make_async_copy(held.at[j, pl.ds(flat * r, TAIL)], outs[j].at[pl.ds(flat * r, TAIL)], osems.at[0]).start()
+
+    def store(c, val):
+        for j in range(n):
+            held[slots[j], c * r:(c + 1) * r] = val[j * r:(j + 1) * r]
+        for j in range(n):
+            rows = pl.ds(c * r, r)
+            pltpu.make_async_copy(held.at[j, rows], outs[j].at[rows], osems.at[0]).start()
+
+    def store_rows(c, val):
+        for i in range(n // 4):
+            held[slots[c * (n // 4) + i], :4 * r] = val[i * 4 * r:(i + 1) * 4 * r]
+        if c == 3:
+            for j in range(n):
+                rows = pl.ds(0, 4 * r)
+                pltpu.make_async_copy(held.at[j, rows], outs[j].at[rows], osems.at[0]).start()
 
     @pl.when(info[5] == 0)
     def _():
+        load(True, 0)
+        load(False, 0)
         for c in range(HALF):
-            val = dot(both(fk, fr, 0 if c < 4 else D), both(bk, br, c * D), 0, 0).astype(BF)
-            for j in range(n):
-                held[slots[j], c * r:(c + 1) * r] = val[j * r:(j + 1) * r]
+            val = dot(operand(True, 0, 0 if c < 4 else 1), operand(False, 0, c), 0, 0).astype(BF)
+            store(c, val)
 
     @pl.when(info[5] != 0)
     def _():
+        load(False, 1)
+        load(True, 1)
         for c in range(HALF):
-            val = dot(both(fk, fr, c * D), both(bk, br, 0 if c < 4 else (c - 3) * D), 0, 0).astype(BF)
+            val = dot(operand(True, 1, c), operand(False, 1, 0 if c < 4 else c - 3), 0, 0).astype(BF)
             if c < 4 and n > 1:
-                for i in range(n // 4):
-                    held[slots[c * (n // 4) + i], :4 * r] = val[i * 4 * r:(i + 1) * 4 * r]
+                store_rows(c, val)
             else:
-                for j in range(n):
-                    held[slots[j], c * r:(c + 1) * r] = val[j * r:(j + 1) * r]
+                store(c, val)
 
     for j in range(n):
-        pltpu.make_async_copy(held.at[j], outs[j], sems.at[j]).start()
-    for j in range(n):
-        pltpu.make_async_copy(held.at[j], outs[j], sems.at[j]).wait()
-
-
-def weight_products(n, info, slots, gv, fk, bk, fr, br):
+        pltpu.make_async_copy(held.at[j], outs[j], osems.at[0]).wait()
+
+
+def weight_products(n, joined, info, slots, gv, fk, bk, fr, br):
     shape = (HALF * (D // n) + TAIL, D)
+    shapes = [jax.ShapeDtypeStruct((n,) + shape, BF)] if joined else [jax.ShapeDtypeStruct(shape, BF)] * n
+    scratch = [pltpu.VMEM((HALF, 2 * ROWS, D), BF), pltpu.VMEM((HALF, 2 * ROWS, D), BF), pltpu.VMEM((n,) + shape, BF),
+               pltpu.SemaphoreType.DMA((2, HALF)), pltpu.SemaphoreType.DMA((1,))]
     return pl.pallas_call(
-        functools.partial(product_kernel, n),
-        out_shape=[jax.ShapeDtypeStruct(shape, BF)] * n,
-        in_specs=[SM, SM] + [VM] * 5,
-        out_specs=[ANYS] * n,
-        scratch_shapes=[pltpu.VMEM((n,) + shape, BF), pltpu.SemaphoreType.DMA((n,))],
+        functools.partial(product_kernel, n, joined),
+        out_shape=shapes,
+        in_specs=[SM, SM, VM] + [ANYS] * 4,
+        out_specs=[ANYS] * len(shapes),
+        scratch_shapes=scratch,
         compiler_params=pltpu.CompilerParams(vmem_limit_bytes=VMEM_LIMIT),
         cost_estimate=pl.CostEstimate(flops=2 * 2 * ROWS * D * D * 6, bytes_accessed=2**24, transcendentals=0),
         name="weight_products",
     )(info, slots, gv, fk, bk, fr, br)
+
+
+def pack_kernel(info, joint, output, up, down, ag, as_, jb, ob, fg, fs, db, ub, block_ref, pair_ref):
+    r = output.shape[0]
+    spot = info[2] * 2 + info[3]
+    for k in range(3):
+        block_ref[k * r:(k + 1) * r, :] = joint[:, k * D:(k + 1) * D].astype(BF)
+    block_ref[3 * r:4 * r, :] = output[...].astype(BF)
+    for k in range(2):
+        block_ref[(4 + k) * r:(5 + k) * r, :] = up[:, k * D:(k + 1) * D].astype(BF)
+        pair_ref[k * r:(k + 1) * r, :] = up[:, (2 + k) * D:(3 + k) * D].astype(BF)
+    block_ref[6 * r:10 * r, :] = down[...].astype(BF)
+
+    def placed(ref, at):
+        wide = ref.shape[1]
+        lane = lax.broadcasted_iota(jnp.int32, (wide, D), 1)
+        entry = lax.broadcasted_iota(jnp.int32, (wide, D), 0)
+        return dot(ref[...].astype(BF), (lane == entry + at * wide).astype(BF))
+
+    zero = jnp.zeros((1, D), F32)
+    jrow = placed(jb, spot % 4)
+    urow = placed(ub, spot % 2)
+    rows = [placed(ag, spot), placed(as_, spot)]
+    rows += [jnp.where(spot // 4 == k, jrow, zero) for k in range(2)]
+    rows += [placed(v, spot) for v in (ob, fg, fs, db)]
+    rows += [jnp.where(spot // 2 == k, urow, zero) for k in range(4)] + [zero] * 4
+    block_ref[10 * r:, :] = jnp.concatenate(rows).astype(BF)
+
+
+def pack(info, *params):
+    r = params[1].shape[0]
+    return pl.pallas_call(
+        pack_kernel,
+        out_shape=[jax.ShapeDtypeStruct((10 * r + TAIL, D), BF), jax.ShapeDtypeStruct((2 * r, D), BF)],
+        in_specs=[SM] + [VM] * 12,
+        out_specs=[VM, VM],
+        compiler_params=pltpu.CompilerParams(vmem_limit_bytes=VMEM_LIMIT),
+        name="pack",
+    )(info, *params)
 
 
 def moved(value, axis, by):
@@ -447,33 +522,54 @@
 
 
 IN, OUT, MID, PAIR = ((0, 1), (3, 2)), ((1, 0), (2, 3)), ((1, 2), (2, 1)), ((0, 1), (1, 0), (2, 3), (3, 2))
-ENDS, MIDS = (0, 3), (1, 2)
-
-
-def along(value, moves):
-    return lax.ppermute(value, "dp", [(2 * a + x, 2 * b + x) for a, b in moves for x in range(2)])
-
-
-def across(value, lines=(0, 1, 2, 3)):
-    return lax.ppermute(value, "dp", [(2 * z + x, 2 * z + 1 - x) for z in lines for x in range(2)])
-
-
-def core_swap(value, lines=(0, 1, 2, 3)):
-    n, peers = lax.axis_size("dp"), lax.axis_size("section")
-    pairs = [(s * n + 2 * z + x, (s ^ 1) * n + 2 * z + x) for s in range(peers) for z in lines for x in range(2)]
-    return lax.ppermute(value, ("section", "dp"), pairs)
-
-
-def gather_blocks(own):
-    one = along(own, PAIR)
-    mid = along(own, MID)
-    far = along(mid, OUT)
-    back = along(one, MID)
-    last = along(back, OUT)
-    column = [own, one, mid, far, back, last]
-    lines = [(0, 1, 2, 3), (0, 1, 2, 3), MIDS, ENDS, MIDS, ENDS]
-    mine = column + [across(b, l) for b, l in zip(column, lines)]
-    return mine, [core_swap(b, l) for b, l in zip(mine, lines * 2)]
+
+
+class Links:
+    def __init__(self, **depth):
+        self.depth = {"x": depth["x"], "in": depth["z"], "mid": depth["z"], "out": depth["z"]}
+        self.ended = {"x": [], "in": [], "mid": [], "out": []}
+
+    def send(self, value, names, axis, pairs):
+        for name in names:
+            done = self.ended[name]
+            if len(done) >= self.depth[name]:
+                value = lax.optimization_barrier((value, done[-self.depth[name]]))[0]
+        got = lax.ppermute(value, axis, pairs)
+        for name in names:
+            self.ended[name].append(got)
+        return got
+
+    def along(self, value, moves):
+        names = {IN: ("in",), OUT: ("out",), MID: ("mid",), PAIR: ("out",)}[moves]
+        return self.send(value, names, "dp", [(2 * a + x, 2 * b + x) for a, b in moves for x in range(2)])
+
+    def across(self, value, core=None):
+        if core is None:
+            return self.send(value, ("x",), "dp", [(i, i ^ 1) for i in range(8)])
+        places = [8 * s + i for s in range(lax.axis_size("section")) if s % 2 == core for i in range(8)]
+        return self.send(value, ("x",), ("section", "dp"), [(i, i ^ 1) for i in places])
+
+
+def gather_blocks(own, pair, middle):
+    net = Links(x=1, z=9)
+    one, mid = net.along(own, PAIR), net.along(own, MID)
+    first = net.across(pair, 0)
+    sent = [net.across(own)]
+    first = first + net.across(pair, 1)
+    both = jnp.concatenate([pair, first])
+    far, back = net.along(mid, OUT), net.along(one, MID)
+    sent.append(net.across(one))
+    both_one, both_mid = net.along(both, PAIR), net.along(both, MID)
+    last = net.along(back, OUT)
+    third = jnp.where(middle, mid, far)
+    sent.append(net.across(third))
+    both_far, both_back = net.along(both_mid, OUT), net.along(both_one, MID)
+    fourth = jnp.where(middle, back, last)
+    sent.append(net.across(fourth))
+    both_last = net.along(both_back, OUT)
+    mine = [own, one, third, fourth] + sent
+    mine += [both, both_one, jnp.where(middle, both_mid, both_far), jnp.where(middle, both_back, both_last)]
+    return mine, [swapped(b) for b in mine]
 
 
 def add(*terms):
@@ -483,15 +579,28 @@
     return total.astype(BF)
 
 
-def scatter_blocks(blocks):
-    s = [add(blocks[k], across(blocks[4 + k])) for k in range(4)]
-    a1 = along(s[0], IN)
-    a2 = along(s[1], IN)
-    b2 = along(add(s[0], a1), MID)
-    a3 = along(s[2], IN)
-    b3 = along(add(s[1], a2), MID)
-    c3 = along(add(s[2], b2), OUT)
-    return add(s[3], a3, b3, c3)
+def scatter_steps(net, blocks, across, zero=None):
+    def own(k):
+        extra = [zero] if zero is not None and k == 1 else []
+        return add(blocks[k], net.across(blocks[4 + k]), *extra) if across else blocks[k]
+
+    s0 = own(0)
+    a1 = net.along(s0, IN)
+    yield
+    s1 = own(1)
+    a2 = net.along(s1, IN)
+    b2 = net.along(add(s0, a1), MID)
+    yield
+    s2 = own(2)
+    a3 = net.along(s2, IN)
+    b3 = net.along(add(s1, a2), MID)
+    c3 = net.along(add(s2, b2), OUT)
+    yield
+    total = add(own(3), a3, b3, c3)
+    if not across:
+        half = total.shape[0] // 2
+        total = add(total[:half], net.across(total[half:]))
+    yield total
 
 
 def shards(tokens, lengths, cotangent, attend_gain, attend_shift, joint_weight, joint_bias, output_weight,
@@ -508,19 +617,21 @@
     spot = lax.axis_index("dp")
     z, column = spot // 2, spot % 2
     middle = (z == 1) | (z == 2)
-    info = jnp.stack([core, 1 - core, z, column, middle.astype(jnp.int32), core]).astype(jnp.int32)
+    info = jnp.stack([core, 1 - core, z, column, middle.astype(jnp.int32), core, 2 + middle]).astype(jnp.int32)
     if lined:
         order = jnp.array([[3, 2, 1, 0], [2, 3, 1, 0], [0, 1, 3, 2], [0, 1, 2, 3]], jnp.int32)[z]
         slots = jnp.stack([order[j // 2] + jnp.where(column == j % 2, 0, 4) for j in range(8)]).astype(jnp.int32)
     else:
         slots = jnp.zeros((1,), jnp.int32)
 
-    tail = vector_tail(n, spot, attend_gain[0], attend_shift[0], joint_bias[0], output_bias[0], feed_gain[0], feed_shift[0],
-                       down_bias[0], up_bias[0])
-    packed = pack_shard(joint_weight[0], output_weight[0], up_weight[0], down_weight[0], tail)
     if lined:
-        wa, wb = gather_blocks(packed)
+        packed, pair = pack(info, joint_weight[0], output_weight[0], up_weight[0], down_weight[0], attend_gain, attend_shift,
+                            joint_bias, output_bias, feed_gain, feed_shift, down_bias, up_bias)
+        wa, wb = gather_blocks(packed, pair, middle)
     else:
+        tail = vector_tail(n, spot, attend_gain[0], attend_shift[0], joint_bias[0], output_bias[0], feed_gain[0],
+                           feed_shift[0], down_bias[0], up_bias[0])
+        packed = pack_shard(joint_weight[0], output_weight[0], up_weight[0], down_weight[0], tail)
         gathered = lax.all_gather(packed, "dp")
         tails = lax.psum(tail.astype(BF).astype(F32), "dp")
         wa, wb = kernel_form(n, gathered, tails), kernel_form(n, swapped(gathered), swapped(tails))
@@ -555,19 +666,24 @@
     behind = mask
     for s in (1, 0):
         g, gv, bk, bs = backward_layers(True, (s,), info, g, mask, saved, wa, wb, behind)
-        products[s] = weight_products(nk, info, slots, gv, kept[s], bk, received[s], swapped(bs))
+        products[s] = weight_products(nk, s == 1 and lined, info, slots if s == 0 else jnp.arange(nk, dtype=jnp.int32),
+                                      gv, kept[s], bk, received[s], swapped(bs))
         behind = products[s][0]
 
     ends = jnp.where(stage == 0, g, leaving)[:seq].reshape(seq, sections, D // sections)
-    pieces = lax.all_to_all(ends, "section", split_axis=1, concat_axis=0, tiled=True).reshape(sections, seq, D // sections)
+    swept = lax.all_to_all(ends, "section", split_axis=1, concat_axis=0, tiled=True)
+    pieces = swept.reshape(sections, seq, D // sections)
     outputs = pieces[sections - 2:]
     token_grad = pieces[:2]
+    zero = jnp.minimum(jnp.abs(swept[0, 0, 0].astype(F32)), 0.0)
 
     reduced = [None, None]
-    for s in (1, 0):
-        if lined:
-            reduced[s] = scatter_blocks(products[s])
-        else:
+    if lined:
+        net = Links(x=2, z=9)
+        reduced[1] = lax.psum_scatter(products[1][0], "dp", scatter_dimension=0)
+        reduced[0] = list(scatter_steps(net, products[0], True, zero))[-1]
+    else:
+        for s in range(2):
             p = products[s][0]
             col = jnp.swapaxes(p[:HALF * D].reshape(HALF, n, r, D), 0, 1).reshape(n, HALF * r, D)
             row = jnp.concatenate([p[:4 * D].reshape(n, 4 * r, D), col[:, 4 * r:]], axis=1)

time: 570 us -> 533 us (0.935)
  starting transfers between devices: 109 us -> 75.8 us
  waiting for transfers between devices: 259 us -> 238 us
  between operations: 7.27 us -> 20.8 us
  blocking collectives: 0 us -> 12 us
  local copies, waits for them, and re-layouts: 23.9 us -> 14.1 us
    ppermute x43 -> x26, starting transfers between devices: 96.8 us -> 62.3 us  [send(): got = lax.ppermute(value, axis, pairs)]
    ppermute x43 -> x26, waiting for transfers between devices: 226 us -> 204 us  [send(): got = lax.ppermute(value, axis, pairs)]
    all_to_all x0 -> x1, blocking collectives: none -> 12 us  [shards(): lax.all_to_all(ends, 'section', split_axis=1, concat_axis=0, tiled=True)]
    all_to_all x1 -> x0, waiting for transfers between devices: 9.3 us -> none  [shards(): lax.all_to_all(ends, 'section', split_axis=1, concat_axis=0, tiled=True)]
    ppermute x4 -> x16, waiting for transfers between devices: 2.98 us -> 12.2 us  [swapped(): return lax.ppermute(value, 'section', [(i, i ^ 1) for i in range(peers)])]
    concatenate x1 -> x0, local copies, waits for them, and re-layouts: 7.52 us -> none  [pack_shard(): return jnp.concatenate(pieces + [down, tail]).astype(BF)]
    pallas_call x2 -> x3, Pallas kernels: 26.3 us -> 28.8 us  [the longest x2 25.1 us: weight_products(): pl.pallas_call(functools.partial(product_kernel, n, joined), out_shape=sh...]
  transfers between devices with their start and end apart: 52 -> 47, of which waited for: 22 -> 23; matrix products, arithmetic and copies ran while one was open for 3% -> 3% of each run, Pallas kernels for 12% -> 10%
where the time goes in v3:
time: 533 us; the launch traced here: 526 us
  waiting for transfers between devices  238 us (45%)
  Pallas kernels  152 us (29%)
  starting transfers between devices  75.8 us (14%)
  between operations  20.8 us (4%)
  local copies, waits for them, and re-layouts  14.1 us (3%)
  other arithmetic  13.3 us (2%)
  blocking collectives  12 us (2%)
    ppermute x26, waiting for transfers between devices, send(): got = lax.ppermute(value, axis, pairs)  204 us
    pallas_call x3, Pallas kernels, backward_layers(): pl.pallas_call(functools.partial(backward_kernel, save, layers, len(wa)),...  74.1 us
    ppermute x26, starting transfers between devices, send(): got = lax.ppermute(value, axis, pairs)  62.3 us
    pallas_call x2, Pallas kernels, forward_stage(): pl.pallas_call(functools.partial(forward_kernel, save, len(wa)), out_shap...  48.8 us
    pallas_call x2, Pallas kernels, weight_products(): pl.pallas_call(functools.partial(product_kernel, n, joined), out_shape=sh...  25.1 us
    ppermute x2, waiting for transfers between devices, moved(): lax.ppermute(value, axis, [(i, i + by) for i in range(peers) if 0 <= i +...  21.4 us
    ppermute x16, waiting for transfers between devices, swapped(): return lax.ppermute(value, 'section', [(i, i ^ 1) for i in range(peers)])  12.2 us
    all_to_all x1, blocking collectives, shards(): lax.all_to_all(ends, 'section', split_axis=1, concat_axis=0, tiled=True)  12 us
  transfers between devices with their start and end apart: 47, of which 23 were waited for; matrix products, arithmetic and copies ran while one was open for 3% of the time, Pallas kernels for 10%

profile of v3, /device:TPU:0, one launch (start us, length us, event | category | flops | bytes accessed | tf_op | source)
XLA Modules:
  0.0 525.9 jit_solution(3055441542099811737)
XLA Ops:
  7.9 3.7 pack.1
  11.6 4.8 collective-permute-start.5
  16.4 1.6 collective-permute-start
  18.8 5.3 %collective-permute-done.5 = bf16[192,768]{1,0:T(8,128)(2,1)S(1)} collective-permute-done((bf16[192,768]{1,0:T(8,128)(2,1)}, bf16[192,768]{1,0:T(8,128)(2,1)S(1)}, u32[]{:S(2)}, u32[]{:S(2)}) %collective-permute-start.5) | collective-permute-done | bytes 294944 | tf_op jit(solution)/shard_map/ppermute | solution.py:537
  24.2 2.3 collective-permute-start.6
  26.5 21.9 %collective-permute-done.rest_1_.rest_11_.rest_7_ = bf16[976,768]{1,0:T(8,128)(2,1)S(1)} collective-permute-done((bf16[976,768]{1,0:T(8,128)(2,1)}, bf16[976,768]{1,0:T(8,128)(2,1)S(1)}, u32[]{:S(2)}, u32[]{:S(2)}) %collective-permute-start) | collective-permute-done | bytes 1499168 | tf_op jit(solution)/shard_map/ppermute | solution.py:537
  50.5 3.7 collective-permute-done.6.rest_4_.rest_14_.rest_10_
  54.8 2.1 collective-permute-start.8
  58.2 25.6 %collective-permute-done.2 = bf16[976,768]{1,0:T(8,128)(2,1)S(1)} collective-permute-done((bf16[976,768]{1,0:T(8,128)(2,1)S(1)}, bf16[976,768]{1,0:T(8,128)(2,1)S(1)}, u32[]{:S(2)}, u32[]{:S(2)}) %collective-permute-start.2) | collective-permute-done | bytes 1499168 | tf_op jit(solution)/shard_map/ppermute | solution.py:537
  84.0 6.1 %collective-permute-done.8.rest_5_.rest_15_.rest_11_ = bf16[976,768]{1,0:T(8,128)(2,1)} collective-permute-done((bf16[976,768]{1,0:T(8,128)(2,1)S(1)}, bf16[976,768]{1,0:T(8,128)(2,1)}, u32[]{:S(2)}, u32[]{:S(2)}) %collective-permute-start.8) | collective-permute-done | bytes 1499168 | tf_op jit(solution)/shard_map/ppermute | solution.py:537
  90.0 2.3 collective-permute-start.9
  94.4 35.5 %collective-permute-done.11.rest_9_.rest_19_.rest_15_ = bf16[384,768]{1,0:T(8,128)(2,1)S(1)} collective-permute-done((bf16[384,768]{1,0:T(8,128)(2,1)S(1)}, bf16[384,768]{1,0:T(8,128)(2,1)S(1)}, u32[]{:S(2)}, u32[]{:S(2)}) %collective-permute-start.11) | collective-permute-done | bytes 589856 | tf_op jit(solution)/shard_map/ppermute | solution.py:537
  132.5 1.3 broadcast_select_fusion.rest_3_.rest_13_.rest_9_
  133.8 1.5 collective-permute-start.10
  136.6 11.9 %collective-permute-done.13 = bf16[384,768]{1,0:T(8,128)(2,1)S(1)} collective-permute-done((bf16[384,768]{1,0:T(8,128)(2,1)S(1)}, bf16[384,768]{1,0:T(8,128)(2,1)S(1)}, u32[]{:S(2)}, u32[]{:S(2)}) %collective-permute-start.13) | collective-permute-done | bytes 589856 | tf_op jit(solution)/shard_map/ppermute | solution.py:537
  148.6 13.2 %collective-permute-done.15 = bf16[384,768]{1,0:T(8,128)(2,1)S(1)} collective-permute-done((bf16[384,768]{1,0:T(8,128)(2,1)S(1)}, bf16[384,768]{1,0:T(8,128)(2,1)S(1)}, u32[]{:S(2)}, u32[]{:S(2)}) %collective-permute-start.15) | collective-permute-done | bytes 589856 | tf_op jit(solution)/shard_map/ppermute | solution.py:537
  165.7 3.2 collective-permute-done.10.rest_7_.rest_17_.rest_13_
  172.2 2.1 collective-permute-done.22.rest_18_.rest_28_.rest_24_
  174.4 2.1 collective-permute-done.23.rest_19_.rest_29_.rest_25_
  177.1 22.8 %forward_stage.2 = (bf16[288,768]{1,0:T(8,128)(2,1)}, bf16[288,768]{1,0:T(8,128)(2,1)}) custom-call(s32[7]{0:T(128)} %stack.55.info, bf16[288,768]{1,0:T(8,128)(2,1)} %pad.8.x_ref, f32[8,288]{1,0:T(8,128)} %iota.16.mask_ref.rest_5_, bf16[976,768]{1,0:T(8,128)(2,1)} %get-tuple-element.56.rest_0_.rest_10_.rest_6_, bf16[976,768]{1,0:T(8,128)(2,1)} %copy-done.4, ...), custom_call_target="tpu_custom_call" | custom-call | flops 8833204224 | bytes 36700160 | tf_op jit(solution)/shard_map/forward_stage/pallas_call | solution.py:224
  200.0 3.6 collective-permute-start.28
  204.4 9.2 %collective-permute-done.28 = bf16[288,768]{1,0:T(8,128)(2,1)S(1)} collective-permute-done((bf16[288,768]{1,0:T(8,128)(2,1)}, bf16[288,768]{1,0:T(8,128)(2,1)S(1)}, u32[]{:S(2)}, u32[]{:S(2)}) %collective-permute-start.28) | collective-permute-done | bytes 442400 | tf_op jit(solution)/shard_map/ppermute | solution.py:490
  214.4 26.0 %forward_stage.3 = (bf16[288,768]{1,0:T(8,128)(2,1)}, bf16[288,768]{1,0:T(8,128)(2,1)}, f32[288,128]{1,0:T(8,128)}, f32[288,768]{1,0:T(8,128)}, bf16[288,2304]{1...) custom-call(s32[7]{0:T(128)} %stack.55.info, ...), custom_call_target="tpu_custom_call" | custom-call | flops 8833204224 | bytes 36700160 | tf_op jit(solution)/shard_map/forward_stage/pallas_call | solution.py:224
  240.4 34.4 %backward_layers.3 = bf16[288,768]{1,0:T(8,128)(2,1)} custom-call(s32[7]{0:T(128)} %stack.55.info, bf16[288,768]{1,0:T(8,128)(2,1)} %pad.7.g_ref, f32[8,288]{1,0:T(8,128)} %iota.16.mask_ref.rest_5_, bf16[288,768]{1,0:T(8,128)(2,1)} %get-tuple-element.62.rest_0_, f32[288,128]{1,0:T(8,128)} %get-tuple-element.63.rest_1_, ...), custom_call_target="tpu_custom_call" | custom-call | flops 9512681472 | bytes 45088768 | tf_op jit(solution)/shard_map/backward_layers/pallas_call | solution.py:355
  276.2 12.3 %collective-permute-done.29 = bf16[288,768]{1,0:T(8,128)(2,1)} collective-permute-done((bf16[288,768]{1,0:T(8,128)(2,1)}, bf16[288,768]{1,0:T(8,128)(2,1)}, u32[]{:S(2)}, u32[]{:S(2)}) %collective-permute-start.29) | collective-permute-done | bytes 442400 | tf_op jit(solution)/shard_map/ppermute | solution.py:490
  288.5 1.9 broadcast_select_fusion.6.g_ref
  290.4 19.9 %backward_layers.4 = (bf16[288,768]{1,0:T(8,128)(2,1)}, f32[16,768]{1,0:T(8,128)}, bf16[288,4608]{1,0:T(8,128)(2,1)}, bf16[288,4608]{1,0:T(8,128)(2,1)}) custom-call(s32[7]{0:T(128)} %stack.55.info, bf16[288,768]{1,0:T(8,128)(2,1)} %broadcast_select_fusion.6.g_ref, f32[8,288]{1,0:T(8,128)} %iota.16.mask_ref.rest_5_, ...), custom_call_target="tpu_custom_call" | custom-call | flops 4756340736 | bytes 22544384 | tf_op jit(solution)/shard_map/backward_layers/pallas_call | solution.py:355
  310.4 5.3 %collective-permute-done.31.br_hbm = bf16[288,4608]{1,0:T(8,128)(2,1)} collective-permute-done((bf16[288,4608]{1,0:T(8,128)(2,1)}, bf16[288,4608]{1,0:T(8,128)(2,1)}, u32[]{:S(2)}, u32[]{:S(2)}) %collective-permute-start.31) | collective-permute-done | bytes 2654240 | tf_op jit(solution)/shard_map/ppermute | solution.py:495
  316.2 12.6 %weight_products.2.rest_5_ = bf16[8,592,768]{2,1,0:T(8,128)(2,1)} custom-call(s32[7]{0:T(128)} %stack.55.info, s32[8]{0:T(128)} %iota.17.slots, f32[16,768]{1,0:T(8,128)} %get-tuple-element.72.gv, bf16[288,4608]{1,0:T(8,128)(2,1)} %get-tuple-element.73.fk_hbm, bf16[288,4608]{1,0:T(8,128)(2,1)} %get-tuple-element.74.bk_hbm, bf16[288,4608]{1,0:T(8,128)(2,1)} %copy-done.19, ...), custom_call_target="tpu_custom_call" | custom-call | flops 4076863488 | bytes 16777216 | tf_op jit(solution)/shard_map/weight_products/pallas_call | solution.py:437
  328.8 1.7 copy-done.28
  330.9 19.8 %backward_layers.5 = (bf16[288,768]{1,0:T(8,128)(2,1)}, f32[16,768]{1,0:T(8,128)}, bf16[288,4608]{1,0:T(8,128)(2,1)}, bf16[288,4608]{1,0:T(8,128)(2,1)}) custom-call(s32[7]{0:T(128)} %stack.55.info, bf16[288,768]{1,0:T(8,128)(2,1)} %get-tuple-element.71.g_ref, f32[8,288]{1,0:T(8,128)} %iota.16.mask_ref.rest_5_, ...), custom_call_target="tpu_custom_call" | custom-call | flops 4756340736 | bytes 22544384 | tf_op jit(solution)/shard_map/backward_layers/pallas_call | solution.py:355
  358.0 12.5 %weight_products.3 = (bf16[592,768]{1,0:T(8,128)(2,1)}, bf16[592,768]{1,0:T(8,128)(2,1)}, bf16[592,768]{1,0:T(8,128)(2,1)}, bf16[592,768]{1,0:T(8,128)(2,1)}, bf...) custom-call(s32[7]{0:T(128)} %stack.55.info, ...), custom_call_target="tpu_custom_call" | custom-call | flops 4076863488 | bytes 16777216 | tf_op jit(solution)/shard_map/weight_products/pallas_call | solution.py:437
  370.6 1.7 collective-permute-start.36
  372.7 21.8 %collective-permute-done.36 = bf16[592,768]{1,0:T(8,128)(2,1)S(1)} collective-permute-done((bf16[592,768]{1,0:T(8,128)(2,1)}, bf16[592,768]{1,0:T(8,128)(2,1)S(1)}, u32[]{:S(2)}, u32[]{:S(2)}) %collective-permute-start.36) | collective-permute-done | bytes 909344 | tf_op jit(solution)/shard_map/ppermute | solution.py:537
  394.4 1.5 add_convert_fusion.3
  395.9 2.6 collective-permute-start.41
  399.3 12.0 %all_to_all.18 = bf16[280,4,192]{2,0,1:T(8,128)(2,1)S(1)} all-to-all(bf16[280,4,192]{2,0,1:T(8,128)(2,1)S(1)} %copy.30), channel_id=1, replica_groups=mesh['section'=4,'dp'=8] {'section'}, dimensions={1} | all-to-all | bytes 860160 | tf_op jit(solution)/shard_map/all_to_all | solution.py:674
  412.4 16.1 %collective-permute-done.34 = bf16[592,768]{1,0:T(8,128)(2,1)} collective-permute-done((bf16[592,768]{1,0:T(8,128)(2,1)}, bf16[592,768]{1,0:T(8,128)(2,1)}, u32[]{:S(2)}, u32[]{:S(2)}) %collective-permute-start.34) | collective-permute-done | bytes 909344 | tf_op jit(solution)/shard_map/ppermute | solution.py:537
  428.5 1.5 add_convert_fusion.5
  430.0 1.5 collective-permute-start.39
  431.5 1.8 collective-permute-start.37
  433.3 1.4 add_convert_fusion.2
  435.9 22.6 %collective-permute-done.39 = bf16[592,768]{1,0:T(8,128)(2,1)S(1)} collective-permute-done((bf16[592,768]{1,0:T(8,128)(2,1)S(1)}, bf16[592,768]{1,0:T(8,128)(2,1)S(1)}, u32[]{:S(2)}, u32[]{:S(2)}) %collective-permute-start.39) | collective-permute-done | bytes 909344 | tf_op jit(solution)/shard_map/ppermute | solution.py:537
  459.5 4.1 collective-permute-done.37
  464.1 1.3 collective-permute-start.43
  465.4 26.6 %collective-permute-start.38 = (bf16[592,768]{1,0:T(8,128)(2,1)S(1)}, bf16[592,768]{1,0:T(8,128)(2,1)S(1)}, u32[]{:S(2)}, u32[]{:S(2)}) collective-permute-start(bf16[592,768]{1,0:T(8,128)(2,1)S(1)} %get-tuple-element.95), channel_id=1, source_target_pairs={{0,2},{1,3},{6,4},{7,5},{8,10},{9,11},{14,12},{15,13},{16,18},{17,... | collective-permute-start | bytes 2727944 | tf_op jit(solution)/shard_map/ppermute | solution.py:537
  492.1 12.8 %collective-permute-done.43 = bf16[592,768]{1,0:T(8,128)(2,1)S(1)} collective-permute-done((bf16[592,768]{1,0:T(8,128)(2,1)S(1)}, bf16[592,768]{1,0:T(8,128)(2,1)S(1)}, u32[]{:S(2)}, u32[]{:S(2)}) %collective-permute-start.43) | collective-permute-done | bytes 909344 | tf_op jit(solution)/shard_map/ppermute | solution.py:537
  506.8 4.2 collective-permute-start.45
  (160 shorter events, 39.4 us)
Async XLA Ops:
  7.2 162.3 %copy-start = (bf16[2,280,768]{2,1,0:T(8,128)(2,1)S(1)}, bf16[2,280,768]{2,1,0:T(8,128)(2,1)}, u32[]{:S(2)}) copy-start(bf16[2,280,768]{2,1,0:T(8,128)(2,1)} %param.16) | copy-start | bytes 2580484
  7.2 499.6 %reduce-scatter.2.cloned.1.call-start = ((), (), s32[]{:S(2)}) async-start(), calls=%async_computation.2 | async-start | bytes 8183808 | tf_op jit(solution)/shard_map/reduce_scatter | solution.py:683
  11.6 12.6 %collective-permute-start.5 = (bf16[192,768]{1,0:T(8,128)(2,1)}, bf16[192,768]{1,0:T(8,128)(2,1)S(1)}, u32[]{:S(2)}, u32[]{:S(2)}) collective-permute-start(bf16[192,768]{1,0:T(8,128)(2,1)} %get-tuple-element.57), channel_id=1, source_target_pairs={{0,1},{1,0},{2,3},{3,2},{4,5},{5,4},{6,7},{7,6},{16,17},{17,16},{1... | collective-permute-start | bytes 884744 | tf_op jit(solution)/shard_map/ppermute | solution.py:537
  16.4 31.9 %collective-permute-start = (bf16[976,768]{1,0:T(8,128)(2,1)}, bf16[976,768]{1,0:T(8,128)(2,1)S(1)}, u32[]{:S(2)}, u32[]{:S(2)}) collective-permute-start(bf16[976,768]{1,0:T(8,128)(2,1)} %get-tuple-element.56.rest_0_.rest_10_.rest_6_), channel_id=1, source_target_pairs={{0,2},{1,3},{2,0},{3,1},{4,6},{5,7},{6,4},{7,5},{8,10},{9,11},{10,... | collective-permute-start | bytes 4497416 | tf_op jit(solution)/shard_map/ppermute | solution.py:537
  18.1 31.1 %collective-permute-start.1 = (bf16[976,768]{1,0:T(8,128)(2,1)}, bf16[976,768]{1,0:T(8,128)(2,1)S(1)}, u32[]{:S(2)}, u32[]{:S(2)}) collective-permute-start(bf16[976,768]{1,0:T(8,128)(2,1)} %get-tuple-element.56.rest_0_.rest_10_.rest_6_), channel_id=1, source_target_pairs={{2,4},{3,5},{4,2},{5,3},{10,12},{11,13},{12,10},{13,11},{18,20},{1... | collective-permute-start | bytes 4497416 | tf_op jit(solution)/shard_map/ppermute | solution.py:537
  24.2 30.0 %collective-permute-start.6 = (bf16[976,768]{1,0:T(8,128)(2,1)}, bf16[976,768]{1,0:T(8,128)(2,1)S(1)}, u32[]{:S(2)}, u32[]{:S(2)}) collective-permute-start(bf16[976,768]{1,0:T(8,128)(2,1)} %get-tuple-element.56.rest_0_.rest_10_.rest_6_), channel_id=1, source_target_pairs={{0,1},{1,0},{2,3},{3,2},{4,5},{5,4},{6,7},{7,6},{8,9},{9,8},{10,11... | collective-permute-start | bytes 4497416 | tf_op jit(solution)/shard_map/ppermute | solution.py:537
  48.4 8.5 %collective-permute-start.3 = (bf16[976,768]{1,0:T(8,128)(2,1)S(1)}, bf16[976,768]{1,0:T(8,128)(2,1)S(1)}, u32[]{:S(2)}, u32[]{:S(2)}) collective-permute-start(bf16[976,768]{1,0:T(8,128)(2,1)S(1)} %collective-permute-done.rest_1_.rest_11_.rest_7_), channel_id=1, source_target_pairs={{2,4},{3,5},{4,2},{5,3},{10,12},{11,13},{12,10},{13,11},{18,20},{1... | collective-permute-start | bytes 4497416 | tf_op jit(solution)/shard_map/ppermute | solution.py:537
  49.2 34.6 %collective-permute-start.2 = (bf16[976,768]{1,0:T(8,128)(2,1)S(1)}, bf16[976,768]{1,0:T(8,128)(2,1)S(1)}, u32[]{:S(2)}, u32[]{:S(2)}) collective-permute-start(bf16[976,768]{1,0:T(8,128)(2,1)S(1)} %collective-permute-done.1), channel_id=1, source_target_pairs={{2,0},{3,1},{4,6},{5,7},{10,8},{11,9},{12,14},{13,15},{18,16},{19,... | collective-permute-start | bytes 4497416 | tf_op jit(solution)/shard_map/ppermute | solution.py:537
  54.1 0.7 collective-permute-start.7
  54.8 35.2 %collective-permute-start.8 = (bf16[976,768]{1,0:T(8,128)(2,1)S(1)}, bf16[976,768]{1,0:T(8,128)(2,1)}, u32[]{:S(2)}, u32[]{:S(2)}) collective-permute-start(bf16[976,768]{1,0:T(8,128)(2,1)S(1)} %collective-permute-done.rest_1_.rest_11_.rest_7_), channel_id=1, source_target_pairs={{0,1},{1,0},{2,3},{3,2},{4,5},{5,4},{6,7},{7,6},{8,9},{9,8},{10,11... | collective-permute-start | bytes 4497416 | tf_op jit(solution)/shard_map/ppermute | solution.py:537
  56.9 73.7 %collective-permute-start.4 = (bf16[976,768]{1,0:T(8,128)(2,1)S(1)}, bf16[976,768]{1,0:T(8,128)(2,1)S(1)}, u32[]{:S(2)}, u32[]{:S(2)}) collective-permute-start(bf16[976,768]{1,0:T(8,128)(2,1)S(1)} %collective-permute-done.3), channel_id=1, source_target_pairs={{2,0},{3,1},{4,6},{5,7},{10,8},{11,9},{12,14},{13,15},{18,16},{19,... | collective-permute-start | bytes 4497416 | tf_op jit(solution)/shard_map/ppermute | solution.py:537
  90.0 41.1 %collective-permute-start.9 = (bf16[976,768]{1,0:T(8,128)(2,1)S(1)}, bf16[976,768]{1,0:T(8,128)(2,1)}, u32[]{:S(2)}, u32[]{:S(2)}) collective-permute-start(bf16[976,768]{1,0:T(8,128)(2,1)S(1)} %broadcast_select_fusion.1.rest_2_.rest_12_.rest_8_), channel_id=1, source_target_pairs={{0,1},{1,0},{2,3},{3,2},{4,5},{5,4},{6,7},{7,6},{8,9},{9,8},{10,11... | collective-permute-start | bytes 4497416 | tf_op jit(solution)/shard_map/ppermute | solution.py:537
  92.4 41.4 %collective-permute-start.16 = (bf16[976,768]{1,0:T(8,128)(2,1)S(1)}, bf16[976,768]{1,0:T(8,128)(2,1)S(1)}, u32[]{:S(2)}, u32[]{:S(2)}) collective-permute-start(bf16[976,768]{1,0:T(8,128)(2,1)S(1)} %copy-done.3), channel_id=1, source_target_pairs={{0,8},{8,0},{16,24},{24,16},{1,9},{9,1},{17,25},{25,17},{2,10},{10... | collective-permute-start | bytes 4497416 | tf_op jit(solution)/shard_map/ppermute | solution.py:495
  92.6 37.3 %collective-permute-start.11 = (bf16[384,768]{1,0:T(8,128)(2,1)S(1)}, bf16[384,768]{1,0:T(8,128)(2,1)S(1)}, u32[]{:S(2)}, u32[]{:S(2)}) collective-permute-start(bf16[384,768]{1,0:T(8,128)(2,1)S(1)} %pad_maximum_fusion.rest_8_.rest_18_.rest_14_), channel_id=1, source_target_pairs={{0,2},{1,3},{2,0},{3,1},{4,6},{5,7},{6,4},{7,5},{8,10},{9,11},{10,... | collective-permute-start | bytes 1769480 | tf_op jit(solution)/shard_map/ppermute | solution.py:537
  93.7 36.2 %collective-permute-start.12 = (bf16[384,768]{1,0:T(8,128)(2,1)S(1)}, bf16[384,768]{1,0:T(8,128)(2,1)S(1)}, u32[]{:S(2)}, u32[]{:S(2)}) collective-permute-start(bf16[384,768]{1,0:T(8,128)(2,1)S(1)} %pad_maximum_fusion.rest_8_.rest_18_.rest_14_), channel_id=1, source_target_pairs={{2,4},{3,5},{4,2},{5,3},{10,12},{11,13},{12,10},{13,11},{18,20},{1... | collective-permute-start | bytes 1769480 | tf_op jit(solution)/shard_map/ppermute | solution.py:537
  129.9 32.5 %collective-permute-start.17 = (bf16[976,768]{1,0:T(8,128)(2,1)S(1)}, bf16[976,768]{1,0:T(8,128)(2,1)S(1)}, u32[]{:S(2)}, u32[]{:S(2)}) collective-permute-start(bf16[976,768]{1,0:T(8,128)(2,1)S(1)} %collective-permute-done.rest_1_.rest_11_.rest_7_), channel_id=1, source_target_pairs={{0,8},{8,0},{16,24},{24,16},{1,9},{9,1},{17,25},{25,17},{2,10},{10... | collective-permute-start | bytes 4497416 | tf_op jit(solution)/shard_map/ppermute | solution.py:495
  129.9 5.4 %collective-permute-start.14 = (bf16[384,768]{1,0:T(8,128)(2,1)S(1)}, bf16[384,768]{1,0:T(8,128)(2,1)S(1)}, u32[]{:S(2)}, u32[]{:S(2)}) collective-permute-start(bf16[384,768]{1,0:T(8,128)(2,1)S(1)} %collective-permute-done.11.rest_9_.rest_19_.rest_15_), channel_id=1, source_target_pairs={{2,4},{3,5},{4,2},{5,3},{10,12},{11,13},{12,10},{13,11},{18,20},{1... | collective-permute-start | bytes 1769480 | tf_op jit(solution)/shard_map/ppermute | solution.py:537
  130.6 33.3 %collective-permute-start.20 = (bf16[976,768]{1,0:T(8,128)(2,1)S(1)}, bf16[976,768]{1,0:T(8,128)(2,1)S(1)}, u32[]{:S(2)}, u32[]{:S(2)}) collective-permute-start(bf16[976,768]{1,0:T(8,128)(2,1)S(1)} %collective-permute-done.6.rest_4_.rest_14_.rest_10_), channel_id=1, source_target_pairs={{0,8},{8,0},{16,24},{24,16},{1,9},{9,1},{17,25},{25,17},{2,10},{10... | collective-permute-start | bytes 4497416 | tf_op jit(solution)/shard_map/ppermute | solution.py:495
  131.2 17.3 %collective-permute-start.13 = (bf16[384,768]{1,0:T(8,128)(2,1)S(1)}, bf16[384,768]{1,0:T(8,128)(2,1)S(1)}, u32[]{:S(2)}, u32[]{:S(2)}) collective-permute-start(bf16[384,768]{1,0:T(8,128)(2,1)S(1)} %collective-permute-done.12), channel_id=1, source_target_pairs={{2,0},{3,1},{4,6},{5,7},{10,8},{11,9},{12,14},{13,15},{18,16},{19,... | collective-permute-start | bytes 1769480 | tf_op jit(solution)/shard_map/ppermute | solution.py:537
  133.8 35.1 %collective-permute-start.10 = (bf16[976,768]{1,0:T(8,128)(2,1)}, bf16[976,768]{1,0:T(8,128)(2,1)}, u32[]{:S(2)}, u32[]{:S(2)}) collective-permute-start(bf16[976,768]{1,0:T(8,128)(2,1)} %broadcast_select_fusion.rest_3_.rest_13_.rest_9_), channel_id=1, source_target_pairs={{0,1},{1,0},{2,3},{3,2},{4,5},{5,4},{6,7},{7,6},{8,9},{9,8},{10,11... | collective-permute-start | bytes 4497416 | tf_op jit(solution)/shard_map/ppermute | solution.py:537
  135.3 26.4 %collective-permute-start.15 = (bf16[384,768]{1,0:T(8,128)(2,1)S(1)}, bf16[384,768]{1,0:T(8,128)(2,1)S(1)}, u32[]{:S(2)}, u32[]{:S(2)}) collective-permute-start(bf16[384,768]{1,0:T(8,128)(2,1)S(1)} %collective-permute-done.14), channel_id=1, source_target_pairs={{2,0},{3,1},{4,6},{5,7},{10,8},{11,9},{12,14},{13,15},{18,16},{19,... | collective-permute-start | bytes 1769480 | tf_op jit(solution)/shard_map/ppermute | solution.py:537
  148.5 13.3 %collective-permute-start.24 = (bf16[384,768]{1,0:T(8,128)(2,1)S(1)}, bf16[384,768]{1,0:T(8,128)(2,1)S(1)}, u32[]{:S(2)}, u32[]{:S(2)}) collective-permute-start(bf16[384,768]{1,0:T(8,128)(2,1)S(1)} %pad_maximum_fusion.rest_8_.rest_18_.rest_14_), channel_id=1, source_target_pairs={{0,8},{8,0},{16,24},{24,16},{1,9},{9,1},{17,25},{25,17},{2,10},{10... | collective-permute-start | bytes 1769480 | tf_op jit(solution)/shard_map/ppermute | solution.py:495
  161.7 2.0 collective-permute-start.25
  161.8 2.7 collective-permute-start.26
  162.4 3.0 collective-permute-start.27
  163.8 7.3 %collective-permute-start.18 = (bf16[976,768]{1,0:T(8,128)(2,1)S(1)}, bf16[976,768]{1,0:T(8,128)(2,1)}, u32[]{:S(2)}, u32[]{:S(2)}) collective-permute-start(bf16[976,768]{1,0:T(8,128)(2,1)S(1)} %broadcast_select_fusion.1.rest_2_.rest_12_.rest_8_), channel_id=1, source_target_pairs={{0,8},{8,0},{16,24},{24,16},{1,9},{9,1},{17,25},{25,17},{2,10},{10... | collective-permute-start | bytes 4497416 | tf_op jit(solution)/shard_map/ppermute | solution.py:495
  163.9 7.2 %collective-permute-start.21 = (bf16[976,768]{1,0:T(8,128)(2,1)}, bf16[976,768]{1,0:T(8,128)(2,1)}, u32[]{:S(2)}, u32[]{:S(2)}) collective-permute-start(bf16[976,768]{1,0:T(8,128)(2,1)} %collective-permute-done.8.rest_5_.rest_15_.rest_11_), channel_id=1, source_target_pairs={{0,8},{8,0},{16,24},{24,16},{1,9},{9,1},{17,25},{25,17},{2,10},{10... | collective-permute-start | bytes 4497416 | tf_op jit(solution)/shard_map/ppermute | solution.py:495
  165.1 7.1 %collective-permute-start.19 = (bf16[976,768]{1,0:T(8,128)(2,1)}, bf16[976,768]{1,0:T(8,128)(2,1)}, u32[]{:S(2)}, u32[]{:S(2)}) collective-permute-start(bf16[976,768]{1,0:T(8,128)(2,1)} %broadcast_select_fusion.rest_3_.rest_13_.rest_9_), channel_id=1, source_target_pairs={{0,8},{8,0},{16,24},{24,16},{1,9},{9,1},{17,25},{25,17},{2,10},{10... | collective-permute-start | bytes 4497416 | tf_op jit(solution)/shard_map/ppermute | solution.py:495
  165.4 8.9 %collective-permute-start.22 = (bf16[976,768]{1,0:T(8,128)(2,1)}, bf16[976,768]{1,0:T(8,128)(2,1)}, u32[]{:S(2)}, u32[]{:S(2)}) collective-permute-start(bf16[976,768]{1,0:T(8,128)(2,1)} %collective-permute-done.9.rest_6_.rest_16_.rest_12_), channel_id=1, source_target_pairs={{0,8},{8,0},{16,24},{24,16},{1,9},{9,1},{17,25},{25,17},{2,10},{10... | collective-permute-start | bytes 4497416 | tf_op jit(solution)/shard_map/ppermute | solution.py:495
  168.9 7.6 %collective-permute-start.23 = (bf16[976,768]{1,0:T(8,128)(2,1)}, bf16[976,768]{1,0:T(8,128)(2,1)}, u32[]{:S(2)}, u32[]{:S(2)}) collective-permute-start(bf16[976,768]{1,0:T(8,128)(2,1)} %collective-permute-done.10.rest_7_.rest_17_.rest_13_), channel_id=1, source_target_pairs={{0,8},{8,0},{16,24},{24,16},{1,9},{9,1},{17,25},{25,17},{2,10},{10... | collective-permute-start | bytes 4497416 | tf_op jit(solution)/shard_map/ppermute | solution.py:495
  200.0 13.6 %collective-permute-start.28 = (bf16[288,768]{1,0:T(8,128)(2,1)}, bf16[288,768]{1,0:T(8,128)(2,1)S(1)}, u32[]{:S(2)}, u32[]{:S(2)}) collective-permute-start(bf16[288,768]{1,0:T(8,128)(2,1)} %get-tuple-element.61), channel_id=1, source_target_pairs={{0,16},{8,24},{1,17},{9,25},{2,18},{10,26},{3,19},{11,27},{4,20},{... | collective-permute-start | bytes 1327112 | tf_op jit(solution)/shard_map/ppermute | solution.py:490
  274.8 13.7 %collective-permute-start.29 = (bf16[288,768]{1,0:T(8,128)(2,1)}, bf16[288,768]{1,0:T(8,128)(2,1)}, u32[]{:S(2)}, u32[]{:S(2)}) collective-permute-start(bf16[288,768]{1,0:T(8,128)(2,1)} %backward_layers.3), channel_id=1, source_target_pairs={{16,0},{24,8},{17,1},{25,9},{18,2},{26,10},{19,3},{27,11},{20,4},{... | collective-permute-start | bytes 1327112 | tf_op jit(solution)/shard_map/ppermute | solution.py:490
  276.1 34.2 %collective-permute-start.30 = (bf16[288,4608]{1,0:T(8,128)(2,1)}, bf16[288,4608]{1,0:T(8,128)(2,1)S(1)}, u32[]{:S(2)}, u32[]{:S(2)}) collective-permute-start(bf16[288,4608]{1,0:T(8,128)(2,1)} %get-tuple-element.75), channel_id=1, source_target_pairs={{0,8},{8,0},{16,24},{24,16},{1,9},{9,1},{17,25},{25,17},{2,10},{10... | collective-permute-start | bytes 7962632 | tf_op jit(solution)/shard_map/ppermute | solution.py:495
  310.3 5.4 %collective-permute-start.31 = (bf16[288,4608]{1,0:T(8,128)(2,1)}, bf16[288,4608]{1,0:T(8,128)(2,1)}, u32[]{:S(2)}, u32[]{:S(2)}) collective-permute-start(bf16[288,4608]{1,0:T(8,128)(2,1)} %get-tuple-element.76), channel_id=1, source_target_pairs={{0,8},{8,0},{16,24},{24,16},{1,9},{9,1},{17,25},{25,17},{2,10},{10... | collective-permute-start | bytes 7962632 | tf_op jit(solution)/shard_map/ppermute | solution.py:495
  330.5 27.5 %collective-permute-start.32 = (bf16[288,4608]{1,0:T(8,128)(2,1)S(1)}, bf16[288,4608]{1,0:T(8,128)(2,1)}, u32[]{:S(2)}, u32[]{:S(2)}) collective-permute-start(bf16[288,4608]{1,0:T(8,128)(2,1)S(1)} %copy-done.28), channel_id=1, source_target_pairs={{0,8},{8,0},{16,24},{24,16},{1,9},{9,1},{17,25},{25,17},{2,10},{10... | collective-permute-start | bytes 7962632 | tf_op jit(solution)/shard_map/ppermute | solution.py:495
  350.7 7.3 %collective-permute-start.33 = (bf16[288,4608]{1,0:T(8,128)(2,1)}, bf16[288,4608]{1,0:T(8,128)(2,1)}, u32[]{:S(2)}, u32[]{:S(2)}) collective-permute-start(bf16[288,4608]{1,0:T(8,128)(2,1)} %get-tuple-element.83), channel_id=1, source_target_pairs={{0,8},{8,0},{16,24},{24,16},{1,9},{9,1},{17,25},{25,17},{2,10},{10... | collective-permute-start | bytes 7962632 | tf_op jit(solution)/shard_map/ppermute | solution.py:495
  370.6 23.9 %collective-permute-start.36 = (bf16[592,768]{1,0:T(8,128)(2,1)}, bf16[592,768]{1,0:T(8,128)(2,1)S(1)}, u32[]{:S(2)}, u32[]{:S(2)}) collective-permute-start(bf16[592,768]{1,0:T(8,128)(2,1)} %get-tuple-element.90), channel_id=1, source_target_pairs={{0,1},{1,0},{2,3},{3,2},{4,5},{5,4},{6,7},{7,6},{8,9},{9,8},{10,11... | collective-permute-start | bytes 2727944 | tf_op jit(solution)/shard_map/ppermute | solution.py:537
  372.3 56.2 %collective-permute-start.34 = (bf16[592,768]{1,0:T(8,128)(2,1)}, bf16[592,768]{1,0:T(8,128)(2,1)}, u32[]{:S(2)}, u32[]{:S(2)}) collective-permute-start(bf16[592,768]{1,0:T(8,128)(2,1)} %get-tuple-element.86), channel_id=1, source_target_pairs={{0,1},{1,0},{2,3},{3,2},{4,5},{5,4},{6,7},{7,6},{8,9},{9,8},{10,11... | collective-permute-start | bytes 2727944 | tf_op jit(solution)/shard_map/ppermute | solution.py:537
  395.9 37.4 %collective-permute-start.41 = (bf16[592,768]{1,0:T(8,128)(2,1)S(1)}, bf16[592,768]{1,0:T(8,128)(2,1)}, u32[]{:S(2)}, u32[]{:S(2)}) collective-permute-start(bf16[592,768]{1,0:T(8,128)(2,1)S(1)} %add_convert_fusion.3), channel_id=1, source_target_pairs={{0,2},{1,3},{6,4},{7,5},{8,10},{9,11},{14,12},{15,13},{16,18},{17,... | collective-permute-start | bytes 2727944 | tf_op jit(solution)/shard_map/ppermute | solution.py:537
  430.0 28.6 %collective-permute-start.39 = (bf16[592,768]{1,0:T(8,128)(2,1)S(1)}, bf16[592,768]{1,0:T(8,128)(2,1)S(1)}, u32[]{:S(2)}, u32[]{:S(2)}) collective-permute-start(bf16[592,768]{1,0:T(8,128)(2,1)S(1)} %add_convert_fusion.5), channel_id=1, source_target_pairs={{0,2},{1,3},{6,4},{7,5},{8,10},{9,11},{14,12},{15,13},{16,18},{17,... | collective-permute-start | bytes 2727944 | tf_op jit(solution)/shard_map/ppermute | solution.py:537
  431.5 32.2 %collective-permute-start.37 = (bf16[592,768]{1,0:T(8,128)(2,1)S(1)}, bf16[592,768]{1,0:T(8,128)(2,1)S(1)}, u32[]{:S(2)}, u32[]{:S(2)}) collective-permute-start(bf16[592,768]{1,0:T(8,128)(2,1)S(1)} %copy-done.30), channel_id=1, source_target_pairs={{0,1},{1,0},{2,3},{3,2},{4,5},{5,4},{6,7},{7,6},{8,9},{9,8},{10,11... | collective-permute-start | bytes 2727944 | tf_op jit(solution)/shard_map/ppermute | solution.py:537
  434.7 29.0 %collective-permute-start.42 = (bf16[592,768]{1,0:T(8,128)(2,1)S(1)}, bf16[592,768]{1,0:T(8,128)(2,1)S(1)}, u32[]{:S(2)}, u32[]{:S(2)}) collective-permute-start(bf16[592,768]{1,0:T(8,128)(2,1)S(1)} %add_convert_fusion.2), channel_id=1, source_target_pairs={{2,4},{3,5},{4,2},{5,3},{10,12},{11,13},{12,10},{13,11},{18,20},{1... | collective-permute-start | bytes 2727944 | tf_op jit(solution)/shard_map/ppermute | solution.py:537
  435.6 56.5 %collective-permute-start.35 = (bf16[592,768]{1,0:T(8,128)(2,1)S(1)}, bf16[592,768]{1,0:T(8,128)(2,1)S(1)}, u32[]{:S(2)}, u32[]{:S(2)}) collective-permute-start(bf16[592,768]{1,0:T(8,128)(2,1)S(1)} %copy-done.29), channel_id=1, source_target_pairs={{0,1},{1,0},{2,3},{3,2},{4,5},{5,4},{6,7},{7,6},{8,9},{9,8},{10,11... | collective-permute-start | bytes 2727944 | tf_op jit(solution)/shard_map/ppermute | solution.py:537
  458.8 33.2 %collective-permute-start.40 = (bf16[592,768]{1,0:T(8,128)(2,1)S(1)}, bf16[592,768]{1,0:T(8,128)(2,1)S(1)}, u32[]{:S(2)}, u32[]{:S(2)}) collective-permute-start(bf16[592,768]{1,0:T(8,128)(2,1)S(1)} %add_convert_fusion.4), channel_id=1, source_target_pairs={{2,4},{3,5},{4,2},{5,3},{10,12},{11,13},{12,10},{13,11},{18,20},{1... | collective-permute-start | bytes 2727944 | tf_op jit(solution)/shard_map/ppermute | solution.py:537
  464.1 40.7 %collective-permute-start.43 = (bf16[592,768]{1,0:T(8,128)(2,1)S(1)}, bf16[592,768]{1,0:T(8,128)(2,1)S(1)}, u32[]{:S(2)}, u32[]{:S(2)}) collective-permute-start(bf16[592,768]{1,0:T(8,128)(2,1)S(1)} %get-tuple-element.94), channel_id=1, source_target_pairs={{2,0},{3,1},{4,6},{5,7},{10,8},{11,9},{12,14},{13,15},{18,16},{19,... | collective-permute-start | bytes 2727944 | tf_op jit(solution)/shard_map/ppermute | solution.py:537
  465.4 39.4 %collective-permute-start.38 = (bf16[592,768]{1,0:T(8,128)(2,1)S(1)}, bf16[592,768]{1,0:T(8,128)(2,1)S(1)}, u32[]{:S(2)}, u32[]{:S(2)}) collective-permute-start(bf16[592,768]{1,0:T(8,128)(2,1)S(1)} %get-tuple-element.95), channel_id=1, source_target_pairs={{0,2},{1,3},{6,4},{7,5},{8,10},{9,11},{14,12},{15,13},{16,18},{17,... | collective-permute-start | bytes 2727944 | tf_op jit(solution)/shard_map/ppermute | solution.py:537
  505.5 6.3 %collective-permute-start.44 = (bf16[592,768]{1,0:T(8,128)(2,1)S(1)}, bf16[592,768]{1,0:T(8,128)(2,1)S(1)}, u32[]{:S(2)}, u32[]{:S(2)}) collective-permute-start(bf16[592,768]{1,0:T(8,128)(2,1)S(1)} %add_convert_fusion), channel_id=1, source_target_pairs={{8,0},{24,16},{9,1},{25,17},{10,2},{26,18},{11,3},{27,19},{12,4},{... | collective-permute-start | bytes 2727944 | tf_op jit(solution)/shard_map/ppermute | solution.py:692
  506.8 5.6 %collective-permute-start.45 = (bf16[592,768]{1,0:T(8,128)(2,1)}, bf16[592,768]{1,0:T(8,128)(2,1)}, u32[]{:S(2)}, u32[]{:S(2)}) collective-permute-start(bf16[592,768]{1,0:T(8,128)(2,1)} %bitcast.52), channel_id=1, source_target_pairs={{0,8},{16,24},{1,9},{17,25},{2,10},{18,26},{3,11},{19,27},{4,12},{... | collective-permute-start | bytes 2727944 | tf_op jit(solution)/shard_map/ppermute | solution.py:692
  (31 other events, 850.3 us)
Sparse Core Ops, SparseCore 0:
  328.9 163.5 reduce-scatter.1

commit v4 on v3

--- a/solution.py
+++ b/solution.py
@@ -24,7 +24,6 @@
 
 ANYS = pl.BlockSpec(memory_space=pl.ANY)
 VM = pl.BlockSpec(memory_space=pltpu.VMEM)
-SM = pl.BlockSpec(memory_space=pltpu.SMEM)
 
 
 def dot(a, b, ca=1, cb=0):
@@ -35,6 +34,23 @@
     mean = jnp.mean(v, axis=-1, keepdims=True)
     cent = v - mean
     return cent, lax.rsqrt(jnp.mean(cent * cent, axis=-1, keepdims=True) + EPS)
+
+
+def here():
+    spot, core = lax.axis_index("dp"), lax.axis_index("section") % 2
+    z, column = spot // 2, spot % 2
+    middle = jnp.where((z == 1) | (z == 2), 1, 0)
+    return [core, 1 - core, z, column, middle, core, 2 + middle]
+
+
+def sending_slots(z, column):
+    orders = ((3, 2, 1, 0), (2, 3, 1, 0), (0, 1, 3, 2), (0, 1, 2, 3))
+    slots = []
+    for j in range(8):
+        a, b, c, d = (o[j // 2] for o in orders)
+        slot = jnp.where(z == 0, a, jnp.where(z == 1, b, jnp.where(z == 2, c, d)))
+        slots.append(slot + jnp.where(column == j % 2, 0, 4))
+    return slots
 
 
 def square(block):
@@ -192,7 +208,8 @@
     return acc.astype(BF)
 
 
-def forward_kernel(save, count, info, x_ref, mask_ref, *rest):
+def forward_kernel(save, count, x_ref, mask_ref, *rest):
+    info = here()
     sets, rest = (rest[:count], rest[count:2 * count]), rest[2 * count:]
     wide = 14 if save else 2
     results, rest = rest[:wide], rest[wide:]
@@ -211,7 +228,7 @@
         c.wait()
 
 
-def forward_stage(save, info, x, mask, wa, wb):
+def forward_stage(save, x, mask, wa, wb):
     def sd(cols, t=BF):
         return jax.ShapeDtypeStruct((ROWS, cols), t)
 
@@ -224,13 +241,13 @@
     return pl.pallas_call(
         functools.partial(forward_kernel, save, len(wa)),
         out_shape=shapes,
-        in_specs=[SM, VM, VM] + [ANYS] * (2 * len(wa)),
+        in_specs=[VM, VM] + [ANYS] * (2 * len(wa)),
         out_specs=specs,
         scratch_shapes=weight_scratch(len(wa)) * 2 + work * 2 + [pltpu.SemaphoreType.DMA((14,))],
         compiler_params=pltpu.CompilerParams(vmem_limit_bytes=VMEM_LIMIT),
         cost_estimate=pl.CostEstimate(flops=2 * ROWS * D * D * 26, bytes_accessed=48 * D * D + 2**23, transcendentals=0),
         name="forward_stage",
-    )(info, x, mask, *wa, *wb)
+    )(x, mask, *wa, *wb)
 
 
 def backward_one(save, core, g_ref, x_ref, lse_ref, mid_ref, j_hbm, gp_hbm, usable, copies, scratch, work, isems, osems, results,
@@ -312,7 +329,8 @@
     return (d_mid + norm_back(x_ref[...].astype(F32), d_n, vec[AG:AG + 1, :], AG)).astype(BF)
 
 
-def backward_kernel(save, layers, count, info, g_ref, mask_ref, *rest):
+def backward_kernel(save, layers, count, g_ref, mask_ref, *rest):
+    info = here()
     m = len(layers)
     kept, rest = [rest[5 * i:5 * i + 5] for i in range(m)], rest[5 * m:]
     rest = rest[1:] if save else rest
@@ -340,7 +358,7 @@
         c.wait()
 
 
-def backward_layers(save, layers, info, g, mask, saved, wa, wb, behind):
+def backward_layers(save, layers, g, mask, saved, wa, wb, behind):
     def sd(cols, t=BF, rows=ROWS):
         return jax.ShapeDtypeStruct((rows, cols), t)
 
@@ -355,21 +373,24 @@
     return pl.pallas_call(
         functools.partial(backward_kernel, save, layers, len(wa)),
         out_shape=shapes,
-        in_specs=[SM, VM, VM] + [VM, VM, VM, ANYS, ANYS] * m + [ANYS] * (save + 2 * len(wa)),
+        in_specs=[VM, VM] + [VM, VM, VM, ANYS, ANYS] * m + [ANYS] * (save + 2 * len(wa)),
         out_specs=specs,
         scratch_shapes=weight_scratch(len(wa)) * m + work * m + [
             pltpu.VMEM((ROWS, D), BF), pltpu.SemaphoreType.DMA((m, 2)), pltpu.SemaphoreType.DMA((5,))],
         compiler_params=pltpu.CompilerParams(vmem_limit_bytes=VMEM_LIMIT),
         cost_estimate=pl.CostEstimate(flops=2 * ROWS * D * D * 14 * m, bytes_accessed=m * (24 * D * D + 2**23), transcendentals=0),
         name="backward_layers",
-    )(info, g, mask, *kept, *([behind] if save else []), *wa, *wb)
-
-
-def product_kernel(n, joined, info, slots, gv, fk_hbm, bk_hbm, fr_hbm, br_hbm, *rest):
-    outs = [rest[0].at[j] for j in range(n)] if joined else rest[:n]
-    f, b, held, isems, osems = rest[-5:]
+    )(g, mask, *kept, *([behind] if save else []), *wa, *wb)
+
+
+def product_kernel(n, direct, behind, gv, fk_hbm, bk_hbm, fr_hbm, br_hbm, *rest):
+    wide = n + 4 * (direct > 0)
+    outs, rest = rest[:wide], rest[wide:]
+    f, b, held, isems, osems = rest[:5]
+    info = here()
+    slots = sending_slots(info[2], info[3]) if n > 1 else [0]
     r = D // n
-    flat = HALF
+    flat = HALF - direct
     loads = {}
 
     def load(first, core):
@@ -392,6 +413,15 @@
         pltpu.make_async_copy(held.at[j, pl.ds(flat * r, TAIL)], outs[j].at[pl.ds(flat * r, TAIL)], osems.at[0]).start()
 
     def store(c, val):
+        if c >= flat:
+            for j in range(n):
+                rest[5][slots[j] % 4, slots[j] // 4, (c - flat) * r:(c - flat + 1) * r] = val[j * r:(j + 1) * r]
+            if c == HALF - 1:
+                for k in range(4):
+                    for far in (0, 1):
+                        rows = pl.ds(far * direct * r, direct * r)
+                        pltpu.make_async_copy(rest[5].at[k, far], outs[n + k].at[rows], osems.at[0]).start()
+            return
         for j in range(n):
             held[slots[j], c * r:(c + 1) * r] = val[j * r:(j + 1) * r]
         for j in range(n):
@@ -427,28 +457,33 @@
 
     for j in range(n):
         pltpu.make_async_copy(held.at[j], outs[j], osems.at[0]).wait()
-
-
-def weight_products(n, joined, info, slots, gv, fk, bk, fr, br):
-    shape = (HALF * (D // n) + TAIL, D)
-    shapes = [jax.ShapeDtypeStruct((n,) + shape, BF)] if joined else [jax.ShapeDtypeStruct(shape, BF)] * n
+    if direct:
+        pltpu.make_async_copy(rest[5], rest[5], osems.at[0]).wait()
+
+
+def weight_products(n, direct, behind, gv, fk, bk, fr, br):
+    shape = ((HALF - direct) * (D // n) + TAIL, D)
+    shapes = [jax.ShapeDtypeStruct(shape, BF)] * n
     scratch = [pltpu.VMEM((HALF, 2 * ROWS, D), BF), pltpu.VMEM((HALF, 2 * ROWS, D), BF), pltpu.VMEM((n,) + shape, BF),
                pltpu.SemaphoreType.DMA((2, HALF)), pltpu.SemaphoreType.DMA((1,))]
+    if direct:
+        shapes += [jax.ShapeDtypeStruct((2 * direct * (D // n), D), BF)] * 4
+        scratch.append(pltpu.VMEM((4, 2, direct * (D // n), D), BF))
     return pl.pallas_call(
-        functools.partial(product_kernel, n, joined),
+        functools.partial(product_kernel, n, direct),
         out_shape=shapes,
-        in_specs=[SM, SM, VM] + [ANYS] * 4,
+        in_specs=[ANYS, VM] + [ANYS] * 4,
         out_specs=[ANYS] * len(shapes),
         scratch_shapes=scratch,
         compiler_params=pltpu.CompilerParams(vmem_limit_bytes=VMEM_LIMIT),
         cost_estimate=pl.CostEstimate(flops=2 * 2 * ROWS * D * D * 6, bytes_accessed=2**24, transcendentals=0),
         name="weight_products",
-    )(info, slots, gv, fk, bk, fr, br)
-
-
-def pack_kernel(info, joint, output, up, down, ag, as_, jb, ob, fg, fs, db, ub, block_ref, pair_ref):
+    )(behind, gv, fk, bk, fr, br)
+
+
+def pack_kernel(joint, output, up, down, ag, as_, jb, ob, fg, fs, db, ub, block_ref, pair_ref):
     r = output.shape[0]
-    spot = info[2] * 2 + info[3]
+    spot = lax.axis_index("dp")
     for k in range(3):
         block_ref[k * r:(k + 1) * r, :] = joint[:, k * D:(k + 1) * D].astype(BF)
     block_ref[3 * r:4 * r, :] = output[...].astype(BF)
@@ -473,16 +508,16 @@
     block_ref[10 * r:, :] = jnp.concatenate(rows).astype(BF)
 
 
-def pack(info, *params):
+def pack(*params):
     r = params[1].shape[0]
     return pl.pallas_call(
         pack_kernel,
         out_shape=[jax.ShapeDtypeStruct((10 * r + TAIL, D), BF), jax.ShapeDtypeStruct((2 * r, D), BF)],
-        in_specs=[SM] + [VM] * 12,
+        in_specs=[VM] * 12,
         out_specs=[VM, VM],
         compiler_params=pltpu.CompilerParams(vmem_limit_bytes=VMEM_LIMIT),
         name="pack",
-    )(info, *params)
+    )(*params)
 
 
 def moved(value, axis, by):
@@ -490,9 +525,13 @@
     return lax.ppermute(value, axis, [(i, i + by) for i in range(peers) if 0 <= i + by < peers])
 
 
+def flipped(value, bit):
+    peers = lax.axis_size("section")
+    return lax.ppermute(value, "section", [(i, i ^ bit) for i in range(peers)])
+
+
 def swapped(value):
-    peers = lax.axis_size("section")
-    return lax.ppermute(value, "section", [(i, i ^ 1) for i in range(peers)])
+    return flipped(value, 1)
 
 
 def vector_tail(n, spot, attend_gain, attend_shift, joint_bias, output_bias, feed_gain, feed_shift, down_bias, up_bias):
@@ -579,10 +618,28 @@
     return total.astype(BF)
 
 
-def scatter_steps(net, blocks, across, zero=None):
+def scatter_rounds(blocks, wide=None, extra=None):
+    net = Links(x=9, z=9)
+    x0 = net.across(blocks[4])
+    s0 = add(blocks[0], x0)
+    b, s0 = lax.optimization_barrier((blocks[5], s0))
+    x1, a1 = net.across(b), net.along(s0, IN)
+    s1, t0 = add(blocks[1], x1), add(s0, a1)
+    if extra is None:
+        b, s1, t0 = lax.optimization_barrier((blocks[6], s1, t0))
+    else:
+        b, s1, t0, extra = lax.optimization_barrier((blocks[6], s1, t0, extra))
+    x2, a2, b2 = net.across(b), net.along(s1, IN), net.along(t0, MID)
+    s2, t1 = add(blocks[2], x2), add(s1, a2)
+    u = add(s2, b2)
+    b, s2, t1, u = lax.optimization_barrier((blocks[7], s2, t1, u))
+    x3, a3, b3, c3 = net.across(b), net.along(s2, IN), net.along(t1, MID), net.along(u, OUT)
+    return add(blocks[3], x3, a3, b3, c3), extra
+
+
+def scatter_steps(net, blocks, across):
     def own(k):
-        extra = [zero] if zero is not None and k == 1 else []
-        return add(blocks[k], net.across(blocks[4 + k]), *extra) if across else blocks[k]
+        return add(blocks[k], net.across(blocks[4 + k])) if across else blocks[k]
 
     s0 = own(0)
     a1 = net.along(s0, IN)
@@ -615,17 +672,10 @@
     core, stage = index % 2, index // 2
     seq = tokens.shape[1]
     spot = lax.axis_index("dp")
-    z, column = spot // 2, spot % 2
+    z = spot // 2
     middle = (z == 1) | (z == 2)
-    info = jnp.stack([core, 1 - core, z, column, middle.astype(jnp.int32), core, 2 + middle]).astype(jnp.int32)
     if lined:
-        order = jnp.array([[3, 2, 1, 0], [2, 3, 1, 0], [0, 1, 3, 2], [0, 1, 2, 3]], jnp.int32)[z]
-        slots = jnp.stack([order[j // 2] + jnp.where(column == j % 2, 0, 4) for j in range(8)]).astype(jnp.int32)
-    else:
-        slots = jnp.zeros((1,), jnp.int32)
-
-    if lined:
-        packed, pair = pack(info, joint_weight[0], output_weight[0], up_weight[0], down_weight[0], attend_gain, attend_shift,
+        packed, pair = pack(joint_weight[0], output_weight[0], up_weight[0], down_weight[0], attend_gain, attend_shift,
                             joint_bias, output_bias, feed_gain, feed_shift, down_bias, up_bias)
         wa, wb = gather_blocks(packed, pair, middle)
     else:
@@ -650,7 +700,7 @@
     x = own_tokens
     for t in range(stages):
         last = t == stages - 1
-        got = forward_stage(last, info, x, mask, wa, wb)
+        got = forward_stage(last, x, mask, wa, wb)
         if not last:
             x = jnp.where(stage == 0, own_tokens, moved(got[1], "section", 2))
     leaving = got[1]
@@ -660,28 +710,33 @@
 
     g = own_cotangent
     for t in range(stages - 1):
-        g = backward_layers(False, (1, 0), info, g, mask, saved, wa, wb, None)[0]
+        g = backward_layers(False, (1, 0), g, mask, saved, wa, wb, None)[0]
         g = jnp.where(stage == stages - 1, own_cotangent, moved(g, "section", -2))
-    products = [None, None]
+    products, operands = [None, None], [None, None]
     behind = mask
     for s in (1, 0):
-        g, gv, bk, bs = backward_layers(True, (s,), info, g, mask, saved, wa, wb, behind)
-        products[s] = weight_products(nk, s == 1 and lined, info, slots if s == 0 else jnp.arange(nk, dtype=jnp.int32),
-                                      gv, kept[s], bk, received[s], swapped(bs))
+        g, gv, bk, bs = backward_layers(True, (s,), g, mask, saved, wa, wb, behind)
+        operands[s] = gv, kept[s], bk, received[s], swapped(bs)
+    behind = g
+    for s in (1, 0):
+        products[s] = list(weight_products(nk, 0 if lined else 0, behind, *operands[s]))
         behind = products[s][0]
 
-    ends = jnp.where(stage == 0, g, leaving)[:seq].reshape(seq, sections, D // sections)
-    swept = lax.all_to_all(ends, "section", split_axis=1, concat_axis=0, tiled=True)
-    pieces = swept.reshape(sections, seq, D // sections)
-    outputs = pieces[sections - 2:]
-    token_grad = pieces[:2]
-    zero = jnp.minimum(jnp.abs(swept[0, 0, 0].astype(F32)), 0.0)
+    g, products[0][-1] = lax.optimization_barrier((g, products[0][-1]))
+    ends = jnp.where(stage == 0, g, leaving)[:seq].reshape(seq, stages, 2, D // sections)
+    kept_half = lax.dynamic_index_in_dim(ends, stage, 1, False)
+    got_half = flipped(lax.dynamic_index_in_dim(ends, 1 - stage, 1, False), 2)
+    halves = jnp.stack([jnp.where(stage == 0, got_half, kept_half), jnp.where(stage == 0, kept_half, got_half)])
+    kept_part = lax.dynamic_index_in_dim(halves, core, 2, False)
+    got_part = flipped(lax.dynamic_index_in_dim(halves, 1 - core, 2, False), 1)
+    parts = jnp.stack([jnp.where(core == 0, kept_part, got_part), jnp.where(core == 0, got_part, kept_part)], axis=1)
 
     reduced = [None, None]
     if lined:
-        net = Links(x=2, z=9)
-        reduced[1] = lax.psum_scatter(products[1][0], "dp", scatter_dimension=0)
-        reduced[0] = list(scatter_steps(net, products[0], True, zero))[-1]
+        net = Links(x=1, z=9)
+        products[1][5], products[0][0] = lax.optimization_barrier((products[1][5], products[0][0]))
+        reduced[1] = list(scatter_steps(net, products[1], True))[-1]
+        reduced[0], parts = scatter_rounds(products[0], None, parts)
     else:
         for s in range(2):
             p = products[s][0]
@@ -703,6 +758,7 @@
     vec = lax.dynamic_slice(v, (0, r * spot), (16, r))
     grad_jb = lax.dynamic_slice(v, (BQ + spot // half, 2 * r * (spot % half)), (1, 2 * r))
     grad_ub = lax.dynamic_slice(v, (UB + spot // quarter, 4 * r * (spot % quarter)), (1, 4 * r))
+    outputs, token_grad = parts[0], parts[1]
     return (outputs, token_grad, vec[AG:AG + 1], vec[AS:AS + 1], grad_joint[None], grad_jb, grad_out[None],
             vec[OB:OB + 1], vec[FG:FG + 1], vec[FS:FS + 1], grad_up[None], grad_ub, grad_down[None], vec[DB:DB + 1])
 

time: 533 us -> 522 us (0.979)
  waiting for transfers between devices: 238 us -> 262 us
  between operations: 20.8 us -> 1.85 us
  blocking collectives: 12 us -> 0 us
    ppermute x26 -> x36, waiting for transfers between devices: 204 us -> 224 us  [send(): got = lax.ppermute(value, axis, pairs)]
    all_to_all x1 -> x0, blocking collectives: 12 us -> none  [shards(): lax.all_to_all(ends, 'section', split_axis=1, concat_axis=0, tiled=True)]
    ppermute x16 -> x18, waiting for transfers between devices: 12.2 us -> 15.4 us  [flipped(): return lax.ppermute(value, 'section', [(i, i ^ bit) for i in range(peers)])]
    ppermute x26 -> x36, starting transfers between devices: 62.3 us -> 61 us  [send(): got = lax.ppermute(value, axis, pairs)]
  transfers between devices with their start and end apart: 47 -> 58, of which waited for: 23 -> 28; matrix products, arithmetic and copies ran while one was open for 3% -> 3% of each run, Pallas kernels for 10% -> 13%
where the time goes in v4:
time: 522 us; the launch traced here: 517 us
  waiting for transfers between devices  262 us (50%)
  Pallas kernels  152 us (29%)
  starting transfers between devices  74.7 us (14%)
  other arithmetic  14.8 us (3%)
  local copies, waits for them, and re-layouts  11.6 us (2%)
    ppermute x36, waiting for transfers between devices, send(): got = lax.ppermute(value, axis, pairs)  224 us
    pallas_call x3, Pallas kernels, backward_layers(): pl.pallas_call(functools.partial(backward_kernel, save, layers, len(wa)),...  74.1 us
    ppermute x36, starting transfers between devices, send(): got = lax.ppermute(value, axis, pairs)  61 us
    pallas_call x2, Pallas kernels, forward_stage(): pl.pallas_call(functools.partial(forward_kernel, save, len(wa)), out_shap...  48.9 us
    pallas_call x2, Pallas kernels, weight_products(): pl.pallas_call(functools.partial(product_kernel, n, direct), out_shape=sh...  25.3 us
    ppermute x2, waiting for transfers between devices, moved(): lax.ppermute(value, axis, [(i, i + by) for i in range(peers) if 0 <= i +...  20.9 us
    ppermute x18, waiting for transfers between devices, flipped(): return lax.ppermute(value, 'section', [(i, i ^ bit) for i in range(peers)])  15.4 us
  transfers between devices with their start and end apart: 58, of which 28 were waited for; matrix products, arithmetic and copies ran while one was open for 3% of the time, Pallas kernels for 13%

profile of v4, /device:TPU:0, one launch (start us, length us, event | category | flops | bytes accessed | tf_op | source)
XLA Modules:
  0.0 517.2 jit_solution(1715053423458146456)
XLA Ops:
  0.7 3.7 pack.1
  4.4 4.8 collective-permute-start.5
  9.3 1.6 collective-permute-start
  11.7 5.4 %collective-permute-done.5 = bf16[192,768]{1,0:T(8,128)(2,1)S(1)} collective-permute-done((bf16[192,768]{1,0:T(8,128)(2,1)}, bf16[192,768]{1,0:T(8,128)(2,1)S(1)}, u32[]{:S(2)}, u32[]{:S(2)}) %collective-permute-start.5) | collective-permute-done | bytes 294944 | tf_op jit(solution)/shard_map/ppermute | solution.py:576
  17.0 2.3 collective-permute-start.6
  19.3 22.0 %collective-permute-done.rest_1_.rest_11_.rest_7_ = bf16[976,768]{1,0:T(8,128)(2,1)} collective-permute-done((bf16[976,768]{1,0:T(8,128)(2,1)}, bf16[976,768]{1,0:T(8,128)(2,1)}, u32[]{:S(2)}, u32[]{:S(2)}) %collective-permute-start) | collective-permute-done | bytes 1499168 | tf_op jit(solution)/shard_map/ppermute | solution.py:576
  41.3 1.8 collective-permute-start.3
  44.4 2.0 collective-permute-done.6.rest_4_.rest_14_.rest_10_
  47.1 1.9 collective-permute-start.8
  50.4 26.4 %collective-permute-done.2 = bf16[976,768]{1,0:T(8,128)(2,1)} collective-permute-done((bf16[976,768]{1,0:T(8,128)(2,1)S(1)}, bf16[976,768]{1,0:T(8,128)(2,1)}, u32[]{:S(2)}, u32[]{:S(2)}) %collective-permute-start.2) | collective-permute-done | bytes 1499168 | tf_op jit(solution)/shard_map/ppermute | solution.py:576
  78.4 2.8 collective-permute-done.8.rest_5_.rest_15_.rest_11_
  81.2 2.0 collective-permute-start.9
  84.9 2.5 collective-permute-start.11
  88.1 34.5 %collective-permute-done.11.rest_9_.rest_19_.rest_15_ = bf16[384,768]{1,0:T(8,128)(2,1)S(1)} collective-permute-done((bf16[384,768]{1,0:T(8,128)(2,1)S(1)}, bf16[384,768]{1,0:T(8,128)(2,1)S(1)}, u32[]{:S(2)}, u32[]{:S(2)}) %collective-permute-start.11) | collective-permute-done | bytes 589856 | tf_op jit(solution)/shard_map/ppermute | solution.py:576
  129.3 12.0 %collective-permute-done.13 = bf16[384,768]{1,0:T(8,128)(2,1)S(1)} collective-permute-done((bf16[384,768]{1,0:T(8,128)(2,1)S(1)}, bf16[384,768]{1,0:T(8,128)(2,1)S(1)}, u32[]{:S(2)}, u32[]{:S(2)}) %collective-permute-start.13) | collective-permute-done | bytes 589856 | tf_op jit(solution)/shard_map/ppermute | solution.py:576
  141.4 13.2 %collective-permute-done.15 = bf16[384,768]{1,0:T(8,128)(2,1)S(1)} collective-permute-done((bf16[384,768]{1,0:T(8,128)(2,1)S(1)}, bf16[384,768]{1,0:T(8,128)(2,1)S(1)}, u32[]{:S(2)}, u32[]{:S(2)}) %collective-permute-start.15) | collective-permute-done | bytes 589856 | tf_op jit(solution)/shard_map/ppermute | solution.py:576
  158.6 3.0 collective-permute-done.10.rest_7_.rest_17_.rest_13_
  165.1 2.1 collective-permute-done.22.rest_18_.rest_28_.rest_24_
  167.2 2.1 collective-permute-done.23.rest_19_.rest_29_.rest_25_
  169.9 22.8 %forward_stage.2 = (bf16[288,768]{1,0:T(8,128)(2,1)}, bf16[288,768]{1,0:T(8,128)(2,1)}) custom-call(bf16[288,768]{1,0:T(8,128)(2,1)} %pad.8.x_ref, f32[8,288]{1,0:T(8,128)} %iota.13.mask_ref.rest_5_, bf16[976,768]{1,0:T(8,128)(2,1)} %get-tuple-element.79.rest_0_.rest_10_.rest_6_, bf16[976,768]{1,0:T(8,128)(2,1)} %collective-permute-done.rest_1_.rest_11_.rest_7_, ...), custom_call_target="tpu_custom_call" | custom-call | flops 8833204224 | bytes 36700160 | tf_op jit(solution)/shard_map/forward_stage/pallas_call | solution.py:241
  192.8 3.6 collective-permute-start.28
  197.2 9.1 %collective-permute-done.28 = bf16[288,768]{1,0:T(8,128)(2,1)S(1)} collective-permute-done((bf16[288,768]{1,0:T(8,128)(2,1)}, bf16[288,768]{1,0:T(8,128)(2,1)S(1)}, u32[]{:S(2)}, u32[]{:S(2)}) %collective-permute-start.28) | collective-permute-done | bytes 442400 | tf_op jit(solution)/shard_map/ppermute | solution.py:525
  207.3 26.1 %forward_stage.3 = (bf16[288,768]{1,0:T(8,128)(2,1)}, bf16[288,768]{1,0:T(8,128)(2,1)}, f32[288,128]{1,0:T(8,128)}, f32[288,768]{1,0:T(8,128)}, bf16[288,2304]{1...) custom-call(bf16[288,768]{1,0:T(8,128)(2,1)} %broadcast_select_fusio, ...), custom_call_target="tpu_custom_call" | custom-call | flops 8833204224 | bytes 36700160 | tf_op jit(solution)/shard_map/forward_stage/pallas_call | solution.py:241
  233.3 34.4 %backward_layers.3 = bf16[288,768]{1,0:T(8,128)(2,1)} custom-call(bf16[288,768]{1,0:T(8,128)(2,1)} %pad.7.g_ref, f32[8,288]{1,0:T(8,128)} %iota.13.mask_ref.rest_5_, bf16[288,768]{1,0:T(8,128)(2,1)} %get-tuple-element.85.rest_0_, f32[288,128]{1,0:T(8,128)} %get-tuple-element.86.rest_1_, f32[288,768]{1,0:T(8,128)} %get-tuple-element.87.rest_2_, ...), custom_call_target="tpu_custom_call" | custom-call | flops 9512681472 | bytes 45088768 | tf_op jit(solution)/shard_map/backward_layers/pallas_call | solution.py:373
  269.6 11.7 %collective-permute-done.29 = bf16[288,768]{1,0:T(8,128)(2,1)S(1)} collective-permute-done((bf16[288,768]{1,0:T(8,128)(2,1)}, bf16[288,768]{1,0:T(8,128)(2,1)S(1)}, u32[]{:S(2)}, u32[]{:S(2)}) %collective-permute-start.29) | collective-permute-done | bytes 442400 | tf_op jit(solution)/shard_map/ppermute | solution.py:525
  282.2 19.8 %backward_layers.4 = (bf16[288,768]{1,0:T(8,128)(2,1)}, f32[16,768]{1,0:T(8,128)}, bf16[288,4608]{1,0:T(8,128)(2,1)}, bf16[288,4608]{1,0:T(8,128)(2,1)}) custom-call(bf16[288,768]{1,0:T(8,128)(2,1)} %broadcast_select_fusion.7.g_ref, f32[8,288]{1,0:T(8,128)} %iota.13.mask_ref.rest_5_, bf16[288,768]{1,0:T(8,128)(2,1)} %get-tuple-element.85.rest_0_, ...), custom_call_target="tpu_custom_call" | custom-call | flops 4756340736 | bytes 22544384 | tf_op jit(solution)/shard_map/backward_layers/pallas_call | solution.py:373
  302.1 19.9 %backward_layers.5 = (bf16[288,768]{1,0:T(8,128)(2,1)}, f32[16,768]{1,0:T(8,128)}, bf16[288,4608]{1,0:T(8,128)(2,1)}, bf16[288,4608]{1,0:T(8,128)(2,1)}) custom-call(bf16[288,768]{1,0:T(8,128)(2,1)} %get-tuple-element.94.g_ref, f32[8,288]{1,0:T(8,128)} %iota.13.mask_ref.rest_5_, bf16[288,768]{1,0:T(8,128)(2,1)} %broadcast_select_fusion.6.x_ref.rest_5_.rest_0_, ...), custom_call_target="tpu_custom_call" | custom-call | flops 4756340736 | bytes 22544384 | tf_op jit(solution)/shard_map/backward_layers/pallas_call | solution.py:373
  324.1 12.7 %weight_products.2 = (bf16[592,768]{1,0:T(8,128)(2,1)}, bf16[592,768]{1,0:T(8,128)(2,1)}, bf16[592,768]{1,0:T(8,128)(2,1)}, bf16[592,768]{1,0:T(8,128)(2,1)}, bf...) custom-call(bf16[288,768]{1,0:T(8,128)(2,1)} %get-tuple-element.117.behi, ...), custom_call_target="tpu_custom_call" | custom-call | flops 4076863488 | bytes 16777216 | tf_op jit(solution)/shard_map/weight_products/pallas_call | solution.py:472
  338.4 12.6 %weight_products.3 = (bf16[592,768]{1,0:T(8,128)(2,1)}, bf16[592,768]{1,0:T(8,128)(2,1)}, bf16[592,768]{1,0:T(8,128)(2,1)}, bf16[592,768]{1,0:T(8,128)(2,1)}, bf...) custom-call(bf16[592,768]{1,0:T(8,128)(2,1)} %get-tuple-element.101.behi, ...), custom_call_target="tpu_custom_call" | custom-call | flops 4076863488 | bytes 16777216 | tf_op jit(solution)/shard_map/weight_products/pallas_call | solution.py:472
  352.7 8.6 %collective-permute-done.37 = bf16[280,2,192]{2,0,1:T(8,128)(2,1)S(1)} collective-permute-done((bf16[280,2,192]{2,0,1:T(8,128)(2,1)S(1)}, bf16[280,2,192]{2,0,1:T(8,128)(2,1)S(1)}, u32[]{:S(2)}, u32[]{:S(2)}) %collective-permute-start.37) | collective-permute-done | bytes 215072 | tf_op jit(solution)/shard_map/ppermute | solution.py:530
  363.4 2.5 collective-permute-start.53
  365.8 13.8 %collective-permute-done.34 = bf16[592,768]{1,0:T(8,128)(2,1)} collective-permute-done((bf16[592,768]{1,0:T(8,128)(2,1)}, bf16[592,768]{1,0:T(8,128)(2,1)}, u32[]{:S(2)}, u32[]{:S(2)}) %collective-permute-start.34) | collective-permute-done | bytes 909344 | tf_op jit(solution)/shard_map/ppermute | solution.py:576
  381.1 2.4 collective-permute-start.36
  385.3 13.7 %collective-permute-done.47 = bf16[592,768]{1,0:T(8,128)(2,1)S(1)} collective-permute-done((bf16[592,768]{1,0:T(8,128)(2,1)S(1)}, bf16[592,768]{1,0:T(8,128)(2,1)S(1)}, u32[]{:S(2)}, u32[]{:S(2)}) %collective-permute-start.47) | collective-permute-done | bytes 909344 | tf_op jit(solution)/shard_map/ppermute | solution.py:576
  400.8 2.3 collective-permute-start.51
  406.1 12.5 %collective-permute-done.35 = bf16[592,768]{1,0:T(8,128)(2,1)S(1)} collective-permute-done((bf16[592,768]{1,0:T(8,128)(2,1)S(1)}, bf16[592,768]{1,0:T(8,128)(2,1)S(1)}, u32[]{:S(2)}, u32[]{:S(2)}) %collective-permute-start.35) | collective-permute-done | bytes 909344 | tf_op jit(solution)/shard_map/ppermute | solution.py:576
  418.8 2.4 collective-permute-start.40
  422.8 15.2 %collective-permute-done.48 = bf16[592,768]{1,0:T(8,128)(2,1)S(1)} collective-permute-done((bf16[592,768]{1,0:T(8,128)(2,1)S(1)}, bf16[592,768]{1,0:T(8,128)(2,1)S(1)}, u32[]{:S(2)}, u32[]{:S(2)}) %collective-permute-start.48) | collective-permute-done | bytes 909344 | tf_op jit(solution)/shard_map/ppermute | solution.py:576
  441.8 2.2 collective-permute-done.40
  444.0 5.4 %collective-permute-start.50 = (bf16[592,768]{1,0:T(8,128)(2,1)S(1)}, bf16[592,768]{1,0:T(8,128)(2,1)S(1)}, u32[]{:S(2)}, u32[]{:S(2)}) collective-permute-start(bf16[592,768]{1,0:T(8,128)(2,1)S(1)} %get-tuple-element.141), channel_id=1, source_target_pairs={{0,2},{1,3},{6,4},{7,5},{8,10},{9,11},{14,12},{15,13},{16,18},{17,... | collective-permute-start | bytes 2727944 | tf_op jit(solution)/shard_map/ppermute | solution.py:576
  449.3 8.2 %collective-permute-done.39 = bf16[592,768]{1,0:T(8,128)(2,1)S(1)} collective-permute-done((bf16[592,768]{1,0:T(8,128)(2,1)S(1)}, bf16[592,768]{1,0:T(8,128)(2,1)S(1)}, u32[]{:S(2)}, u32[]{:S(2)}) %collective-permute-start.39) | collective-permute-done | bytes 909344 | tf_op jit(solution)/shard_map/ppermute | solution.py:576
  461.8 15.2 %collective-permute-done.49 = bf16[592,768]{1,0:T(8,128)(2,1)S(1)} collective-permute-done((bf16[592,768]{1,0:T(8,128)(2,1)S(1)}, bf16[592,768]{1,0:T(8,128)(2,1)S(1)}, u32[]{:S(2)}, u32[]{:S(2)}) %collective-permute-start.49) | collective-permute-done | bytes 909344 | tf_op jit(solution)/shard_map/ppermute | solution.py:576
  477.0 2.3 collective-permute-start.43
  481.9 2.2 collective-permute-start.57
  484.2 11.6 %collective-permute-done.42 = bf16[592,768]{1,0:T(8,128)(2,1)S(1)} collective-permute-done((bf16[592,768]{1,0:T(8,128)(2,1)S(1)}, bf16[592,768]{1,0:T(8,128)(2,1)S(1)}, u32[]{:S(2)}, u32[]{:S(2)}) %collective-permute-start.42) | collective-permute-done | bytes 909344 | tf_op jit(solution)/shard_map/ppermute | solution.py:576
  495.8 1.7 collective-permute-done.43
  497.6 6.8 %collective-permute-done.45 = bf16[592,768]{1,0:T(8,128)(2,1)S(1)} collective-permute-done((bf16[592,768]{1,0:T(8,128)(2,1)S(1)}, bf16[592,768]{1,0:T(8,128)(2,1)S(1)}, u32[]{:S(2)}, u32[]{:S(2)}) %collective-permute-start.45) | collective-permute-done | bytes 909344 | tf_op jit(solution)/shard_map/ppermute | solution.py:576
  507.2 2.3 collective-permute-done.56
  (197 shorter events, 65.2 us)
Async XLA Ops:
  4.4 12.6 %collective-permute-start.5 = (bf16[192,768]{1,0:T(8,128)(2,1)}, bf16[192,768]{1,0:T(8,128)(2,1)S(1)}, u32[]{:S(2)}, u32[]{:S(2)}) collective-permute-start(bf16[192,768]{1,0:T(8,128)(2,1)} %get-tuple-element.80), channel_id=1, source_target_pairs={{0,1},{1,0},{2,3},{3,2},{4,5},{5,4},{6,7},{7,6},{16,17},{17,16},{1... | collective-permute-start | bytes 884744 | tf_op jit(solution)/shard_map/ppermute | solution.py:576
  9.3 32.1 %collective-permute-start = (bf16[976,768]{1,0:T(8,128)(2,1)}, bf16[976,768]{1,0:T(8,128)(2,1)}, u32[]{:S(2)}, u32[]{:S(2)}) collective-permute-start(bf16[976,768]{1,0:T(8,128)(2,1)} %get-tuple-element.79.rest_0_.rest_10_.rest_6_), channel_id=1, source_target_pairs={{0,2},{1,3},{2,0},{3,1},{4,6},{5,7},{6,4},{7,5},{8,10},{9,11},{10,... | collective-permute-start | bytes 4497416 | tf_op jit(solution)/shard_map/ppermute | solution.py:576
  10.9 32.2 %collective-permute-start.1 = (bf16[976,768]{1,0:T(8,128)(2,1)}, bf16[976,768]{1,0:T(8,128)(2,1)S(1)}, u32[]{:S(2)}, u32[]{:S(2)}) collective-permute-start(bf16[976,768]{1,0:T(8,128)(2,1)} %get-tuple-element.79.rest_0_.rest_10_.rest_6_), channel_id=1, source_target_pairs={{2,4},{3,5},{4,2},{5,3},{10,12},{11,13},{12,10},{13,11},{18,20},{1... | collective-permute-start | bytes 4497416 | tf_op jit(solution)/shard_map/ppermute | solution.py:576
  17.0 29.4 %collective-permute-start.6 = (bf16[976,768]{1,0:T(8,128)(2,1)}, bf16[976,768]{1,0:T(8,128)(2,1)}, u32[]{:S(2)}, u32[]{:S(2)}) collective-permute-start(bf16[976,768]{1,0:T(8,128)(2,1)} %get-tuple-element.79.rest_0_.rest_10_.rest_6_), channel_id=1, source_target_pairs={{0,1},{1,0},{2,3},{3,2},{4,5},{5,4},{6,7},{7,6},{8,9},{9,8},{10,11... | collective-permute-start | bytes 4497416 | tf_op jit(solution)/shard_map/ppermute | solution.py:576
  43.1 33.7 %collective-permute-start.2 = (bf16[976,768]{1,0:T(8,128)(2,1)S(1)}, bf16[976,768]{1,0:T(8,128)(2,1)}, u32[]{:S(2)}, u32[]{:S(2)}) collective-permute-start(bf16[976,768]{1,0:T(8,128)(2,1)S(1)} %collective-permute-done.1), channel_id=1, source_target_pairs={{2,0},{3,1},{4,6},{5,7},{10,8},{11,9},{12,14},{13,15},{18,16},{19,... | collective-permute-start | bytes 4497416 | tf_op jit(solution)/shard_map/ppermute | solution.py:576
  47.1 34.1 %collective-permute-start.8 = (bf16[976,768]{1,0:T(8,128)(2,1)}, bf16[976,768]{1,0:T(8,128)(2,1)}, u32[]{:S(2)}, u32[]{:S(2)}) collective-permute-start(bf16[976,768]{1,0:T(8,128)(2,1)} %collective-permute-done.rest_1_.rest_11_.rest_7_), channel_id=1, source_target_pairs={{0,1},{1,0},{2,3},{3,2},{4,5},{5,4},{6,7},{7,6},{8,9},{9,8},{10,11... | collective-permute-start | bytes 4497416 | tf_op jit(solution)/shard_map/ppermute | solution.py:576
  49.0 74.3 %collective-permute-start.4 = (bf16[976,768]{1,0:T(8,128)(2,1)}, bf16[976,768]{1,0:T(8,128)(2,1)S(1)}, u32[]{:S(2)}, u32[]{:S(2)}) collective-permute-start(bf16[976,768]{1,0:T(8,128)(2,1)} %collective-permute-done.3), channel_id=1, source_target_pairs={{2,0},{3,1},{4,6},{5,7},{10,8},{11,9},{12,14},{13,15},{18,16},{19,... | collective-permute-start | bytes 4497416 | tf_op jit(solution)/shard_map/ppermute | solution.py:576
  81.2 42.7 %collective-permute-start.9 = (bf16[976,768]{1,0:T(8,128)(2,1)S(1)}, bf16[976,768]{1,0:T(8,128)(2,1)}, u32[]{:S(2)}, u32[]{:S(2)}) collective-permute-start(bf16[976,768]{1,0:T(8,128)(2,1)S(1)} %broadcast_select_fusion.1.rest_2_.rest_12_.rest_8_), channel_id=1, source_target_pairs={{0,1},{1,0},{2,3},{3,2},{4,5},{5,4},{6,7},{7,6},{8,9},{9,8},{10,11... | collective-permute-start | bytes 4497416 | tf_op jit(solution)/shard_map/ppermute | solution.py:576
  83.2 43.3 %collective-permute-start.16 = (bf16[976,768]{1,0:T(8,128)(2,1)S(1)}, bf16[976,768]{1,0:T(8,128)(2,1)S(1)}, u32[]{:S(2)}, u32[]{:S(2)}) collective-permute-start(bf16[976,768]{1,0:T(8,128)(2,1)S(1)} %copy-done.3), channel_id=1, source_target_pairs={{0,8},{8,0},{16,24},{24,16},{1,9},{9,1},{17,25},{25,17},{2,10},{10... | collective-permute-start | bytes 4497416 | tf_op jit(solution)/shard_map/ppermute | solution.py:530
  84.9 37.7 %collective-permute-start.11 = (bf16[384,768]{1,0:T(8,128)(2,1)S(1)}, bf16[384,768]{1,0:T(8,128)(2,1)S(1)}, u32[]{:S(2)}, u32[]{:S(2)}) collective-permute-start(bf16[384,768]{1,0:T(8,128)(2,1)S(1)} %pad_maximum_fusion.rest_8_.rest_18_.rest_14_), channel_id=1, source_target_pairs={{0,2},{1,3},{2,0},{3,1},{4,6},{5,7},{6,4},{7,5},{8,10},{9,11},{10,... | collective-permute-start | bytes 1769480 | tf_op jit(solution)/shard_map/ppermute | solution.py:576
  87.4 35.2 %collective-permute-start.12 = (bf16[384,768]{1,0:T(8,128)(2,1)S(1)}, bf16[384,768]{1,0:T(8,128)(2,1)S(1)}, u32[]{:S(2)}, u32[]{:S(2)}) collective-permute-start(bf16[384,768]{1,0:T(8,128)(2,1)S(1)} %pad_maximum_fusion.rest_8_.rest_18_.rest_14_), channel_id=1, source_target_pairs={{2,4},{3,5},{4,2},{5,3},{10,12},{11,13},{12,10},{13,11},{18,20},{1... | collective-permute-start | bytes 1769480 | tf_op jit(solution)/shard_map/ppermute | solution.py:576
  122.6 32.7 %collective-permute-start.17 = (bf16[976,768]{1,0:T(8,128)(2,1)}, bf16[976,768]{1,0:T(8,128)(2,1)S(1)}, u32[]{:S(2)}, u32[]{:S(2)}) collective-permute-start(bf16[976,768]{1,0:T(8,128)(2,1)} %collective-permute-done.rest_1_.rest_11_.rest_7_), channel_id=1, source_target_pairs={{0,8},{8,0},{16,24},{24,16},{1,9},{9,1},{17,25},{25,17},{2,10},{10... | collective-permute-start | bytes 4497416 | tf_op jit(solution)/shard_map/ppermute | solution.py:530
  123.3 33.4 %collective-permute-start.20 = (bf16[976,768]{1,0:T(8,128)(2,1)}, bf16[976,768]{1,0:T(8,128)(2,1)S(1)}, u32[]{:S(2)}, u32[]{:S(2)}) collective-permute-start(bf16[976,768]{1,0:T(8,128)(2,1)} %collective-permute-done.6.rest_4_.rest_14_.rest_10_), channel_id=1, source_target_pairs={{0,8},{8,0},{16,24},{24,16},{1,9},{9,1},{17,25},{25,17},{2,10},{10... | collective-permute-start | bytes 4497416 | tf_op jit(solution)/shard_map/ppermute | solution.py:530
  123.9 17.4 %collective-permute-start.13 = (bf16[384,768]{1,0:T(8,128)(2,1)S(1)}, bf16[384,768]{1,0:T(8,128)(2,1)S(1)}, u32[]{:S(2)}, u32[]{:S(2)}) collective-permute-start(bf16[384,768]{1,0:T(8,128)(2,1)S(1)} %collective-permute-done.12), channel_id=1, source_target_pairs={{2,0},{3,1},{4,6},{5,7},{10,8},{11,9},{12,14},{13,15},{18,16},{19,... | collective-permute-start | bytes 1769480 | tf_op jit(solution)/shard_map/ppermute | solution.py:576
  126.5 35.1 %collective-permute-start.10 = (bf16[976,768]{1,0:T(8,128)(2,1)}, bf16[976,768]{1,0:T(8,128)(2,1)}, u32[]{:S(2)}, u32[]{:S(2)}) collective-permute-start(bf16[976,768]{1,0:T(8,128)(2,1)} %broadcast_select_fusion.rest_3_.rest_13_.rest_9_), channel_id=1, source_target_pairs={{0,1},{1,0},{2,3},{3,2},{4,5},{5,4},{6,7},{7,6},{8,9},{9,8},{10,11... | collective-permute-start | bytes 4497416 | tf_op jit(solution)/shard_map/ppermute | solution.py:576
  128.0 26.5 %collective-permute-start.15 = (bf16[384,768]{1,0:T(8,128)(2,1)S(1)}, bf16[384,768]{1,0:T(8,128)(2,1)S(1)}, u32[]{:S(2)}, u32[]{:S(2)}) collective-permute-start(bf16[384,768]{1,0:T(8,128)(2,1)S(1)} %collective-permute-done.14), channel_id=1, source_target_pairs={{2,0},{3,1},{4,6},{5,7},{10,8},{11,9},{12,14},{13,15},{18,16},{19,... | collective-permute-start | bytes 1769480 | tf_op jit(solution)/shard_map/ppermute | solution.py:576
  141.3 13.4 %collective-permute-start.24 = (bf16[384,768]{1,0:T(8,128)(2,1)S(1)}, bf16[384,768]{1,0:T(8,128)(2,1)S(1)}, u32[]{:S(2)}, u32[]{:S(2)}) collective-permute-start(bf16[384,768]{1,0:T(8,128)(2,1)S(1)} %pad_maximum_fusion.rest_8_.rest_18_.rest_14_), channel_id=1, source_target_pairs={{0,8},{8,0},{16,24},{24,16},{1,9},{9,1},{17,25},{25,17},{2,10},{10... | collective-permute-start | bytes 1769480 | tf_op jit(solution)/shard_map/ppermute | solution.py:530
  158.3 8.9 %collective-permute-start.22 = (bf16[976,768]{1,0:T(8,128)(2,1)}, bf16[976,768]{1,0:T(8,128)(2,1)}, u32[]{:S(2)}, u32[]{:S(2)}) collective-permute-start(bf16[976,768]{1,0:T(8,128)(2,1)} %collective-permute-done.9.rest_6_.rest_16_.rest_12_), channel_id=1, source_target_pairs={{0,8},{8,0},{16,24},{24,16},{1,9},{9,1},{17,25},{25,17},{2,10},{10... | collective-permute-start | bytes 4497416 | tf_op jit(solution)/shard_map/ppermute | solution.py:530
  161.6 7.7 %collective-permute-start.23 = (bf16[976,768]{1,0:T(8,128)(2,1)}, bf16[976,768]{1,0:T(8,128)(2,1)}, u32[]{:S(2)}, u32[]{:S(2)}) collective-permute-start(bf16[976,768]{1,0:T(8,128)(2,1)} %collective-permute-done.10.rest_7_.rest_17_.rest_13_), channel_id=1, source_target_pairs={{0,8},{8,0},{16,24},{24,16},{1,9},{9,1},{17,25},{25,17},{2,10},{10... | collective-permute-start | bytes 4497416 | tf_op jit(solution)/shard_map/ppermute | solution.py:530
  192.8 13.6 %collective-permute-start.28 = (bf16[288,768]{1,0:T(8,128)(2,1)}, bf16[288,768]{1,0:T(8,128)(2,1)S(1)}, u32[]{:S(2)}, u32[]{:S(2)}) collective-permute-start(bf16[288,768]{1,0:T(8,128)(2,1)} %get-tuple-element.84), channel_id=1, source_target_pairs={{0,16},{8,24},{1,17},{9,25},{2,18},{10,26},{3,19},{11,27},{4,20},{... | collective-permute-start | bytes 1327112 | tf_op jit(solution)/shard_map/ppermute | solution.py:525
  267.7 13.6 %collective-permute-start.29 = (bf16[288,768]{1,0:T(8,128)(2,1)}, bf16[288,768]{1,0:T(8,128)(2,1)S(1)}, u32[]{:S(2)}, u32[]{:S(2)}) collective-permute-start(bf16[288,768]{1,0:T(8,128)(2,1)} %backward_layers.3), channel_id=1, source_target_pairs={{16,0},{24,8},{17,1},{25,9},{18,2},{26,10},{19,3},{27,11},{20,4},{... | collective-permute-start | bytes 1327112 | tf_op jit(solution)/shard_map/ppermute | solution.py:525
  269.0 53.6 %collective-permute-start.30 = (bf16[288,4608]{1,0:T(8,128)(2,1)}, bf16[288,4608]{1,0:T(8,128)(2,1)}, u32[]{:S(2)}, u32[]{:S(2)}) collective-permute-start(bf16[288,4608]{1,0:T(8,128)(2,1)} %get-tuple-element.99), channel_id=1, source_target_pairs={{0,8},{8,0},{16,24},{24,16},{1,9},{9,1},{17,25},{25,17},{2,10},{10... | collective-permute-start | bytes 7962632 | tf_op jit(solution)/shard_map/ppermute | solution.py:530
  269.1 69.3 %collective-permute-start.32 = (bf16[288,4608]{1,0:T(8,128)(2,1)}, bf16[288,4608]{1,0:T(8,128)(2,1)}, u32[]{:S(2)}, u32[]{:S(2)}) collective-permute-start(bf16[288,4608]{1,0:T(8,128)(2,1)} %get-tuple-element.105), channel_id=1, source_target_pairs={{0,8},{8,0},{16,24},{24,16},{1,9},{9,1},{17,25},{25,17},{2,10},{10... | collective-permute-start | bytes 7962632 | tf_op jit(solution)/shard_map/ppermute | solution.py:530
  302.0 20.6 %collective-permute-start.31 = (bf16[288,4608]{1,0:T(8,128)(2,1)}, bf16[288,4608]{1,0:T(8,128)(2,1)S(1)}, u32[]{:S(2)}, u32[]{:S(2)}) collective-permute-start(bf16[288,4608]{1,0:T(8,128)(2,1)} %get-tuple-element.100), channel_id=1, source_target_pairs={{0,8},{8,0},{16,24},{24,16},{1,9},{9,1},{17,25},{25,17},{2,10},{10... | collective-permute-start | bytes 7962632 | tf_op jit(solution)/shard_map/ppermute | solution.py:530
  322.0 16.4 %collective-permute-start.33 = (bf16[288,4608]{1,0:T(8,128)(2,1)}, bf16[288,4608]{1,0:T(8,128)(2,1)}, u32[]{:S(2)}, u32[]{:S(2)}) collective-permute-start(bf16[288,4608]{1,0:T(8,128)(2,1)} %get-tuple-element.106), channel_id=1, source_target_pairs={{0,8},{8,0},{16,24},{24,16},{1,9},{9,1},{17,25},{25,17},{2,10},{10... | collective-permute-start | bytes 7962632 | tf_op jit(solution)/shard_map/ppermute | solution.py:530
  336.8 24.7 %collective-permute-start.46 = (bf16[592,768]{1,0:T(8,128)(2,1)}, bf16[592,768]{1,0:T(8,128)(2,1)S(1)}, u32[]{:S(2)}, u32[]{:S(2)}) collective-permute-start(bf16[592,768]{1,0:T(8,128)(2,1)} %get-tuple-element.134), channel_id=1, source_target_pairs={{0,1},{1,0},{2,3},{3,2},{4,5},{5,4},{6,7},{7,6},{8,9},{9,8},{10,11... | collective-permute-start | bytes 2727944 | tf_op jit(solution)/shard_map/ppermute | solution.py:576
  351.5 28.1 %collective-permute-start.34 = (bf16[592,768]{1,0:T(8,128)(2,1)}, bf16[592,768]{1,0:T(8,128)(2,1)}, u32[]{:S(2)}, u32[]{:S(2)}) collective-permute-start(bf16[592,768]{1,0:T(8,128)(2,1)} %get-tuple-element.113), channel_id=1, source_target_pairs={{0,1},{1,0},{2,3},{3,2},{4,5},{5,4},{6,7},{7,6},{8,9},{9,8},{10,11... | collective-permute-start | bytes 2727944 | tf_op jit(solution)/shard_map/ppermute | solution.py:576
  352.6 8.7 %collective-permute-start.37 = (bf16[280,2,192]{2,0,1:T(8,128)(2,1)S(1)}, bf16[280,2,192]{2,0,1:T(8,128)(2,1)S(1)}, u32[]{:S(2)}, u32[]{:S(2)}) collective-permute-start(bf16[280,2,192]{2,0,1:T(8,128)(2,1)S(1)} %bitcast.52), channel_id=1, source_target_pairs={{0,16},{8,24},{16,0},{24,8},{1,17},{9,25},{17,1},{25,9},{2,18},{10... | collective-permute-start | bytes 645128 | tf_op jit(solution)/shard_map/ppermute | solution.py:530
  361.4 22.1 %collective-permute-start.38 = (bf16[2,280,192]{2,1,0:T(8,128)(2,1)S(1)}, bf16[2,280,192]{2,1,0:T(8,128)(2,1)S(1)}, u32[]{:S(2)}, u32[]{:S(2)}) collective-permute-start(bf16[2,280,192]{2,1,0:T(8,128)(2,1)S(1)} %fusion.1), channel_id=1, source_target_pairs={{0,8},{8,0},{16,24},{24,16},{1,9},{9,1},{17,25},{25,17},{2,10},{10... | collective-permute-start | bytes 645128 | tf_op jit(solution)/shard_map/ppermute | solution.py:530
  361.5 37.5 %collective-permute-start.47 = (bf16[592,768]{1,0:T(8,128)(2,1)S(1)}, bf16[592,768]{1,0:T(8,128)(2,1)S(1)}, u32[]{:S(2)}, u32[]{:S(2)}) collective-permute-start(bf16[592,768]{1,0:T(8,128)(2,1)S(1)} %copy-done.36), channel_id=1, source_target_pairs={{0,1},{1,0},{2,3},{3,2},{4,5},{5,4},{6,7},{7,6},{8,9},{9,8},{10,11... | collective-permute-start | bytes 2727944 | tf_op jit(solution)/shard_map/ppermute | solution.py:576
  363.4 39.8 %collective-permute-start.53 = (bf16[592,768]{1,0:T(8,128)(2,1)S(1)}, bf16[592,768]{1,0:T(8,128)(2,1)S(1)}, u32[]{:S(2)}, u32[]{:S(2)}) collective-permute-start(bf16[592,768]{1,0:T(8,128)(2,1)S(1)} %add_convert_fusion.3), channel_id=1, source_target_pairs={{0,2},{1,3},{6,4},{7,5},{8,10},{9,11},{14,12},{15,13},{16,18},{17,... | collective-permute-start | bytes 2727944 | tf_op jit(solution)/shard_map/ppermute | solution.py:576
  381.1 24.7 %collective-permute-start.36 = (bf16[592,768]{1,0:T(8,128)(2,1)S(1)}, bf16[592,768]{1,0:T(8,128)(2,1)S(1)}, u32[]{:S(2)}, u32[]{:S(2)}) collective-permute-start(bf16[592,768]{1,0:T(8,128)(2,1)S(1)} %add_convert_fusion.14), channel_id=1, source_target_pairs={{0,2},{1,3},{6,4},{7,5},{8,10},{9,11},{14,12},{15,13},{16,18},{17,... | collective-permute-start | bytes 2727944 | tf_op jit(solution)/shard_map/ppermute | solution.py:576
  383.6 34.9 %collective-permute-start.35 = (bf16[592,768]{1,0:T(8,128)(2,1)S(1)}, bf16[592,768]{1,0:T(8,128)(2,1)S(1)}, u32[]{:S(2)}, u32[]{:S(2)}) collective-permute-start(bf16[592,768]{1,0:T(8,128)(2,1)S(1)} %copy-done.35), channel_id=1, source_target_pairs={{0,1},{1,0},{2,3},{3,2},{4,5},{5,4},{6,7},{7,6},{8,9},{9,8},{10,11... | collective-permute-start | bytes 2727944 | tf_op jit(solution)/shard_map/ppermute | solution.py:576
  399.0 39.0 %collective-permute-start.48 = (bf16[592,768]{1,0:T(8,128)(2,1)S(1)}, bf16[592,768]{1,0:T(8,128)(2,1)S(1)}, u32[]{:S(2)}, u32[]{:S(2)}) collective-permute-start(bf16[592,768]{1,0:T(8,128)(2,1)S(1)} %copy-done.34), channel_id=1, source_target_pairs={{0,1},{1,0},{2,3},{3,2},{4,5},{5,4},{6,7},{7,6},{8,9},{9,8},{10,11... | collective-permute-start | bytes 2727944 | tf_op jit(solution)/shard_map/ppermute | solution.py:576
  400.8 37.9 %collective-permute-start.51 = (bf16[592,768]{1,0:T(8,128)(2,1)S(1)}, bf16[592,768]{1,0:T(8,128)(2,1)S(1)}, u32[]{:S(2)}, u32[]{:S(2)}) collective-permute-start(bf16[592,768]{1,0:T(8,128)(2,1)S(1)} %add_convert_fusion.5), channel_id=1, source_target_pairs={{0,2},{1,3},{6,4},{7,5},{8,10},{9,11},{14,12},{15,13},{16,18},{17,... | collective-permute-start | bytes 2727944 | tf_op jit(solution)/shard_map/ppermute | solution.py:576
  403.4 37.2 %collective-permute-start.54 = (bf16[592,768]{1,0:T(8,128)(2,1)S(1)}, bf16[592,768]{1,0:T(8,128)(2,1)S(1)}, u32[]{:S(2)}, u32[]{:S(2)}) collective-permute-start(bf16[592,768]{1,0:T(8,128)(2,1)S(1)} %add_convert_fusion.2), channel_id=1, source_target_pairs={{2,4},{3,5},{4,2},{5,3},{10,12},{11,13},{12,10},{13,11},{18,20},{1... | collective-permute-start | bytes 2727944 | tf_op jit(solution)/shard_map/ppermute | solution.py:576
  418.8 25.2 %collective-permute-start.40 = (bf16[592,768]{1,0:T(8,128)(2,1)S(1)}, bf16[592,768]{1,0:T(8,128)(2,1)S(1)}, u32[]{:S(2)}, u32[]{:S(2)}) collective-permute-start(bf16[592,768]{1,0:T(8,128)(2,1)S(1)} %add_convert_fusion.13), channel_id=1, source_target_pairs={{0,2},{1,3},{6,4},{7,5},{8,10},{9,11},{14,12},{15,13},{16,18},{17,... | collective-permute-start | bytes 2727944 | tf_op jit(solution)/shard_map/ppermute | solution.py:576
  421.2 36.3 %collective-permute-start.39 = (bf16[592,768]{1,0:T(8,128)(2,1)S(1)}, bf16[592,768]{1,0:T(8,128)(2,1)S(1)}, u32[]{:S(2)}, u32[]{:S(2)}) collective-permute-start(bf16[592,768]{1,0:T(8,128)(2,1)S(1)} %copy-done.33), channel_id=1, source_target_pairs={{0,1},{1,0},{2,3},{3,2},{4,5},{5,4},{6,7},{7,6},{8,9},{9,8},{10,11... | collective-permute-start | bytes 2727944 | tf_op jit(solution)/shard_map/ppermute | solution.py:576
  438.0 21.0 %collective-permute-start.41 = (bf16[592,768]{1,0:T(8,128)(2,1)S(1)}, bf16[592,768]{1,0:T(8,128)(2,1)S(1)}, u32[]{:S(2)}, u32[]{:S(2)}) collective-permute-start(bf16[592,768]{1,0:T(8,128)(2,1)S(1)} %add_convert_fusion.12), channel_id=1, source_target_pairs={{2,4},{3,5},{4,2},{5,3},{10,12},{11,13},{12,10},{13,11},{18,20},{1... | collective-permute-start | bytes 2727944 | tf_op jit(solution)/shard_map/ppermute | solution.py:576
  438.7 38.2 %collective-permute-start.49 = (bf16[592,768]{1,0:T(8,128)(2,1)S(1)}, bf16[592,768]{1,0:T(8,128)(2,1)S(1)}, u32[]{:S(2)}, u32[]{:S(2)}) collective-permute-start(bf16[592,768]{1,0:T(8,128)(2,1)S(1)} %copy-done.32), channel_id=1, source_target_pairs={{0,1},{1,0},{2,3},{3,2},{4,5},{5,4},{6,7},{7,6},{8,9},{9,8},{10,11... | collective-permute-start | bytes 2727944 | tf_op jit(solution)/shard_map/ppermute | solution.py:576
  440.6 38.7 %collective-permute-start.52 = (bf16[592,768]{1,0:T(8,128)(2,1)S(1)}, bf16[592,768]{1,0:T(8,128)(2,1)S(1)}, u32[]{:S(2)}, u32[]{:S(2)}) collective-permute-start(bf16[592,768]{1,0:T(8,128)(2,1)S(1)} %add_convert_fusion.4), channel_id=1, source_target_pairs={{2,4},{3,5},{4,2},{5,3},{10,12},{11,13},{12,10},{13,11},{18,20},{1... | collective-permute-start | bytes 2727944 | tf_op jit(solution)/shard_map/ppermute | solution.py:576
  444.0 36.0 %collective-permute-start.50 = (bf16[592,768]{1,0:T(8,128)(2,1)S(1)}, bf16[592,768]{1,0:T(8,128)(2,1)S(1)}, u32[]{:S(2)}, u32[]{:S(2)}) collective-permute-start(bf16[592,768]{1,0:T(8,128)(2,1)S(1)} %get-tuple-element.141), channel_id=1, source_target_pairs={{0,2},{1,3},{6,4},{7,5},{8,10},{9,11},{14,12},{15,13},{16,18},{17,... | collective-permute-start | bytes 2727944 | tf_op jit(solution)/shard_map/ppermute | solution.py:576
  457.5 23.8 %collective-permute-start.55 = (bf16[592,768]{1,0:T(8,128)(2,1)S(1)}, bf16[592,768]{1,0:T(8,128)(2,1)S(1)}, u32[]{:S(2)}, u32[]{:S(2)}) collective-permute-start(bf16[592,768]{1,0:T(8,128)(2,1)S(1)} %get-tuple-element.140), channel_id=1, source_target_pairs={{2,0},{3,1},{4,6},{5,7},{10,8},{11,9},{12,14},{13,15},{18,16},{19,... | collective-permute-start | bytes 2727944 | tf_op jit(solution)/shard_map/ppermute | solution.py:576
  460.2 35.6 %collective-permute-start.42 = (bf16[592,768]{1,0:T(8,128)(2,1)S(1)}, bf16[592,768]{1,0:T(8,128)(2,1)S(1)}, u32[]{:S(2)}, u32[]{:S(2)}) collective-permute-start(bf16[592,768]{1,0:T(8,128)(2,1)S(1)} %copy-done.31), channel_id=1, source_target_pairs={{0,1},{1,0},{2,3},{3,2},{4,5},{5,4},{6,7},{7,6},{8,9},{9,8},{10,11... | collective-permute-start | bytes 2727944 | tf_op jit(solution)/shard_map/ppermute | solution.py:576
  477.0 20.6 %collective-permute-start.43 = (bf16[592,768]{1,0:T(8,128)(2,1)S(1)}, bf16[592,768]{1,0:T(8,128)(2,1)S(1)}, u32[]{:S(2)}, u32[]{:S(2)}) collective-permute-start(bf16[592,768]{1,0:T(8,128)(2,1)S(1)} %get-tuple-element.127), channel_id=1, source_target_pairs={{0,2},{1,3},{6,4},{7,5},{8,10},{9,11},{14,12},{15,13},{16,18},{17,... | collective-permute-start | bytes 2727944 | tf_op jit(solution)/shard_map/ppermute | solution.py:576
  479.3 18.3 %collective-permute-start.44 = (bf16[592,768]{1,0:T(8,128)(2,1)S(1)}, bf16[592,768]{1,0:T(8,128)(2,1)S(1)}, u32[]{:S(2)}, u32[]{:S(2)}) collective-permute-start(bf16[592,768]{1,0:T(8,128)(2,1)S(1)} %add_convert_fusion.10), channel_id=1, source_target_pairs={{2,4},{3,5},{4,2},{5,3},{10,12},{11,13},{12,10},{13,11},{18,20},{1... | collective-permute-start | bytes 2727944 | tf_op jit(solution)/shard_map/ppermute | solution.py:576
  480.0 24.3 %collective-permute-start.45 = (bf16[592,768]{1,0:T(8,128)(2,1)S(1)}, bf16[592,768]{1,0:T(8,128)(2,1)S(1)}, u32[]{:S(2)}, u32[]{:S(2)}) collective-permute-start(bf16[592,768]{1,0:T(8,128)(2,1)S(1)} %get-tuple-element.129), channel_id=1, source_target_pairs={{2,0},{3,1},{4,6},{5,7},{10,8},{11,9},{12,14},{13,15},{18,16},{19,... | collective-permute-start | bytes 2727944 | tf_op jit(solution)/shard_map/ppermute | solution.py:576
  481.9 25.2 %collective-permute-start.57 = (bf16[592,768]{1,0:T(8,128)(2,1)S(1)}, bf16[592,768]{1,0:T(8,128)(2,1)}, u32[]{:S(2)}, u32[]{:S(2)}) collective-permute-start(bf16[592,768]{1,0:T(8,128)(2,1)S(1)} %add_convert_fusion), channel_id=1, source_target_pairs={{0,8},{16,24},{1,9},{17,25},{2,10},{18,26},{3,11},{19,27},{4,12},{... | collective-permute-start | bytes 2727944 | tf_op jit(solution)/shard_map/ppermute | solution.py:747
  (48 other events, 890.9 us)

commit v5 on v4

--- a/solution.py
+++ b/solution.py
@@ -208,10 +208,10 @@
     return acc.astype(BF)
 
 
-def forward_kernel(save, count, x_ref, mask_ref, *rest):
+def forward_kernel(save, count, x_ref, came_ref, mask_ref, *rest):
     info = here()
     sets, rest = (rest[:count], rest[count:2 * count]), rest[2 * count:]
-    wide = 14 if save else 2
+    wide = 15 if save else 2
     results, rest = rest[:wide], rest[wide:]
     scratch = [rest[0:4], rest[4:8]]
     rest = rest[8:]
@@ -219,6 +219,9 @@
     usable = mask_ref[0:1, :] > 0.5
     outs = []
     x = x_ref[...]
+    if save:
+        x = jnp.where(lax.axis_index("section") < 2, x, came_ref[...])
+        results[14][...] = x
     for s in range(2):
         work, rest = rest[:7], rest[7:]
         saved = results[2 + 6 * s:8 + 6 * s] if save else ()
@@ -228,7 +231,7 @@
         c.wait()
 
 
-def forward_stage(save, x, mask, wa, wb):
+def forward_stage(save, x, came, mask, wa, wb):
     def sd(cols, t=BF):
         return jax.ShapeDtypeStruct((ROWS, cols), t)
 
@@ -236,18 +239,20 @@
     if save:
         shapes += [sd(PAIRED, F32), sd(D, F32), sd(3 * D), sd(FF), sd(WIDE), sd(WIDE)] * 2
         specs += ([VM, VM] + [ANYS] * 4) * 2
+        shapes.append(sd(D))
+        specs.append(VM)
     work = [pltpu.VMEM((ROWS, 3 * D), BF), pltpu.VMEM((ROWS, D), BF), pltpu.VMEM((ROWS, FF), BF),
             pltpu.VMEM((ROWS, FF), BF), pltpu.VMEM((ROWS, D), BF), pltpu.VMEM((ROWS, D), BF), pltpu.VMEM((16, D), F32)]
     return pl.pallas_call(
         functools.partial(forward_kernel, save, len(wa)),
         out_shape=shapes,
-        in_specs=[VM, VM] + [ANYS] * (2 * len(wa)),
+        in_specs=[VM, VM, VM] + [ANYS] * (2 * len(wa)),
         out_specs=specs,
         scratch_shapes=weight_scratch(len(wa)) * 2 + work * 2 + [pltpu.SemaphoreType.DMA((14,))],
         compiler_params=pltpu.CompilerParams(vmem_limit_bytes=VMEM_LIMIT),
         cost_estimate=pl.CostEstimate(flops=2 * ROWS * D * D * 26, bytes_accessed=48 * D * D + 2**23, transcendentals=0),
         name="forward_stage",
-    )(x, mask, *wa, *wb)
+    )(x, came, mask, *wa, *wb)
 
 
 def backward_one(save, core, g_ref, x_ref, lse_ref, mid_ref, j_hbm, gp_hbm, usable, copies, scratch, work, isems, osems, results,
@@ -520,6 +525,57 @@
     )(*params)
 
 
+def finish_kernel(red0, red1, sent0, sent1, up, joint, out, down, ag, as_, jb, ob, fg, fs, db, ub):
+    r = out.shape[0]
+    spot, core = lax.axis_index("dp"), lax.axis_index("section") % 2
+
+    def taken(rows, wide, at):
+        entry = lax.broadcasted_iota(jnp.int32, (D, wide), 0)
+        lane = lax.broadcasted_iota(jnp.int32, (D, wide), 1)
+        pick = (entry == lane + at * wide).astype(F32)
+        return lax.dot_general(rows, pick, (((1,), (0,)), ((), ())), precision=lax.Precision.HIGHEST,
+                               preferred_element_type=F32)
+
+    def write(a, b):
+        for k in range(4):
+            up[:, k * D:(k + 1) * D] = a[k * r:(k + 1) * r, :].astype(F32)
+        for k in range(2):
+            joint[:, k * D:(k + 1) * D] = a[(4 + k) * r:(5 + k) * r, :].astype(F32)
+        joint[:, 2 * D:] = b[5 * r:6 * r, :].astype(F32)
+        down[...] = b[:4 * r, :].astype(F32)
+        out[...] = b[4 * r:5 * r, :].astype(F32)
+        v = a[6 * r:, :].astype(F32) + b[6 * r:, :].astype(F32)
+        own = taken(v, r, spot)
+        for ref, row in ((ag, AG), (as_, AS), (ob, OB), (fg, FG), (fs, FS), (db, DB)):
+            ref[...] = own[row:row + 1]
+        half = taken(v, 2 * r, spot % 4)
+        jb[...] = jnp.where(spot // 4 == 0, half[BQ:BQ + 1], half[BV:BV + 1])
+        most = taken(v, 4 * r, spot % 2)
+        place = spot // 2
+        ub[...] = jnp.where(place == 0, most[UB:UB + 1], jnp.where(place == 1, most[UB + 1:UB + 2], jnp.where(
+            place == 2, most[UB + 2:UB + 3], most[UB + 3:UB + 4])))
+
+    @pl.when(core == 0)
+    def _():
+        write(red0, sent0)
+
+    @pl.when(core != 0)
+    def _():
+        write(sent1, red1)
+
+
+def finish(r, reduced, sent):
+    shapes = [(r, FF), (r, 3 * D), (r, D), (4 * r, D), (1, r), (1, r), (1, 2 * r), (1, r), (1, r), (1, r), (1, r), (1, 4 * r)]
+    return pl.pallas_call(
+        finish_kernel,
+        out_shape=[jax.ShapeDtypeStruct(shape, F32) for shape in shapes],
+        in_specs=[VM] * 4,
+        out_specs=[VM] * 12,
+        compiler_params=pltpu.CompilerParams(vmem_limit_bytes=VMEM_LIMIT),
+        name="finish",
+    )(*reduced, *sent)
+
+
 def moved(value, axis, by):
     peers = lax.axis_size(axis)
     return lax.ppermute(value, axis, [(i, i + by) for i in range(peers) if 0 <= i + by < peers])
@@ -618,46 +674,38 @@
     return total.astype(BF)
 
 
-def scatter_rounds(blocks, wide=None, extra=None):
-    net = Links(x=9, z=9)
-    x0 = net.across(blocks[4])
-    s0 = add(blocks[0], x0)
-    b, s0 = lax.optimization_barrier((blocks[5], s0))
+def scatter_both(p, q, extra):
+    chain, net = Links(x=1, z=9), Links(x=9, z=9)
+    p[5], q[0] = lax.optimization_barrier((p[5], q[0]))
+    ps = []
+    for k in range(3):
+        ps.append(jnp.concatenate([add(p[k], chain.across(p[4 + k])), p[8 + k]]))
+        if k == 0:
+            pa1 = chain.along(ps[0], IN)
+        elif k == 1:
+            pa2 = chain.along(ps[1], IN)
+            pb2 = chain.along(add(ps[0], pa1), MID)
+        else:
+            pa3 = chain.along(ps[2], IN)
+            pb3 = chain.along(add(ps[1], pa2), MID)
+            pc3 = chain.along(add(ps[2], pb2), OUT)
+    px3 = chain.across(p[7])
+    x0 = net.across(q[4])
+    s0 = add(q[0], x0)
+    b, s0 = lax.optimization_barrier((q[5], s0))
     x1, a1 = net.across(b), net.along(s0, IN)
-    s1, t0 = add(blocks[1], x1), add(s0, a1)
-    if extra is None:
-        b, s1, t0 = lax.optimization_barrier((blocks[6], s1, t0))
-    else:
-        b, s1, t0, extra = lax.optimization_barrier((blocks[6], s1, t0, extra))
-    x2, a2, b2 = net.across(b), net.along(s1, IN), net.along(t0, MID)
-    s2, t1 = add(blocks[2], x2), add(s1, a2)
+    s1, t0 = add(q[1], x1), add(s0, a1)
+    b, own, s1, t0, extra = lax.optimization_barrier((q[6], q[7], s1, t0, extra))
+    x2, a2, b2, x3 = net.across(b), net.along(s1, IN), net.along(t0, MID), net.across(own)
+    s2, t1 = add(q[2], x2), add(s1, a2)
     u = add(s2, b2)
-    b, s2, t1, u = lax.optimization_barrier((blocks[7], s2, t1, u))
-    x3, a3, b3, c3 = net.across(b), net.along(s2, IN), net.along(t1, MID), net.along(u, OUT)
-    return add(blocks[3], x3, a3, b3, c3), extra
-
-
-def scatter_steps(net, blocks, across):
-    def own(k):
-        return add(blocks[k], net.across(blocks[4 + k])) if across else blocks[k]
-
-    s0 = own(0)
-    a1 = net.along(s0, IN)
-    yield
-    s1 = own(1)
-    a2 = net.along(s1, IN)
-    b2 = net.along(add(s0, a1), MID)
-    yield
-    s2 = own(2)
-    a3 = net.along(s2, IN)
-    b3 = net.along(add(s1, a2), MID)
-    c3 = net.along(add(s2, b2), OUT)
-    yield
-    total = add(own(3), a3, b3, c3)
-    if not across:
-        half = total.shape[0] // 2
-        total = add(total[:half], net.across(total[half:]))
-    yield total
+    s2, t1, u = lax.optimization_barrier((s2, t1, u))
+    a3, b3, c3 = net.along(s2, IN), net.along(t1, MID), net.along(u, OUT)
+    total = add(jnp.concatenate([add(p[3], px3), p[11]]), pa3, pb3, pc3)
+    rows, pair = p[3].shape[0], p[11].shape[0] // 2
+    late = add(total[rows:rows + pair], net.across(total[rows + pair:]))
+    first = jnp.concatenate([total[:rows - TAIL], late, total[rows - TAIL:rows]])
+    return first, add(q[3], x3, a3, b3, c3), extra
 
 
 def shards(tokens, lengths, cotangent, attend_gain, attend_shift, joint_weight, joint_bias, output_weight,
@@ -697,13 +745,13 @@
     own_tokens = padded(own_pair(tokens))
     own_cotangent = padded(own_pair(cotangent))
 
-    x = own_tokens
-    for t in range(stages):
-        last = t == stages - 1
-        got = forward_stage(last, x, mask, wa, wb)
-        if not last:
-            x = jnp.where(stage == 0, own_tokens, moved(got[1], "section", 2))
-    leaving = got[1]
+    came = own_tokens
+    for _ in range(stages - 1):
+        came = moved(forward_stage(False, came, came, mask, wa, wb)[1], "section", 2)
+        if stages > 2:
+            came = jnp.where(stage == 0, own_tokens, came)
+    got = forward_stage(True, own_tokens, came, mask, wa, wb)
+    x, leaving = got[14], got[1]
     saved = [(x, *got[2:6]), (got[0], *got[8:12])]
     kept = [got[6], got[12]]
     received = [swapped(got[7]), swapped(got[13])]
@@ -719,7 +767,7 @@
         operands[s] = gv, kept[s], bk, received[s], swapped(bs)
     behind = g
     for s in (1, 0):
-        products[s] = list(weight_products(nk, 0 if lined else 0, behind, *operands[s]))
+        products[s] = list(weight_products(nk, 2 * s if lined else 0, behind, *operands[s]))
         behind = products[s][0]
 
     g, products[0][-1] = lax.optimization_barrier((g, products[0][-1]))
@@ -733,10 +781,7 @@
 
     reduced = [None, None]
     if lined:
-        net = Links(x=1, z=9)
-        products[1][5], products[0][0] = lax.optimization_barrier((products[1][5], products[0][0]))
-        reduced[1] = list(scatter_steps(net, products[1], True))[-1]
-        reduced[0], parts = scatter_rounds(products[0], None, parts)
+        reduced[1], reduced[0], parts = scatter_both(products[1], products[0], parts)
     else:
         for s in range(2):
             p = products[s][0]
@@ -745,6 +790,10 @@
             total = lax.psum_scatter(jnp.where(core == 0, col, row), "dp", scatter_dimension=0)
             reduced[s] = jnp.concatenate([total, lax.psum(p[HALF * D:], "dp")])
     sent = [lax.ppermute(reduced[s], "section", [(i, i ^ 1) for i in range(sections) if i % 2 != s]) for s in range(2)]
+    outputs, token_grad = parts[0], parts[1]
+    if lined:
+        up, joint, out, down, ag, as_, jb, ob, fg, fs, db, ub = finish(r, reduced, sent)
+        return (outputs, token_grad, ag, as_, joint[None], jb, out[None], ob, fg, fs, up[None], ub, down[None], db)
     keep = jnp.where(core == 0, reduced[0], reduced[1])
     away = jnp.where(core == 0, sent[0], sent[1])
     first = jnp.where(core == 0, keep, away).astype(F32)
@@ -758,7 +807,6 @@
     vec = lax.dynamic_slice(v, (0, r * spot), (16, r))
     grad_jb = lax.dynamic_slice(v, (BQ + spot // half, 2 * r * (spot % half)), (1, 2 * r))
     grad_ub = lax.dynamic_slice(v, (UB + spot // quarter, 4 * r * (spot % quarter)), (1, 4 * r))
-    outputs, token_grad = parts[0], parts[1]
     return (outputs, token_grad, vec[AG:AG + 1], vec[AS:AS + 1], grad_joint[None], grad_jb, grad_out[None],
             vec[OB:OB + 1], vec[FG:FG + 1], vec[FS:FS + 1], grad_up[None], grad_ub, grad_down[None], vec[DB:DB + 1])
 

time: 522 us -> 518 us (level)
  Pallas kernels: 152 us -> 158 us
    pallas_call x0 -> x1, Pallas kernels: none -> 5.41 us  [finish(): pl.pallas_call(finish_kernel, out_shape=[jax.ShapeDtypeStruct(shape, F32)...]
    ppermute x36 -> x37, waiting for transfers between devices: 224 us -> 225 us  [send(): got = lax.ppermute(value, axis, pairs)]
    ppermute x36 -> x37, starting transfers between devices: 61 us -> 60.5 us  [send(): got = lax.ppermute(value, axis, pairs)]
  transfers between devices with their start and end apart: 58 -> 59, of which waited for: 28 -> 30; matrix products, arithmetic and copies ran while one was open for 3% -> 3% of each run, Pallas kernels for 13% -> 13%
where the time goes in v5:
time: 518 us; the launch traced here: 513 us
  waiting for transfers between devices  259 us (50%)
  Pallas kernels  158 us (31%)
  starting transfers between devices  74.9 us (14%)
  other arithmetic  9.85 us (2%)
  local copies, waits for them, and re-layouts  9.19 us (2%)
    ppermute x37, waiting for transfers between devices, send(): got = lax.ppermute(value, axis, pairs)  225 us
    pallas_call x3, Pallas kernels, backward_layers(): pl.pallas_call(functools.partial(backward_kernel, save, layers, len(wa)),...  74.1 us
    ppermute x37, starting transfers between devices, send(): got = lax.ppermute(value, axis, pairs)  60.5 us
    pallas_call x2, Pallas kernels, forward_stage(): pl.pallas_call(functools.partial(forward_kernel, save, len(wa)), out_shap...  49.2 us
    pallas_call x2, Pallas kernels, weight_products(): pl.pallas_call(functools.partial(product_kernel, n, direct), out_shape=sh...  25.7 us
    ppermute x2, waiting for transfers between devices, moved(): lax.ppermute(value, axis, [(i, i + by) for i in range(peers) if 0 <= i +...  20.9 us
    ppermute x18, waiting for transfers between devices, flipped(): return lax.ppermute(value, 'section', [(i, i ^ bit) for i in range(peers)])  12.3 us
  transfers between devices with their start and end apart: 59, of which 30 were waited for; matrix products, arithmetic and copies ran while one was open for 3% of the time, Pallas kernels for 13%

profile of v5, /device:TPU:0, one launch (start us, length us, event | category | flops | bytes accessed | tf_op | source)
XLA Modules:
  0.0 513.3 jit_solution(18044494802245665899)
XLA Ops:
  0.7 3.7 pack.1
  4.4 4.8 collective-permute-start.5
  11.7 5.4 %collective-permute-done.5 = bf16[192,768]{1,0:T(8,128)(2,1)S(1)} collective-permute-done((bf16[192,768]{1,0:T(8,128)(2,1)}, bf16[192,768]{1,0:T(8,128)(2,1)S(1)}, u32[]{:S(2)}, u32[]{:S(2)}) %collective-permute-start.5) | collective-permute-done | bytes 294944 | tf_op jit(solution)/shard_map/ppermute | solution.py:632
  17.0 2.3 collective-permute-start.6
  19.3 22.0 %collective-permute-done.rest_1_.rest_11_.rest_7_ = bf16[976,768]{1,0:T(8,128)(2,1)} collective-permute-done((bf16[976,768]{1,0:T(8,128)(2,1)}, bf16[976,768]{1,0:T(8,128)(2,1)}, u32[]{:S(2)}, u32[]{:S(2)}) %collective-permute-start) | collective-permute-done | bytes 1499168 | tf_op jit(solution)/shard_map/ppermute | solution.py:632
  44.4 2.0 collective-permute-done.6.rest_4_.rest_14_.rest_10_
  47.1 1.9 collective-permute-start.8
  50.4 26.4 %collective-permute-done.2 = bf16[976,768]{1,0:T(8,128)(2,1)} collective-permute-done((bf16[976,768]{1,0:T(8,128)(2,1)S(1)}, bf16[976,768]{1,0:T(8,128)(2,1)}, u32[]{:S(2)}, u32[]{:S(2)}) %collective-permute-start.2) | collective-permute-done | bytes 1499168 | tf_op jit(solution)/shard_map/ppermute | solution.py:632
  78.4 2.8 collective-permute-done.8.rest_5_.rest_15_.rest_11_
  81.2 2.0 collective-permute-start.9
  84.9 2.5 collective-permute-start.11
  88.1 34.5 %collective-permute-done.11.rest_9_.rest_19_.rest_15_ = bf16[384,768]{1,0:T(8,128)(2,1)S(1)} collective-permute-done((bf16[384,768]{1,0:T(8,128)(2,1)S(1)}, bf16[384,768]{1,0:T(8,128)(2,1)S(1)}, u32[]{:S(2)}, u32[]{:S(2)}) %collective-permute-start.11) | collective-permute-done | bytes 589856 | tf_op jit(solution)/shard_map/ppermute | solution.py:632
  129.3 12.0 %collective-permute-done.13 = bf16[384,768]{1,0:T(8,128)(2,1)S(1)} collective-permute-done((bf16[384,768]{1,0:T(8,128)(2,1)S(1)}, bf16[384,768]{1,0:T(8,128)(2,1)S(1)}, u32[]{:S(2)}, u32[]{:S(2)}) %collective-permute-start.13) | collective-permute-done | bytes 589856 | tf_op jit(solution)/shard_map/ppermute | solution.py:632
  141.4 13.2 %collective-permute-done.15 = bf16[384,768]{1,0:T(8,128)(2,1)S(1)} collective-permute-done((bf16[384,768]{1,0:T(8,128)(2,1)S(1)}, bf16[384,768]{1,0:T(8,128)(2,1)S(1)}, u32[]{:S(2)}, u32[]{:S(2)}) %collective-permute-start.15) | collective-permute-done | bytes 589856 | tf_op jit(solution)/shard_map/ppermute | solution.py:632
  158.9 2.7 collective-permute-done.10.rest_7_.rest_17_.rest_13_
  165.1 2.1 collective-permute-done.22.rest_18_.rest_28_.rest_24_
  167.2 2.1 collective-permute-done.23.rest_19_.rest_29_.rest_25_
  169.9 22.9 %forward_stage.2 = (bf16[288,768]{1,0:T(8,128)(2,1)}, bf16[288,768]{1,0:T(8,128)(2,1)}) custom-call(bf16[288,768]{1,0:T(8,128)(2,1)} %pad.8.x_ref.came_ref, bf16[288,768]{1,0:T(8,128)(2,1)} %pad.8.x_ref.came_ref, f32[8,288]{1,0:T(8,128)} %iota.13.mask_ref.rest_5_, bf16[976,768]{1,0:T(8,128)(2,1)} %get-tuple-element.96.rest_0_.rest_10_.rest_6_, ...), custom_call_target="tpu_custom_call" | custom-call | flops 8833204224 | bytes 36700160 | tf_op jit(solution)/shard_map/forward_stage/pallas_call | solution.py:246
  192.9 3.5 collective-permute-start.28
  197.2 9.1 %collective-permute-done.28.came_ref = bf16[288,768]{1,0:T(8,128)(2,1)S(1)} collective-permute-done((bf16[288,768]{1,0:T(8,128)(2,1)}, bf16[288,768]{1,0:T(8,128)(2,1)S(1)}, u32[]{:S(2)}, u32[]{:S(2)}) %collective-permute-start.28) | collective-permute-done | bytes 442400 | tf_op jit(solution)/shard_map/ppermute | solution.py:581
  207.1 26.3 %forward_stage.3 = (bf16[288,768]{1,0:T(8,128)(2,1)}, bf16[288,768]{1,0:T(8,128)(2,1)}, f32[288,128]{1,0:T(8,128)}, f32[288,768]{1,0:T(8,128)}, bf16[288,2304]{1...) custom-call(bf16[288,768]{1,0:T(8,128)(2,1)} %pad.8.x_ref.came_ref, ...), custom_call_target="tpu_custom_call" | custom-call | flops 8833204224 | bytes 36700160 | tf_op jit(solution)/shard_map/forward_stage/pallas_call | solution.py:246
  233.5 34.3 %backward_layers.3 = bf16[288,768]{1,0:T(8,128)(2,1)} custom-call(bf16[288,768]{1,0:T(8,128)(2,1)} %pad.7.g_ref, f32[8,288]{1,0:T(8,128)} %iota.13.mask_ref.rest_5_, bf16[288,768]{1,0:T(8,128)(2,1)} %get-tuple-element.102.rest_0_, f32[288,128]{1,0:T(8,128)} %get-tuple-element.103.rest_1_, f32[288,768]{1,0:T(8,128)} %get-tuple-element.104.rest_2_, ...), custom_call_target="tpu_custom_call" | custom-call | flops 9512681472 | bytes 45088768 | tf_op jit(solution)/shard_map/backward_layers/pallas_call | solution.py:378
  269.7 11.7 %collective-permute-done.29 = bf16[288,768]{1,0:T(8,128)(2,1)S(1)} collective-permute-done((bf16[288,768]{1,0:T(8,128)(2,1)}, bf16[288,768]{1,0:T(8,128)(2,1)S(1)}, u32[]{:S(2)}, u32[]{:S(2)}) %collective-permute-start.29) | collective-permute-done | bytes 442400 | tf_op jit(solution)/shard_map/ppermute | solution.py:581
  282.3 19.8 %backward_layers.4 = (bf16[288,768]{1,0:T(8,128)(2,1)}, f32[16,768]{1,0:T(8,128)}, bf16[288,4608]{1,0:T(8,128)(2,1)}, bf16[288,4608]{1,0:T(8,128)(2,1)}) custom-call(bf16[288,768]{1,0:T(8,128)(2,1)} %broadcast_select_fusion.4.g_ref, f32[8,288]{1,0:T(8,128)} %iota.13.mask_ref.rest_5_, bf16[288,768]{1,0:T(8,128)(2,1)} %get-tuple-element.102.rest_0_, ...), custom_call_target="tpu_custom_call" | custom-call | flops 4756340736 | bytes 22544384 | tf_op jit(solution)/shard_map/backward_layers/pallas_call | solution.py:378
  302.2 19.9 %backward_layers.5 = (bf16[288,768]{1,0:T(8,128)(2,1)}, f32[16,768]{1,0:T(8,128)}, bf16[288,4608]{1,0:T(8,128)(2,1)}, bf16[288,4608]{1,0:T(8,128)(2,1)}) custom-call(bf16[288,768]{1,0:T(8,128)(2,1)} %get-tuple-element.112.g_ref, f32[8,288]{1,0:T(8,128)} %iota.13.mask_ref.rest_5_, bf16[288,768]{1,0:T(8,128)(2,1)} %get-tuple-element.107.rest_5_.rest_0_, ...), custom_call_target="tpu_custom_call" | custom-call | flops 4756340736 | bytes 22544384 | tf_op jit(solution)/shard_map/backward_layers/pallas_call | solution.py:378
  324.2 13.1 %weight_products.2 = (bf16[400,768]{1,0:T(8,128)(2,1)}, bf16[400,768]{1,0:T(8,128)(2,1)}, bf16[400,768]{1,0:T(8,128)(2,1)}, bf16[400,768]{1,0:T(8,128)(2,1)}, bf...) custom-call(bf16[288,768]{1,0:T(8,128)(2,1)} %get-tuple-element.136., ...), custom_call_target="tpu_custom_call" | custom-call | flops 4076863488 | bytes 16777216 | tf_op jit(solution)/shard_map/weight_products/pallas_call | solution.py:477
  338.9 12.6 %weight_products.3 = (bf16[592,768]{1,0:T(8,128)(2,1)}, bf16[592,768]{1,0:T(8,128)(2,1)}, bf16[592,768]{1,0:T(8,128)(2,1)}, bf16[592,768]{1,0:T(8,128)(2,1)}, bf...) custom-call(bf16[400,768]{1,0:T(8,128)(2,1)} %get-tuple-element.119.behi, ...), custom_call_target="tpu_custom_call" | custom-call | flops 4076863488 | bytes 16777216 | tf_op jit(solution)/shard_map/weight_products/pallas_call | solution.py:477
  354.0 2.5 collective-permute-start.53
  356.5 5.4 %collective-permute-done.37 = bf16[280,2,192]{2,0,1:T(8,128)(2,1)S(1)} collective-permute-done((bf16[280,2,192]{2,0,1:T(8,128)(2,1)S(1)}, bf16[280,2,192]{2,0,1:T(8,128)(2,1)S(1)}, u32[]{:S(2)}, u32[]{:S(2)}) %collective-permute-start.37) | collective-permute-done | bytes 215072 | tf_op jit(solution)/shard_map/ppermute | solution.py:586
  363.6 11.7 %collective-permute-done.34 = bf16[592,768]{1,0:T(8,128)(2,1)S(1)} collective-permute-done((bf16[592,768]{1,0:T(8,128)(2,1)}, bf16[592,768]{1,0:T(8,128)(2,1)S(1)}, u32[]{:S(2)}, u32[]{:S(2)}) %collective-permute-start.34) | collective-permute-done | bytes 909344 | tf_op jit(solution)/shard_map/ppermute | solution.py:632
  375.6 2.5 collective-permute-start.36
  379.0 9.5 %collective-permute-done.47 = bf16[400,768]{1,0:T(8,128)(2,1)S(1)} collective-permute-done((bf16[400,768]{1,0:T(8,128)(2,1)S(1)}, bf16[400,768]{1,0:T(8,128)(2,1)S(1)}, u32[]{:S(2)}, u32[]{:S(2)}) %collective-permute-start.47) | collective-permute-done | bytes 614432 | tf_op jit(solution)/shard_map/ppermute | solution.py:632
  389.3 2.4 collective-permute-start.51
  393.0 9.8 %collective-permute-done.36 = bf16[592,768]{1,0:T(8,128)(2,1)S(1)} collective-permute-done((bf16[592,768]{1,0:T(8,128)(2,1)S(1)}, bf16[592,768]{1,0:T(8,128)(2,1)S(1)}, u32[]{:S(2)}, u32[]{:S(2)}) %collective-permute-start.36) | collective-permute-done | bytes 909344 | tf_op jit(solution)/shard_map/ppermute | solution.py:632
  403.1 4.9 collective-permute-done.35
  408.2 2.5 collective-permute-start.41
  411.4 9.8 %collective-permute-done.48 = bf16[400,768]{1,0:T(8,128)(2,1)S(1)} collective-permute-done((bf16[400,768]{1,0:T(8,128)(2,1)S(1)}, bf16[400,768]{1,0:T(8,128)(2,1)S(1)}, u32[]{:S(2)}, u32[]{:S(2)}) %collective-permute-start.48) | collective-permute-done | bytes 614432 | tf_op jit(solution)/shard_map/ppermute | solution.py:632
  422.1 6.5 %collective-permute-done.51 = bf16[784,768]{1,0:T(8,128)(2,1)S(1)} collective-permute-done((bf16[784,768]{1,0:T(8,128)(2,1)S(1)}, bf16[784,768]{1,0:T(8,128)(2,1)S(1)}, u32[]{:S(2)}, u32[]{:S(2)}) %collective-permute-start.51) | collective-permute-done | bytes 1204256 | tf_op jit(solution)/shard_map/ppermute | solution.py:632
  428.6 4.5 collective-permute-start.50
  434.7 13.4 %collective-permute-done.41 = bf16[592,768]{1,0:T(8,128)(2,1)S(1)} collective-permute-done((bf16[592,768]{1,0:T(8,128)(2,1)S(1)}, bf16[592,768]{1,0:T(8,128)(2,1)S(1)}, u32[]{:S(2)}, u32[]{:S(2)}) %collective-permute-start.41) | collective-permute-done | bytes 909344 | tf_op jit(solution)/shard_map/ppermute | solution.py:632
  452.3 13.9 %collective-permute-done.49 = bf16[400,768]{1,0:T(8,128)(2,1)S(1)} collective-permute-done((bf16[400,768]{1,0:T(8,128)(2,1)S(1)}, bf16[400,768]{1,0:T(8,128)(2,1)S(1)}, u32[]{:S(2)}, u32[]{:S(2)}) %collective-permute-start.49) | collective-permute-done | bytes 614432 | tf_op jit(solution)/shard_map/ppermute | solution.py:632
  466.3 4.7 collective-permute-start.43
  470.9 3.0 collective-permute-done.50
  478.4 6.5 %collective-permute-done.39 = bf16[592,768]{1,0:T(8,128)(2,1)S(1)} collective-permute-done((bf16[592,768]{1,0:T(8,128)(2,1)S(1)}, bf16[592,768]{1,0:T(8,128)(2,1)S(1)}, u32[]{:S(2)}, u32[]{:S(2)}) %collective-permute-start.39) | collective-permute-done | bytes 909344 | tf_op jit(solution)/shard_map/ppermute | solution.py:632
  484.9 6.9 %collective-permute-done.43 = bf16[592,768]{1,0:T(8,128)(2,1)S(1)} collective-permute-done((bf16[592,768]{1,0:T(8,128)(2,1)S(1)}, bf16[592,768]{1,0:T(8,128)(2,1)S(1)}, u32[]{:S(2)}, u32[]{:S(2)}) %collective-permute-start.43) | collective-permute-done | bytes 909344 | tf_op jit(solution)/shard_map/ppermute | solution.py:632
  491.8 7.5 %collective-permute-done.45 = bf16[592,768]{1,0:T(8,128)(2,1)S(1)} collective-permute-done((bf16[592,768]{1,0:T(8,128)(2,1)S(1)}, bf16[592,768]{1,0:T(8,128)(2,1)S(1)}, u32[]{:S(2)}, u32[]{:S(2)}) %collective-permute-start.45) | collective-permute-done | bytes 909344 | tf_op jit(solution)/shard_map/ppermute | solution.py:632
  501.5 3.1 collective-permute-start.58
  507.6 5.4 %finish.1 = (f32[96,3072]{1,0:T(8,128)}, f32[96,2304]{1,0:T(8,128)}, f32[96,768]{1,0:T(8,128)}, f32[384,768]{1,0:T(8,128)}, f32[1,96]{1,0:T(1,128)}, /*index=5*/...) custom-call(bf16[592,768]{1,0:T(8,128)(2,1)} %copy-done.16, ...), custom_call_target="tpu_custom_call" | custom-call | tf_op jit(solution)/shard_map/finish/pallas_call | solution.py:569
  (214 shorter events, 59.1 us)
Async XLA Ops:
  4.4 12.6 %collective-permute-start.5 = (bf16[192,768]{1,0:T(8,128)(2,1)}, bf16[192,768]{1,0:T(8,128)(2,1)S(1)}, u32[]{:S(2)}, u32[]{:S(2)}) collective-permute-start(bf16[192,768]{1,0:T(8,128)(2,1)} %get-tuple-element.97), channel_id=1, source_target_pairs={{0,1},{1,0},{2,3},{3,2},{4,5},{5,4},{6,7},{7,6},{16,17},{17,16},{1... | collective-permute-start | bytes 884744 | tf_op jit(solution)/shard_map/ppermute | solution.py:632
  9.3 32.1 %collective-permute-start = (bf16[976,768]{1,0:T(8,128)(2,1)}, bf16[976,768]{1,0:T(8,128)(2,1)}, u32[]{:S(2)}, u32[]{:S(2)}) collective-permute-start(bf16[976,768]{1,0:T(8,128)(2,1)} %get-tuple-element.96.rest_0_.rest_10_.rest_6_), channel_id=1, source_target_pairs={{0,2},{1,3},{2,0},{3,1},{4,6},{5,7},{6,4},{7,5},{8,10},{9,11},{10,... | collective-permute-start | bytes 4497416 | tf_op jit(solution)/shard_map/ppermute | solution.py:632
  10.9 32.2 %collective-permute-start.1 = (bf16[976,768]{1,0:T(8,128)(2,1)}, bf16[976,768]{1,0:T(8,128)(2,1)S(1)}, u32[]{:S(2)}, u32[]{:S(2)}) collective-permute-start(bf16[976,768]{1,0:T(8,128)(2,1)} %get-tuple-element.96.rest_0_.rest_10_.rest_6_), channel_id=1, source_target_pairs={{2,4},{3,5},{4,2},{5,3},{10,12},{11,13},{12,10},{13,11},{18,20},{1... | collective-permute-start | bytes 4497416 | tf_op jit(solution)/shard_map/ppermute | solution.py:632
  17.0 29.4 %collective-permute-start.6 = (bf16[976,768]{1,0:T(8,128)(2,1)}, bf16[976,768]{1,0:T(8,128)(2,1)}, u32[]{:S(2)}, u32[]{:S(2)}) collective-permute-start(bf16[976,768]{1,0:T(8,128)(2,1)} %get-tuple-element.96.rest_0_.rest_10_.rest_6_), channel_id=1, source_target_pairs={{0,1},{1,0},{2,3},{3,2},{4,5},{5,4},{6,7},{7,6},{8,9},{9,8},{10,11... | collective-permute-start | bytes 4497416 | tf_op jit(solution)/shard_map/ppermute | solution.py:632
  43.1 33.7 %collective-permute-start.2 = (bf16[976,768]{1,0:T(8,128)(2,1)S(1)}, bf16[976,768]{1,0:T(8,128)(2,1)}, u32[]{:S(2)}, u32[]{:S(2)}) collective-permute-start(bf16[976,768]{1,0:T(8,128)(2,1)S(1)} %collective-permute-done.1), channel_id=1, source_target_pairs={{2,0},{3,1},{4,6},{5,7},{10,8},{11,9},{12,14},{13,15},{18,16},{19,... | collective-permute-start | bytes 4497416 | tf_op jit(solution)/shard_map/ppermute | solution.py:632
  47.1 34.1 %collective-permute-start.8 = (bf16[976,768]{1,0:T(8,128)(2,1)}, bf16[976,768]{1,0:T(8,128)(2,1)}, u32[]{:S(2)}, u32[]{:S(2)}) collective-permute-start(bf16[976,768]{1,0:T(8,128)(2,1)} %collective-permute-done.rest_1_.rest_11_.rest_7_), channel_id=1, source_target_pairs={{0,1},{1,0},{2,3},{3,2},{4,5},{5,4},{6,7},{7,6},{8,9},{9,8},{10,11... | collective-permute-start | bytes 4497416 | tf_op jit(solution)/shard_map/ppermute | solution.py:632
  49.0 74.3 %collective-permute-start.4 = (bf16[976,768]{1,0:T(8,128)(2,1)}, bf16[976,768]{1,0:T(8,128)(2,1)S(1)}, u32[]{:S(2)}, u32[]{:S(2)}) collective-permute-start(bf16[976,768]{1,0:T(8,128)(2,1)} %collective-permute-done.3), channel_id=1, source_target_pairs={{2,0},{3,1},{4,6},{5,7},{10,8},{11,9},{12,14},{13,15},{18,16},{19,... | collective-permute-start | bytes 4497416 | tf_op jit(solution)/shard_map/ppermute | solution.py:632
  81.2 42.7 %collective-permute-start.9 = (bf16[976,768]{1,0:T(8,128)(2,1)S(1)}, bf16[976,768]{1,0:T(8,128)(2,1)}, u32[]{:S(2)}, u32[]{:S(2)}) collective-permute-start(bf16[976,768]{1,0:T(8,128)(2,1)S(1)} %broadcast_select_fusion.1.rest_2_.rest_12_.rest_8_), channel_id=1, source_target_pairs={{0,1},{1,0},{2,3},{3,2},{4,5},{5,4},{6,7},{7,6},{8,9},{9,8},{10,11... | collective-permute-start | bytes 4497416 | tf_op jit(solution)/shard_map/ppermute | solution.py:632
  83.2 43.3 %collective-permute-start.16 = (bf16[976,768]{1,0:T(8,128)(2,1)S(1)}, bf16[976,768]{1,0:T(8,128)(2,1)S(1)}, u32[]{:S(2)}, u32[]{:S(2)}) collective-permute-start(bf16[976,768]{1,0:T(8,128)(2,1)S(1)} %copy-done.3), channel_id=1, source_target_pairs={{0,8},{8,0},{16,24},{24,16},{1,9},{9,1},{17,25},{25,17},{2,10},{10... | collective-permute-start | bytes 4497416 | tf_op jit(solution)/shard_map/ppermute | solution.py:586
  84.9 37.7 %collective-permute-start.11 = (bf16[384,768]{1,0:T(8,128)(2,1)S(1)}, bf16[384,768]{1,0:T(8,128)(2,1)S(1)}, u32[]{:S(2)}, u32[]{:S(2)}) collective-permute-start(bf16[384,768]{1,0:T(8,128)(2,1)S(1)} %pad_maximum_fusion.4.rest_8_.rest_18_.rest_14_), channel_id=1, source_target_pairs={{0,2},{1,3},{2,0},{3,1},{4,6},{5,7},{6,4},{7,5},{8,10},{9,11},{10,... | collective-permute-start | bytes 1769480 | tf_op jit(solution)/shard_map/ppermute | solution.py:632
  87.4 35.2 %collective-permute-start.12 = (bf16[384,768]{1,0:T(8,128)(2,1)S(1)}, bf16[384,768]{1,0:T(8,128)(2,1)S(1)}, u32[]{:S(2)}, u32[]{:S(2)}) collective-permute-start(bf16[384,768]{1,0:T(8,128)(2,1)S(1)} %pad_maximum_fusion.4.rest_8_.rest_18_.rest_14_), channel_id=1, source_target_pairs={{2,4},{3,5},{4,2},{5,3},{10,12},{11,13},{12,10},{13,11},{18,20},{1... | collective-permute-start | bytes 1769480 | tf_op jit(solution)/shard_map/ppermute | solution.py:632
  122.6 32.7 %collective-permute-start.17 = (bf16[976,768]{1,0:T(8,128)(2,1)}, bf16[976,768]{1,0:T(8,128)(2,1)S(1)}, u32[]{:S(2)}, u32[]{:S(2)}) collective-permute-start(bf16[976,768]{1,0:T(8,128)(2,1)} %collective-permute-done.rest_1_.rest_11_.rest_7_), channel_id=1, source_target_pairs={{0,8},{8,0},{16,24},{24,16},{1,9},{9,1},{17,25},{25,17},{2,10},{10... | collective-permute-start | bytes 4497416 | tf_op jit(solution)/shard_map/ppermute | solution.py:586
  123.3 33.4 %collective-permute-start.20 = (bf16[976,768]{1,0:T(8,128)(2,1)}, bf16[976,768]{1,0:T(8,128)(2,1)S(1)}, u32[]{:S(2)}, u32[]{:S(2)}) collective-permute-start(bf16[976,768]{1,0:T(8,128)(2,1)} %collective-permute-done.6.rest_4_.rest_14_.rest_10_), channel_id=1, source_target_pairs={{0,8},{8,0},{16,24},{24,16},{1,9},{9,1},{17,25},{25,17},{2,10},{10... | collective-permute-start | bytes 4497416 | tf_op jit(solution)/shard_map/ppermute | solution.py:586
  123.9 17.4 %collective-permute-start.13 = (bf16[384,768]{1,0:T(8,128)(2,1)S(1)}, bf16[384,768]{1,0:T(8,128)(2,1)S(1)}, u32[]{:S(2)}, u32[]{:S(2)}) collective-permute-start(bf16[384,768]{1,0:T(8,128)(2,1)S(1)} %collective-permute-done.12), channel_id=1, source_target_pairs={{2,0},{3,1},{4,6},{5,7},{10,8},{11,9},{12,14},{13,15},{18,16},{19,... | collective-permute-start | bytes 1769480 | tf_op jit(solution)/shard_map/ppermute | solution.py:632
  126.5 35.1 %collective-permute-start.10 = (bf16[976,768]{1,0:T(8,128)(2,1)}, bf16[976,768]{1,0:T(8,128)(2,1)}, u32[]{:S(2)}, u32[]{:S(2)}) collective-permute-start(bf16[976,768]{1,0:T(8,128)(2,1)} %broadcast_select_fusion.rest_3_.rest_13_.rest_9_), channel_id=1, source_target_pairs={{0,1},{1,0},{2,3},{3,2},{4,5},{5,4},{6,7},{7,6},{8,9},{9,8},{10,11... | collective-permute-start | bytes 4497416 | tf_op jit(solution)/shard_map/ppermute | solution.py:632
  128.0 26.5 %collective-permute-start.15 = (bf16[384,768]{1,0:T(8,128)(2,1)S(1)}, bf16[384,768]{1,0:T(8,128)(2,1)S(1)}, u32[]{:S(2)}, u32[]{:S(2)}) collective-permute-start(bf16[384,768]{1,0:T(8,128)(2,1)S(1)} %collective-permute-done.14), channel_id=1, source_target_pairs={{2,0},{3,1},{4,6},{5,7},{10,8},{11,9},{12,14},{13,15},{18,16},{19,... | collective-permute-start | bytes 1769480 | tf_op jit(solution)/shard_map/ppermute | solution.py:632
  141.3 13.4 %collective-permute-start.24 = (bf16[384,768]{1,0:T(8,128)(2,1)S(1)}, bf16[384,768]{1,0:T(8,128)(2,1)S(1)}, u32[]{:S(2)}, u32[]{:S(2)}) collective-permute-start(bf16[384,768]{1,0:T(8,128)(2,1)S(1)} %pad_maximum_fusion.4.rest_8_.rest_18_.rest_14_), channel_id=1, source_target_pairs={{0,8},{8,0},{16,24},{24,16},{1,9},{9,1},{17,25},{25,17},{2,10},{10... | collective-permute-start | bytes 1769480 | tf_op jit(solution)/shard_map/ppermute | solution.py:586
  158.5 8.7 %collective-permute-start.22 = (bf16[976,768]{1,0:T(8,128)(2,1)}, bf16[976,768]{1,0:T(8,128)(2,1)}, u32[]{:S(2)}, u32[]{:S(2)}) collective-permute-start(bf16[976,768]{1,0:T(8,128)(2,1)} %collective-permute-done.9.rest_6_.rest_16_.rest_12_), channel_id=1, source_target_pairs={{0,8},{8,0},{16,24},{24,16},{1,9},{9,1},{17,25},{25,17},{2,10},{10... | collective-permute-start | bytes 4497416 | tf_op jit(solution)/shard_map/ppermute | solution.py:586
  161.6 7.7 %collective-permute-start.23 = (bf16[976,768]{1,0:T(8,128)(2,1)}, bf16[976,768]{1,0:T(8,128)(2,1)}, u32[]{:S(2)}, u32[]{:S(2)}) collective-permute-start(bf16[976,768]{1,0:T(8,128)(2,1)} %collective-permute-done.10.rest_7_.rest_17_.rest_13_), channel_id=1, source_target_pairs={{0,8},{8,0},{16,24},{24,16},{1,9},{9,1},{17,25},{25,17},{2,10},{10... | collective-permute-start | bytes 4497416 | tf_op jit(solution)/shard_map/ppermute | solution.py:586
  192.9 13.5 %collective-permute-start.28 = (bf16[288,768]{1,0:T(8,128)(2,1)}, bf16[288,768]{1,0:T(8,128)(2,1)S(1)}, u32[]{:S(2)}, u32[]{:S(2)}) collective-permute-start(bf16[288,768]{1,0:T(8,128)(2,1)} %get-tuple-element.101), channel_id=1, source_target_pairs={{0,16},{8,24},{1,17},{9,25},{2,18},{10,26},{3,19},{11,27},{4,20},{... | collective-permute-start | bytes 1327112 | tf_op jit(solution)/shard_map/ppermute | solution.py:581
  267.8 13.6 %collective-permute-start.29 = (bf16[288,768]{1,0:T(8,128)(2,1)}, bf16[288,768]{1,0:T(8,128)(2,1)S(1)}, u32[]{:S(2)}, u32[]{:S(2)}) collective-permute-start(bf16[288,768]{1,0:T(8,128)(2,1)} %backward_layers.3), channel_id=1, source_target_pairs={{16,0},{24,8},{17,1},{25,9},{18,2},{26,10},{19,3},{27,11},{20,4},{... | collective-permute-start | bytes 1327112 | tf_op jit(solution)/shard_map/ppermute | solution.py:581
  269.1 53.6 %collective-permute-start.30 = (bf16[288,4608]{1,0:T(8,128)(2,1)}, bf16[288,4608]{1,0:T(8,128)(2,1)}, u32[]{:S(2)}, u32[]{:S(2)}) collective-permute-start(bf16[288,4608]{1,0:T(8,128)(2,1)} %get-tuple-element.117), channel_id=1, source_target_pairs={{0,8},{8,0},{16,24},{24,16},{1,9},{9,1},{17,25},{25,17},{2,10},{10... | collective-permute-start | bytes 7962632 | tf_op jit(solution)/shard_map/ppermute | solution.py:586
  269.2 69.6 %collective-permute-start.32 = (bf16[288,4608]{1,0:T(8,128)(2,1)}, bf16[288,4608]{1,0:T(8,128)(2,1)}, u32[]{:S(2)}, u32[]{:S(2)}) collective-permute-start(bf16[288,4608]{1,0:T(8,128)(2,1)} %get-tuple-element.123), channel_id=1, source_target_pairs={{0,8},{8,0},{16,24},{24,16},{1,9},{9,1},{17,25},{25,17},{2,10},{10... | collective-permute-start | bytes 7962632 | tf_op jit(solution)/shard_map/ppermute | solution.py:586
  302.2 20.5 %collective-permute-start.31 = (bf16[288,4608]{1,0:T(8,128)(2,1)}, bf16[288,4608]{1,0:T(8,128)(2,1)S(1)}, u32[]{:S(2)}, u32[]{:S(2)}) collective-permute-start(bf16[288,4608]{1,0:T(8,128)(2,1)} %get-tuple-element.118), channel_id=1, source_target_pairs={{0,8},{8,0},{16,24},{24,16},{1,9},{9,1},{17,25},{25,17},{2,10},{10... | collective-permute-start | bytes 7962632 | tf_op jit(solution)/shard_map/ppermute | solution.py:586
  322.1 16.7 %collective-permute-start.33 = (bf16[288,4608]{1,0:T(8,128)(2,1)}, bf16[288,4608]{1,0:T(8,128)(2,1)}, u32[]{:S(2)}, u32[]{:S(2)}) collective-permute-start(bf16[288,4608]{1,0:T(8,128)(2,1)} %get-tuple-element.124), channel_id=1, source_target_pairs={{0,8},{8,0},{16,24},{24,16},{1,9},{9,1},{17,25},{25,17},{2,10},{10... | collective-permute-start | bytes 7962632 | tf_op jit(solution)/shard_map/ppermute | solution.py:586
  337.4 16.3 %collective-permute-start.46 = (bf16[400,768]{1,0:T(8,128)(2,1)}, bf16[400,768]{1,0:T(8,128)(2,1)S(1)}, u32[]{:S(2)}, u32[]{:S(2)}) collective-permute-start(bf16[400,768]{1,0:T(8,128)(2,1)} %get-tuple-element.152), channel_id=1, source_target_pairs={{0,1},{1,0},{2,3},{3,2},{4,5},{5,4},{6,7},{7,6},{8,9},{9,8},{10,11... | collective-permute-start | bytes 1843208 | tf_op jit(solution)/shard_map/ppermute | solution.py:632
  352.0 23.3 %collective-permute-start.34 = (bf16[592,768]{1,0:T(8,128)(2,1)}, bf16[592,768]{1,0:T(8,128)(2,1)S(1)}, u32[]{:S(2)}, u32[]{:S(2)}) collective-permute-start(bf16[592,768]{1,0:T(8,128)(2,1)} %get-tuple-element.133), channel_id=1, source_target_pairs={{0,1},{1,0},{2,3},{3,2},{4,5},{5,4},{6,7},{7,6},{8,9},{9,8},{10,11... | collective-permute-start | bytes 2727944 | tf_op jit(solution)/shard_map/ppermute | solution.py:632
  353.1 8.7 %collective-permute-start.37 = (bf16[280,2,192]{2,0,1:T(8,128)(2,1)S(1)}, bf16[280,2,192]{2,0,1:T(8,128)(2,1)S(1)}, u32[]{:S(2)}, u32[]{:S(2)}) collective-permute-start(bf16[280,2,192]{2,0,1:T(8,128)(2,1)S(1)} %bitcast.48), channel_id=1, source_target_pairs={{0,16},{8,24},{16,0},{24,8},{1,17},{9,25},{17,1},{25,9},{2,18},{10... | collective-permute-start | bytes 645128 | tf_op jit(solution)/shard_map/ppermute | solution.py:586
  354.0 37.8 %collective-permute-start.53 = (bf16[784,768]{1,0:T(8,128)(2,1)S(1)}, bf16[784,768]{1,0:T(8,128)(2,1)S(1)}, u32[]{:S(2)}, u32[]{:S(2)}) collective-permute-start(bf16[784,768]{1,0:T(8,128)(2,1)S(1)} %pad_maximum_fusion.2), channel_id=1, source_target_pairs={{0,2},{1,3},{6,4},{7,5},{8,10},{9,11},{14,12},{15,13},{16,18},{17,... | collective-permute-start | bytes 3612680 | tf_op jit(solution)/shard_map/ppermute | solution.py:632
  362.0 16.1 %collective-permute-start.38 = (bf16[2,280,192]{2,1,0:T(8,128)(2,1)S(1)}, bf16[2,280,192]{2,1,0:T(8,128)(2,1)S(1)}, u32[]{:S(2)}, u32[]{:S(2)}) collective-permute-start(bf16[2,280,192]{2,1,0:T(8,128)(2,1)S(1)} %fusion.1), channel_id=1, source_target_pairs={{0,8},{8,0},{16,24},{24,16},{1,9},{9,1},{17,25},{25,17},{2,10},{10... | collective-permute-start | bytes 645128 | tf_op jit(solution)/shard_map/ppermute | solution.py:586
  362.1 26.4 %collective-permute-start.47 = (bf16[400,768]{1,0:T(8,128)(2,1)S(1)}, bf16[400,768]{1,0:T(8,128)(2,1)S(1)}, u32[]{:S(2)}, u32[]{:S(2)}) collective-permute-start(bf16[400,768]{1,0:T(8,128)(2,1)S(1)} %copy-done.42), channel_id=1, source_target_pairs={{0,1},{1,0},{2,3},{3,2},{4,5},{5,4},{6,7},{7,6},{8,9},{9,8},{10,11... | collective-permute-start | bytes 1843208 | tf_op jit(solution)/shard_map/ppermute | solution.py:632
  375.6 27.2 %collective-permute-start.36 = (bf16[592,768]{1,0:T(8,128)(2,1)S(1)}, bf16[592,768]{1,0:T(8,128)(2,1)S(1)}, u32[]{:S(2)}, u32[]{:S(2)}) collective-permute-start(bf16[592,768]{1,0:T(8,128)(2,1)S(1)} %add_convert_fusion.10), channel_id=1, source_target_pairs={{0,2},{1,3},{6,4},{7,5},{8,10},{9,11},{14,12},{15,13},{16,18},{17,... | collective-permute-start | bytes 2727944 | tf_op jit(solution)/shard_map/ppermute | solution.py:632
  378.3 29.7 %collective-permute-start.35 = (bf16[592,768]{1,0:T(8,128)(2,1)S(1)}, bf16[592,768]{1,0:T(8,128)(2,1)S(1)}, u32[]{:S(2)}, u32[]{:S(2)}) collective-permute-start(bf16[592,768]{1,0:T(8,128)(2,1)S(1)} %copy-done.39), channel_id=1, source_target_pairs={{0,1},{1,0},{2,3},{3,2},{4,5},{5,4},{6,7},{7,6},{8,9},{9,8},{10,11... | collective-permute-start | bytes 2727944 | tf_op jit(solution)/shard_map/ppermute | solution.py:632
  388.5 32.6 %collective-permute-start.48 = (bf16[400,768]{1,0:T(8,128)(2,1)S(1)}, bf16[400,768]{1,0:T(8,128)(2,1)S(1)}, u32[]{:S(2)}, u32[]{:S(2)}) collective-permute-start(bf16[400,768]{1,0:T(8,128)(2,1)S(1)} %copy-done.41), channel_id=1, source_target_pairs={{0,1},{1,0},{2,3},{3,2},{4,5},{5,4},{6,7},{7,6},{8,9},{9,8},{10,11... | collective-permute-start | bytes 1843208 | tf_op jit(solution)/shard_map/ppermute | solution.py:632
  389.3 39.3 %collective-permute-start.51 = (bf16[784,768]{1,0:T(8,128)(2,1)S(1)}, bf16[784,768]{1,0:T(8,128)(2,1)S(1)}, u32[]{:S(2)}, u32[]{:S(2)}) collective-permute-start(bf16[784,768]{1,0:T(8,128)(2,1)S(1)} %pad_maximum_fusion.1), channel_id=1, source_target_pairs={{0,2},{1,3},{6,4},{7,5},{8,10},{9,11},{14,12},{15,13},{16,18},{17,... | collective-permute-start | bytes 3612680 | tf_op jit(solution)/shard_map/ppermute | solution.py:632
  392.1 41.3 %collective-permute-start.54 = (bf16[784,768]{1,0:T(8,128)(2,1)S(1)}, bf16[784,768]{1,0:T(8,128)(2,1)S(1)}, u32[]{:S(2)}, u32[]{:S(2)}) collective-permute-start(bf16[784,768]{1,0:T(8,128)(2,1)S(1)} %add_convert_fusion.2), channel_id=1, source_target_pairs={{2,4},{3,5},{4,2},{5,3},{10,12},{11,13},{12,10},{13,11},{18,20},{1... | collective-permute-start | bytes 3612680 | tf_op jit(solution)/shard_map/ppermute | solution.py:632
  408.2 39.9 %collective-permute-start.41 = (bf16[592,768]{1,0:T(8,128)(2,1)S(1)}, bf16[592,768]{1,0:T(8,128)(2,1)S(1)}, u32[]{:S(2)}, u32[]{:S(2)}) collective-permute-start(bf16[592,768]{1,0:T(8,128)(2,1)S(1)} %add_convert_fusion.9), channel_id=1, source_target_pairs={{0,2},{1,3},{6,4},{7,5},{8,10},{9,11},{14,12},{15,13},{16,18},{17,... | collective-permute-start | bytes 2727944 | tf_op jit(solution)/shard_map/ppermute | solution.py:632
  410.7 38.7 %collective-permute-start.40 = (bf16[592,768]{1,0:T(8,128)(2,1)S(1)}, bf16[592,768]{1,0:T(8,128)(2,1)S(1)}, u32[]{:S(2)}, u32[]{:S(2)}) collective-permute-start(bf16[592,768]{1,0:T(8,128)(2,1)S(1)} %copy-done.38), channel_id=1, source_target_pairs={{0,1},{1,0},{2,3},{3,2},{4,5},{5,4},{6,7},{7,6},{8,9},{9,8},{10,11... | collective-permute-start | bytes 2727944 | tf_op jit(solution)/shard_map/ppermute | solution.py:632
  421.1 30.0 %collective-permute-start.42 = (bf16[592,768]{1,0:T(8,128)(2,1)S(1)}, bf16[592,768]{1,0:T(8,128)(2,1)S(1)}, u32[]{:S(2)}, u32[]{:S(2)}) collective-permute-start(bf16[592,768]{1,0:T(8,128)(2,1)S(1)} %add_convert_fusion.8), channel_id=1, source_target_pairs={{2,4},{3,5},{4,2},{5,3},{10,12},{11,13},{12,10},{13,11},{18,20},{1... | collective-permute-start | bytes 2727944 | tf_op jit(solution)/shard_map/ppermute | solution.py:632
  428.6 45.3 %collective-permute-start.50 = (bf16[784,768]{1,0:T(8,128)(2,1)S(1)}, bf16[784,768]{1,0:T(8,128)(2,1)S(1)}, u32[]{:S(2)}, u32[]{:S(2)}) collective-permute-start(bf16[784,768]{1,0:T(8,128)(2,1)S(1)} %pad_maximum_fusion), channel_id=1, source_target_pairs={{0,2},{1,3},{6,4},{7,5},{8,10},{9,11},{14,12},{15,13},{16,18},{17,... | collective-permute-start | bytes 3612680 | tf_op jit(solution)/shard_map/ppermute | solution.py:632
  433.5 41.2 %collective-permute-start.52 = (bf16[784,768]{1,0:T(8,128)(2,1)S(1)}, bf16[784,768]{1,0:T(8,128)(2,1)S(1)}, u32[]{:S(2)}, u32[]{:S(2)}) collective-permute-start(bf16[784,768]{1,0:T(8,128)(2,1)S(1)} %add_convert_fusion.3), channel_id=1, source_target_pairs={{2,4},{3,5},{4,2},{5,3},{10,12},{11,13},{12,10},{13,11},{18,20},{1... | collective-permute-start | bytes 3612680 | tf_op jit(solution)/shard_map/ppermute | solution.py:632
  448.1 28.0 %collective-permute-start.55 = (bf16[784,768]{1,0:T(8,128)(2,1)S(1)}, bf16[784,768]{1,0:T(8,128)(2,1)S(1)}, u32[]{:S(2)}, u32[]{:S(2)}) collective-permute-start(bf16[784,768]{1,0:T(8,128)(2,1)S(1)} %add_convert_fusion.1), channel_id=1, source_target_pairs={{2,0},{3,1},{4,6},{5,7},{10,8},{11,9},{12,14},{13,15},{18,16},{19,... | collective-permute-start | bytes 3612680 | tf_op jit(solution)/shard_map/ppermute | solution.py:632
  449.4 16.9 %collective-permute-start.49 = (bf16[400,768]{1,0:T(8,128)(2,1)S(1)}, bf16[400,768]{1,0:T(8,128)(2,1)S(1)}, u32[]{:S(2)}, u32[]{:S(2)}) collective-permute-start(bf16[400,768]{1,0:T(8,128)(2,1)S(1)} %copy-done.40), channel_id=1, source_target_pairs={{0,1},{1,0},{2,3},{3,2},{4,5},{5,4},{6,7},{7,6},{8,9},{9,8},{10,11... | collective-permute-start | bytes 1843208 | tf_op jit(solution)/shard_map/ppermute | solution.py:632
  451.2 33.7 %collective-permute-start.39 = (bf16[592,768]{1,0:T(8,128)(2,1)S(1)}, bf16[592,768]{1,0:T(8,128)(2,1)S(1)}, u32[]{:S(2)}, u32[]{:S(2)}) collective-permute-start(bf16[592,768]{1,0:T(8,128)(2,1)S(1)} %copy-done.37), channel_id=1, source_target_pairs={{0,1},{1,0},{2,3},{3,2},{4,5},{5,4},{6,7},{7,6},{8,9},{9,8},{10,11... | collective-permute-start | bytes 2727944 | tf_op jit(solution)/shard_map/ppermute | solution.py:632
  466.3 25.6 %collective-permute-start.43 = (bf16[592,768]{1,0:T(8,128)(2,1)S(1)}, bf16[592,768]{1,0:T(8,128)(2,1)S(1)}, u32[]{:S(2)}, u32[]{:S(2)}) collective-permute-start(bf16[592,768]{1,0:T(8,128)(2,1)S(1)} %get-tuple-element.145), channel_id=1, source_target_pairs={{0,2},{1,3},{6,4},{7,5},{8,10},{9,11},{14,12},{15,13},{16,18},{17,... | collective-permute-start | bytes 2727944 | tf_op jit(solution)/shard_map/ppermute | solution.py:632
  473.9 17.9 %collective-permute-start.44 = (bf16[592,768]{1,0:T(8,128)(2,1)S(1)}, bf16[592,768]{1,0:T(8,128)(2,1)S(1)}, u32[]{:S(2)}, u32[]{:S(2)}) collective-permute-start(bf16[592,768]{1,0:T(8,128)(2,1)S(1)} %add_convert_fusion.6), channel_id=1, source_target_pairs={{2,4},{3,5},{4,2},{5,3},{10,12},{11,13},{12,10},{13,11},{18,20},{1... | collective-permute-start | bytes 2727944 | tf_op jit(solution)/shard_map/ppermute | solution.py:632
  474.6 24.7 %collective-permute-start.45 = (bf16[592,768]{1,0:T(8,128)(2,1)S(1)}, bf16[592,768]{1,0:T(8,128)(2,1)S(1)}, u32[]{:S(2)}, u32[]{:S(2)}) collective-permute-start(bf16[592,768]{1,0:T(8,128)(2,1)S(1)} %get-tuple-element.147), channel_id=1, source_target_pairs={{2,0},{3,1},{4,6},{5,7},{10,8},{11,9},{12,14},{13,15},{18,16},{19,... | collective-permute-start | bytes 2727944 | tf_op jit(solution)/shard_map/ppermute | solution.py:632
  476.9 24.4 %collective-permute-start.56 = (bf16[192,768]{1,0:T(8,128)(2,1)S(1)}, bf16[192,768]{1,0:T(8,128)(2,1)S(1)}, u32[]{:S(2)}, u32[]{:S(2)}) collective-permute-start(bf16[192,768]{1,0:T(8,128)(2,1)S(1)} %slice.32), channel_id=1, source_target_pairs={{0,1},{1,0},{2,3},{3,2},{4,5},{5,4},{6,7},{7,6},{8,9},{9,8},{10,11... | collective-permute-start | bytes 884744 | tf_op jit(solution)/shard_map/ppermute | solution.py:632
  (56 other events, 892.2 us)

commit v6 on v5

--- a/solution.py
+++ b/solution.py
@@ -201,10 +201,9 @@
         if save:
             act[:, cols] = a
             gp[:, cols] = (phi + h * jnp.exp(-0.5 * h * h) * 0.3989422804014327).astype(BF)
+            hand_on(act.at[:, pl.ds(b * D, D)], False, b * D)
+            flush(gp.at[:, pl.ds(b * D, D)], gp_hbm.at[:, pl.ds(b * D, D)])
         acc = acc + dot(a, square(wd[b]))
-    if save:
-        hand_on(act, False, 0)
-        flush(gp, gp_hbm)
     return acc.astype(BF)
 
 
@@ -248,7 +247,7 @@
         out_shape=shapes,
         in_specs=[VM, VM, VM] + [ANYS] * (2 * len(wa)),
         out_specs=specs,
-        scratch_shapes=weight_scratch(len(wa)) * 2 + work * 2 + [pltpu.SemaphoreType.DMA((14,))],
+        scratch_shapes=weight_scratch(len(wa)) * 2 + work * 2 + [pltpu.SemaphoreType.DMA((32,))],
         compiler_params=pltpu.CompilerParams(vmem_limit_bytes=VMEM_LIMIT),
         cost_estimate=pl.CostEstimate(flops=2 * ROWS * D * D * 26, bytes_accessed=48 * D * D + 2**23, transcendentals=0),
         name="forward_stage",
@@ -645,12 +644,11 @@
         return self.send(value, ("x",), ("section", "dp"), [(i, i ^ 1) for i in places])
 
 
-def gather_blocks(own, pair, middle):
+def gather_blocks(own, pair, middle, others):
     net = Links(x=1, z=9)
     one, mid = net.along(own, PAIR), net.along(own, MID)
-    first = net.across(pair, 0)
     sent = [net.across(own)]
-    first = first + net.across(pair, 1)
+    first = net.across(pair)
     both = jnp.concatenate([pair, first])
     far, back = net.along(mid, OUT), net.along(one, MID)
     sent.append(net.across(one))
@@ -658,13 +656,15 @@
     last = net.along(back, OUT)
     third = jnp.where(middle, mid, far)
     sent.append(net.across(third))
-    both_far, both_back = net.along(both_mid, OUT), net.along(both_one, MID)
     fourth = jnp.where(middle, back, last)
     sent.append(net.across(fourth))
+    both_one, both_mid, fourth = lax.optimization_barrier((both_one, both_mid, fourth))
+    both_far, both_back = net.along(both_mid, OUT), net.along(both_one, MID)
     both_last = net.along(both_back, OUT)
+    third, *others = lax.optimization_barrier((third, *others))
     mine = [own, one, third, fourth] + sent
     mine += [both, both_one, jnp.where(middle, both_mid, both_far), jnp.where(middle, both_back, both_last)]
-    return mine, [swapped(b) for b in mine]
+    return mine, [swapped(b) for b in mine], others
 
 
 def add(*terms):
@@ -722,10 +722,22 @@
     spot = lax.axis_index("dp")
     z = spot // 2
     middle = (z == 1) | (z == 2)
+    def own_pair(a):
+        return lax.dynamic_index_in_dim(a, core, 0, False)
+
+    def padded(a):
+        return jnp.pad(a, ((0, ROWS - seq), (0, 0)))
+
+    places = lax.broadcasted_iota(jnp.int32, (8, ROWS), 1)
+    mask = (((places < own_pair(lengths)) | (places >= CAPTION)) & (places < seq)).astype(F32)
+    own_tokens = padded(own_pair(tokens))
+    own_cotangent = padded(own_pair(cotangent))
+
     if lined:
         packed, pair = pack(joint_weight[0], output_weight[0], up_weight[0], down_weight[0], attend_gain, attend_shift,
                             joint_bias, output_bias, feed_gain, feed_shift, down_bias, up_bias)
-        wa, wb = gather_blocks(packed, pair, middle)
+        wa, wb, others = gather_blocks(packed, pair, middle, (own_tokens, own_cotangent, mask))
+        own_tokens, own_cotangent, mask = others
     else:
         tail = vector_tail(n, spot, attend_gain[0], attend_shift[0], joint_bias[0], output_bias[0], feed_gain[0],
                            feed_shift[0], down_bias[0], up_bias[0])
@@ -733,17 +745,6 @@
         gathered = lax.all_gather(packed, "dp")
         tails = lax.psum(tail.astype(BF).astype(F32), "dp")
         wa, wb = kernel_form(n, gathered, tails), kernel_form(n, swapped(gathered), swapped(tails))
-
-    def own_pair(a):
-        return lax.dynamic_index_in_dim(a, core, 0, False)
-
-    def padded(a):
-        return jnp.pad(a, ((0, ROWS - seq), (0, 0)))
-
-    places = lax.broadcasted_iota(jnp.int32, (8, ROWS), 1)
-    mask = (((places < own_pair(lengths)) | (places >= CAPTION)) & (places < seq)).astype(F32)
-    own_tokens = padded(own_pair(tokens))
-    own_cotangent = padded(own_pair(cotangent))
 
     came = own_tokens
     for _ in range(stages - 1):

time: 518 us -> 512 us (0.988)
  waiting for transfers between devices: 259 us -> 253 us
    ppermute x37 -> x36, waiting for transfers between devices: 225 us -> 220 us  [send(): got = lax.ppermute(value, axis, pairs)]
    ppermute x37 -> x36, starting transfers between devices: 60.5 us -> 61.3 us  [send(): got = lax.ppermute(value, axis, pairs)]
  transfers between devices with their start and end apart: 59 -> 58, of which waited for: 30 -> 30; matrix products, arithmetic and copies ran while one was open for 3% -> 3% of each run, Pallas kernels for 13% -> 13%
where the time goes in v6:
time: 512 us; the launch traced here: 507 us
  waiting for transfers between devices  253 us (49%)
  Pallas kernels  158 us (31%)
  starting transfers between devices  73.7 us (14%)
  local copies, waits for them, and re-layouts  10.6 us (2%)
  other arithmetic  9.99 us (2%)
    ppermute x36, waiting for transfers between devices, send(): got = lax.ppermute(value, axis, pairs)  220 us
    pallas_call x3, Pallas kernels, backward_layers(): pl.pallas_call(functools.partial(backward_kernel, save, layers, len(wa)),...  74.2 us
    ppermute x36, starting transfers between devices, send(): got = lax.ppermute(value, axis, pairs)  61.3 us
    pallas_call x2, Pallas kernels, forward_stage(): pl.pallas_call(functools.partial(forward_kernel, save, len(wa)), out_shap...  48.6 us
    pallas_call x2, Pallas kernels, weight_products(): pl.pallas_call(functools.partial(product_kernel, n, direct), out_shape=sh...  25.7 us
    ppermute x2, waiting for transfers between devices, moved(): lax.ppermute(value, axis, [(i, i + by) for i in range(peers) if 0 <= i +...  21.6 us
    ppermute x18, waiting for transfers between devices, flipped(): return lax.ppermute(value, 'section', [(i, i ^ bit) for i in range(peers)])  10.3 us
  transfers between devices with their start and end apart: 58, of which 30 were waited for; matrix products, arithmetic and copies ran while one was open for 3% of the time, Pallas kernels for 13%

profile of v6, /device:TPU:0, one launch (start us, length us, event | category | flops | bytes accessed | tf_op | source)
XLA Modules:
  0.0 507.4 jit_solution(13225089062021673592)
XLA Ops:
  0.6 3.7 pack.1
  4.3 3.0 collective-permute-start.2
  9.7 30.8 %collective-permute-done.2.rest_1_.rest_11_.rest_7_ = bf16[976,768]{1,0:T(8,128)(2,1)} collective-permute-done((bf16[976,768]{1,0:T(8,128)(2,1)}, bf16[976,768]{1,0:T(8,128)(2,1)}, u32[]{:S(2)}, u32[]{:S(2)}) %collective-permute-start.2) | collective-permute-done | bytes 1499168 | tf_op jit(solution)/shard_map/ppermute | solution.py:631
  40.5 1.8 collective-permute-start.7
  43.6 1.7 collective-permute-start.4
  45.3 6.7 %collective-permute-done.4 = bf16[192,768]{1,0:T(8,128)(2,1)S(1)} collective-permute-done((bf16[192,768]{1,0:T(8,128)(2,1)}, bf16[192,768]{1,0:T(8,128)(2,1)S(1)}, u32[]{:S(2)}, u32[]{:S(2)}) %collective-permute-start.4) | collective-permute-done | bytes 294944 | tf_op jit(solution)/shard_map/ppermute | solution.py:631
  54.7 24.2 %collective-permute-done.1 = bf16[976,768]{1,0:T(8,128)(2,1)} collective-permute-done((bf16[976,768]{1,0:T(8,128)(2,1)S(1)}, bf16[976,768]{1,0:T(8,128)(2,1)}, u32[]{:S(2)}, u32[]{:S(2)}) %collective-permute-start.1) | collective-permute-done | bytes 1499168 | tf_op jit(solution)/shard_map/ppermute | solution.py:631
  80.4 5.0 collective-permute-done.9.rest_5_.rest_15_.rest_11_
  88.4 4.2 collective-permute-start.5
  92.6 20.8 %collective-permute-done.8 = bf16[976,768]{1,0:T(8,128)(2,1)} collective-permute-done((bf16[976,768]{1,0:T(8,128)(2,1)}, bf16[976,768]{1,0:T(8,128)(2,1)}, u32[]{:S(2)}, u32[]{:S(2)}) %collective-permute-start.8) | collective-permute-done | bytes 1499168 | tf_op jit(solution)/shard_map/ppermute | solution.py:631
  118.8 1.6 broadcast_select_fusion.rest_3_.rest_13_.rest_9_
  120.5 3.0 collective-permute-done.5.rest_9_.rest_19_.rest_15_
  125.0 2.2 collective-permute-done.23.rest_20_.rest_30_.rest_26_
  131.3 16.1 %collective-permute-done.12 = bf16[384,768]{1,0:T(8,128)(2,1)S(1)} collective-permute-done((bf16[384,768]{1,0:T(8,128)(2,1)S(1)}, bf16[384,768]{1,0:T(8,128)(2,1)S(1)}, u32[]{:S(2)}, u32[]{:S(2)}) %collective-permute-start.12) | collective-permute-done | bytes 589856 | tf_op jit(solution)/shard_map/ppermute | solution.py:631
  147.4 8.5 %collective-permute-done.11.rest_7_.rest_17_.rest_13_ = bf16[976,768]{1,0:T(8,128)(2,1)S(1)} collective-permute-done((bf16[976,768]{1,0:T(8,128)(2,1)S(1)}, bf16[976,768]{1,0:T(8,128)(2,1)S(1)}, u32[]{:S(2)}, u32[]{:S(2)}) %collective-permute-start.11) | collective-permute-done | bytes 1499168 | tf_op jit(solution)/shard_map/ppermute | solution.py:631
  155.9 4.1 collective-permute-done.14
  165.0 23.0 %forward_stage.2 = (bf16[288,768]{1,0:T(8,128)(2,1)}, bf16[288,768]{1,0:T(8,128)(2,1)}) custom-call(bf16[288,768]{1,0:T(8,128)(2,1)} %pad.7.x_ref.came_ref, bf16[288,768]{1,0:T(8,128)(2,1)} %pad.7.x_ref.came_ref, f32[8,288]{1,0:T(8,128)} %iota.13.mask_ref.rest_5_, bf16[976,768]{1,0:T(8,128)(2,1)} %get-tuple-element.100.rest_0_.rest_10_.rest_6_, ...), custom_call_target="tpu_custom_call" | custom-call | flops 8833204224 | bytes 36700160 | tf_op jit(solution)/shard_map/forward_stage/pallas_call | solution.py:245
  188.0 3.5 collective-permute-start.27
  191.5 10.0 %collective-permute-done.27.came_ref = bf16[288,768]{1,0:T(8,128)(2,1)S(1)} collective-permute-done((bf16[288,768]{1,0:T(8,128)(2,1)}, bf16[288,768]{1,0:T(8,128)(2,1)S(1)}, u32[]{:S(2)}, u32[]{:S(2)}) %collective-permute-start.27) | collective-permute-done | bytes 442400 | tf_op jit(solution)/shard_map/ppermute | solution.py:580
  202.3 25.6 %forward_stage.3 = (bf16[288,768]{1,0:T(8,128)(2,1)}, bf16[288,768]{1,0:T(8,128)(2,1)}, f32[288,128]{1,0:T(8,128)}, f32[288,768]{1,0:T(8,128)}, bf16[288,2304]{1...) custom-call(bf16[288,768]{1,0:T(8,128)(2,1)} %pad.7.x_ref.came_ref, ...), custom_call_target="tpu_custom_call" | custom-call | flops 8833204224 | bytes 36700160 | tf_op jit(solution)/shard_map/forward_stage/pallas_call | solution.py:245
  227.9 34.5 %backward_layers.3 = bf16[288,768]{1,0:T(8,128)(2,1)} custom-call(bf16[288,768]{1,0:T(8,128)(2,1)} %pad.8.g_ref, f32[8,288]{1,0:T(8,128)} %iota.13.mask_ref.rest_5_, bf16[288,768]{1,0:T(8,128)(2,1)} %get-tuple-element.114.rest_0_, f32[288,128]{1,0:T(8,128)} %get-tuple-element.115.rest_1_, f32[288,768]{1,0:T(8,128)} %get-tuple-element.116.rest_2_, ...), custom_call_target="tpu_custom_call" | custom-call | flops 9512681472 | bytes 45088768 | tf_op jit(solution)/shard_map/backward_layers/pallas_call | solution.py:377
  264.3 11.6 %collective-permute-done.28 = bf16[288,768]{1,0:T(8,128)(2,1)S(1)} collective-permute-done((bf16[288,768]{1,0:T(8,128)(2,1)}, bf16[288,768]{1,0:T(8,128)(2,1)S(1)}, u32[]{:S(2)}, u32[]{:S(2)}) %collective-permute-start.28) | collective-permute-done | bytes 442400 | tf_op jit(solution)/shard_map/ppermute | solution.py:580
  276.8 19.8 %backward_layers.4 = (bf16[288,768]{1,0:T(8,128)(2,1)}, f32[16,768]{1,0:T(8,128)}, bf16[288,4608]{1,0:T(8,128)(2,1)}, bf16[288,4608]{1,0:T(8,128)(2,1)}) custom-call(bf16[288,768]{1,0:T(8,128)(2,1)} %broadcast_select_fusion.4.g_ref, f32[8,288]{1,0:T(8,128)} %iota.13.mask_ref.rest_5_, bf16[288,768]{1,0:T(8,128)(2,1)} %get-tuple-element.114.rest_0_, ...), custom_call_target="tpu_custom_call" | custom-call | flops 4756340736 | bytes 22544384 | tf_op jit(solution)/shard_map/backward_layers/pallas_call | solution.py:377
  296.7 19.9 %backward_layers.5 = (bf16[288,768]{1,0:T(8,128)(2,1)}, f32[16,768]{1,0:T(8,128)}, bf16[288,4608]{1,0:T(8,128)(2,1)}, bf16[288,4608]{1,0:T(8,128)(2,1)}) custom-call(bf16[288,768]{1,0:T(8,128)(2,1)} %get-tuple-element.124.g_ref, f32[8,288]{1,0:T(8,128)} %iota.13.mask_ref.rest_5_, bf16[288,768]{1,0:T(8,128)(2,1)} %get-tuple-element.119.rest_5_.rest_0_, ...), custom_call_target="tpu_custom_call" | custom-call | flops 4756340736 | bytes 22544384 | tf_op jit(solution)/shard_map/backward_layers/pallas_call | solution.py:377
  317.1 13.1 %weight_products.2 = (bf16[400,768]{1,0:T(8,128)(2,1)}, bf16[400,768]{1,0:T(8,128)(2,1)}, bf16[400,768]{1,0:T(8,128)(2,1)}, bf16[400,768]{1,0:T(8,128)(2,1)}, bf...) custom-call(bf16[288,768]{1,0:T(8,128)(2,1)} %get-tuple-element.148., ...), custom_call_target="tpu_custom_call" | custom-call | flops 4076863488 | bytes 16777216 | tf_op jit(solution)/shard_map/weight_products/pallas_call | solution.py:476
  331.8 12.6 %weight_products.3 = (bf16[592,768]{1,0:T(8,128)(2,1)}, bf16[592,768]{1,0:T(8,128)(2,1)}, bf16[592,768]{1,0:T(8,128)(2,1)}, bf16[592,768]{1,0:T(8,128)(2,1)}, bf...) custom-call(bf16[400,768]{1,0:T(8,128)(2,1)} %get-tuple-element.131.behi, ...), custom_call_target="tpu_custom_call" | custom-call | flops 4076863488 | bytes 16777216 | tf_op jit(solution)/shard_map/weight_products/pallas_call | solution.py:476
  347.0 3.6 collective-permute-start.52
  350.6 4.8 collective-permute-done.36
  357.1 11.5 %collective-permute-done.33 = bf16[592,768]{1,0:T(8,128)(2,1)S(1)} collective-permute-done((bf16[592,768]{1,0:T(8,128)(2,1)S(1)}, bf16[592,768]{1,0:T(8,128)(2,1)S(1)}, u32[]{:S(2)}, u32[]{:S(2)}) %collective-permute-start.33) | collective-permute-done | bytes 909344 | tf_op jit(solution)/shard_map/ppermute | solution.py:631
  368.9 3.6 collective-permute-start.35
  373.3 8.4 %collective-permute-done.46 = bf16[400,768]{1,0:T(8,128)(2,1)S(1)} collective-permute-done((bf16[400,768]{1,0:T(8,128)(2,1)S(1)}, bf16[400,768]{1,0:T(8,128)(2,1)S(1)}, u32[]{:S(2)}, u32[]{:S(2)}) %collective-permute-start.46) | collective-permute-done | bytes 614432 | tf_op jit(solution)/shard_map/ppermute | solution.py:631
  382.6 3.4 collective-permute-start.50
  387.3 9.5 %collective-permute-done.35 = bf16[592,768]{1,0:T(8,128)(2,1)S(1)} collective-permute-done((bf16[592,768]{1,0:T(8,128)(2,1)S(1)}, bf16[592,768]{1,0:T(8,128)(2,1)S(1)}, u32[]{:S(2)}, u32[]{:S(2)}) %collective-permute-start.35) | collective-permute-done | bytes 909344 | tf_op jit(solution)/shard_map/ppermute | solution.py:631
  397.1 4.1 collective-permute-done.34
  401.5 3.6 collective-permute-start.40
  405.7 8.6 %collective-permute-done.47 = bf16[400,768]{1,0:T(8,128)(2,1)S(1)} collective-permute-done((bf16[400,768]{1,0:T(8,128)(2,1)S(1)}, bf16[400,768]{1,0:T(8,128)(2,1)S(1)}, u32[]{:S(2)}, u32[]{:S(2)}) %collective-permute-start.47) | collective-permute-done | bytes 614432 | tf_op jit(solution)/shard_map/ppermute | solution.py:631
  415.4 7.3 %collective-permute-done.50 = bf16[784,768]{1,0:T(8,128)(2,1)S(1)} collective-permute-done((bf16[784,768]{1,0:T(8,128)(2,1)S(1)}, bf16[784,768]{1,0:T(8,128)(2,1)S(1)}, u32[]{:S(2)}, u32[]{:S(2)}) %collective-permute-start.50) | collective-permute-done | bytes 1204256 | tf_op jit(solution)/shard_map/ppermute | solution.py:631
  422.7 4.5 collective-permute-start.49
  428.7 13.4 %collective-permute-done.40 = bf16[592,768]{1,0:T(8,128)(2,1)S(1)} collective-permute-done((bf16[592,768]{1,0:T(8,128)(2,1)S(1)}, bf16[592,768]{1,0:T(8,128)(2,1)S(1)}, u32[]{:S(2)}, u32[]{:S(2)}) %collective-permute-start.40) | collective-permute-done | bytes 909344 | tf_op jit(solution)/shard_map/ppermute | solution.py:631
  443.4 1.6 collective-permute-start.48
  446.3 14.0 %collective-permute-done.48 = bf16[400,768]{1,0:T(8,128)(2,1)S(1)} collective-permute-done((bf16[400,768]{1,0:T(8,128)(2,1)S(1)}, bf16[400,768]{1,0:T(8,128)(2,1)S(1)}, u32[]{:S(2)}, u32[]{:S(2)}) %collective-permute-start.48) | collective-permute-done | bytes 614432 | tf_op jit(solution)/shard_map/ppermute | solution.py:631
  460.3 4.7 collective-permute-start.42
  465.0 3.0 collective-permute-done.49
  472.9 6.9 %collective-permute-done.38 = bf16[592,768]{1,0:T(8,128)(2,1)S(1)} collective-permute-done((bf16[592,768]{1,0:T(8,128)(2,1)S(1)}, bf16[592,768]{1,0:T(8,128)(2,1)S(1)}, u32[]{:S(2)}, u32[]{:S(2)}) %collective-permute-start.38) | collective-permute-done | bytes 909344 | tf_op jit(solution)/shard_map/ppermute | solution.py:631
  479.8 6.8 %collective-permute-done.42 = bf16[592,768]{1,0:T(8,128)(2,1)S(1)} collective-permute-done((bf16[592,768]{1,0:T(8,128)(2,1)S(1)}, bf16[592,768]{1,0:T(8,128)(2,1)S(1)}, u32[]{:S(2)}, u32[]{:S(2)}) %collective-permute-start.42) | collective-permute-done | bytes 909344 | tf_op jit(solution)/shard_map/ppermute | solution.py:631
  486.6 6.9 %collective-permute-done.44 = bf16[592,768]{1,0:T(8,128)(2,1)S(1)} collective-permute-done((bf16[592,768]{1,0:T(8,128)(2,1)S(1)}, bf16[592,768]{1,0:T(8,128)(2,1)S(1)}, u32[]{:S(2)}, u32[]{:S(2)}) %collective-permute-start.44) | collective-permute-done | bytes 909344 | tf_op jit(solution)/shard_map/ppermute | solution.py:631
  495.7 3.1 collective-permute-start.57
  501.8 5.4 %finish.1 = (f32[96,3072]{1,0:T(8,128)}, f32[96,2304]{1,0:T(8,128)}, f32[96,768]{1,0:T(8,128)}, f32[384,768]{1,0:T(8,128)}, f32[1,96]{1,0:T(1,128)}, /*index=5*/...) custom-call(bf16[592,768]{1,0:T(8,128)(2,1)} %copy-done.16, ...), custom_call_target="tpu_custom_call" | custom-call | tf_op jit(solution)/shard_map/finish/pallas_call | solution.py:568
  (211 shorter events, 55.7 us)
Async XLA Ops:
  4.3 36.2 %collective-permute-start.2 = (bf16[976,768]{1,0:T(8,128)(2,1)}, bf16[976,768]{1,0:T(8,128)(2,1)}, u32[]{:S(2)}, u32[]{:S(2)}) collective-permute-start(bf16[976,768]{1,0:T(8,128)(2,1)} %get-tuple-element.100.rest_0_.rest_10_.rest_6_), channel_id=1, source_target_pairs={{0,2},{1,3},{2,0},{3,1},{4,6},{5,7},{6,4},{7,5},{8,10},{9,11},{10,... | collective-permute-start | bytes 4497416 | tf_op jit(solution)/shard_map/ppermute | solution.py:631
  7.4 34.9 %collective-permute-start = (bf16[976,768]{1,0:T(8,128)(2,1)}, bf16[976,768]{1,0:T(8,128)(2,1)S(1)}, u32[]{:S(2)}, u32[]{:S(2)}) collective-permute-start(bf16[976,768]{1,0:T(8,128)(2,1)} %get-tuple-element.100.rest_0_.rest_10_.rest_6_), channel_id=1, source_target_pairs={{2,4},{3,5},{4,2},{5,3},{10,12},{11,13},{12,10},{13,11},{18,20},{1... | collective-permute-start | bytes 4497416 | tf_op jit(solution)/shard_map/ppermute | solution.py:631
  8.1 35.4 %collective-permute-start.3 = (bf16[976,768]{1,0:T(8,128)(2,1)}, bf16[976,768]{1,0:T(8,128)(2,1)}, u32[]{:S(2)}, u32[]{:S(2)}) collective-permute-start(bf16[976,768]{1,0:T(8,128)(2,1)} %get-tuple-element.100.rest_0_.rest_10_.rest_6_), channel_id=1, source_target_pairs={{0,1},{1,0},{2,3},{3,2},{4,5},{5,4},{6,7},{7,6},{8,9},{9,8},{10,11... | collective-permute-start | bytes 4497416 | tf_op jit(solution)/shard_map/ppermute | solution.py:631
  40.5 12.9 %collective-permute-start.7 = (bf16[976,768]{1,0:T(8,128)(2,1)}, bf16[976,768]{1,0:T(8,128)(2,1)}, u32[]{:S(2)}, u32[]{:S(2)}) collective-permute-start(bf16[976,768]{1,0:T(8,128)(2,1)} %collective-permute-done.2.rest_1_.rest_11_.rest_7_), channel_id=1, source_target_pairs={{2,4},{3,5},{4,2},{5,3},{10,12},{11,13},{12,10},{13,11},{18,20},{1... | collective-permute-start | bytes 4497416 | tf_op jit(solution)/shard_map/ppermute | solution.py:631
  42.3 36.6 %collective-permute-start.1 = (bf16[976,768]{1,0:T(8,128)(2,1)S(1)}, bf16[976,768]{1,0:T(8,128)(2,1)}, u32[]{:S(2)}, u32[]{:S(2)}) collective-permute-start(bf16[976,768]{1,0:T(8,128)(2,1)S(1)} %collective-permute-done), channel_id=1, source_target_pairs={{2,0},{3,1},{4,6},{5,7},{10,8},{11,9},{12,14},{13,15},{18,16},{19,... | collective-permute-start | bytes 4497416 | tf_op jit(solution)/shard_map/ppermute | solution.py:631
  52.0 33.4 %collective-permute-start.9 = (bf16[976,768]{1,0:T(8,128)(2,1)}, bf16[976,768]{1,0:T(8,128)(2,1)S(1)}, u32[]{:S(2)}, u32[]{:S(2)}) collective-permute-start(bf16[976,768]{1,0:T(8,128)(2,1)} %collective-permute-done.2.rest_1_.rest_11_.rest_7_), channel_id=1, source_target_pairs={{0,1},{1,0},{2,3},{3,2},{4,5},{5,4},{6,7},{7,6},{8,9},{9,8},{10,11... | collective-permute-start | bytes 4497416 | tf_op jit(solution)/shard_map/ppermute | solution.py:631
  53.4 35.1 %collective-permute-start.15 = (bf16[976,768]{1,0:T(8,128)(2,1)}, bf16[976,768]{1,0:T(8,128)(2,1)}, u32[]{:S(2)}, u32[]{:S(2)}) collective-permute-start(bf16[976,768]{1,0:T(8,128)(2,1)} %get-tuple-element.100.rest_0_.rest_10_.rest_6_), channel_id=1, source_target_pairs={{0,8},{8,0},{16,24},{24,16},{1,9},{9,1},{17,25},{25,17},{2,10},{10... | collective-permute-start | bytes 4497416 | tf_op jit(solution)/shard_map/ppermute | solution.py:585
  53.4 60.0 %collective-permute-start.8 = (bf16[976,768]{1,0:T(8,128)(2,1)}, bf16[976,768]{1,0:T(8,128)(2,1)}, u32[]{:S(2)}, u32[]{:S(2)}) collective-permute-start(bf16[976,768]{1,0:T(8,128)(2,1)} %collective-permute-done.7), channel_id=1, source_target_pairs={{2,0},{3,1},{4,6},{5,7},{10,8},{11,9},{12,14},{13,15},{18,16},{19,... | collective-permute-start | bytes 4497416 | tf_op jit(solution)/shard_map/ppermute | solution.py:631
  85.4 35.0 %collective-permute-start.10 = (bf16[976,768]{1,0:T(8,128)(2,1)S(1)}, bf16[976,768]{1,0:T(8,128)(2,1)}, u32[]{:S(2)}, u32[]{:S(2)}) collective-permute-start(bf16[976,768]{1,0:T(8,128)(2,1)S(1)} %broadcast_select_fusion.1.rest_2_.rest_12_.rest_8_), channel_id=1, source_target_pairs={{0,1},{1,0},{2,3},{3,2},{4,5},{5,4},{6,7},{7,6},{8,9},{9,8},{10,11... | collective-permute-start | bytes 4497416 | tf_op jit(solution)/shard_map/ppermute | solution.py:631
  87.2 40.9 %collective-permute-start.16 = (bf16[976,768]{1,0:T(8,128)(2,1)}, bf16[976,768]{1,0:T(8,128)(2,1)}, u32[]{:S(2)}, u32[]{:S(2)}) collective-permute-start(bf16[976,768]{1,0:T(8,128)(2,1)} %collective-permute-done.2.rest_1_.rest_11_.rest_7_), channel_id=1, source_target_pairs={{0,8},{8,0},{16,24},{24,16},{1,9},{9,1},{17,25},{25,17},{2,10},{10... | collective-permute-start | bytes 4497416 | tf_op jit(solution)/shard_map/ppermute | solution.py:585
  87.2 41.0 %collective-permute-start.19 = (bf16[976,768]{1,0:T(8,128)(2,1)}, bf16[976,768]{1,0:T(8,128)(2,1)}, u32[]{:S(2)}, u32[]{:S(2)}) collective-permute-start(bf16[976,768]{1,0:T(8,128)(2,1)} %collective-permute-done.3.rest_4_.rest_14_.rest_10_), channel_id=1, source_target_pairs={{0,8},{8,0},{16,24},{24,16},{1,9},{9,1},{17,25},{25,17},{2,10},{10... | collective-permute-start | bytes 4497416 | tf_op jit(solution)/shard_map/ppermute | solution.py:585
  88.4 35.1 %collective-permute-start.5 = (bf16[384,768]{1,0:T(8,128)(2,1)}, bf16[384,768]{1,0:T(8,128)(2,1)}, u32[]{:S(2)}, u32[]{:S(2)}) collective-permute-start(bf16[384,768]{1,0:T(8,128)(2,1)} %constant_dynamic-update-slice_fusion.rest_8_.rest_18_.rest_14_), channel_id=1, source_target_pairs={{0,2},{1,3},{2,0},{3,1},{4,6},{5,7},{6,4},{7,5},{8,10},{9,11},{10,... | collective-permute-start | bytes 1769480 | tf_op jit(solution)/shard_map/ppermute | solution.py:631
  113.4 11.6 %collective-permute-start.6 = (bf16[384,768]{1,0:T(8,128)(2,1)}, bf16[384,768]{1,0:T(8,128)(2,1)S(1)}, u32[]{:S(2)}, u32[]{:S(2)}) collective-permute-start(bf16[384,768]{1,0:T(8,128)(2,1)} %constant_dynamic-update-slice_fusion.rest_8_.rest_18_.rest_14_), channel_id=1, source_target_pairs={{2,4},{3,5},{4,2},{5,3},{10,12},{11,13},{12,10},{13,11},{18,20},{1... | collective-permute-start | bytes 1769480 | tf_op jit(solution)/shard_map/ppermute | solution.py:631
  120.4 10.4 %collective-permute-start.17 = (bf16[976,768]{1,0:T(8,128)(2,1)S(1)}, bf16[976,768]{1,0:T(8,128)(2,1)S(1)}, u32[]{:S(2)}, u32[]{:S(2)}) collective-permute-start(bf16[976,768]{1,0:T(8,128)(2,1)S(1)} %broadcast_select_fusion.1.rest_2_.rest_12_.rest_8_), channel_id=1, source_target_pairs={{0,8},{8,0},{16,24},{24,16},{1,9},{9,1},{17,25},{25,17},{2,10},{10... | collective-permute-start | bytes 4497416 | tf_op jit(solution)/shard_map/ppermute | solution.py:585
  123.5 32.3 %collective-permute-start.11 = (bf16[976,768]{1,0:T(8,128)(2,1)S(1)}, bf16[976,768]{1,0:T(8,128)(2,1)S(1)}, u32[]{:S(2)}, u32[]{:S(2)}) collective-permute-start(bf16[976,768]{1,0:T(8,128)(2,1)S(1)} %broadcast_select_fusion.rest_3_.rest_13_.rest_9_), channel_id=1, source_target_pairs={{0,1},{1,0},{2,3},{3,2},{4,5},{5,4},{6,7},{7,6},{8,9},{9,8},{10,11... | collective-permute-start | bytes 4497416 | tf_op jit(solution)/shard_map/ppermute | solution.py:631
  128.1 32.1 %collective-permute-start.20 = (bf16[976,768]{1,0:T(8,128)(2,1)S(1)}, bf16[976,768]{1,0:T(8,128)(2,1)S(1)}, u32[]{:S(2)}, u32[]{:S(2)}) collective-permute-start(bf16[976,768]{1,0:T(8,128)(2,1)S(1)} %copy-done.3), channel_id=1, source_target_pairs={{0,8},{8,0},{16,24},{24,16},{1,9},{9,1},{17,25},{25,17},{2,10},{10... | collective-permute-start | bytes 4497416 | tf_op jit(solution)/shard_map/ppermute | solution.py:585
  128.2 19.2 %collective-permute-start.12 = (bf16[384,768]{1,0:T(8,128)(2,1)S(1)}, bf16[384,768]{1,0:T(8,128)(2,1)S(1)}, u32[]{:S(2)}, u32[]{:S(2)}) collective-permute-start(bf16[384,768]{1,0:T(8,128)(2,1)S(1)} %collective-permute-done.6), channel_id=1, source_target_pairs={{2,0},{3,1},{4,6},{5,7},{10,8},{11,9},{12,14},{13,15},{18,16},{19,... | collective-permute-start | bytes 1769480 | tf_op jit(solution)/shard_map/ppermute | solution.py:631
  129.5 30.5 %collective-permute-start.14 = (bf16[384,768]{1,0:T(8,128)(2,1)S(1)}, bf16[384,768]{1,0:T(8,128)(2,1)S(1)}, u32[]{:S(2)}, u32[]{:S(2)}) collective-permute-start(bf16[384,768]{1,0:T(8,128)(2,1)S(1)} %collective-permute-done.13), channel_id=1, source_target_pairs={{2,0},{3,1},{4,6},{5,7},{10,8},{11,9},{12,14},{13,15},{18,16},{19,... | collective-permute-start | bytes 1769480 | tf_op jit(solution)/shard_map/ppermute | solution.py:631
  130.8 32.0 %collective-permute-start.18 = (bf16[976,768]{1,0:T(8,128)(2,1)S(1)}, bf16[976,768]{1,0:T(8,128)(2,1)S(1)}, u32[]{:S(2)}, u32[]{:S(2)}) collective-permute-start(bf16[976,768]{1,0:T(8,128)(2,1)S(1)} %broadcast_select_fusion.rest_3_.rest_13_.rest_9_), channel_id=1, source_target_pairs={{0,8},{8,0},{16,24},{24,16},{1,9},{9,1},{17,25},{25,17},{2,10},{10... | collective-permute-start | bytes 4497416 | tf_op jit(solution)/shard_map/ppermute | solution.py:585
  147.4 16.8 %collective-permute-start.21 = (bf16[976,768]{1,0:T(8,128)(2,1)}, bf16[976,768]{1,0:T(8,128)(2,1)}, u32[]{:S(2)}, u32[]{:S(2)}) collective-permute-start(bf16[976,768]{1,0:T(8,128)(2,1)} %collective-permute-done.10.rest_6_.rest_16_.rest_12_), channel_id=1, source_target_pairs={{0,8},{8,0},{16,24},{24,16},{1,9},{9,1},{17,25},{25,17},{2,10},{10... | collective-permute-start | bytes 4497416 | tf_op jit(solution)/shard_map/ppermute | solution.py:585
  188.0 13.5 %collective-permute-start.27 = (bf16[288,768]{1,0:T(8,128)(2,1)}, bf16[288,768]{1,0:T(8,128)(2,1)S(1)}, u32[]{:S(2)}, u32[]{:S(2)}) collective-permute-start(bf16[288,768]{1,0:T(8,128)(2,1)} %get-tuple-element.113), channel_id=1, source_target_pairs={{0,16},{8,24},{1,17},{9,25},{2,18},{10,26},{3,19},{11,27},{4,20},{... | collective-permute-start | bytes 1327112 | tf_op jit(solution)/shard_map/ppermute | solution.py:580
  262.4 13.5 %collective-permute-start.28 = (bf16[288,768]{1,0:T(8,128)(2,1)}, bf16[288,768]{1,0:T(8,128)(2,1)S(1)}, u32[]{:S(2)}, u32[]{:S(2)}) collective-permute-start(bf16[288,768]{1,0:T(8,128)(2,1)} %backward_layers.3), channel_id=1, source_target_pairs={{16,0},{24,8},{17,1},{25,9},{18,2},{26,10},{19,3},{27,11},{20,4},{... | collective-permute-start | bytes 1327112 | tf_op jit(solution)/shard_map/ppermute | solution.py:580
  263.7 53.4 %collective-permute-start.29 = (bf16[288,4608]{1,0:T(8,128)(2,1)}, bf16[288,4608]{1,0:T(8,128)(2,1)}, u32[]{:S(2)}, u32[]{:S(2)}) collective-permute-start(bf16[288,4608]{1,0:T(8,128)(2,1)} %get-tuple-element.129), channel_id=1, source_target_pairs={{0,8},{8,0},{16,24},{24,16},{1,9},{9,1},{17,25},{25,17},{2,10},{10... | collective-permute-start | bytes 7962632 | tf_op jit(solution)/shard_map/ppermute | solution.py:585
  263.8 67.9 %collective-permute-start.31 = (bf16[288,4608]{1,0:T(8,128)(2,1)S(1)}, bf16[288,4608]{1,0:T(8,128)(2,1)}, u32[]{:S(2)}, u32[]{:S(2)}) collective-permute-start(bf16[288,4608]{1,0:T(8,128)(2,1)S(1)} %copy-done.35), channel_id=1, source_target_pairs={{0,8},{8,0},{16,24},{24,16},{1,9},{9,1},{17,25},{25,17},{2,10},{10... | collective-permute-start | bytes 7962632 | tf_op jit(solution)/shard_map/ppermute | solution.py:585
  296.6 20.5 %collective-permute-start.30 = (bf16[288,4608]{1,0:T(8,128)(2,1)}, bf16[288,4608]{1,0:T(8,128)(2,1)}, u32[]{:S(2)}, u32[]{:S(2)}) collective-permute-start(bf16[288,4608]{1,0:T(8,128)(2,1)} %get-tuple-element.130), channel_id=1, source_target_pairs={{0,8},{8,0},{16,24},{24,16},{1,9},{9,1},{17,25},{25,17},{2,10},{10... | collective-permute-start | bytes 7962632 | tf_op jit(solution)/shard_map/ppermute | solution.py:585
  316.6 15.2 %collective-permute-start.32 = (bf16[288,4608]{1,0:T(8,128)(2,1)}, bf16[288,4608]{1,0:T(8,128)(2,1)}, u32[]{:S(2)}, u32[]{:S(2)}) collective-permute-start(bf16[288,4608]{1,0:T(8,128)(2,1)} %get-tuple-element.136), channel_id=1, source_target_pairs={{0,8},{8,0},{16,24},{24,16},{1,9},{9,1},{17,25},{25,17},{2,10},{10... | collective-permute-start | bytes 7962632 | tf_op jit(solution)/shard_map/ppermute | solution.py:585
  330.3 16.4 %collective-permute-start.45 = (bf16[400,768]{1,0:T(8,128)(2,1)}, bf16[400,768]{1,0:T(8,128)(2,1)S(1)}, u32[]{:S(2)}, u32[]{:S(2)}) collective-permute-start(bf16[400,768]{1,0:T(8,128)(2,1)} %get-tuple-element.164), channel_id=1, source_target_pairs={{0,1},{1,0},{2,3},{3,2},{4,5},{5,4},{6,7},{7,6},{8,9},{9,8},{10,11... | collective-permute-start | bytes 1843208 | tf_op jit(solution)/shard_map/ppermute | solution.py:631
  345.6 23.0 %collective-permute-start.33 = (bf16[592,768]{1,0:T(8,128)(2,1)S(1)}, bf16[592,768]{1,0:T(8,128)(2,1)S(1)}, u32[]{:S(2)}, u32[]{:S(2)}) collective-permute-start(bf16[592,768]{1,0:T(8,128)(2,1)S(1)} %copy-done.39), channel_id=1, source_target_pairs={{0,1},{1,0},{2,3},{3,2},{4,5},{5,4},{6,7},{7,6},{8,9},{9,8},{10,11... | collective-permute-start | bytes 2727944 | tf_op jit(solution)/shard_map/ppermute | solution.py:631
  347.0 39.1 %collective-permute-start.52 = (bf16[784,768]{1,0:T(8,128)(2,1)S(1)}, bf16[784,768]{1,0:T(8,128)(2,1)S(1)}, u32[]{:S(2)}, u32[]{:S(2)}) collective-permute-start(bf16[784,768]{1,0:T(8,128)(2,1)S(1)} %pad_maximum_fusion.2), channel_id=1, source_target_pairs={{0,2},{1,3},{6,4},{7,5},{8,10},{9,11},{14,12},{15,13},{16,18},{17,... | collective-permute-start | bytes 3612680 | tf_op jit(solution)/shard_map/ppermute | solution.py:631
  355.5 17.0 %collective-permute-start.37 = (bf16[2,280,192]{2,1,0:T(8,128)(2,1)S(1)}, bf16[2,280,192]{2,1,0:T(8,128)(2,1)S(1)}, u32[]{:S(2)}, u32[]{:S(2)}) collective-permute-start(bf16[2,280,192]{2,1,0:T(8,128)(2,1)S(1)} %fusion.1), channel_id=1, source_target_pairs={{0,8},{8,0},{16,24},{24,16},{1,9},{9,1},{17,25},{25,17},{2,10},{10... | collective-permute-start | bytes 645128 | tf_op jit(solution)/shard_map/ppermute | solution.py:585
  355.6 26.2 %collective-permute-start.46 = (bf16[400,768]{1,0:T(8,128)(2,1)S(1)}, bf16[400,768]{1,0:T(8,128)(2,1)S(1)}, u32[]{:S(2)}, u32[]{:S(2)}) collective-permute-start(bf16[400,768]{1,0:T(8,128)(2,1)S(1)} %copy-done.42), channel_id=1, source_target_pairs={{0,1},{1,0},{2,3},{3,2},{4,5},{5,4},{6,7},{7,6},{8,9},{9,8},{10,11... | collective-permute-start | bytes 1843208 | tf_op jit(solution)/shard_map/ppermute | solution.py:631
  368.9 28.0 %collective-permute-start.35 = (bf16[592,768]{1,0:T(8,128)(2,1)S(1)}, bf16[592,768]{1,0:T(8,128)(2,1)S(1)}, u32[]{:S(2)}, u32[]{:S(2)}) collective-permute-start(bf16[592,768]{1,0:T(8,128)(2,1)S(1)} %add_convert_fusion.10), channel_id=1, source_target_pairs={{0,2},{1,3},{6,4},{7,5},{8,10},{9,11},{14,12},{15,13},{16,18},{17,... | collective-permute-start | bytes 2727944 | tf_op jit(solution)/shard_map/ppermute | solution.py:631
  372.7 28.5 %collective-permute-start.34 = (bf16[592,768]{1,0:T(8,128)(2,1)S(1)}, bf16[592,768]{1,0:T(8,128)(2,1)S(1)}, u32[]{:S(2)}, u32[]{:S(2)}) collective-permute-start(bf16[592,768]{1,0:T(8,128)(2,1)S(1)} %copy-done.38), channel_id=1, source_target_pairs={{0,1},{1,0},{2,3},{3,2},{4,5},{5,4},{6,7},{7,6},{8,9},{9,8},{10,11... | collective-permute-start | bytes 2727944 | tf_op jit(solution)/shard_map/ppermute | solution.py:631
  381.7 32.6 %collective-permute-start.47 = (bf16[400,768]{1,0:T(8,128)(2,1)S(1)}, bf16[400,768]{1,0:T(8,128)(2,1)S(1)}, u32[]{:S(2)}, u32[]{:S(2)}) collective-permute-start(bf16[400,768]{1,0:T(8,128)(2,1)S(1)} %copy-done.41), channel_id=1, source_target_pairs={{0,1},{1,0},{2,3},{3,2},{4,5},{5,4},{6,7},{7,6},{8,9},{9,8},{10,11... | collective-permute-start | bytes 1843208 | tf_op jit(solution)/shard_map/ppermute | solution.py:631
  382.6 40.0 %collective-permute-start.50 = (bf16[784,768]{1,0:T(8,128)(2,1)S(1)}, bf16[784,768]{1,0:T(8,128)(2,1)S(1)}, u32[]{:S(2)}, u32[]{:S(2)}) collective-permute-start(bf16[784,768]{1,0:T(8,128)(2,1)S(1)} %pad_maximum_fusion.1), channel_id=1, source_target_pairs={{0,2},{1,3},{6,4},{7,5},{8,10},{9,11},{14,12},{15,13},{16,18},{17,... | collective-permute-start | bytes 3612680 | tf_op jit(solution)/shard_map/ppermute | solution.py:631
  386.5 41.0 %collective-permute-start.53 = (bf16[784,768]{1,0:T(8,128)(2,1)S(1)}, bf16[784,768]{1,0:T(8,128)(2,1)S(1)}, u32[]{:S(2)}, u32[]{:S(2)}) collective-permute-start(bf16[784,768]{1,0:T(8,128)(2,1)S(1)} %add_convert_fusion.2), channel_id=1, source_target_pairs={{2,4},{3,5},{4,2},{5,3},{10,12},{11,13},{12,10},{13,11},{18,20},{1... | collective-permute-start | bytes 3612680 | tf_op jit(solution)/shard_map/ppermute | solution.py:631
  401.5 40.7 %collective-permute-start.40 = (bf16[592,768]{1,0:T(8,128)(2,1)S(1)}, bf16[592,768]{1,0:T(8,128)(2,1)S(1)}, u32[]{:S(2)}, u32[]{:S(2)}) collective-permute-start(bf16[592,768]{1,0:T(8,128)(2,1)S(1)} %add_convert_fusion.9), channel_id=1, source_target_pairs={{0,2},{1,3},{6,4},{7,5},{8,10},{9,11},{14,12},{15,13},{16,18},{17,... | collective-permute-start | bytes 2727944 | tf_op jit(solution)/shard_map/ppermute | solution.py:631
  405.1 38.3 %collective-permute-start.39 = (bf16[592,768]{1,0:T(8,128)(2,1)S(1)}, bf16[592,768]{1,0:T(8,128)(2,1)S(1)}, u32[]{:S(2)}, u32[]{:S(2)}) collective-permute-start(bf16[592,768]{1,0:T(8,128)(2,1)S(1)} %copy-done.37), channel_id=1, source_target_pairs={{0,1},{1,0},{2,3},{3,2},{4,5},{5,4},{6,7},{7,6},{8,9},{9,8},{10,11... | collective-permute-start | bytes 2727944 | tf_op jit(solution)/shard_map/ppermute | solution.py:631
  414.4 30.9 %collective-permute-start.41 = (bf16[592,768]{1,0:T(8,128)(2,1)S(1)}, bf16[592,768]{1,0:T(8,128)(2,1)S(1)}, u32[]{:S(2)}, u32[]{:S(2)}) collective-permute-start(bf16[592,768]{1,0:T(8,128)(2,1)S(1)} %add_convert_fusion.8), channel_id=1, source_target_pairs={{2,4},{3,5},{4,2},{5,3},{10,12},{11,13},{12,10},{13,11},{18,20},{1... | collective-permute-start | bytes 2727944 | tf_op jit(solution)/shard_map/ppermute | solution.py:631
  422.7 45.3 %collective-permute-start.49 = (bf16[784,768]{1,0:T(8,128)(2,1)S(1)}, bf16[784,768]{1,0:T(8,128)(2,1)S(1)}, u32[]{:S(2)}, u32[]{:S(2)}) collective-permute-start(bf16[784,768]{1,0:T(8,128)(2,1)S(1)} %pad_maximum_fusion), channel_id=1, source_target_pairs={{0,2},{1,3},{6,4},{7,5},{8,10},{9,11},{14,12},{15,13},{16,18},{17,... | collective-permute-start | bytes 3612680 | tf_op jit(solution)/shard_map/ppermute | solution.py:631
  427.5 41.2 %collective-permute-start.51 = (bf16[784,768]{1,0:T(8,128)(2,1)S(1)}, bf16[784,768]{1,0:T(8,128)(2,1)S(1)}, u32[]{:S(2)}, u32[]{:S(2)}) collective-permute-start(bf16[784,768]{1,0:T(8,128)(2,1)S(1)} %add_convert_fusion.3), channel_id=1, source_target_pairs={{2,4},{3,5},{4,2},{5,3},{10,12},{11,13},{12,10},{13,11},{18,20},{1... | collective-permute-start | bytes 3612680 | tf_op jit(solution)/shard_map/ppermute | solution.py:631
  442.1 28.7 %collective-permute-start.54 = (bf16[784,768]{1,0:T(8,128)(2,1)S(1)}, bf16[784,768]{1,0:T(8,128)(2,1)S(1)}, u32[]{:S(2)}, u32[]{:S(2)}) collective-permute-start(bf16[784,768]{1,0:T(8,128)(2,1)S(1)} %add_convert_fusion.1), channel_id=1, source_target_pairs={{2,0},{3,1},{4,6},{5,7},{10,8},{11,9},{12,14},{13,15},{18,16},{19,... | collective-permute-start | bytes 3612680 | tf_op jit(solution)/shard_map/ppermute | solution.py:631
  443.4 16.9 %collective-permute-start.48 = (bf16[400,768]{1,0:T(8,128)(2,1)S(1)}, bf16[400,768]{1,0:T(8,128)(2,1)S(1)}, u32[]{:S(2)}, u32[]{:S(2)}) collective-permute-start(bf16[400,768]{1,0:T(8,128)(2,1)S(1)} %copy-done.40), channel_id=1, source_target_pairs={{0,1},{1,0},{2,3},{3,2},{4,5},{5,4},{6,7},{7,6},{8,9},{9,8},{10,11... | collective-permute-start | bytes 1843208 | tf_op jit(solution)/shard_map/ppermute | solution.py:631
  445.3 34.5 %collective-permute-start.38 = (bf16[592,768]{1,0:T(8,128)(2,1)S(1)}, bf16[592,768]{1,0:T(8,128)(2,1)S(1)}, u32[]{:S(2)}, u32[]{:S(2)}) collective-permute-start(bf16[592,768]{1,0:T(8,128)(2,1)S(1)} %copy-done.36), channel_id=1, source_target_pairs={{0,1},{1,0},{2,3},{3,2},{4,5},{5,4},{6,7},{7,6},{8,9},{9,8},{10,11... | collective-permute-start | bytes 2727944 | tf_op jit(solution)/shard_map/ppermute | solution.py:631
  460.3 26.2 %collective-permute-start.42 = (bf16[592,768]{1,0:T(8,128)(2,1)S(1)}, bf16[592,768]{1,0:T(8,128)(2,1)S(1)}, u32[]{:S(2)}, u32[]{:S(2)}) collective-permute-start(bf16[592,768]{1,0:T(8,128)(2,1)S(1)} %get-tuple-element.157), channel_id=1, source_target_pairs={{0,2},{1,3},{6,4},{7,5},{8,10},{9,11},{14,12},{15,13},{16,18},{17,... | collective-permute-start | bytes 2727944 | tf_op jit(solution)/shard_map/ppermute | solution.py:631
  467.9 18.6 %collective-permute-start.43 = (bf16[592,768]{1,0:T(8,128)(2,1)S(1)}, bf16[592,768]{1,0:T(8,128)(2,1)S(1)}, u32[]{:S(2)}, u32[]{:S(2)}) collective-permute-start(bf16[592,768]{1,0:T(8,128)(2,1)S(1)} %add_convert_fusion.6), channel_id=1, source_target_pairs={{2,4},{3,5},{4,2},{5,3},{10,12},{11,13},{12,10},{13,11},{18,20},{1... | collective-permute-start | bytes 2727944 | tf_op jit(solution)/shard_map/ppermute | solution.py:631
  468.7 24.8 %collective-permute-start.44 = (bf16[592,768]{1,0:T(8,128)(2,1)S(1)}, bf16[592,768]{1,0:T(8,128)(2,1)S(1)}, u32[]{:S(2)}, u32[]{:S(2)}) collective-permute-start(bf16[592,768]{1,0:T(8,128)(2,1)S(1)} %get-tuple-element.159), channel_id=1, source_target_pairs={{2,0},{3,1},{4,6},{5,7},{10,8},{11,9},{12,14},{13,15},{18,16},{19,... | collective-permute-start | bytes 2727944 | tf_op jit(solution)/shard_map/ppermute | solution.py:631
  471.6 23.9 %collective-permute-start.55 = (bf16[192,768]{1,0:T(8,128)(2,1)S(1)}, bf16[192,768]{1,0:T(8,128)(2,1)S(1)}, u32[]{:S(2)}, u32[]{:S(2)}) collective-permute-start(bf16[192,768]{1,0:T(8,128)(2,1)S(1)} %slice.32), channel_id=1, source_target_pairs={{0,1},{1,0},{2,3},{3,2},{4,5},{5,4},{6,7},{7,6},{8,9},{9,8},{10,11... | collective-permute-start | bytes 884744 | tf_op jit(solution)/shard_map/ppermute | solution.py:631
  (55 other events, 653.4 us)

commit v7 on v6

--- a/solution.py
+++ b/solution.py
@@ -382,7 +382,7 @@
         scratch_shapes=weight_scratch(len(wa)) * m + work * m + [
             pltpu.VMEM((ROWS, D), BF), pltpu.SemaphoreType.DMA((m, 2)), pltpu.SemaphoreType.DMA((5,))],
         compiler_params=pltpu.CompilerParams(vmem_limit_bytes=VMEM_LIMIT),
-        cost_estimate=pl.CostEstimate(flops=2 * ROWS * D * D * 14 * m, bytes_accessed=m * (24 * D * D + 2**23), transcendentals=0),
+        cost_estimate=pl.CostEstimate(flops=2 * 10**10, bytes_accessed=2**24, transcendentals=0),
         name="backward_layers",
     )(g, mask, *kept, *([behind] if save else []), *wa, *wb)
 
@@ -480,7 +480,7 @@
         out_specs=[ANYS] * len(shapes),
         scratch_shapes=scratch,
         compiler_params=pltpu.CompilerParams(vmem_limit_bytes=VMEM_LIMIT),
-        cost_estimate=pl.CostEstimate(flops=2 * 2 * ROWS * D * D * 6, bytes_accessed=2**24, transcendentals=0),
+        cost_estimate=pl.CostEstimate(flops=13 * 10**9, bytes_accessed=2**24, transcendentals=0),
         name="weight_products",
     )(behind, gv, fk, bk, fr, br)
 
@@ -524,7 +524,7 @@
     )(*params)
 
 
-def finish_kernel(red0, red1, sent0, sent1, up, joint, out, down, ag, as_, jb, ob, fg, fs, db, ub):
+def finish_kernel(red0, red1, sent0, sent1, up, joint, out, down, ag, as_, jb, ob, fg, fs, db, ub, first, second, sems):
     r = out.shape[0]
     spot, core = lax.axis_index("dp"), lax.axis_index("section") % 2
 
@@ -556,11 +556,17 @@
 
     @pl.when(core == 0)
     def _():
-        write(red0, sent0)
+        pltpu.make_async_copy(red0, first, sems.at[0]).start()
+        pltpu.make_async_copy(sent0, second, sems.at[1]).start()
 
     @pl.when(core != 0)
     def _():
-        write(sent1, red1)
+        pltpu.make_async_copy(sent1, first, sems.at[0]).start()
+        pltpu.make_async_copy(red1, second, sems.at[1]).start()
+
+    pltpu.make_async_copy(red0, first, sems.at[0]).wait()
+    pltpu.make_async_copy(red0, second, sems.at[1]).wait()
+    write(first, second)
 
 
 def finish(r, reduced, sent):
@@ -568,8 +574,9 @@
     return pl.pallas_call(
         finish_kernel,
         out_shape=[jax.ShapeDtypeStruct(shape, F32) for shape in shapes],
-        in_specs=[VM] * 4,
+        in_specs=[ANYS] * 4,
         out_specs=[VM] * 12,
+        scratch_shapes=[pltpu.VMEM(reduced[0].shape, BF)] * 2 + [pltpu.SemaphoreType.DMA((2,))],
         compiler_params=pltpu.CompilerParams(vmem_limit_bytes=VMEM_LIMIT),
         name="finish",
     )(*reduced, *sent)

time: 512 us -> 511 us (level)
  starting transfers between devices: 73.7 us -> 67.5 us
    ppermute x36, starting transfers between devices: 61.3 us -> 55.2 us  [send(): got = lax.ppermute(value, axis, pairs)]
  transfers between devices with their start and end apart: 58 -> 58, of which waited for: 30 -> 31; matrix products, arithmetic and copies ran while one was open for 3% -> 3% of each run, Pallas kernels for 13% -> 13%
where the time goes in v7:
time: 511 us; the launch traced here: 506 us
  waiting for transfers between devices  258 us (50%)
  Pallas kernels  157 us (31%)
  starting transfers between devices  67.5 us (13%)
  local copies, waits for them, and re-layouts  11.8 us (2%)
  other arithmetic  9.87 us (2%)
    ppermute x36, waiting for transfers between devices, send(): got = lax.ppermute(value, axis, pairs)  224 us
    pallas_call x3, Pallas kernels, backward_layers(): pl.pallas_call(functools.partial(backward_kernel, save, layers, len(wa)),...  74.2 us
    ppermute x36, starting transfers between devices, send(): got = lax.ppermute(value, axis, pairs)  55.2 us
    pallas_call x2, Pallas kernels, forward_stage(): pl.pallas_call(functools.partial(forward_kernel, save, len(wa)), out_shap...  48.7 us
    pallas_call x2, Pallas kernels, weight_products(): pl.pallas_call(functools.partial(product_kernel, n, direct), out_shape=sh...  25.7 us
    ppermute x2, waiting for transfers between devices, moved(): lax.ppermute(value, axis, [(i, i + by) for i in range(peers) if 0 <= i +...  21.6 us
    ppermute x18, waiting for transfers between devices, flipped(): return lax.ppermute(value, 'section', [(i, i ^ bit) for i in range(peers)])  11.8 us
  transfers between devices with their start and end apart: 58, of which 31 were waited for; matrix products, arithmetic and copies ran while one was open for 3% of the time, Pallas kernels for 13%

profile of v7, /device:TPU:0, one launch (start us, length us, event | category | flops | bytes accessed | tf_op | source)
XLA Modules:
  0.0 506.4 jit_solution(11753653292725636516)
XLA Ops:
  0.6 3.7 pack.1
  4.3 3.0 collective-permute-start.2
  8.1 1.6 collective-permute-start.3
  9.7 30.8 %collective-permute-done.2.rest_1_.rest_11_.rest_7_ = bf16[976,768]{1,0:T(8,128)(2,1)} collective-permute-done((bf16[976,768]{1,0:T(8,128)(2,1)}, bf16[976,768]{1,0:T(8,128)(2,1)}, u32[]{:S(2)}, u32[]{:S(2)}) %collective-permute-start.2) | collective-permute-done | bytes 1499168 | tf_op jit(solution)/shard_map/ppermute | solution.py:638
  44.3 6.7 %collective-permute-done.4 = bf16[192,768]{1,0:T(8,128)(2,1)S(1)} collective-permute-done((bf16[192,768]{1,0:T(8,128)(2,1)}, bf16[192,768]{1,0:T(8,128)(2,1)S(1)}, u32[]{:S(2)}, u32[]{:S(2)}) %collective-permute-start.4) | collective-permute-done | bytes 294944 | tf_op jit(solution)/shard_map/ppermute | solution.py:638
  53.7 25.4 %collective-permute-done.1 = bf16[976,768]{1,0:T(8,128)(2,1)} collective-permute-done((bf16[976,768]{1,0:T(8,128)(2,1)S(1)}, bf16[976,768]{1,0:T(8,128)(2,1)}, u32[]{:S(2)}, u32[]{:S(2)}) %collective-permute-start.1) | collective-permute-done | bytes 1499168 | tf_op jit(solution)/shard_map/ppermute | solution.py:638
  80.7 3.8 collective-permute-done.9.rest_5_.rest_15_.rest_11_
  87.6 5.1 %collective-permute-start.5 = (bf16[384,768]{1,0:T(8,128)(2,1)}, bf16[384,768]{1,0:T(8,128)(2,1)}, u32[]{:S(2)}, u32[]{:S(2)}) collective-permute-start(bf16[384,768]{1,0:T(8,128)(2,1)} %constant_dynamic-update-slice_fusion.rest_8_.rest_18_.rest_14_), channel_id=1, source_target_pairs={{0,2},{1,3},{2,0},{3,1},{4,6},{5,7},{6,4},{7,5},{8,10},{9,11},{10,... | collective-permute-start | bytes 1769480 | tf_op jit(solution)/shard_map/ppermute | solution.py:638
  92.6 20.5 %collective-permute-done.8 = bf16[976,768]{1,0:T(8,128)(2,1)} collective-permute-done((bf16[976,768]{1,0:T(8,128)(2,1)S(1)}, bf16[976,768]{1,0:T(8,128)(2,1)}, u32[]{:S(2)}, u32[]{:S(2)}) %collective-permute-start.8) | collective-permute-done | bytes 1499168 | tf_op jit(solution)/shard_map/ppermute | solution.py:638
  118.4 1.5 broadcast_select_fusion.rest_3_.rest_13_.rest_9_
  120.1 3.4 collective-permute-done.5.rest_9_.rest_19_.rest_15_
  125.0 2.2 collective-permute-done.23.rest_20_.rest_30_.rest_26_
  131.3 14.6 %collective-permute-done.12 = bf16[384,768]{1,0:T(8,128)(2,1)S(1)} collective-permute-done((bf16[384,768]{1,0:T(8,128)(2,1)S(1)}, bf16[384,768]{1,0:T(8,128)(2,1)S(1)}, u32[]{:S(2)}, u32[]{:S(2)}) %collective-permute-start.12) | collective-permute-done | bytes 589856 | tf_op jit(solution)/shard_map/ppermute | solution.py:638
  145.9 10.3 %collective-permute-done.11.rest_7_.rest_17_.rest_13_ = bf16[976,768]{1,0:T(8,128)(2,1)S(1)} collective-permute-done((bf16[976,768]{1,0:T(8,128)(2,1)S(1)}, bf16[976,768]{1,0:T(8,128)(2,1)S(1)}, u32[]{:S(2)}, u32[]{:S(2)}) %collective-permute-start.11) | collective-permute-done | bytes 1499168 | tf_op jit(solution)/shard_map/ppermute | solution.py:638
  156.2 3.1 collective-permute-done.14
  165.5 23.1 %forward_stage.2 = (bf16[288,768]{1,0:T(8,128)(2,1)}, bf16[288,768]{1,0:T(8,128)(2,1)}) custom-call(bf16[288,768]{1,0:T(8,128)(2,1)} %pad.7.x_ref.came_ref, bf16[288,768]{1,0:T(8,128)(2,1)} %pad.7.x_ref.came_ref, f32[8,288]{1,0:T(8,128)} %iota.13.mask_ref.rest_5_, bf16[976,768]{1,0:T(8,128)(2,1)} %get-tuple-element.100.rest_0_.rest_10_.rest_6_, ...), custom_call_target="tpu_custom_call" | custom-call | flops 8833204224 | bytes 36700160 | tf_op jit(solution)/shard_map/forward_stage/pallas_call | solution.py:245
  188.6 3.4 collective-permute-start.27
  192.0 10.0 %collective-permute-done.27.came_ref = bf16[288,768]{1,0:T(8,128)(2,1)S(1)} collective-permute-done((bf16[288,768]{1,0:T(8,128)(2,1)}, bf16[288,768]{1,0:T(8,128)(2,1)S(1)}, u32[]{:S(2)}, u32[]{:S(2)}) %collective-permute-start.27) | collective-permute-done | bytes 442400 | tf_op jit(solution)/shard_map/ppermute | solution.py:587
  202.8 25.6 %forward_stage.3 = (bf16[288,768]{1,0:T(8,128)(2,1)}, bf16[288,768]{1,0:T(8,128)(2,1)}, f32[288,128]{1,0:T(8,128)}, f32[288,768]{1,0:T(8,128)}, bf16[288,2304]{1...) custom-call(bf16[288,768]{1,0:T(8,128)(2,1)} %pad.7.x_ref.came_ref, ...), custom_call_target="tpu_custom_call" | custom-call | flops 8833204224 | bytes 36700160 | tf_op jit(solution)/shard_map/forward_stage/pallas_call | solution.py:245
  228.5 34.5 %backward_layers.3 = bf16[288,768]{1,0:T(8,128)(2,1)} custom-call(bf16[288,768]{1,0:T(8,128)(2,1)} %pad.8.g_ref, f32[8,288]{1,0:T(8,128)} %iota.13.mask_ref.rest_5_, bf16[288,768]{1,0:T(8,128)(2,1)} %get-tuple-element.114.rest_0_, f32[288,128]{1,0:T(8,128)} %get-tuple-element.115.rest_1_, f32[288,768]{1,0:T(8,128)} %get-tuple-element.116.rest_2_, ...), custom_call_target="tpu_custom_call" | custom-call | flops 20000000000 | bytes 16777216 | tf_op jit(solution)/shard_map/backward_layers/pallas_call | solution.py:377
  264.9 11.6 %collective-permute-done.28 = bf16[288,768]{1,0:T(8,128)(2,1)S(1)} collective-permute-done((bf16[288,768]{1,0:T(8,128)(2,1)}, bf16[288,768]{1,0:T(8,128)(2,1)S(1)}, u32[]{:S(2)}, u32[]{:S(2)}) %collective-permute-start.28) | collective-permute-done | bytes 442400 | tf_op jit(solution)/shard_map/ppermute | solution.py:587
  277.3 19.8 %backward_layers.4 = (bf16[288,768]{1,0:T(8,128)(2,1)}, f32[16,768]{1,0:T(8,128)}, bf16[288,4608]{1,0:T(8,128)(2,1)}, bf16[288,4608]{1,0:T(8,128)(2,1)}) custom-call(bf16[288,768]{1,0:T(8,128)(2,1)} %broadcast_select_fusion.4.g_ref, f32[8,288]{1,0:T(8,128)} %iota.13.mask_ref.rest_5_, bf16[288,768]{1,0:T(8,128)(2,1)} %get-tuple-element.114.rest_0_, ...), custom_call_target="tpu_custom_call" | custom-call | flops 20000000000 | bytes 16777216 | tf_op jit(solution)/shard_map/backward_layers/pallas_call | solution.py:377
  297.2 19.9 %backward_layers.5 = (bf16[288,768]{1,0:T(8,128)(2,1)}, f32[16,768]{1,0:T(8,128)}, bf16[288,4608]{1,0:T(8,128)(2,1)}, bf16[288,4608]{1,0:T(8,128)(2,1)}) custom-call(bf16[288,768]{1,0:T(8,128)(2,1)} %get-tuple-element.124.g_ref, f32[8,288]{1,0:T(8,128)} %iota.13.mask_ref.rest_5_, bf16[288,768]{1,0:T(8,128)(2,1)} %get-tuple-element.119.rest_5_.rest_0_, ...), custom_call_target="tpu_custom_call" | custom-call | flops 20000000000 | bytes 16777216 | tf_op jit(solution)/shard_map/backward_layers/pallas_call | solution.py:377
  317.6 13.1 %weight_products.2 = (bf16[400,768]{1,0:T(8,128)(2,1)}, bf16[400,768]{1,0:T(8,128)(2,1)}, bf16[400,768]{1,0:T(8,128)(2,1)}, bf16[400,768]{1,0:T(8,128)(2,1)}, bf...) custom-call(bf16[288,768]{1,0:T(8,128)(2,1)} %get-tuple-element.148., ...), custom_call_target="tpu_custom_call" | custom-call | flops 12999999488 | bytes 16777216 | tf_op jit(solution)/shard_map/weight_products/pallas_call | solution.py:476
  330.8 1.6 collective-permute-start.45
  332.4 12.6 %weight_products.3 = (bf16[592,768]{1,0:T(8,128)(2,1)}, bf16[592,768]{1,0:T(8,128)(2,1)}, bf16[592,768]{1,0:T(8,128)(2,1)}, bf16[592,768]{1,0:T(8,128)(2,1)}, bf...) custom-call(bf16[400,768]{1,0:T(8,128)(2,1)} %get-tuple-element.131.behi, ...), custom_call_target="tpu_custom_call" | custom-call | flops 12999999488 | bytes 16777216 | tf_op jit(solution)/shard_map/weight_products/pallas_call | solution.py:476
  347.5 2.1 collective-permute-start.52
  349.6 6.3 %collective-permute-done.36 = bf16[280,2,192]{2,0,1:T(8,128)(2,1)S(1)} collective-permute-done((bf16[280,2,192]{2,0,1:T(8,128)(2,1)S(1)}, bf16[280,2,192]{2,0,1:T(8,128)(2,1)S(1)}, u32[]{:S(2)}, u32[]{:S(2)}) %collective-permute-start.36) | collective-permute-done | bytes 215072 | tf_op jit(solution)/shard_map/ppermute | solution.py:592
  356.1 1.6 collective-permute-start.46
  357.7 11.5 %collective-permute-done.33 = bf16[592,768]{1,0:T(8,128)(2,1)S(1)} collective-permute-done((bf16[592,768]{1,0:T(8,128)(2,1)S(1)}, bf16[592,768]{1,0:T(8,128)(2,1)S(1)}, u32[]{:S(2)}, u32[]{:S(2)}) %collective-permute-start.33) | collective-permute-done | bytes 909344 | tf_op jit(solution)/shard_map/ppermute | solution.py:638
  369.4 2.0 collective-permute-start.35
  372.3 10.0 %collective-permute-done.46 = bf16[400,768]{1,0:T(8,128)(2,1)S(1)} collective-permute-done((bf16[400,768]{1,0:T(8,128)(2,1)S(1)}, bf16[400,768]{1,0:T(8,128)(2,1)S(1)}, u32[]{:S(2)}, u32[]{:S(2)}) %collective-permute-start.46) | collective-permute-done | bytes 614432 | tf_op jit(solution)/shard_map/ppermute | solution.py:638
  383.1 2.0 collective-permute-start.50
  386.3 9.5 %collective-permute-done.35 = bf16[592,768]{1,0:T(8,128)(2,1)S(1)} collective-permute-done((bf16[592,768]{1,0:T(8,128)(2,1)S(1)}, bf16[592,768]{1,0:T(8,128)(2,1)S(1)}, u32[]{:S(2)}, u32[]{:S(2)}) %collective-permute-start.35) | collective-permute-done | bytes 909344 | tf_op jit(solution)/shard_map/ppermute | solution.py:638
  396.1 5.7 %collective-permute-done.34 = bf16[592,768]{1,0:T(8,128)(2,1)S(1)} collective-permute-done((bf16[592,768]{1,0:T(8,128)(2,1)S(1)}, bf16[592,768]{1,0:T(8,128)(2,1)S(1)}, u32[]{:S(2)}, u32[]{:S(2)}) %collective-permute-start.34) | collective-permute-done | bytes 909344 | tf_op jit(solution)/shard_map/ppermute | solution.py:638
  402.0 2.0 collective-permute-start.40
  404.8 10.2 %collective-permute-done.47 = bf16[400,768]{1,0:T(8,128)(2,1)S(1)} collective-permute-done((bf16[400,768]{1,0:T(8,128)(2,1)S(1)}, bf16[400,768]{1,0:T(8,128)(2,1)S(1)}, u32[]{:S(2)}, u32[]{:S(2)}) %collective-permute-start.47) | collective-permute-done | bytes 614432 | tf_op jit(solution)/shard_map/ppermute | solution.py:638
  415.9 5.7 %collective-permute-done.50 = bf16[784,768]{1,0:T(8,128)(2,1)S(1)} collective-permute-done((bf16[784,768]{1,0:T(8,128)(2,1)S(1)}, bf16[784,768]{1,0:T(8,128)(2,1)S(1)}, u32[]{:S(2)}, u32[]{:S(2)}) %collective-permute-start.50) | collective-permute-done | bytes 1204256 | tf_op jit(solution)/shard_map/ppermute | solution.py:638
  421.7 4.5 collective-permute-start.49
  427.7 13.4 %collective-permute-done.40 = bf16[592,768]{1,0:T(8,128)(2,1)S(1)} collective-permute-done((bf16[592,768]{1,0:T(8,128)(2,1)S(1)}, bf16[592,768]{1,0:T(8,128)(2,1)S(1)}, u32[]{:S(2)}, u32[]{:S(2)}) %collective-permute-start.40) | collective-permute-done | bytes 909344 | tf_op jit(solution)/shard_map/ppermute | solution.py:638
  445.3 14.0 %collective-permute-done.48 = bf16[400,768]{1,0:T(8,128)(2,1)S(1)} collective-permute-done((bf16[400,768]{1,0:T(8,128)(2,1)S(1)}, bf16[400,768]{1,0:T(8,128)(2,1)S(1)}, u32[]{:S(2)}, u32[]{:S(2)}) %collective-permute-start.48) | collective-permute-done | bytes 614432 | tf_op jit(solution)/shard_map/ppermute | solution.py:638
  459.3 4.7 collective-permute-start.42
  464.0 3.0 collective-permute-done.49
  471.9 6.9 %collective-permute-done.38 = bf16[592,768]{1,0:T(8,128)(2,1)S(1)} collective-permute-done((bf16[592,768]{1,0:T(8,128)(2,1)S(1)}, bf16[592,768]{1,0:T(8,128)(2,1)S(1)}, u32[]{:S(2)}, u32[]{:S(2)}) %collective-permute-start.38) | collective-permute-done | bytes 909344 | tf_op jit(solution)/shard_map/ppermute | solution.py:638
  478.8 6.8 %collective-permute-done.42 = bf16[592,768]{1,0:T(8,128)(2,1)S(1)} collective-permute-done((bf16[592,768]{1,0:T(8,128)(2,1)S(1)}, bf16[592,768]{1,0:T(8,128)(2,1)S(1)}, u32[]{:S(2)}, u32[]{:S(2)}) %collective-permute-start.42) | collective-permute-done | bytes 909344 | tf_op jit(solution)/shard_map/ppermute | solution.py:638
  485.6 7.7 %collective-permute-done.44 = bf16[592,768]{1,0:T(8,128)(2,1)S(1)} collective-permute-done((bf16[592,768]{1,0:T(8,128)(2,1)S(1)}, bf16[592,768]{1,0:T(8,128)(2,1)S(1)}, u32[]{:S(2)}, u32[]{:S(2)}) %collective-permute-start.44) | collective-permute-done | bytes 909344 | tf_op jit(solution)/shard_map/ppermute | solution.py:638
  495.4 3.1 collective-permute-start.57
  501.5 4.6 finish.1
  (213 shorter events, 56.5 us)
Async XLA Ops:
  4.3 36.2 %collective-permute-start.2 = (bf16[976,768]{1,0:T(8,128)(2,1)}, bf16[976,768]{1,0:T(8,128)(2,1)}, u32[]{:S(2)}, u32[]{:S(2)}) collective-permute-start(bf16[976,768]{1,0:T(8,128)(2,1)} %get-tuple-element.100.rest_0_.rest_10_.rest_6_), channel_id=1, source_target_pairs={{0,2},{1,3},{2,0},{3,1},{4,6},{5,7},{6,4},{7,5},{8,10},{9,11},{10,... | collective-permute-start | bytes 4497416 | tf_op jit(solution)/shard_map/ppermute | solution.py:638
  7.4 33.9 %collective-permute-start = (bf16[976,768]{1,0:T(8,128)(2,1)}, bf16[976,768]{1,0:T(8,128)(2,1)S(1)}, u32[]{:S(2)}, u32[]{:S(2)}) collective-permute-start(bf16[976,768]{1,0:T(8,128)(2,1)} %get-tuple-element.100.rest_0_.rest_10_.rest_6_), channel_id=1, source_target_pairs={{2,4},{3,5},{4,2},{5,3},{10,12},{11,13},{12,10},{13,11},{18,20},{1... | collective-permute-start | bytes 4497416 | tf_op jit(solution)/shard_map/ppermute | solution.py:638
  8.1 34.7 %collective-permute-start.3 = (bf16[976,768]{1,0:T(8,128)(2,1)}, bf16[976,768]{1,0:T(8,128)(2,1)}, u32[]{:S(2)}, u32[]{:S(2)}) collective-permute-start(bf16[976,768]{1,0:T(8,128)(2,1)} %get-tuple-element.100.rest_0_.rest_10_.rest_6_), channel_id=1, source_target_pairs={{0,1},{1,0},{2,3},{3,2},{4,5},{5,4},{6,7},{7,6},{8,9},{9,8},{10,11... | collective-permute-start | bytes 4497416 | tf_op jit(solution)/shard_map/ppermute | solution.py:638
  40.5 11.9 %collective-permute-start.7 = (bf16[976,768]{1,0:T(8,128)(2,1)}, bf16[976,768]{1,0:T(8,128)(2,1)S(1)}, u32[]{:S(2)}, u32[]{:S(2)}) collective-permute-start(bf16[976,768]{1,0:T(8,128)(2,1)} %collective-permute-done.2.rest_1_.rest_11_.rest_7_), channel_id=1, source_target_pairs={{2,4},{3,5},{4,2},{5,3},{10,12},{11,13},{12,10},{13,11},{18,20},{1... | collective-permute-start | bytes 4497416 | tf_op jit(solution)/shard_map/ppermute | solution.py:638
  41.3 37.8 %collective-permute-start.1 = (bf16[976,768]{1,0:T(8,128)(2,1)S(1)}, bf16[976,768]{1,0:T(8,128)(2,1)}, u32[]{:S(2)}, u32[]{:S(2)}) collective-permute-start(bf16[976,768]{1,0:T(8,128)(2,1)S(1)} %collective-permute-done), channel_id=1, source_target_pairs={{2,0},{3,1},{4,6},{5,7},{10,8},{11,9},{12,14},{13,15},{18,16},{19,... | collective-permute-start | bytes 4497416 | tf_op jit(solution)/shard_map/ppermute | solution.py:638
  51.0 33.4 %collective-permute-start.9 = (bf16[976,768]{1,0:T(8,128)(2,1)}, bf16[976,768]{1,0:T(8,128)(2,1)}, u32[]{:S(2)}, u32[]{:S(2)}) collective-permute-start(bf16[976,768]{1,0:T(8,128)(2,1)} %collective-permute-done.2.rest_1_.rest_11_.rest_7_), channel_id=1, source_target_pairs={{0,1},{1,0},{2,3},{3,2},{4,5},{5,4},{6,7},{7,6},{8,9},{9,8},{10,11... | collective-permute-start | bytes 4497416 | tf_op jit(solution)/shard_map/ppermute | solution.py:638
  52.4 35.2 %collective-permute-start.15 = (bf16[976,768]{1,0:T(8,128)(2,1)}, bf16[976,768]{1,0:T(8,128)(2,1)}, u32[]{:S(2)}, u32[]{:S(2)}) collective-permute-start(bf16[976,768]{1,0:T(8,128)(2,1)} %get-tuple-element.100.rest_0_.rest_10_.rest_6_), channel_id=1, source_target_pairs={{0,8},{8,0},{16,24},{24,16},{1,9},{9,1},{17,25},{25,17},{2,10},{10... | collective-permute-start | bytes 4497416 | tf_op jit(solution)/shard_map/ppermute | solution.py:592
  52.4 60.7 %collective-permute-start.8 = (bf16[976,768]{1,0:T(8,128)(2,1)S(1)}, bf16[976,768]{1,0:T(8,128)(2,1)}, u32[]{:S(2)}, u32[]{:S(2)}) collective-permute-start(bf16[976,768]{1,0:T(8,128)(2,1)S(1)} %collective-permute-done.7), channel_id=1, source_target_pairs={{2,0},{3,1},{4,6},{5,7},{10,8},{11,9},{12,14},{13,15},{18,16},{19,... | collective-permute-start | bytes 4497416 | tf_op jit(solution)/shard_map/ppermute | solution.py:638
  84.4 35.6 %collective-permute-start.10 = (bf16[976,768]{1,0:T(8,128)(2,1)S(1)}, bf16[976,768]{1,0:T(8,128)(2,1)}, u32[]{:S(2)}, u32[]{:S(2)}) collective-permute-start(bf16[976,768]{1,0:T(8,128)(2,1)S(1)} %broadcast_select_fusion.1.rest_2_.rest_12_.rest_8_), channel_id=1, source_target_pairs={{0,1},{1,0},{2,3},{3,2},{4,5},{5,4},{6,7},{7,6},{8,9},{9,8},{10,11... | collective-permute-start | bytes 4497416 | tf_op jit(solution)/shard_map/ppermute | solution.py:638
  86.3 41.8 %collective-permute-start.16 = (bf16[976,768]{1,0:T(8,128)(2,1)}, bf16[976,768]{1,0:T(8,128)(2,1)}, u32[]{:S(2)}, u32[]{:S(2)}) collective-permute-start(bf16[976,768]{1,0:T(8,128)(2,1)} %collective-permute-done.2.rest_1_.rest_11_.rest_7_), channel_id=1, source_target_pairs={{0,8},{8,0},{16,24},{24,16},{1,9},{9,1},{17,25},{25,17},{2,10},{10... | collective-permute-start | bytes 4497416 | tf_op jit(solution)/shard_map/ppermute | solution.py:592
  86.3 41.9 %collective-permute-start.19 = (bf16[976,768]{1,0:T(8,128)(2,1)}, bf16[976,768]{1,0:T(8,128)(2,1)}, u32[]{:S(2)}, u32[]{:S(2)}) collective-permute-start(bf16[976,768]{1,0:T(8,128)(2,1)} %collective-permute-done.3.rest_4_.rest_14_.rest_10_), channel_id=1, source_target_pairs={{0,8},{8,0},{16,24},{24,16},{1,9},{9,1},{17,25},{25,17},{2,10},{10... | collective-permute-start | bytes 4497416 | tf_op jit(solution)/shard_map/ppermute | solution.py:592
  87.6 36.0 %collective-permute-start.5 = (bf16[384,768]{1,0:T(8,128)(2,1)}, bf16[384,768]{1,0:T(8,128)(2,1)}, u32[]{:S(2)}, u32[]{:S(2)}) collective-permute-start(bf16[384,768]{1,0:T(8,128)(2,1)} %constant_dynamic-update-slice_fusion.rest_8_.rest_18_.rest_14_), channel_id=1, source_target_pairs={{0,2},{1,3},{2,0},{3,1},{4,6},{5,7},{6,4},{7,5},{8,10},{9,11},{10,... | collective-permute-start | bytes 1769480 | tf_op jit(solution)/shard_map/ppermute | solution.py:638
  113.1 11.9 %collective-permute-start.6 = (bf16[384,768]{1,0:T(8,128)(2,1)}, bf16[384,768]{1,0:T(8,128)(2,1)S(1)}, u32[]{:S(2)}, u32[]{:S(2)}) collective-permute-start(bf16[384,768]{1,0:T(8,128)(2,1)} %constant_dynamic-update-slice_fusion.rest_8_.rest_18_.rest_14_), channel_id=1, source_target_pairs={{2,4},{3,5},{4,2},{5,3},{10,12},{11,13},{12,10},{13,11},{18,20},{1... | collective-permute-start | bytes 1769480 | tf_op jit(solution)/shard_map/ppermute | solution.py:638
  120.0 10.8 %collective-permute-start.17 = (bf16[976,768]{1,0:T(8,128)(2,1)S(1)}, bf16[976,768]{1,0:T(8,128)(2,1)S(1)}, u32[]{:S(2)}, u32[]{:S(2)}) collective-permute-start(bf16[976,768]{1,0:T(8,128)(2,1)S(1)} %broadcast_select_fusion.1.rest_2_.rest_12_.rest_8_), channel_id=1, source_target_pairs={{0,8},{8,0},{16,24},{24,16},{1,9},{9,1},{17,25},{25,17},{2,10},{10... | collective-permute-start | bytes 4497416 | tf_op jit(solution)/shard_map/ppermute | solution.py:592
  123.5 32.6 %collective-permute-start.11 = (bf16[976,768]{1,0:T(8,128)(2,1)S(1)}, bf16[976,768]{1,0:T(8,128)(2,1)S(1)}, u32[]{:S(2)}, u32[]{:S(2)}) collective-permute-start(bf16[976,768]{1,0:T(8,128)(2,1)S(1)} %broadcast_select_fusion.rest_3_.rest_13_.rest_9_), channel_id=1, source_target_pairs={{0,1},{1,0},{2,3},{3,2},{4,5},{5,4},{6,7},{7,6},{8,9},{9,8},{10,11... | collective-permute-start | bytes 4497416 | tf_op jit(solution)/shard_map/ppermute | solution.py:638
  128.1 31.4 %collective-permute-start.20 = (bf16[976,768]{1,0:T(8,128)(2,1)}, bf16[976,768]{1,0:T(8,128)(2,1)S(1)}, u32[]{:S(2)}, u32[]{:S(2)}) collective-permute-start(bf16[976,768]{1,0:T(8,128)(2,1)} %collective-permute-done.9.rest_5_.rest_15_.rest_11_), channel_id=1, source_target_pairs={{0,8},{8,0},{16,24},{24,16},{1,9},{9,1},{17,25},{25,17},{2,10},{10... | collective-permute-start | bytes 4497416 | tf_op jit(solution)/shard_map/ppermute | solution.py:592
  128.2 17.7 %collective-permute-start.12 = (bf16[384,768]{1,0:T(8,128)(2,1)S(1)}, bf16[384,768]{1,0:T(8,128)(2,1)S(1)}, u32[]{:S(2)}, u32[]{:S(2)}) collective-permute-start(bf16[384,768]{1,0:T(8,128)(2,1)S(1)} %collective-permute-done.6), channel_id=1, source_target_pairs={{2,0},{3,1},{4,6},{5,7},{10,8},{11,9},{12,14},{13,15},{18,16},{19,... | collective-permute-start | bytes 1769480 | tf_op jit(solution)/shard_map/ppermute | solution.py:638
  129.5 29.8 %collective-permute-start.14 = (bf16[384,768]{1,0:T(8,128)(2,1)S(1)}, bf16[384,768]{1,0:T(8,128)(2,1)S(1)}, u32[]{:S(2)}, u32[]{:S(2)}) collective-permute-start(bf16[384,768]{1,0:T(8,128)(2,1)S(1)} %collective-permute-done.13), channel_id=1, source_target_pairs={{2,0},{3,1},{4,6},{5,7},{10,8},{11,9},{12,14},{13,15},{18,16},{19,... | collective-permute-start | bytes 1769480 | tf_op jit(solution)/shard_map/ppermute | solution.py:638
  130.8 31.3 %collective-permute-start.18 = (bf16[976,768]{1,0:T(8,128)(2,1)S(1)}, bf16[976,768]{1,0:T(8,128)(2,1)S(1)}, u32[]{:S(2)}, u32[]{:S(2)}) collective-permute-start(bf16[976,768]{1,0:T(8,128)(2,1)S(1)} %broadcast_select_fusion.rest_3_.rest_13_.rest_9_), channel_id=1, source_target_pairs={{0,8},{8,0},{16,24},{24,16},{1,9},{9,1},{17,25},{25,17},{2,10},{10... | collective-permute-start | bytes 4497416 | tf_op jit(solution)/shard_map/ppermute | solution.py:592
  145.9 17.7 %collective-permute-start.21 = (bf16[976,768]{1,0:T(8,128)(2,1)}, bf16[976,768]{1,0:T(8,128)(2,1)S(1)}, u32[]{:S(2)}, u32[]{:S(2)}) collective-permute-start(bf16[976,768]{1,0:T(8,128)(2,1)} %collective-permute-done.10.rest_6_.rest_16_.rest_12_), channel_id=1, source_target_pairs={{0,8},{8,0},{16,24},{24,16},{1,9},{9,1},{17,25},{25,17},{2,10},{10... | collective-permute-start | bytes 4497416 | tf_op jit(solution)/shard_map/ppermute | solution.py:592
  188.6 13.4 %collective-permute-start.27 = (bf16[288,768]{1,0:T(8,128)(2,1)}, bf16[288,768]{1,0:T(8,128)(2,1)S(1)}, u32[]{:S(2)}, u32[]{:S(2)}) collective-permute-start(bf16[288,768]{1,0:T(8,128)(2,1)} %get-tuple-element.113), channel_id=1, source_target_pairs={{0,16},{8,24},{1,17},{9,25},{2,18},{10,26},{3,19},{11,27},{4,20},{... | collective-permute-start | bytes 1327112 | tf_op jit(solution)/shard_map/ppermute | solution.py:587
  263.0 13.5 %collective-permute-start.28 = (bf16[288,768]{1,0:T(8,128)(2,1)}, bf16[288,768]{1,0:T(8,128)(2,1)S(1)}, u32[]{:S(2)}, u32[]{:S(2)}) collective-permute-start(bf16[288,768]{1,0:T(8,128)(2,1)} %backward_layers.3), channel_id=1, source_target_pairs={{16,0},{24,8},{17,1},{25,9},{18,2},{26,10},{19,3},{27,11},{20,4},{... | collective-permute-start | bytes 1327112 | tf_op jit(solution)/shard_map/ppermute | solution.py:587
  264.3 53.3 %collective-permute-start.29 = (bf16[288,4608]{1,0:T(8,128)(2,1)}, bf16[288,4608]{1,0:T(8,128)(2,1)}, u32[]{:S(2)}, u32[]{:S(2)}) collective-permute-start(bf16[288,4608]{1,0:T(8,128)(2,1)} %get-tuple-element.129), channel_id=1, source_target_pairs={{0,8},{8,0},{16,24},{24,16},{1,9},{9,1},{17,25},{25,17},{2,10},{10... | collective-permute-start | bytes 7962632 | tf_op jit(solution)/shard_map/ppermute | solution.py:592
  264.4 68.0 %collective-permute-start.31 = (bf16[288,4608]{1,0:T(8,128)(2,1)S(1)}, bf16[288,4608]{1,0:T(8,128)(2,1)}, u32[]{:S(2)}, u32[]{:S(2)}) collective-permute-start(bf16[288,4608]{1,0:T(8,128)(2,1)S(1)} %copy-done.27), channel_id=1, source_target_pairs={{0,8},{8,0},{16,24},{24,16},{1,9},{9,1},{17,25},{25,17},{2,10},{10... | collective-permute-start | bytes 7962632 | tf_op jit(solution)/shard_map/ppermute | solution.py:592
  297.1 20.5 %collective-permute-start.30 = (bf16[288,4608]{1,0:T(8,128)(2,1)}, bf16[288,4608]{1,0:T(8,128)(2,1)}, u32[]{:S(2)}, u32[]{:S(2)}) collective-permute-start(bf16[288,4608]{1,0:T(8,128)(2,1)} %get-tuple-element.130), channel_id=1, source_target_pairs={{0,8},{8,0},{16,24},{24,16},{1,9},{9,1},{17,25},{25,17},{2,10},{10... | collective-permute-start | bytes 7962632 | tf_op jit(solution)/shard_map/ppermute | solution.py:592
  317.1 15.3 %collective-permute-start.32 = (bf16[288,4608]{1,0:T(8,128)(2,1)}, bf16[288,4608]{1,0:T(8,128)(2,1)}, u32[]{:S(2)}, u32[]{:S(2)}) collective-permute-start(bf16[288,4608]{1,0:T(8,128)(2,1)} %get-tuple-element.136), channel_id=1, source_target_pairs={{0,8},{8,0},{16,24},{24,16},{1,9},{9,1},{17,25},{25,17},{2,10},{10... | collective-permute-start | bytes 7962632 | tf_op jit(solution)/shard_map/ppermute | solution.py:592
  330.8 16.4 %collective-permute-start.45 = (bf16[400,768]{1,0:T(8,128)(2,1)}, bf16[400,768]{1,0:T(8,128)(2,1)S(1)}, u32[]{:S(2)}, u32[]{:S(2)}) collective-permute-start(bf16[400,768]{1,0:T(8,128)(2,1)} %get-tuple-element.164), channel_id=1, source_target_pairs={{0,1},{1,0},{2,3},{3,2},{4,5},{5,4},{6,7},{7,6},{8,9},{9,8},{10,11... | collective-permute-start | bytes 1843208 | tf_op jit(solution)/shard_map/ppermute | solution.py:638
  346.1 23.0 %collective-permute-start.33 = (bf16[592,768]{1,0:T(8,128)(2,1)S(1)}, bf16[592,768]{1,0:T(8,128)(2,1)S(1)}, u32[]{:S(2)}, u32[]{:S(2)}) collective-permute-start(bf16[592,768]{1,0:T(8,128)(2,1)S(1)} %copy-done.36), channel_id=1, source_target_pairs={{0,1},{1,0},{2,3},{3,2},{4,5},{5,4},{6,7},{7,6},{8,9},{9,8},{10,11... | collective-permute-start | bytes 2727944 | tf_op jit(solution)/shard_map/ppermute | solution.py:638
  347.5 37.6 %collective-permute-start.52 = (bf16[784,768]{1,0:T(8,128)(2,1)S(1)}, bf16[784,768]{1,0:T(8,128)(2,1)S(1)}, u32[]{:S(2)}, u32[]{:S(2)}) collective-permute-start(bf16[784,768]{1,0:T(8,128)(2,1)S(1)} %pad_maximum_fusion.2), channel_id=1, source_target_pairs={{0,2},{1,3},{6,4},{7,5},{8,10},{9,11},{14,12},{15,13},{16,18},{17,... | collective-permute-start | bytes 3612680 | tf_op jit(solution)/shard_map/ppermute | solution.py:638
  356.0 15.5 %collective-permute-start.37 = (bf16[2,280,192]{2,1,0:T(8,128)(2,1)S(1)}, bf16[2,280,192]{2,1,0:T(8,128)(2,1)S(1)}, u32[]{:S(2)}, u32[]{:S(2)}) collective-permute-start(bf16[2,280,192]{2,1,0:T(8,128)(2,1)S(1)} %fusion.1), channel_id=1, source_target_pairs={{0,8},{8,0},{16,24},{24,16},{1,9},{9,1},{17,25},{25,17},{2,10},{10... | collective-permute-start | bytes 645128 | tf_op jit(solution)/shard_map/ppermute | solution.py:592
  356.1 26.2 %collective-permute-start.46 = (bf16[400,768]{1,0:T(8,128)(2,1)S(1)}, bf16[400,768]{1,0:T(8,128)(2,1)S(1)}, u32[]{:S(2)}, u32[]{:S(2)}) collective-permute-start(bf16[400,768]{1,0:T(8,128)(2,1)S(1)} %copy-done.39), channel_id=1, source_target_pairs={{0,1},{1,0},{2,3},{3,2},{4,5},{5,4},{6,7},{7,6},{8,9},{9,8},{10,11... | collective-permute-start | bytes 1843208 | tf_op jit(solution)/shard_map/ppermute | solution.py:638
  369.4 26.4 %collective-permute-start.35 = (bf16[592,768]{1,0:T(8,128)(2,1)S(1)}, bf16[592,768]{1,0:T(8,128)(2,1)S(1)}, u32[]{:S(2)}, u32[]{:S(2)}) collective-permute-start(bf16[592,768]{1,0:T(8,128)(2,1)S(1)} %add_convert_fusion.10), channel_id=1, source_target_pairs={{0,2},{1,3},{6,4},{7,5},{8,10},{9,11},{14,12},{15,13},{16,18},{17,... | collective-permute-start | bytes 2727944 | tf_op jit(solution)/shard_map/ppermute | solution.py:638
  371.7 30.1 %collective-permute-start.34 = (bf16[592,768]{1,0:T(8,128)(2,1)S(1)}, bf16[592,768]{1,0:T(8,128)(2,1)S(1)}, u32[]{:S(2)}, u32[]{:S(2)}) collective-permute-start(bf16[592,768]{1,0:T(8,128)(2,1)S(1)} %copy-done.35), channel_id=1, source_target_pairs={{0,1},{1,0},{2,3},{3,2},{4,5},{5,4},{6,7},{7,6},{8,9},{9,8},{10,11... | collective-permute-start | bytes 2727944 | tf_op jit(solution)/shard_map/ppermute | solution.py:638
  382.3 32.6 %collective-permute-start.47 = (bf16[400,768]{1,0:T(8,128)(2,1)S(1)}, bf16[400,768]{1,0:T(8,128)(2,1)S(1)}, u32[]{:S(2)}, u32[]{:S(2)}) collective-permute-start(bf16[400,768]{1,0:T(8,128)(2,1)S(1)} %copy-done.38), channel_id=1, source_target_pairs={{0,1},{1,0},{2,3},{3,2},{4,5},{5,4},{6,7},{7,6},{8,9},{9,8},{10,11... | collective-permute-start | bytes 1843208 | tf_op jit(solution)/shard_map/ppermute | solution.py:638
  383.1 38.6 %collective-permute-start.50 = (bf16[784,768]{1,0:T(8,128)(2,1)S(1)}, bf16[784,768]{1,0:T(8,128)(2,1)S(1)}, u32[]{:S(2)}, u32[]{:S(2)}) collective-permute-start(bf16[784,768]{1,0:T(8,128)(2,1)S(1)} %pad_maximum_fusion.1), channel_id=1, source_target_pairs={{0,2},{1,3},{6,4},{7,5},{8,10},{9,11},{14,12},{15,13},{16,18},{17,... | collective-permute-start | bytes 3612680 | tf_op jit(solution)/shard_map/ppermute | solution.py:638
  385.5 41.0 %collective-permute-start.53 = (bf16[784,768]{1,0:T(8,128)(2,1)S(1)}, bf16[784,768]{1,0:T(8,128)(2,1)S(1)}, u32[]{:S(2)}, u32[]{:S(2)}) collective-permute-start(bf16[784,768]{1,0:T(8,128)(2,1)S(1)} %add_convert_fusion.2), channel_id=1, source_target_pairs={{2,4},{3,5},{4,2},{5,3},{10,12},{11,13},{12,10},{13,11},{18,20},{1... | collective-permute-start | bytes 3612680 | tf_op jit(solution)/shard_map/ppermute | solution.py:638
  402.0 39.1 %collective-permute-start.40 = (bf16[592,768]{1,0:T(8,128)(2,1)S(1)}, bf16[592,768]{1,0:T(8,128)(2,1)S(1)}, u32[]{:S(2)}, u32[]{:S(2)}) collective-permute-start(bf16[592,768]{1,0:T(8,128)(2,1)S(1)} %add_convert_fusion.9), channel_id=1, source_target_pairs={{0,2},{1,3},{6,4},{7,5},{8,10},{9,11},{14,12},{15,13},{16,18},{17,... | collective-permute-start | bytes 2727944 | tf_op jit(solution)/shard_map/ppermute | solution.py:638
  404.1 38.3 %collective-permute-start.39 = (bf16[592,768]{1,0:T(8,128)(2,1)S(1)}, bf16[592,768]{1,0:T(8,128)(2,1)S(1)}, u32[]{:S(2)}, u32[]{:S(2)}) collective-permute-start(bf16[592,768]{1,0:T(8,128)(2,1)S(1)} %copy-done.34), channel_id=1, source_target_pairs={{0,1},{1,0},{2,3},{3,2},{4,5},{5,4},{6,7},{7,6},{8,9},{9,8},{10,11... | collective-permute-start | bytes 2727944 | tf_op jit(solution)/shard_map/ppermute | solution.py:638
  414.9 29.3 %collective-permute-start.41 = (bf16[592,768]{1,0:T(8,128)(2,1)S(1)}, bf16[592,768]{1,0:T(8,128)(2,1)S(1)}, u32[]{:S(2)}, u32[]{:S(2)}) collective-permute-start(bf16[592,768]{1,0:T(8,128)(2,1)S(1)} %add_convert_fusion.8), channel_id=1, source_target_pairs={{2,4},{3,5},{4,2},{5,3},{10,12},{11,13},{12,10},{13,11},{18,20},{1... | collective-permute-start | bytes 2727944 | tf_op jit(solution)/shard_map/ppermute | solution.py:638
  421.7 45.3 %collective-permute-start.49 = (bf16[784,768]{1,0:T(8,128)(2,1)S(1)}, bf16[784,768]{1,0:T(8,128)(2,1)S(1)}, u32[]{:S(2)}, u32[]{:S(2)}) collective-permute-start(bf16[784,768]{1,0:T(8,128)(2,1)S(1)} %pad_maximum_fusion), channel_id=1, source_target_pairs={{0,2},{1,3},{6,4},{7,5},{8,10},{9,11},{14,12},{15,13},{16,18},{17,... | collective-permute-start | bytes 3612680 | tf_op jit(solution)/shard_map/ppermute | solution.py:638
  426.5 41.2 %collective-permute-start.51 = (bf16[784,768]{1,0:T(8,128)(2,1)S(1)}, bf16[784,768]{1,0:T(8,128)(2,1)S(1)}, u32[]{:S(2)}, u32[]{:S(2)}) collective-permute-start(bf16[784,768]{1,0:T(8,128)(2,1)S(1)} %add_convert_fusion.3), channel_id=1, source_target_pairs={{2,4},{3,5},{4,2},{5,3},{10,12},{11,13},{12,10},{13,11},{18,20},{1... | collective-permute-start | bytes 3612680 | tf_op jit(solution)/shard_map/ppermute | solution.py:638
  441.1 28.7 %collective-permute-start.54 = (bf16[784,768]{1,0:T(8,128)(2,1)S(1)}, bf16[784,768]{1,0:T(8,128)(2,1)S(1)}, u32[]{:S(2)}, u32[]{:S(2)}) collective-permute-start(bf16[784,768]{1,0:T(8,128)(2,1)S(1)} %add_convert_fusion.1), channel_id=1, source_target_pairs={{2,0},{3,1},{4,6},{5,7},{10,8},{11,9},{12,14},{13,15},{18,16},{19,... | collective-permute-start | bytes 3612680 | tf_op jit(solution)/shard_map/ppermute | solution.py:638
  442.5 16.9 %collective-permute-start.48 = (bf16[400,768]{1,0:T(8,128)(2,1)S(1)}, bf16[400,768]{1,0:T(8,128)(2,1)S(1)}, u32[]{:S(2)}, u32[]{:S(2)}) collective-permute-start(bf16[400,768]{1,0:T(8,128)(2,1)S(1)} %copy-done.37), channel_id=1, source_target_pairs={{0,1},{1,0},{2,3},{3,2},{4,5},{5,4},{6,7},{7,6},{8,9},{9,8},{10,11... | collective-permute-start | bytes 1843208 | tf_op jit(solution)/shard_map/ppermute | solution.py:638
  444.2 34.6 %collective-permute-start.38 = (bf16[592,768]{1,0:T(8,128)(2,1)S(1)}, bf16[592,768]{1,0:T(8,128)(2,1)S(1)}, u32[]{:S(2)}, u32[]{:S(2)}) collective-permute-start(bf16[592,768]{1,0:T(8,128)(2,1)S(1)} %copy-done.33), channel_id=1, source_target_pairs={{0,1},{1,0},{2,3},{3,2},{4,5},{5,4},{6,7},{7,6},{8,9},{9,8},{10,11... | collective-permute-start | bytes 2727944 | tf_op jit(solution)/shard_map/ppermute | solution.py:638
  459.3 26.2 %collective-permute-start.42 = (bf16[592,768]{1,0:T(8,128)(2,1)S(1)}, bf16[592,768]{1,0:T(8,128)(2,1)S(1)}, u32[]{:S(2)}, u32[]{:S(2)}) collective-permute-start(bf16[592,768]{1,0:T(8,128)(2,1)S(1)} %get-tuple-element.157), channel_id=1, source_target_pairs={{0,2},{1,3},{6,4},{7,5},{8,10},{9,11},{14,12},{15,13},{16,18},{17,... | collective-permute-start | bytes 2727944 | tf_op jit(solution)/shard_map/ppermute | solution.py:638
  466.9 18.6 %collective-permute-start.43 = (bf16[592,768]{1,0:T(8,128)(2,1)S(1)}, bf16[592,768]{1,0:T(8,128)(2,1)S(1)}, u32[]{:S(2)}, u32[]{:S(2)}) collective-permute-start(bf16[592,768]{1,0:T(8,128)(2,1)S(1)} %add_convert_fusion.6), channel_id=1, source_target_pairs={{2,4},{3,5},{4,2},{5,3},{10,12},{11,13},{12,10},{13,11},{18,20},{1... | collective-permute-start | bytes 2727944 | tf_op jit(solution)/shard_map/ppermute | solution.py:638
  467.7 25.6 %collective-permute-start.44 = (bf16[592,768]{1,0:T(8,128)(2,1)S(1)}, bf16[592,768]{1,0:T(8,128)(2,1)S(1)}, u32[]{:S(2)}, u32[]{:S(2)}) collective-permute-start(bf16[592,768]{1,0:T(8,128)(2,1)S(1)} %get-tuple-element.159), channel_id=1, source_target_pairs={{2,0},{3,1},{4,6},{5,7},{10,8},{11,9},{12,14},{13,15},{18,16},{19,... | collective-permute-start | bytes 2727944 | tf_op jit(solution)/shard_map/ppermute | solution.py:638
  470.6 24.6 %collective-permute-start.55 = (bf16[192,768]{1,0:T(8,128)(2,1)S(1)}, bf16[192,768]{1,0:T(8,128)(2,1)S(1)}, u32[]{:S(2)}, u32[]{:S(2)}) collective-permute-start(bf16[192,768]{1,0:T(8,128)(2,1)S(1)} %slice.32), channel_id=1, source_target_pairs={{0,1},{1,0},{2,3},{3,2},{4,5},{5,4},{6,7},{7,6},{8,9},{9,8},{10,11... | collective-permute-start | bytes 884744 | tf_op jit(solution)/shard_map/ppermute | solution.py:638
  (56 other events, 692.2 us)
